TPU v7x, 256 devices: a whole 4x4x8 slice. The times are simulated.
256 devices in a mesh: dp: 256 (over y, x, z, core).
Axes of the slice: x: 4, y: 4, z: 8, core: 2. Of those that a mesh axis runs over, the one named last changes fastest.
Arguments:
- telemetry_pooled_features: bfloat16 [32768, 1152], P('dp')
- picture_pooled_features: bfloat16 [32768, 1152], P('dp')
- telemetry_projection_weights: bfloat16 [1152, 1152], replicated, may hold values from -0.1875 to 0.1875
- picture_projection_weights: bfloat16 [1152, 1152], replicated, may hold values from -0.1875 to 0.1875
- positive_position: int32 [32768], P('dp'), may hold values from 0 to 127, as said below
- logarithmic_scale_param: float32 [1], replicated, may hold values from 0.7 to 1.5
- affinity_shift: float32 [1], replicated, may hold values from -3 to -1
Outputs:
- grad_w_text: bfloat16 [1152, 1152], replicated
- grad_w_image: bfloat16 [1152, 1152], replicated
Inputs may be any that keep to these rules, and one draw needn't show every extreme that they name: `positive_position`: most rows name themselves; some name another row of their block, so that an image may be the positive of several texts or of none. The first and last row of every block name themselves.
All inputs are finite; a program needn't handle non-finite values.
Results may differ from a plain program's by a relative error of at most 0.0063.
Values may be sent and summed in bfloat16 or wider, within the bound.
No kernel may reach another device: no remote copies, remote signals or barrier semaphores. Data moves between devices by JAX's collectives and lax.ppermute only.
A program may use at most 128 MiB of HBM per device.

v0:
```python
import jax
import jax.numpy as jnp
from jax import lax
from jax.sharding import PartitionSpec as P

HALF = 3


epsilon = 1e-06


def from_behind(block, axis, distance):
    devices = range(lax.axis_size(axis))
    route = [((i - distance) % len(devices), i) for i in devices]
    return lax.ppermute(block, axis, route)


def embed(features, weight):
    projected = jnp.dot(features, weight, preferred_element_type=jnp.float32)
    length = jnp.sqrt(jnp.sum(projected * projected, axis=-1, keepdims=True) + epsilon)
    return (projected / length, length)


def pull_back(gradient, unit_rows, length):
    radial = jnp.sum(gradient * unit_rows, axis=-1, keepdims=True)
    return ((gradient - unit_rows * radial) / length).astype(jnp.bfloat16)


def pair_factors(
    telemetry_vectors, picture_group_entries, affinity_scale, affinity_additive_term, match_targets
):
    similarity_array = lax.dot_general(
        telemetry_vectors,
        picture_group_entries,
        (((1,), (1,)), ((), ())),
        preferred_element_type=jnp.float32,
    )
    affinity_array = affinity_scale * similarity_array + affinity_additive_term
    return (jax.nn.sigmoid(affinity_array) - match_targets).astype(jnp.bfloat16)


def telemetry_tower_entries(match_coefficient, picture_group_entries, affinity_scale):
    return affinity_scale * jnp.dot(
        match_coefficient, picture_group_entries, preferred_element_type=jnp.float32
    )


def picture_tower_entries(match_coefficient, telemetry_vectors, affinity_scale):
    return affinity_scale * lax.dot_general(
        match_coefficient,
        telemetry_vectors,
        (((0,), (0,)), ((), ())),
        preferred_element_type=jnp.float32,
    )


def pair_gradient(
    telemetry_vectors, picture_group_entries, affinity_scale, affinity_additive_term, match_targets
):
    match_coefficient = pair_factors(
        telemetry_vectors,
        picture_group_entries,
        affinity_scale,
        affinity_additive_term,
        match_targets,
    )
    return (
        telemetry_tower_entries(match_coefficient, picture_group_entries, affinity_scale),
        picture_tower_entries(match_coefficient, telemetry_vectors, affinity_scale),
    )


def on_device(
    telemetry_pooled_features,
    picture_pooled_features,
    telemetry_projection_weights,
    picture_projection_weights,
    positive_position,
    logarithmic_scale_param,
    affinity_shift,
):
    row_count = telemetry_pooled_features.shape[0]
    text_unit, text_norm = embed(telemetry_pooled_features, telemetry_projection_weights)
    image_unit, image_norm = embed(picture_pooled_features, picture_projection_weights)
    telemetry_vectors = text_unit.astype(jnp.bfloat16)
    image_emb = image_unit.astype(jnp.bfloat16)
    affinity_scale = jnp.exp(logarithmic_scale_param[0])
    affinity_additive_term = affinity_shift[0]
    labels = (positive_position[:, None] == jnp.arange(row_count, dtype=jnp.int32)[None, :]).astype(
        jnp.float32
    )
    nothing = jnp.float32(0.0)
    empty = jnp.zeros(image_unit.shape, jnp.float32)
    current_group = from_behind(image_emb, "dp", -HALF)
    carried = empty
    telemetry_derivative = empty
    for block_step in range(2 * HALF + 1):
        match_targets = labels if block_step == HALF else nothing
        text_portion, picture_share = pair_gradient(
            telemetry_vectors, current_group, affinity_scale, affinity_additive_term, match_targets
        )
        telemetry_derivative = telemetry_derivative + text_portion
        carried = carried + picture_share
        if block_step < 2 * HALF:
            current_group = from_behind(current_group, "dp", 1)
            carried = from_behind(carried, "dp", 1)
    image_grad = from_behind(carried, "dp", -HALF)
    text_back = pull_back(telemetry_derivative, text_unit, text_norm)
    image_back = pull_back(image_grad, image_unit, image_norm)
    head_text = lax.dot_general(
        telemetry_pooled_features,
        text_back,
        (((0,), (0,)), ((), ())),
        preferred_element_type=jnp.float32,
    )
    head_image = lax.dot_general(
        picture_pooled_features,
        image_back,
        (((0,), (0,)), ((), ())),
        preferred_element_type=jnp.float32,
    )
    stacked = jnp.stack([head_text, head_image]).reshape(-1, 128)
    shares = lax.psum_scatter(stacked, "dp", scatter_dimension=0, tiled=True).astype(jnp.bfloat16)
    joined = lax.all_gather(shares, "dp", axis=0, tiled=True).reshape(
        2, telemetry_projection_weights.shape[0], telemetry_projection_weights.shape[1]
    )
    return (joined[0], joined[1])


def solution(mesh):
    return jax.shard_map(
        on_device,
        mesh=mesh,
        in_specs=(P("dp", None), P("dp", None), P(), P(), P("dp"), P(), P()),
        out_specs=(P(), P()),
        check_vma=False,
    )
```

profile of v0, /device:TPU:1, one launch (start us, length us, event | category | flops | bytes accessed | tf_op | source)
XLA Modules:
  0.0 1236.8 jit_solution(13223676128228621498)
XLA Ops:
  7.2 1.7 copy-done
  8.9 1.6 multiply_reduce_fusion.2
  10.7 11.7 collective-permute-start
  22.4 2.5 multiply_reduce_fusion.3
  26.4 5.6 collective-permute-done
  32.7 9.9 collective-permute-done.1
  42.6 2.5 collective-permute-start.2
  46.0 6.4 collective-permute-done.2
  52.9 2.2 collective-permute-done.8
  55.1 2.6 collective-permute-start.9
  57.9 6.0 collective-permute-done.3
  64.5 6.3 collective-permute-done.9
  71.2 4.3 collective-permute-done.4
  76.1 9.7 collective-permute-done.10
  86.1 2.2 collective-permute-done.5
  88.9 11.7 collective-permute-done.11
  101.0 2.2 collective-permute-done.6
  103.7 11.7 collective-permute-done.12
  118.5 9.8 collective-permute-done.13
  129.5 4.6 pad_maximum_fusion
  134.1 12.7 %copy.10 = f32[2,1152,1152]{2,1,0:T(8,128)} copy(f32[2,1152,1152]{1,2,0:T(8,128)} %pad_maximum_fusion) | data formatting | bytes 21233664 | tf_op jit(solution)/shard_map/stack | solution.py:122
  146.8 11.2 reshape.28
  158.1 726.4 %fusion = f32[96,128]{1,0:T(8,128)S(1)} fusion(f32[20736,128]{1,0:T(8,128)} %reshape.28), kind=kCustom, calls=%all-reduce-scatter | all-reduce-scatter fusion | flops 3145729 | bytes 10665984
  884.5 2.4 collective-permute-start.14
  886.8 13.3 %collective-permute-start.15 = (bf16[96,128]{1,0:T(8,128)(2,1)S(1)}, bf16[96,128]{1,0:T(8,128)(2,1)S(1)}, u32[]{:S(2)}, u32[]{:S(2)}) collective-permute-start(bf16[96,128]{1,0:T(8,128)(2,1)S(1)} %convert.78), channel_id=1, source_target_pairs={{0,2},{1,3},{2,4},{3,5},{4,6},{5,7},{6,8},{7,9},{8,10},{9,11},{10,... | collective-permute-start | bytes 73736
  900.1 13.1 %collective-permute-start.16 = (bf16[96,128]{1,0:T(8,128)(2,1)S(1)}, bf16[96,128]{1,0:T(8,128)(2,1)S(1)}, u32[]{:S(2)}, u32[]{:S(2)}) collective-permute-start(bf16[96,128]{1,0:T(8,128)(2,1)S(1)} %convert.78), channel_id=1, source_target_pairs={{0,3},{1,4},{2,5},{3,6},{4,7},{5,8},{6,9},{7,10},{8,11},{9,12},{10... | collective-permute-start | bytes 73736
  913.2 13.1 %collective-permute-start.17 = (bf16[96,128]{1,0:T(8,128)(2,1)S(1)}, bf16[96,128]{1,0:T(8,128)(2,1)S(1)}, u32[]{:S(2)}, u32[]{:S(2)}) collective-permute-start(bf16[96,128]{1,0:T(8,128)(2,1)S(1)} %convert.78), channel_id=1, source_target_pairs={{0,4},{1,5},{2,6},{3,7},{4,8},{5,9},{6,10},{7,11},{8,12},{9,13},{1... | collective-permute-start | bytes 73736
  926.4 10.6 collective-permute-start.53
  937.8 13.6 %collective-permute-start.18 = (bf16[96,128]{1,0:T(8,128)(2,1)S(1)}, bf16[96,128]{1,0:T(8,128)(2,1)S(1)}, u32[]{:S(2)}, u32[]{:S(2)}) collective-permute-start(bf16[96,128]{1,0:T(8,128)(2,1)S(1)} %convert.78), channel_id=1, source_target_pairs={{0,5},{1,6},{2,7},{3,8},{4,9},{5,10},{6,11},{7,12},{8,13},{9,14},{... | collective-permute-start | bytes 73736
  951.5 13.1 %collective-permute-start.19 = (bf16[96,128]{1,0:T(8,128)(2,1)S(1)}, bf16[96,128]{1,0:T(8,128)(2,1)S(1)}, u32[]{:S(2)}, u32[]{:S(2)}) collective-permute-start(bf16[96,128]{1,0:T(8,128)(2,1)S(1)} %convert.78), channel_id=1, source_target_pairs={{0,6},{1,7},{2,8},{3,9},{4,10},{5,11},{6,12},{7,13},{8,14},{9,15},... | collective-permute-start | bytes 73736
  964.6 13.1 %collective-permute-start.20 = (bf16[96,128]{1,0:T(8,128)(2,1)S(1)}, bf16[96,128]{1,0:T(8,128)(2,1)S(1)}, u32[]{:S(2)}, u32[]{:S(2)}) collective-permute-start(bf16[96,128]{1,0:T(8,128)(2,1)S(1)} %convert.78), channel_id=1, source_target_pairs={{0,7},{1,8},{2,9},{3,10},{4,11},{5,12},{6,13},{7,14},{8,15},{9,16}... | collective-permute-start | bytes 73736
  977.8 8.1 collective-permute-start.21
  985.9 2.8 collective-permute-start.22
  988.8 6.5 collective-permute-start.23
  995.3 4.1 collective-permute-start.24
  999.5 2.3 collective-permute-start.25
  1001.8 3.4 collective-permute-start.26
  1005.2 6.1 collective-permute-start.27
  1011.4 3.8 collective-permute-start.28
  1015.1 3.1 collective-permute-start.29
  1018.3 3.6 collective-permute-start.30
  1023.3 3.8 collective-permute-start.32
  1027.2 6.4 collective-permute-start.33
  1033.6 6.9 collective-permute-start.34
  1041.8 6.8 collective-permute-start.36
  1048.5 4.5 collective-permute-start.37
  1053.1 3.9 collective-permute-start.38
  1056.9 4.0 collective-permute-start.39
  1060.9 2.3 collective-permute-start.40
  1064.6 2.0 collective-permute-start.42
  1066.6 1.5 collective-permute-start.43
  1069.4 1.6 collective-permute-start.45
  1071.0 3.2 collective-permute-start.46
  1074.3 1.5 collective-permute-start.47
  1075.7 3.4 collective-permute-start.48
  1079.1 1.6 collective-permute-start.49
  1080.8 2.2 collective-permute-start.50
  1083.0 1.6 collective-permute-start.51
  1084.7 2.7 collective-permute-start.52
  1088.3 7.5 concatenate
  1096.5 115.9 %all-gather.3.cloned.1.call-done = bf16[256,81,128]{2,1,0:T(8,128)(2,1)} async-done(((bf16[1,81,128]{2,1,0:T(8,128)(2,1)}), bf16[256,81,128]{2,1,0:T(8,128)(2,1)}) %all-gather.3.cloned.1.call-update) | async-done | bytes 5308432 | tf_op jit(solution)/shard_map/all_gather | solution.py:124
  1212.4 6.1 fusion.53
  1218.5 5.8 squeeze.11
  1224.3 5.7 squeeze.12
  (103 shorter events, 17.8 us)
Async XLA Ops:
  7.2 1.8 copy-start
  7.2 1205.2 %all-gather.3.cloned.1.call-start = ((), (), s32[]{:S(2)}) async-start(), calls=%async_computation | async-start | bytes 5789696 | tf_op jit(solution)/shard_map/all_gather | solution.py:124
  10.7 21.3 %collective-permute-start = (bf16[128,1152]{1,0:T(8,128)(2,1)S(1)}, bf16[128,1152]{1,0:T(8,128)(2,1)S(1)}, u32[]{:S(2)}, u32[]{:S(2)}) collective-permute-start(bf16[128,1152]{1,0:T(8,128)(2,1)S(1)} %fusion.52), channel_id=1, source_target_pairs={{3,0},{4,1},{5,2},{6,3},{7,4},{8,5},{9,6},{10,7},{11,8},{12,9},{13... | collective-permute-start | bytes 884744 | tf_op jit(solution)/shard_map/ppermute | solution.py:15
  26.3 37.6 %copy-start.4 = (s32[128]{0:T(128)S(1)}, s32[128]{0:T(128)}, u32[]{:S(2)}) copy-start(s32[128]{0:T(128)} %param.11) | copy-start | bytes 1540
  32.5 12.8 %collective-permute-start.7 = (f32[128,1152]{1,0:T(8,128)S(1)}, f32[128,1152]{1,0:T(8,128)S(1)}, u32[]{:S(2)}, u32[]{:S(2)}) collective-permute-start(f32[128,1152]{1,0:T(8,128)S(1)} %convolution_multiply_fusion.6), channel_id=1, source_target_pairs={{255,0},{0,1},{1,2},{2,3},{3,4},{4,5},{5,6},{6,7},{7,8},{8,9},{9,1... | collective-permute-start | bytes 1769480 | tf_op jit(solution)/shard_map/ppermute | solution.py:15
  32.6 10.0 collective-permute-start.1
  42.6 9.8 collective-permute-start.2
  45.6 9.4 collective-permute-start.8
  52.4 11.6 collective-permute-start.3
  55.1 15.7 %collective-permute-start.9 = (f32[128,1152]{1,0:T(8,128)S(1)}, f32[128,1152]{1,0:T(8,128)S(1)}, u32[]{:S(2)}, u32[]{:S(2)}) collective-permute-start(f32[128,1152]{1,0:T(8,128)S(1)} %add.129), channel_id=1, source_target_pairs={{255,0},{0,1},{1,2},{2,3},{3,4},{4,5},{5,6},{6,7},{7,8},{8,9},{9,1... | collective-permute-start | bytes 1769480 | tf_op jit(solution)/shard_map/ppermute | solution.py:15
  63.9 11.6 collective-permute-start.4
  70.9 14.8 %collective-permute-start.10 = (f32[128,1152]{1,0:T(8,128)S(1)}, f32[128,1152]{1,0:T(8,128)S(1)}, u32[]{:S(2)}, u32[]{:S(2)}) collective-permute-start(f32[128,1152]{1,0:T(8,128)S(1)} %add.130), channel_id=1, source_target_pairs={{255,0},{0,1},{1,2},{2,3},{3,4},{4,5},{5,6},{6,7},{7,8},{8,9},{9,1... | collective-permute-start | bytes 1769480 | tf_op jit(solution)/shard_map/ppermute | solution.py:15
  75.5 12.8 %collective-permute-start.5 = (bf16[128,1152]{1,0:T(8,128)(2,1)S(1)}, bf16[128,1152]{1,0:T(8,128)(2,1)S(1)}, u32[]{:S(2)}, u32[]{:S(2)}) collective-permute-start(bf16[128,1152]{1,0:T(8,128)(2,1)S(1)} %collective-permute-done.4), channel_id=1, source_target_pairs={{255,0},{0,1},{1,2},{2,3},{3,4},{4,5},{5,6},{6,7},{7,8},{8,9},{9,1... | collective-permute-start | bytes 884744 | tf_op jit(solution)/shard_map/ppermute | solution.py:15
  85.8 14.8 %collective-permute-start.11 = (f32[128,1152]{1,0:T(8,128)S(1)}, f32[128,1152]{1,0:T(8,128)S(1)}, u32[]{:S(2)}, u32[]{:S(2)}) collective-permute-start(f32[128,1152]{1,0:T(8,128)S(1)} %add.131), channel_id=1, source_target_pairs={{255,0},{0,1},{1,2},{2,3},{3,4},{4,5},{5,6},{6,7},{7,8},{8,9},{9,1... | collective-permute-start | bytes 1769480 | tf_op jit(solution)/shard_map/ppermute | solution.py:15
  88.3 14.9 %collective-permute-start.6 = (bf16[128,1152]{1,0:T(8,128)(2,1)S(1)}, bf16[128,1152]{1,0:T(8,128)(2,1)S(1)}, u32[]{:S(2)}, u32[]{:S(2)}) collective-permute-start(bf16[128,1152]{1,0:T(8,128)(2,1)S(1)} %collective-permute-done.5), channel_id=1, source_target_pairs={{255,0},{0,1},{1,2},{2,3},{3,4},{4,5},{5,6},{6,7},{7,8},{8,9},{9,1... | collective-permute-start | bytes 884744 | tf_op jit(solution)/shard_map/ppermute | solution.py:15
  88.8 28.7 %copy-start.2 = (bf16[128,1152]{1,0:T(8,128)(2,1)S(1)}, bf16[128,1152]{1,0:T(8,128)(2,1)}, u32[]{:S(2)}) copy-start(bf16[128,1152]{1,0:T(8,128)(2,1)} %param.7) | copy-start | bytes 884740
  100.7 14.8 %collective-permute-start.12 = (f32[128,1152]{1,0:T(8,128)S(1)}, f32[128,1152]{1,0:T(8,128)S(1)}, u32[]{:S(2)}, u32[]{:S(2)}) collective-permute-start(f32[128,1152]{1,0:T(8,128)S(1)} %add.132), channel_id=1, source_target_pairs={{255,0},{0,1},{1,2},{2,3},{3,4},{4,5},{5,6},{6,7},{7,8},{8,9},{9,1... | collective-permute-start | bytes 1769480 | tf_op jit(solution)/shard_map/ppermute | solution.py:15
  115.5 12.8 %collective-permute-start.13 = (f32[128,1152]{1,0:T(8,128)S(1)}, f32[128,1152]{1,0:T(8,128)S(1)}, u32[]{:S(2)}, u32[]{:S(2)}) collective-permute-start(f32[128,1152]{1,0:T(8,128)S(1)} %add.133), channel_id=1, source_target_pairs={{3,0},{4,1},{5,2},{6,3},{7,4},{8,5},{9,6},{10,7},{11,8},{12,9},{13... | collective-permute-start | bytes 1769480 | tf_op jit(solution)/shard_map/ppermute | solution.py:15
  117.1 11.4 copy-start.3
  884.5 67.0 %collective-permute-start.14 = (bf16[96,128]{1,0:T(8,128)(2,1)S(1)}, bf16[96,128]{1,0:T(8,128)(2,1)S(1)}, u32[]{:S(2)}, u32[]{:S(2)}) collective-permute-start(bf16[96,128]{1,0:T(8,128)(2,1)S(1)} %convert.78), channel_id=1, source_target_pairs={{0,1},{1,2},{2,3},{3,4},{4,5},{5,6},{6,7},{7,8},{8,9},{9,10},{10,1... | collective-permute-start | bytes 73736
  886.8 77.8 %collective-permute-start.15 = (bf16[96,128]{1,0:T(8,128)(2,1)S(1)}, bf16[96,128]{1,0:T(8,128)(2,1)S(1)}, u32[]{:S(2)}, u32[]{:S(2)}) collective-permute-start(bf16[96,128]{1,0:T(8,128)(2,1)S(1)} %convert.78), channel_id=1, source_target_pairs={{0,2},{1,3},{2,4},{3,5},{4,6},{5,7},{6,8},{7,9},{8,10},{9,11},{10,... | collective-permute-start | bytes 73736
  900.1 77.7 %collective-permute-start.16 = (bf16[96,128]{1,0:T(8,128)(2,1)S(1)}, bf16[96,128]{1,0:T(8,128)(2,1)S(1)}, u32[]{:S(2)}, u32[]{:S(2)}) collective-permute-start(bf16[96,128]{1,0:T(8,128)(2,1)S(1)} %convert.78), channel_id=1, source_target_pairs={{0,3},{1,4},{2,5},{3,6},{4,7},{5,8},{6,9},{7,10},{8,11},{9,12},{10... | collective-permute-start | bytes 73736
  913.2 72.7 %collective-permute-start.17 = (bf16[96,128]{1,0:T(8,128)(2,1)S(1)}, bf16[96,128]{1,0:T(8,128)(2,1)S(1)}, u32[]{:S(2)}, u32[]{:S(2)}) collective-permute-start(bf16[96,128]{1,0:T(8,128)(2,1)S(1)} %convert.78), channel_id=1, source_target_pairs={{0,4},{1,5},{2,6},{3,7},{4,8},{5,9},{6,10},{7,11},{8,12},{9,13},{1... | collective-permute-start | bytes 73736
  926.4 11.5 collective-permute-start.53
  937.8 50.9 %collective-permute-start.18 = (bf16[96,128]{1,0:T(8,128)(2,1)S(1)}, bf16[96,128]{1,0:T(8,128)(2,1)S(1)}, u32[]{:S(2)}, u32[]{:S(2)}) collective-permute-start(bf16[96,128]{1,0:T(8,128)(2,1)S(1)} %convert.78), channel_id=1, source_target_pairs={{0,5},{1,6},{2,7},{3,8},{4,9},{5,10},{6,11},{7,12},{8,13},{9,14},{... | collective-permute-start | bytes 73736
  951.5 43.8 %collective-permute-start.19 = (bf16[96,128]{1,0:T(8,128)(2,1)S(1)}, bf16[96,128]{1,0:T(8,128)(2,1)S(1)}, u32[]{:S(2)}, u32[]{:S(2)}) collective-permute-start(bf16[96,128]{1,0:T(8,128)(2,1)S(1)} %convert.78), channel_id=1, source_target_pairs={{0,6},{1,7},{2,8},{3,9},{4,10},{5,11},{6,12},{7,13},{8,14},{9,15},... | collective-permute-start | bytes 73736
  964.6 34.8 %collective-permute-start.20 = (bf16[96,128]{1,0:T(8,128)(2,1)S(1)}, bf16[96,128]{1,0:T(8,128)(2,1)S(1)}, u32[]{:S(2)}, u32[]{:S(2)}) collective-permute-start(bf16[96,128]{1,0:T(8,128)(2,1)S(1)} %convert.78), channel_id=1, source_target_pairs={{0,7},{1,8},{2,9},{3,10},{4,11},{5,12},{6,13},{7,14},{8,15},{9,16}... | collective-permute-start | bytes 73736
  977.8 24.0 %collective-permute-start.21 = (bf16[96,128]{1,0:T(8,128)(2,1)S(1)}, bf16[96,128]{1,0:T(8,128)(2,1)S(1)}, u32[]{:S(2)}, u32[]{:S(2)}) collective-permute-start(bf16[96,128]{1,0:T(8,128)(2,1)S(1)} %convert.78), channel_id=1, source_target_pairs={{0,8},{1,9},{2,10},{3,11},{4,12},{5,13},{6,14},{7,15},{8,16},{9,17... | collective-permute-start | bytes 73736
  985.9 19.3 %collective-permute-start.22 = (bf16[96,128]{1,0:T(8,128)(2,1)S(1)}, bf16[96,128]{1,0:T(8,128)(2,1)S(1)}, u32[]{:S(2)}, u32[]{:S(2)}) collective-permute-start(bf16[96,128]{1,0:T(8,128)(2,1)S(1)} %convert.78), channel_id=1, source_target_pairs={{0,9},{1,10},{2,11},{3,12},{4,13},{5,14},{6,15},{7,16},{8,17},{9,1... | collective-permute-start | bytes 73736
  988.8 22.6 %collective-permute-start.23 = (bf16[96,128]{1,0:T(8,128)(2,1)S(1)}, bf16[96,128]{1,0:T(8,128)(2,1)S(1)}, u32[]{:S(2)}, u32[]{:S(2)}) collective-permute-start(bf16[96,128]{1,0:T(8,128)(2,1)S(1)} %convert.78), channel_id=1, source_target_pairs={{0,10},{1,11},{2,12},{3,13},{4,14},{5,15},{6,16},{7,17},{8,18},{9,... | collective-permute-start | bytes 73736
  995.3 19.8 %collective-permute-start.24 = (bf16[96,128]{1,0:T(8,128)(2,1)S(1)}, bf16[96,128]{1,0:T(8,128)(2,1)S(1)}, u32[]{:S(2)}, u32[]{:S(2)}) collective-permute-start(bf16[96,128]{1,0:T(8,128)(2,1)S(1)} %convert.78), channel_id=1, source_target_pairs={{0,11},{1,12},{2,13},{3,14},{4,15},{5,16},{6,17},{7,18},{8,19},{9,... | collective-permute-start | bytes 73736
  999.5 18.8 %collective-permute-start.25 = (bf16[96,128]{1,0:T(8,128)(2,1)S(1)}, bf16[96,128]{1,0:T(8,128)(2,1)S(1)}, u32[]{:S(2)}, u32[]{:S(2)}) collective-permute-start(bf16[96,128]{1,0:T(8,128)(2,1)S(1)} %convert.78), channel_id=1, source_target_pairs={{0,12},{1,13},{2,14},{3,15},{4,16},{5,17},{6,18},{7,19},{8,20},{9,... | collective-permute-start | bytes 73736
  1001.8 20.1 %collective-permute-start.26 = (bf16[96,128]{1,0:T(8,128)(2,1)S(1)}, bf16[96,128]{1,0:T(8,128)(2,1)S(1)}, u32[]{:S(2)}, u32[]{:S(2)}) collective-permute-start(bf16[96,128]{1,0:T(8,128)(2,1)S(1)} %convert.78), channel_id=1, source_target_pairs={{0,13},{1,14},{2,15},{3,16},{4,17},{5,18},{6,19},{7,20},{8,21},{9,... | collective-permute-start | bytes 73736
  1005.2 18.1 %collective-permute-start.27 = (bf16[96,128]{1,0:T(8,128)(2,1)S(1)}, bf16[96,128]{1,0:T(8,128)(2,1)S(1)}, u32[]{:S(2)}, u32[]{:S(2)}) collective-permute-start(bf16[96,128]{1,0:T(8,128)(2,1)S(1)} %convert.78), channel_id=1, source_target_pairs={{0,14},{1,15},{2,16},{3,17},{4,18},{5,19},{6,20},{7,21},{8,22},{9,... | collective-permute-start | bytes 73736
  1011.4 15.8 %collective-permute-start.28 = (bf16[96,128]{1,0:T(8,128)(2,1)S(1)}, bf16[96,128]{1,0:T(8,128)(2,1)S(1)}, u32[]{:S(2)}, u32[]{:S(2)}) collective-permute-start(bf16[96,128]{1,0:T(8,128)(2,1)S(1)} %convert.78), channel_id=1, source_target_pairs={{0,15},{1,16},{2,17},{3,18},{4,19},{5,20},{6,21},{7,22},{8,23},{9,... | collective-permute-start | bytes 73736
  1015.1 18.4 %collective-permute-start.29 = (bf16[96,128]{1,0:T(8,128)(2,1)S(1)}, bf16[96,128]{1,0:T(8,128)(2,1)S(1)}, u32[]{:S(2)}, u32[]{:S(2)}) collective-permute-start(bf16[96,128]{1,0:T(8,128)(2,1)S(1)} %convert.78), channel_id=1, source_target_pairs={{0,16},{1,17},{2,18},{3,19},{4,20},{5,21},{6,22},{7,23},{8,24},{9,... | collective-permute-start | bytes 73736
  1018.3 22.2 %collective-permute-start.30 = (bf16[96,128]{1,0:T(8,128)(2,1)S(1)}, bf16[96,128]{1,0:T(8,128)(2,1)S(1)}, u32[]{:S(2)}, u32[]{:S(2)}) collective-permute-start(bf16[96,128]{1,0:T(8,128)(2,1)S(1)} %convert.78), channel_id=1, source_target_pairs={{0,17},{1,18},{2,19},{3,20},{4,21},{5,22},{6,23},{7,24},{8,25},{9,... | collective-permute-start | bytes 73736
  1021.9 19.9 %collective-permute-start.31 = (bf16[96,128]{1,0:T(8,128)(2,1)S(1)}, bf16[96,128]{1,0:T(8,128)(2,1)S(1)}, u32[]{:S(2)}, u32[]{:S(2)}) collective-permute-start(bf16[96,128]{1,0:T(8,128)(2,1)S(1)} %convert.78), channel_id=1, source_target_pairs={{0,18},{1,19},{2,20},{3,21},{4,22},{5,23},{6,24},{7,25},{8,26},{9,... | collective-permute-start | bytes 73736
  1023.3 25.2 %collective-permute-start.32 = (bf16[96,128]{1,0:T(8,128)(2,1)S(1)}, bf16[96,128]{1,0:T(8,128)(2,1)S(1)}, u32[]{:S(2)}, u32[]{:S(2)}) collective-permute-start(bf16[96,128]{1,0:T(8,128)(2,1)S(1)} %convert.78), channel_id=1, source_target_pairs={{0,19},{1,20},{2,21},{3,22},{4,23},{5,24},{6,25},{7,26},{8,27},{9,... | collective-permute-start | bytes 73736
  1027.2 25.9 %collective-permute-start.33 = (bf16[96,128]{1,0:T(8,128)(2,1)S(1)}, bf16[96,128]{1,0:T(8,128)(2,1)S(1)}, u32[]{:S(2)}, u32[]{:S(2)}) collective-permute-start(bf16[96,128]{1,0:T(8,128)(2,1)S(1)} %convert.78), channel_id=1, source_target_pairs={{0,20},{1,21},{2,22},{3,23},{4,24},{5,25},{6,26},{7,27},{8,28},{9,... | collective-permute-start | bytes 73736
  1033.6 23.4 %collective-permute-start.34 = (bf16[96,128]{1,0:T(8,128)(2,1)S(1)}, bf16[96,128]{1,0:T(8,128)(2,1)S(1)}, u32[]{:S(2)}, u32[]{:S(2)}) collective-permute-start(bf16[96,128]{1,0:T(8,128)(2,1)S(1)} %convert.78), channel_id=1, source_target_pairs={{0,21},{1,22},{2,23},{3,24},{4,25},{5,26},{6,27},{7,28},{8,29},{9,... | collective-permute-start | bytes 73736
  1040.4 20.5 %collective-permute-start.35 = (bf16[96,128]{1,0:T(8,128)(2,1)S(1)}, bf16[96,128]{1,0:T(8,128)(2,1)S(1)}, u32[]{:S(2)}, u32[]{:S(2)}) collective-permute-start(bf16[96,128]{1,0:T(8,128)(2,1)S(1)} %convert.78), channel_id=1, source_target_pairs={{0,22},{1,23},{2,24},{3,25},{4,26},{5,27},{6,28},{7,29},{8,30},{9,... | collective-permute-start | bytes 73736
  1041.8 21.5 %collective-permute-start.36 = (bf16[96,128]{1,0:T(8,128)(2,1)S(1)}, bf16[96,128]{1,0:T(8,128)(2,1)S(1)}, u32[]{:S(2)}, u32[]{:S(2)}) collective-permute-start(bf16[96,128]{1,0:T(8,128)(2,1)S(1)} %convert.78), channel_id=1, source_target_pairs={{0,23},{1,24},{2,25},{3,26},{4,27},{5,28},{6,29},{7,30},{8,31},{9,... | collective-permute-start | bytes 73736
  1048.5 16.1 %collective-permute-start.37 = (bf16[96,128]{1,0:T(8,128)(2,1)S(1)}, bf16[96,128]{1,0:T(8,128)(2,1)S(1)}, u32[]{:S(2)}, u32[]{:S(2)}) collective-permute-start(bf16[96,128]{1,0:T(8,128)(2,1)S(1)} %convert.78), channel_id=1, source_target_pairs={{0,24},{1,25},{2,26},{3,27},{4,28},{5,29},{6,30},{7,31},{8,32},{9,... | collective-permute-start | bytes 73736
  1053.1 13.5 %collective-permute-start.38 = (bf16[96,128]{1,0:T(8,128)(2,1)S(1)}, bf16[96,128]{1,0:T(8,128)(2,1)S(1)}, u32[]{:S(2)}, u32[]{:S(2)}) collective-permute-start(bf16[96,128]{1,0:T(8,128)(2,1)S(1)} %convert.78), channel_id=1, source_target_pairs={{0,25},{1,26},{2,27},{3,28},{4,29},{5,30},{6,31},{7,32},{8,33},{9,... | collective-permute-start | bytes 73736
  1056.9 11.1 collective-permute-start.39
  1060.9 8.4 collective-permute-start.40
  1063.3 7.7 collective-permute-start.41
  1064.6 9.7 collective-permute-start.42
  1066.6 9.2 collective-permute-start.43
  1068.1 11.1 collective-permute-start.44
  1069.4 11.4 collective-permute-start.45
  1071.0 12.0 collective-permute-start.46
  1074.3 10.4 collective-permute-start.47
  1075.7 11.6 collective-permute-start.48
  1079.1 8.3 collective-permute-start.49
  1080.8 6.6 collective-permute-start.50
  1083.0 4.4 collective-permute-start.51
  1084.7 3.6 collective-permute-start.52
  1218.5 11.5 copy-start.1
Sparse Core Ops, SparseCore 0:
  1096.6 115.7 all-gather.2
where the time goes:
time: 1240 us
  blocking collectives  726 us (59%)
  starting transfers between devices  220 us (18%)
  waiting for transfers between devices  206 us (17%)
  local copies, waits for them, and re-layouts  51.5 us (4%)
  between operations  16.4 us (1%)
    unnamed x1, blocking collectives  726 us
    unnamed x40, starting transfers between devices  201 us
    all_gather x1, waiting for transfers between devices, on_device(): lax.all_gather(shares, 'dp', axis=0, tiled=True)  116 us
    ppermute x14, waiting for transfers between devices, from_behind(): return lax.ppermute(block, axis, route)  88.1 us
  transfers between devices with their start and end apart: 55, of which 16 were waited for; matrix products, arithmetic and copies ran while one was open for 1% of the time, Pallas kernels for 0%

commit v1 on v0

v1 whole, which is shorter than its diff:
```python
import jax
import jax.numpy as jnp
from jax import lax
from jax.sharding import PartitionSpec as P

NY, NX, NZ = 4, 4, 8
N = 2 * NX * NY * NZ
epsilon = 1e-06
bf16, f32 = jnp.bfloat16, jnp.float32


def index(y, x, z, c):
    return ((y * NX + x) * NZ + z) * 2 + c


PLANES = [
    [index(y, x, z, c) for y in range(NY) for x in range(NX)] for z in range(NZ) for c in range(2)
]
LINES = [
    [index(y, x, z, c) for z in range(NZ)]
    for y in range(NY)
    for x in range(NX)
    for c in range(2)
]
SWAP = [(i, i ^ 1) for i in range(N)]


def shifted(distance):
    return [(i, (i + distance) % N) for i in range(N)]


def embed(features, weight):
    projected = jnp.dot(features, weight, preferred_element_type=f32)
    length = jnp.sqrt(jnp.sum(projected * projected, axis=-1, keepdims=True) + epsilon)
    return projected / length, length


def pull_back(gradient, unit_rows, length):
    radial = jnp.sum(gradient * unit_rows, axis=-1, keepdims=True)
    return ((gradient - unit_rows * radial) / length).astype(bf16)


def contract(a, b, da, db):
    return lax.dot_general(a, b, (((da,), (db,)), ((), ())), preferred_element_type=f32)


def exchange(parts, groups):
    return lax.all_to_all(parts, "dp", 0, 0, axis_index_groups=groups, tiled=True)


def to_tiles(matrix):
    rows, columns = matrix.shape
    return (
        matrix.reshape(rows // 8, 8, columns // 128, 128)
        .transpose(0, 2, 1, 3)
        .reshape(-1, 8, 128)
    )


def from_tiles(tiles, rows, columns):
    return (
        tiles.reshape(rows // 8, columns // 128, 8, 128)
        .transpose(0, 2, 1, 3)
        .reshape(rows, columns)
    )


def on_device(text_x, image_x, text_w, image_w, position, log_scale, shift):
    rows = text_x.shape[0]
    depth, width = text_w.shape
    core = lax.rem(lax.axis_index("dp"), 2)
    scale = jnp.exp(log_scale[0])
    bias = shift[0]
    with jax.named_scope("band_exchange"):
        below = lax.ppermute(text_x, "dp", shifted(2))
        above = lax.ppermute(text_x, "dp", shifted(-2))
        far = lax.ppermute(
            text_x, "dp", [(i, (i + 3) % N if i % 2 else (i - 3) % N) for i in range(N)]
        )
        partner = lax.ppermute(text_x, "dp", SWAP)
        below_partner = lax.ppermute(below, "dp", SWAP)
        above_partner = lax.ppermute(above, "dp", SWAP)
    image_unit, image_norm = embed(image_x, image_w)
    image_emb = image_unit.astype(bf16)
    labels = (position[:, None] == jnp.arange(rows, dtype=jnp.int32)[None, :]).astype(f32)

    def visit(block, targets):
        unit, norm = embed(block, text_w)
        emb = unit.astype(bf16)
        logits = scale * contract(emb, image_emb, 1, 1) + bias
        sigmoid = jax.nn.sigmoid(logits)
        coefficient = (sigmoid - targets).astype(bf16)
        text_grad = scale * jnp.dot(coefficient, image_emb, preferred_element_type=f32)
        return pull_back(text_grad, unit, norm), scale * contract(coefficient, emb, 0, 0)

    with jax.named_scope("near_blocks"):
        near = jnp.concatenate([text_x, partner])
        targets = jnp.concatenate([labels, jnp.zeros_like(labels)])
        near_back, image_grad = visit(near, targets)
    with jax.named_scope("far_blocks"):
        others = jnp.concatenate([below, above, far, below_partner, above_partner])
        others_back, image_share = visit(others, 0.0)
        image_grad = image_grad + image_share
    image_back = pull_back(image_grad, image_unit, image_norm)
    with jax.named_scope("heads"):
        head_text = contract(
            jnp.concatenate([near, others]), jnp.concatenate([near_back, others_back]), 0, 0
        )
        head_image = contract(image_x, image_back, 0, 0)
        mine = jnp.where(core == 0, head_text, head_image)
        theirs = jnp.where(core == 0, head_image, head_text).astype(bf16)
        total = mine + lax.ppermute(theirs, "dp", SWAP).astype(f32)
    with jax.named_scope("sum_planes"):
        tiles = to_tiles(total.astype(bf16))
        slices = exchange(tiles, PLANES).reshape(NX * NY, -1, 8, 128)
        part = jnp.sum(slices.astype(f32), axis=0).astype(bf16)
    count = part.shape[0]
    each = -(-count // NZ)
    with jax.named_scope("sum_lines"):
        part = jnp.concatenate([part, jnp.zeros((each * NZ - count, 8, 128), bf16)])
        part = exchange(part, LINES).reshape(NZ, each, 8, 128)
        part = jnp.sum(part.astype(f32), axis=0).astype(bf16)
    with jax.named_scope("share_lines"):
        part = exchange(jnp.tile(part, (NZ, 1, 1)), LINES)[:count]
    with jax.named_scope("share_planes"):
        whole = exchange(jnp.tile(part, (NX * NY, 1, 1)), PLANES)
        mine = from_tiles(whole, depth, width)
    with jax.named_scope("finish"):
        theirs = lax.ppermute(mine, "dp", SWAP)
        return jnp.where(core == 0, mine, theirs), jnp.where(core == 0, theirs, mine)


def solution(mesh):
    return jax.shard_map(
        on_device,
        mesh=mesh,
        in_specs=(P("dp", None), P("dp", None), P(), P(), P("dp"), P(), P()),
        out_specs=(P(), P()),
        check_vma=False,
    )
```

time: 1240 us -> 158 us (0.13)
  blocking collectives: 726 us -> 96.2 us
  starting transfers between devices: 220 us -> 22.3 us
  waiting for transfers between devices: 206 us -> 9.54 us
  local copies, waits for them, and re-layouts: 51.5 us -> 6.12 us
  between operations: 16.4 us -> 2.25 us
    unnamed x1 -> x0, blocking collectives: 726 us -> none
    unnamed x40 -> x0, starting transfers between devices: 201 us -> none
    all_gather x1 -> x0, waiting for transfers between devices: 116 us -> none  [on_device(): lax.all_gather(shares, 'dp', axis=0, tiled=True)]
    all_to_all x0 -> x4, blocking collectives: none -> 96.2 us  [exchange(): lax.all_to_all(parts, 'dp', 0, 0, axis_index_groups=groups, tiled=True)]
    ppermute x14 -> x8, waiting for transfers between devices: 88.1 us -> 9.54 us  [the longest x1 4.94 us: on_device(): total = mine + lax.ppermute(theirs, 'dp', SWAP).astype(f32)]
  transfers between devices with their start and end apart: 55 -> 8, of which waited for: 16 -> 2; matrix products, arithmetic and copies ran while one was open for 1% -> 7% of each run, Pallas kernels for 0% -> 0%
where the time goes in v1:
time: 158 us
  blocking collectives  96.2 us (61%)
  starting transfers between devices  22.3 us (14%)
  matrix products  14.5 us (9%)
  waiting for transfers between devices  9.54 us (6%)
  other arithmetic  6.86 us (4%)
  local copies, waits for them, and re-layouts  6.12 us (4%)
  between operations  2.25 us (1%)
    all_to_all x4, blocking collectives, exchange(): lax.all_to_all(parts, 'dp', 0, 0, axis_index_groups=groups, tiled=True)  96.2 us
    dot_general x3, matrix products, embed(): projected = jnp.dot(features, weight, preferred_element_type=f32)  7.06 us
    ppermute x1, starting transfers between devices, on_device(): above = lax.ppermute(text_x, 'dp', shifted(-2))  6.76 us
    dot_general x6, matrix products, contract(): lax.dot_general(a, b, (((da,), (db,)), ((), ())), preferred_element_type=...  6.26 us
    unnamed x16, local copies, waits for them, and re-layouts  5.66 us
    ppermute x1, waiting for transfers between devices, on_device(): total = mine + lax.ppermute(theirs, 'dp', SWAP).astype(f32)  4.94 us
    ppermute x1, starting transfers between devices, on_device(): theirs = lax.ppermute(mine, 'dp', SWAP)  4.76 us
    ppermute x1, waiting for transfers between devices, on_device(): theirs = lax.ppermute(mine, 'dp', SWAP)  4.58 us
  transfers between devices with their start and end apart: 8, of which 2 were waited for; matrix products, arithmetic and copies ran while one was open for 7% of the time, Pallas kernels for 0%

profile of v1, /device:TPU:1, one launch (start us, length us, event | category | flops | bytes accessed | tf_op | source)
XLA Modules:
  0.0 157.8 jit_solution(17491677786618670504)
XLA Ops:
  0.6 0.0 copy-start
  0.6 0.0 copy-start.4
  0.7 4.5 %collective-permute-start.3 = (bf16[128,1152]{1,0:T(8,128)(2,1)}, bf16[128,1152]{1,0:T(8,128)(2,1)}, u32[]{:S(2)}, u32[]{:S(2)}) collective-permute-start(bf16[128,1152]{1,0:T(8,128)(2,1)} %param.7), channel_id=1, source_target_pairs={{0,253},{1,4},{2,255},{3,6},{4,1},{5,8},{6,3},{7,10},{8,5},{9,12},... | collective-permute-start | bytes 884744 | tf_op jit(solution)/shard_map/band_exchange/ppermute | solution.py:77
  5.1 6.8 %collective-permute-start.2 = (bf16[128,1152]{1,0:T(8,128)(2,1)}, bf16[128,1152]{1,0:T(8,128)(2,1)}, u32[]{:S(2)}, u32[]{:S(2)}) collective-permute-start(bf16[128,1152]{1,0:T(8,128)(2,1)} %param.7), channel_id=1, source_target_pairs={{0,254},{1,255},{2,0},{3,1},{4,2},{5,3},{6,4},{7,5},{8,6},{9,7},{1... | collective-permute-start | bytes 884744 | tf_op jit(solution)/shard_map/band_exchange/ppermute | solution.py:76
  11.9 0.0 collective-permute-start.1
  11.9 2.8 %collective-permute-start = (bf16[128,1152]{1,0:T(8,128)(2,1)}, bf16[128,1152]{1,0:T(8,128)(2,1)}, u32[]{:S(2)}, u32[]{:S(2)}) collective-permute-start(bf16[128,1152]{1,0:T(8,128)(2,1)} %param.7), channel_id=1, source_target_pairs={{0,1},{1,0},{2,3},{3,2},{4,5},{5,4},{6,7},{7,6},{8,9},{9,8},{10,11... | collective-permute-start | bytes 884744 | tf_op jit(solution)/shard_map/band_exchange/ppermute | solution.py:80
  14.7 2.5 %multiply_reduce_fusion.5 = (f32[128]{0:T(128)S(1)}, f32[128,1152]{1,0:T(8,128)S(1)}) fusion(bf16[128,1152]{1,0:T(8,128)(2,1)} %param.8, bf16[1152,1152]{1,0:T(8,128)(2,1)} %param.10), kind=kOutput, calls=%fused_computation.44 | convolution fusion | flops 340033408 | bytes 3539456 | tf_op jit(solution)/shard_map/dot_general | solution.py:33
  17.2 0.0 copy-start.2
  17.2 0.5 copy-done.2
  17.8 0.1 fusion.31
  17.9 0.0 copy-done.4
  17.9 0.1 iota_compare_fusion
  19.3 1.0 constant_dynamic-update-slice_fusion.6
  20.3 0.0 collective-permute-done
  20.3 0.0 copy-done
  20.3 2.1 %multiply_reduce_fusion.3 = (f32[256]{0:T(256)S(1)}, f32[256,1152]{1,0:T(8,128)S(1)}) fusion(bf16[1152,1152]{1,0:T(8,128)(2,1)S(1)} %copy-done, bf16[128,1152]{1,0:T(8,128)(2,1)} %collective-permute-done, bf16[128,1152]{1,0:T(8,128)(2,1)} %param.7), kind=kOutput, calls=%fused_computation.25 | convolution fusion | flops 681246464 | bytes 4424704 | tf_op jit(solution)/shard_map/near_blocks/dot_general | solution.py:33
  22.5 0.4 fusion.17
  22.9 0.4 multiply_reduce_fusion.2
  23.3 0.3 divide_convert_fusion.1
  23.6 0.0 collective-permute-done.2
  23.6 2.1 %collective-permute-start.5 = (bf16[128,1152]{1,0:T(8,128)(2,1)}, bf16[128,1152]{1,0:T(8,128)(2,1)S(1)}, u32[]{:S(2)}, u32[]{:S(2)}) collective-permute-start(bf16[128,1152]{1,0:T(8,128)(2,1)} %collective-permute-done.2), channel_id=1, source_target_pairs={{0,1},{1,0},{2,3},{3,2},{4,5},{5,4},{6,7},{7,6},{8,9},{9,8},{10,11... | collective-permute-start | bytes 884744 | tf_op jit(solution)/shard_map/band_exchange/ppermute | solution.py:82
  25.7 0.0 collective-permute-done.1
  25.7 1.3 collective-permute-start.4
  27.1 1.0 constant_dynamic-update-slice_fusion.5
  28.0 1.0 constant_dynamic-update-slice_fusion.4
  29.1 1.0 constant_dynamic-update-slice_fusion.3
  30.1 0.0 collective-permute-done.3
  30.1 1.0 constant_dynamic-update-slice_fusion.2
  31.1 0.0 collective-permute-done.4
  31.1 0.1 constant_dynamic-update-slice_fusion.1
  31.2 0.0 collective-permute-done.5
  31.2 0.1 constant_dynamic-update-slice_fusion
  31.3 2.4 %multiply_reduce_fusion.1 = (f32[640]{0:T(1024)S(1)}, f32[640,1152]{1,0:T(8,128)S(1)}) fusion(bf16[640,1152]{1,0:T(8,128)(2,1)S(1)} %get-tuple-element.5, bf16[1152,1152]{1,0:T(8,128)(2,1)S(1)} %copy-done), kind=kOutput, calls=%fused_computation.6 | convolution fusion | flops 1700167040 | bytes 7080448 | tf_op jit(solution)/shard_map/far_blocks/dot_general | solution.py:33
  33.7 0.6 fusion.10
  34.3 0.5 fusion.18
  34.9 0.0 copy-start.3
  34.9 0.8 multiply_reduce_fusion
  35.6 0.0 copy-done.3
  35.6 0.4 multiply_reduce_fusion.4
  36.1 0.5 divide_convert_fusion
  36.6 0.0 copy-start.1
  36.6 3.2 %fusion.1 = f32[1152,1152]{1,0:T(8,128)S(1)} fusion(bf16[896,1152]{1,0:T(8,128)(2,1)S(1)} %get-tuple-element.4, bf16[640,1152]{1,0:T(8,128)(2,1)S(1)} %divide_convert_fusion, bf16[256,1152]{1,0:T(8,128)(2,1)S(1)} %divide_convert_fusion.1), kind=kOutput, calls=%fused_computation.12 | convolution fusion | flops 2382299136 | bytes 9437184 | tf_op jit(solution)/shard_map/heads/dot_general | solution.py:44
  39.9 0.0 copy-done.1
  39.9 1.0 select_convert_fusion
  40.9 0.1 collective-permute-start.6
  41.0 4.9 %collective-permute-done.6 = bf16[1152,1152]{1,0:T(8,128)(2,1)S(1)} collective-permute-done((bf16[1152,1152]{1,0:T(8,128)(2,1)S(1)}, bf16[1152,1152]{1,0:T(8,128)(2,1)S(1)}, u32[]{:S(2)}, u32[]{:S(2)}) %collective-permute-start.6) | collective-permute-done | bytes 2654240 | tf_op jit(solution)/shard_map/heads/ppermute | solution.py:112
  46.0 0.8 add_convert_fusion
  46.8 37.6 %all_to_all.20 = bf16[1296,8,128]{2,1,0:T(8,128)(2,1)} all-to-all(bf16[1296,8,128]{2,1,0:T(8,128)(2,1)S(1)} %bitcast.35), channel_id=1, replica_groups={{0,16,32,48,64,80,96,112,128,144,160,176,192,208,224,240},{1,17,33,49,6..., dimensions={0} | all-to-all | bytes 5308416 | tf_op jit(solution)/shard_map/sum_planes/all_to_all | solution.py:48
  84.4 2.1 %reduce_sum.84 = bf16[81,8,128]{2,1,0:T(8,128)(2,1)S(1)} reduce(bf16[16,81,8,128]{3,2,1,0:T(8,128)(2,1)} %bitcast.37, bf16[]{:T(256)} %constant.25.clone.1), dimensions={0}, to_apply=%region_6.7 | reduce | flops 1244160 | bytes 2820098 | tf_op jit(solution)/shard_map/sum_planes/reduce_sum | solution.py:116
  86.5 13.7 %all_to_all.21 = bf16[88,8,128]{2,1,0:T(8,128)(2,1)S(1)} all-to-all(bf16[88,8,128]{2,1,0:T(8,128)(2,1)S(1)} %concatenate.27), channel_id=1, replica_groups={{0,2,4,6,8,10,12,14},{1,3,5,7,9,11,13,15},{16,18,20,22,24,26,28,30},{17..., dimensions={0} | all-to-all | bytes 360448 | tf_op jit(solution)/shard_map/sum_lines/all_to_all | solution.py:48
  100.3 10.8 %all_to_all.22 = bf16[88,8,128]{2,1,0:T(8,128)(2,1)S(1)} all-to-all(bf16[88,8,128]{2,1,0:T(8,128)(2,1)S(1)} %bitcast.41), channel_id=1, replica_groups={{0,2,4,6,8,10,12,14},{1,3,5,7,9,11,13,15},{16,18,20,22,24,26,28,30},{17..., dimensions={0} | all-to-all | bytes 360448 | tf_op jit(solution)/shard_map/share_lines/all_to_all | solution.py:48
  111.1 0.3 tile.20
  111.5 34.1 %all_to_all.23 = bf16[1296,8,128]{2,1,0:T(8,128)(2,1)S(1)} all-to-all(bf16[1296,8,128]{2,1,0:T(8,128)(2,1)S(1)} %bitcast.36), channel_id=1, replica_groups={{0,16,32,48,64,80,96,112,128,144,160,176,192,208,224,240},{1,17,33,49,6..., dimensions={0} | all-to-all | bytes 5308416 | tf_op jit(solution)/shard_map/share_planes/all_to_all | solution.py:48
  145.6 4.8 %collective-permute-start.7 = (bf16[1152,1152]{1,0:T(8,128)(2,1)S(1)}, bf16[1152,1152]{1,0:T(8,128)(2,1)S(1)}, u32[]{:S(2)}, u32[]{:S(2)}) collective-permute-start(bf16[1152,1152]{1,0:T(8,128)(2,1)S(1)} %bitcast.38), channel_id=1, source_target_pairs={{0,1},{1,0},{2,3},{3,2},{4,5},{5,4},{6,7},{7,6},{8,9},{9,8},{10,11... | collective-permute-start | bytes 7962632 | tf_op jit(solution)/shard_map/finish/ppermute | solution.py:129
  150.4 4.6 %collective-permute-done.7 = bf16[1152,1152]{1,0:T(8,128)(2,1)S(1)} collective-permute-done((bf16[1152,1152]{1,0:T(8,128)(2,1)S(1)}, bf16[1152,1152]{1,0:T(8,128)(2,1)S(1)}, u32[]{:S(2)}, u32[]{:S(2)}) %collective-permute-start.7) | collective-permute-done | bytes 2654240 | tf_op jit(solution)/shard_map/finish/ppermute | solution.py:129
  154.9 2.9 %broadcast_select_fusion = (bf16[1152,1152]{1,0:T(8,128)(2,1)}, bf16[1152,1152]{1,0:T(8,128)(2,1)}) fusion(bf16[1152,1152]{1,0:T(8,128)(2,1)S(1)} %collective-permute-done.7, bf16[1152,1152]{1,0:T(8,128)(2,1)S(1)} %bitcast.39, pred[]{:T(512)S(6)} %eq.8), kind=kLoop, calls=%fused_computation.8 | loop fusion | flops 2654208 | bytes 10616833 | tf_op jit(solution)/shard_map/finish/jit(_where)/select_n | solution.py:130
  (7 shorter events, 0.1 us)
Async XLA Ops:
  0.6 19.7 %copy-start = (bf16[1152,1152]{1,0:T(8,128)(2,1)S(1)}, bf16[1152,1152]{1,0:T(8,128)(2,1)}, u32[]{:S(2)}) copy-start(bf16[1152,1152]{1,0:T(8,128)(2,1)} %param.9) | copy-start | bytes 7962628
  0.6 17.2 %copy-start.4 = (s32[128]{0:T(128)S(1)}, s32[128]{0:T(128)}, u32[]{:S(2)}) copy-start(s32[128]{0:T(128)} %param.11) | copy-start | bytes 1540
  0.7 29.4 %collective-permute-start.3 = (bf16[128,1152]{1,0:T(8,128)(2,1)}, bf16[128,1152]{1,0:T(8,128)(2,1)}, u32[]{:S(2)}, u32[]{:S(2)}) collective-permute-start(bf16[128,1152]{1,0:T(8,128)(2,1)} %param.7), channel_id=1, source_target_pairs={{0,253},{1,4},{2,255},{3,6},{4,1},{5,8},{6,3},{7,10},{8,5},{9,12},... | collective-permute-start | bytes 884744 | tf_op jit(solution)/shard_map/band_exchange/ppermute | solution.py:77
  5.1 18.5 %collective-permute-start.2 = (bf16[128,1152]{1,0:T(8,128)(2,1)}, bf16[128,1152]{1,0:T(8,128)(2,1)}, u32[]{:S(2)}, u32[]{:S(2)}) collective-permute-start(bf16[128,1152]{1,0:T(8,128)(2,1)} %param.7), channel_id=1, source_target_pairs={{0,254},{1,255},{2,0},{3,1},{4,2},{5,3},{6,4},{7,5},{8,6},{9,7},{1... | collective-permute-start | bytes 884744 | tf_op jit(solution)/shard_map/band_exchange/ppermute | solution.py:76
  11.9 13.9 %collective-permute-start.1 = (bf16[128,1152]{1,0:T(8,128)(2,1)}, bf16[128,1152]{1,0:T(8,128)(2,1)}, u32[]{:S(2)}, u32[]{:S(2)}) collective-permute-start(bf16[128,1152]{1,0:T(8,128)(2,1)} %param.7), channel_id=1, source_target_pairs={{0,2},{1,3},{2,4},{3,5},{4,6},{5,7},{6,8},{7,9},{8,10},{9,11},{10,... | collective-permute-start | bytes 884744 | tf_op jit(solution)/shard_map/band_exchange/ppermute | solution.py:75
  11.9 8.4 %collective-permute-start = (bf16[128,1152]{1,0:T(8,128)(2,1)}, bf16[128,1152]{1,0:T(8,128)(2,1)}, u32[]{:S(2)}, u32[]{:S(2)}) collective-permute-start(bf16[128,1152]{1,0:T(8,128)(2,1)} %param.7), channel_id=1, source_target_pairs={{0,1},{1,0},{2,3},{3,2},{4,5},{5,4},{6,7},{7,6},{8,9},{9,8},{10,11... | collective-permute-start | bytes 884744 | tf_op jit(solution)/shard_map/band_exchange/ppermute | solution.py:80
  17.2 0.5 copy-start.2
  23.6 7.6 %collective-permute-start.5 = (bf16[128,1152]{1,0:T(8,128)(2,1)}, bf16[128,1152]{1,0:T(8,128)(2,1)S(1)}, u32[]{:S(2)}, u32[]{:S(2)}) collective-permute-start(bf16[128,1152]{1,0:T(8,128)(2,1)} %collective-permute-done.2), channel_id=1, source_target_pairs={{0,1},{1,0},{2,3},{3,2},{4,5},{5,4},{6,7},{7,6},{8,9},{9,8},{10,11... | collective-permute-start | bytes 884744 | tf_op jit(solution)/shard_map/band_exchange/ppermute | solution.py:82
  25.7 5.4 %collective-permute-start.4 = (bf16[128,1152]{1,0:T(8,128)(2,1)}, bf16[128,1152]{1,0:T(8,128)(2,1)S(1)}, u32[]{:S(2)}, u32[]{:S(2)}) collective-permute-start(bf16[128,1152]{1,0:T(8,128)(2,1)} %collective-permute-done.1), channel_id=1, source_target_pairs={{0,1},{1,0},{2,3},{3,2},{4,5},{5,4},{6,7},{7,6},{8,9},{9,8},{10,11... | collective-permute-start | bytes 884744 | tf_op jit(solution)/shard_map/band_exchange/ppermute | solution.py:81
  34.9 0.8 copy-start.3
  36.6 3.3 %copy-start.1 = (bf16[128,1152]{1,0:T(8,128)(2,1)S(1)}, bf16[128,1152]{1,0:T(8,128)(2,1)}, u32[]{:S(2)}) copy-start(bf16[128,1152]{1,0:T(8,128)(2,1)} %param.8) | copy-start | bytes 884740
  40.9 5.0 %collective-permute-start.6 = (bf16[1152,1152]{1,0:T(8,128)(2,1)S(1)}, bf16[1152,1152]{1,0:T(8,128)(2,1)S(1)}, u32[]{:S(2)}, u32[]{:S(2)}) collective-permute-start(bf16[1152,1152]{1,0:T(8,128)(2,1)S(1)} %get-tuple-element.26), channel_id=1, source_target_pairs={{0,1},{1,0},{2,3},{3,2},{4,5},{5,4},{6,7},{7,6},{8,9},{9,8},{10,11... | collective-permute-start | bytes 7962632 | tf_op jit(solution)/shard_map/heads/ppermute | solution.py:112
  145.6 9.3 %collective-permute-start.7 = (bf16[1152,1152]{1,0:T(8,128)(2,1)S(1)}, bf16[1152,1152]{1,0:T(8,128)(2,1)S(1)}, u32[]{:S(2)}, u32[]{:S(2)}) collective-permute-start(bf16[1152,1152]{1,0:T(8,128)(2,1)S(1)} %bitcast.38), channel_id=1, source_target_pairs={{0,1},{1,0},{2,3},{3,2},{4,5},{5,4},{6,7},{7,6},{8,9},{9,8},{10,11... | collective-permute-start | bytes 7962632 | tf_op jit(solution)/shard_map/finish/ppermute | solution.py:129

commit v2 on v1

v2 whole, which is shorter than its diff:
```python
import functools

import jax
import jax.numpy as jnp
from jax import lax
from jax.experimental import pallas as pl
from jax.experimental.pallas import tpu as pltpu
from jax.sharding import PartitionSpec as P

NY, NX, NZ, CORES = 4, 4, 8, 2
N = NY * NX * NZ * CORES
epsilon = 1e-06
bf16, f32 = jnp.bfloat16, jnp.float32
MIB = 1 << 20


def index(y, x, z, c):
    return ((y % NY * NX + x % NX) * NZ + z % NZ) * CORES + c


PLACES = [
    (y, x, z, c) for y in range(NY) for x in range(NX) for z in range(NZ) for c in range(CORES)
]


def route(move):
    return [(index(*place), index(*move(*place))) for place in PLACES]


def groups(key):
    found = {}
    for place in PLACES:
        found.setdefault(key(*place), []).append(index(*place))
    return list(found.values())


def along_first(step):
    return route(lambda y, x, z, c: (y, x + step, z, c) if c == 0 else (y + step, x, z, c))


SWAP = route(lambda y, x, z, c: (y, x, z, 1 - c))
RIGHT, LEFT = along_first(1), along_first(-1)
SECOND = groups(lambda y, x, z, c: (c, z, x if c == 0 else y))
LINES = groups(lambda y, x, z, c: (c, x, y))
FAR = [(i, (i + 3) % N if i % 2 else (i - 3) % N) for i in range(N)]


def shifted(distance):
    return [(i, (i + distance) % N) for i in range(N)]


def send(block, pairs):
    return lax.ppermute(block, "dp", pairs)


def exchange(parts, members):
    return lax.all_to_all(parts, "dp", 0, 0, axis_index_groups=members, tiled=True)


def call(body, outs, scratch=(), limit=32):
    def run(scalars, *arrays):
        smem = [pl.BlockSpec(memory_space=pltpu.SMEM)] * len(scalars)
        vmem = [pl.BlockSpec(memory_space=pltpu.VMEM)] * len(arrays)
        return pl.pallas_call(
            body,
            out_shape=[jax.ShapeDtypeStruct(s, d) for s, d in outs],
            in_specs=smem + vmem,
            out_specs=[pl.BlockSpec(memory_space=pltpu.VMEM)] * len(outs),
            scratch_shapes=list(scratch),
            compiler_params=pltpu.CompilerParams(vmem_limit_bytes=limit * MIB),
        )(*scalars, *[pltpu.with_memory_space_constraint(a, pltpu.VMEM) for a in arrays])

    return run


def embed(features, weight):
    projected = jnp.dot(features, weight, preferred_element_type=f32)
    length = jnp.sqrt(jnp.sum(projected * projected, axis=-1, keepdims=True) + epsilon)
    return projected / length, length


def pull_back(gradient, unit_rows, length):
    radial = jnp.sum(gradient * unit_rows, axis=-1, keepdims=True)
    return ((gradient - unit_rows * radial) / length).astype(bf16)


def contract(a, b, da, db):
    return lax.dot_general(a, b, (((da,), (db,)), ((), ())), preferred_element_type=f32)


def near_kernel(
    place, factors, text_own, text_other, image_own, image_other, text_w, image_w, target,
    image_emb, image_unit, image_norm, text_back, image_grad,
):
    scale, bias = factors[0], factors[1]
    unit, norm = embed(jnp.concatenate([image_own[...], image_other[...]]), image_w[...])
    emb = unit.astype(bf16)
    image_emb[...] = emb
    image_unit[...] = unit
    image_norm[...] = norm
    unit, norm = embed(jnp.concatenate([text_own[...], text_other[...]]), text_w[...])
    text_emb = unit.astype(bf16)
    logits = scale * contract(text_emb, emb, 1, 1) + bias
    labels = (lax.broadcasted_iota(jnp.int32, logits.shape, 1) == target[...]).astype(f32)
    coefficient = (jax.nn.sigmoid(logits) - labels).astype(bf16)

    @pl.when(place[0] == 0)
    def _():
        gradient = scale * jnp.dot(coefficient, emb, preferred_element_type=f32)
        text_back[...] = pull_back(gradient, unit, norm)

    @pl.when(place[0] != 0)
    def _():
        image_grad[...] = contract(coefficient, text_emb, 0, 0)


def far_kernel(
    place, factors, text_own, text_other, below, below_other, above, above_other, far, far_other,
    image_own, image_other, text_w, image_emb, image_unit, image_norm, text_back, image_grad,
    own, right_top, right_bottom, left_top, left_bottom, far_right, far_left,
    xs, backs, grad, head,
):
    rows, width = text_own.shape
    depth = head.shape[0]
    scale, bias = factors[0], factors[1]
    for k, (a, b) in enumerate([(below, below_other), (above, above_other), (far, far_other)]):
        x = jnp.concatenate([a[...], b[...]])
        unit, norm = embed(x, text_w[...])
        emb = unit.astype(bf16)
        logits = scale * contract(emb, image_emb[...], 1, 1) + bias
        sigmoid = jax.nn.sigmoid(logits)
        if k == 2:
            row = lax.broadcasted_iota(jnp.int32, logits.shape, 0) < rows
            column = lax.broadcasted_iota(jnp.int32, logits.shape, 1) < rows
            sigmoid = jnp.where(row == column, sigmoid, 0.0)
        coefficient = sigmoid.astype(bf16)

        @pl.when(place[0] == 0)
        def _():
            gradient = scale * jnp.dot(coefficient, image_emb[...], preferred_element_type=f32)
            at = pl.ds(2 * rows * k, 2 * rows)
            backs[at, :] = pull_back(gradient, unit, norm)
            xs[at, :] = x

        @pl.when(place[0] != 0)
        def _():
            share = contract(coefficient, emb, 0, 0)
            if k == 0:
                grad[...] = image_grad[...] + share
            else:
                grad[...] = grad[...] + share

    step = depth // 3

    @pl.when(place[0] == 0)
    def _():
        at = 6 * rows
        xs[pl.ds(at, rows), :] = text_own[...]
        xs[pl.ds(at + rows, rows), :] = text_other[...]
        backs[pl.ds(at, 2 * rows), :] = text_back[...]
        for k in range(3):
            at = pl.ds(k * step, step)
            head[at, :] = contract(xs[:, at], backs[...], 0, 0)

    @pl.when(place[0] != 0)
    def _():
        back = pull_back(scale * grad[...], image_unit[...], image_norm[...])
        backs[pl.ds(0, 2 * rows), :] = back
        xs[pl.ds(0, rows), :] = image_own[...]
        xs[pl.ds(rows, rows), :] = image_other[...]
        for k in range(3):
            at = pl.ds(k * step, step)
            head[at, :] = contract(xs[pl.ds(0, 2 * rows), at], back, 0, 0)

    slab = depth // 4
    half = slab // 2

    def part(turn, upper, size):
        start = lax.rem(place[1] + turn, 4) * slab + upper
        return head[pl.ds(pl.multiple_of(start, 16), size), :].astype(bf16)

    far_right[...] = part(2, 0, half)
    far_left[...] = part(2, half, half)
    right_top[...] = part(1, 0, half)
    right_bottom[...] = part(1, half, half)
    left_top[...] = part(3, 0, half)
    left_bottom[...] = part(3, half, half)
    own[...] = part(0, 0, slab)


def add_kernel(a, b, c, d, ab, cd):
    ab[...] = (a[...].astype(f32) + b[...].astype(f32)).astype(bf16)
    cd[...] = (c[...].astype(f32) + d[...].astype(f32)).astype(bf16)


def join_kernel(own, a_top, a_bottom, b_top, b_bottom, out):
    half = a_top.shape[0]
    upper, lower = pl.ds(0, half), pl.ds(half, half)
    out[upper, :] = (
        own[upper, :].astype(f32) + a_top[...].astype(f32) + b_top[...].astype(f32)
    ).astype(bf16)
    out[lower, :] = (
        own[lower, :].astype(f32) + a_bottom[...].astype(f32) + b_bottom[...].astype(f32)
    ).astype(bf16)


def write_kernel(*refs):
    mine, theirs, (text, image, sems) = refs[:5], refs[5:10], refs[10:]
    me = lax.axis_index("dp")
    core = lax.rem(me, CORES)
    x = lax.rem(me // (NZ * CORES), NX)
    y = me // (NX * NZ * CORES)
    slab = mine[0].shape[0]
    half = slab // 2

    def copies(pieces, position, out, first):
        turns = [(0, 0), (3, 0), (1, 0), (2, 0), (2, half)]
        return [
            pltpu.make_async_copy(
                piece,
                out.at[
                    pl.ds(
                        pl.multiple_of(lax.rem(position + turn, 4) * slab + upper, 16),
                        piece.shape[0],
                    ),
                    :,
                ],
                sems.at[first + k],
            )
            for k, (piece, (turn, upper)) in enumerate(zip(pieces, turns))
        ]

    def go(moves):
        for move in moves:
            move.start()
        for move in moves:
            move.wait()

    @pl.when(core == 0)
    def _():
        go(copies(mine, x, text, 0) + copies(theirs, y, image, 5))

    @pl.when(core != 0)
    def _():
        go(copies(mine, y, image, 0) + copies(theirs, x, text, 5))


def on_device(text_x, image_x, text_w, image_w, position, log_scale, shift):
    rows, width = text_x.shape
    depth = text_w.shape[0]
    slab = depth // 4
    half = slab // 2
    me = lax.axis_index("dp")
    core = lax.rem(me, CORES)
    x = lax.rem(me // (NZ * CORES), NX)
    y = me // (NX * NZ * CORES)
    place = jnp.stack([core, jnp.where(core == 0, x, y)]).astype(jnp.int32)
    factors = jnp.concatenate([jnp.exp(log_scale), shift])
    with jax.named_scope("band_exchange"):
        below = send(text_x, shifted(2))
        above = send(text_x, shifted(-2))
        far = send(text_x, FAR)
        text_other = send(text_x, SWAP)
        image_other = send(image_x, SWAP)
        target = jnp.concatenate([position, send(position, SWAP) + rows])[:, None]
        below_other = send(below, SWAP)
        above_other = send(above, SWAP)
        far_other = send(far, SWAP)
    near = call(
        near_kernel,
        [
            ((2 * rows, width), bf16),
            ((2 * rows, width), f32),
            ((2 * rows, 1), f32),
            ((2 * rows, width), bf16),
            ((2 * rows, width), f32),
        ],
    )
    with jax.named_scope("near"):
        known = near(
            (place, factors), text_x, text_other, image_x, image_other, text_w, image_w, target
        )
    halves = ((half, width), bf16)
    far_call = call(
        far_kernel,
        [((slab, width), bf16)] + [halves] * 6,
        [
            pltpu.VMEM((8 * rows, depth), bf16),
            pltpu.VMEM((8 * rows, width), bf16),
            pltpu.VMEM((2 * rows, width), f32),
            pltpu.VMEM((depth, width), f32),
        ],
    )
    with jax.named_scope("far"):
        own, right_top, right_bottom, left_top, left_bottom, far_right, far_left = far_call(
            (place, factors), text_x, text_other, below, below_other, above, above_other, far,
            far_other, image_x, image_other, text_w, *known,
        )
    with jax.named_scope("sum_first"):
        from_left = send(far_right, RIGHT)
        from_right = send(far_left, LEFT)
        a_bottom = send(right_bottom, RIGHT)
        b_top = send(left_top, LEFT)
        right_top, left_bottom = call(add_kernel, [halves] * 2)(
            (), right_top, from_left, left_bottom, from_right
        )
        a_top = send(right_top, RIGHT)
        b_bottom = send(left_bottom, LEFT)
        [part] = call(join_kernel, [((slab, width), bf16)])(
            (), own, a_top, a_bottom, b_top, b_bottom
        )
    with jax.named_scope("sum_second"):
        part = exchange(part.reshape(4, slab // 4, width), SECOND)
        part = jnp.sum(part.astype(f32), axis=0).astype(bf16)
    with jax.named_scope("sum_lines"):
        tiles = (
            part.reshape(slab // 32, 8, width // 128, 128).transpose(0, 2, 1, 3).reshape(-1, 8, 128)
        )
        count = tiles.shape[0]
        each = -(-count // NZ)
        tiles = jnp.concatenate([tiles, jnp.zeros((each * NZ - count, 8, 128), bf16)])
        tiles = exchange(tiles, LINES).reshape(NZ, each, 8, 128)
        tiles = jnp.sum(tiles.astype(f32), axis=0).astype(bf16)
    with jax.named_scope("share_lines"):
        tiles = exchange(jnp.tile(tiles, (NZ, 1, 1)), LINES)[:count]
        part = (
            tiles.reshape(slab // 32, width // 128, 8, 128).transpose(0, 2, 1, 3).reshape(-1, width)
        )
    with jax.named_scope("share_second"):
        whole = exchange(jnp.tile(part[None], (4, 1, 1)), SECOND)
        own = whole.reshape(slab, width)
    with jax.named_scope("share_first"):
        left = send(own, RIGHT)
        right = send(own, LEFT)
        own_other = send(own, SWAP)
        across_top = send(left[:half], RIGHT)
        across_bottom = send(right[half:], LEFT)
        mine = [own, left, right, across_top, across_bottom]
        theirs = [own_other] + [send(piece, SWAP) for piece in mine[1:]]
    with jax.named_scope("write"):
        return pl.pallas_call(
            write_kernel,
            out_shape=[jax.ShapeDtypeStruct((depth, width), bf16)] * 2,
            in_specs=[pl.BlockSpec(memory_space=pl.ANY)] * 10,
            out_specs=[pl.BlockSpec(memory_space=pl.ANY)] * 2,
            scratch_shapes=[pltpu.SemaphoreType.DMA((10,))],
        )(*mine, *theirs)


def solution(mesh):
    return jax.shard_map(
        on_device,
        mesh=mesh,
        in_specs=(P("dp", None), P("dp", None), P(), P(), P("dp"), P(), P()),
        out_specs=(P(), P()),
        check_vma=False,
    )
```

time: 158 us -> 307 us (1.94)
  Pallas kernels: 0 us -> 175 us
  blocking collectives: 96.2 us -> 43.7 us
  starting transfers between devices: 22.3 us -> 70.3 us
  matrix products: 14.5 us -> 0 us
  other arithmetic: 6.86 us -> 0.95 us
    pallas_call x0 -> x5, Pallas kernels: none -> 175 us  [the longest x1 162 us: on_device(): pl.pallas_call(write_kernel, out_shape=[jax.ShapeDtypeStruct((depth, widt...]
    all_to_all x4, blocking collectives: 96.2 us -> 43.7 us  [exchange(): lax.all_to_all(parts, 'dp', 0, 0, axis_index_groups=members, tiled=True)]
    ppermute x8 -> x24, starting transfers between devices: 22.3 us -> 70.3 us  [send(): return lax.ppermute(block, 'dp', pairs)]
    dot_general x11 -> x0, matrix products: 14.5 us -> none  [the longest x3 7.06 us: embed(): projected = jnp.dot(features, weight, preferred_element_type=f32)]
    ppermute x8 -> x24, waiting for transfers between devices: 9.54 us -> 7.8 us  [send(): return lax.ppermute(block, 'dp', pairs)]
    unnamed x16 -> x26, local copies, waits for them, and re-layouts: 5.66 us -> 6.18 us
  transfers between devices with their start and end apart: 8 -> 24, of which waited for: 2 -> 4; matrix products, arithmetic and copies ran while one was open for 7% -> 0% of each run, Pallas kernels for 0% -> 1%
where the time goes in v2:
time: 307 us; the launch traced here: 306 us
  Pallas kernels  175 us (57%)
  starting transfers between devices  70.3 us (23%)
  blocking collectives  43.7 us (14%)
  waiting for transfers between devices  7.8 us (3%)
  local copies, waits for them, and re-layouts  6.46 us (2%)
    pallas_call x1, Pallas kernels, on_device(): pl.pallas_call(write_kernel, out_shape=[jax.ShapeDtypeStruct((depth, widt...  162 us
    ppermute x24, starting transfers between devices, send(): return lax.ppermute(block, 'dp', pairs)  70.3 us
    all_to_all x4, blocking collectives, exchange(): lax.all_to_all(parts, 'dp', 0, 0, axis_index_groups=members, tiled=True)  43.7 us
    pallas_call x4, Pallas kernels, run(): pl.pallas_call(body, out_shape=[jax.ShapeDtypeStruct(s, d) for s, d in ou...  12.8 us
    ppermute x24, waiting for transfers between devices, send(): return lax.ppermute(block, 'dp', pairs)  7.8 us
    unnamed x26, local copies, waits for them, and re-layouts  6.18 us
  transfers between devices with their start and end apart: 24, of which 4 were waited for; matrix products, arithmetic and copies ran while one was open for 0% of the time, Pallas kernels for 1%

profile of v2, /device:TPU:1, one launch (start us, length us, event | category | flops | bytes accessed | tf_op | source)
XLA Modules:
  0.0 306.4 jit_solution(16768000567613827431)
XLA Ops:
  0.6 4.5 %collective-permute-start.5 = (bf16[128,1152]{1,0:T(8,128)(2,1)}, bf16[128,1152]{1,0:T(8,128)(2,1)S(1)}, u32[]{:S(2)}, u32[]{:S(2)}) collective-permute-start(bf16[128,1152]{1,0:T(8,128)(2,1)} %text_own.3), channel_id=1, source_target_pairs={{0,253},{1,4},{2,255},{3,6},{4,1},{5,8},{6,3},{7,10},{8,5},{9,12},... | collective-permute-start | bytes 884744 | tf_op jit(solution)/shard_map/band_exchange/ppermute | solution.py:53
  5.1 6.8 %collective-permute-start.3 = (bf16[128,1152]{1,0:T(8,128)(2,1)}, bf16[128,1152]{1,0:T(8,128)(2,1)S(1)}, u32[]{:S(2)}, u32[]{:S(2)}) collective-permute-start(bf16[128,1152]{1,0:T(8,128)(2,1)} %text_own.3), channel_id=1, source_target_pairs={{0,254},{1,255},{2,0},{3,1},{4,2},{5,3},{6,4},{7,5},{8,6},{9,7},{1... | collective-permute-start | bytes 884744 | tf_op jit(solution)/shard_map/band_exchange/ppermute | solution.py:53
  11.9 0.0 collective-permute-start.1
  11.9 2.8 collective-permute-start
  14.6 0.0 collective-permute-start.8
  16.0 0.1 pad_maximum_fusion.factors
  16.1 0.1 pad_add_fusion.1.place
  16.1 0.0 collective-permute-done.8
  16.1 0.5 collective-permute-start.7
  16.7 0.0 collective-permute-done.5.far
  16.7 5.9 %collective-permute-start.6 = (bf16[128,1152]{1,0:T(8,128)(2,1)S(1)}, bf16[128,1152]{1,0:T(8,128)(2,1)S(1)}, u32[]{:S(2)}, u32[]{:S(2)}) collective-permute-start(bf16[128,1152]{1,0:T(8,128)(2,1)S(1)} %collective-permute-done.5.far), channel_id=1, source_target_pairs={{0,1},{1,0},{2,3},{3,2},{4,5},{5,4},{6,7},{7,6},{8,9},{9,8},{10,11... | collective-permute-start | bytes 884744 | tf_op jit(solution)/shard_map/band_exchange/ppermute | solution.py:53
  22.6 0.0 collective-permute-done.3.above
  22.6 3.2 %collective-permute-start.4 = (bf16[128,1152]{1,0:T(8,128)(2,1)S(1)}, bf16[128,1152]{1,0:T(8,128)(2,1)S(1)}, u32[]{:S(2)}, u32[]{:S(2)}) collective-permute-start(bf16[128,1152]{1,0:T(8,128)(2,1)S(1)} %collective-permute-done.3.above), channel_id=1, source_target_pairs={{0,1},{1,0},{2,3},{3,2},{4,5},{5,4},{6,7},{7,6},{8,9},{9,8},{10,11... | collective-permute-start | bytes 884744 | tf_op jit(solution)/shard_map/band_exchange/ppermute | solution.py:53
  25.7 0.0 collective-permute-done.1.below
  25.7 1.2 collective-permute-start.2
  26.9 0.7 pad_add_fusion
  27.6 0.1 copy.10.target
  27.7 0.0 collective-permute-done.7.image_other
  27.7 0.0 collective-permute-done.text_other
  27.8 0.0 copy-start
  27.8 1.7 copy-done
  29.5 1.7 copy-done.1
  31.3 1.0 copy-done.2
  32.2 1.0 copy-done.3
  33.2 3.6 %near.1 = (bf16[256,1152]{1,0:T(8,128)(2,1)S(1)}, f32[256,1152]{1,0:T(8,128)S(1)}, f32[256,1]{1,0:T(8,128)S(1)}, bf16[256,1152]{1,0:T(8,128)(2,1)S(1)}, f32[256,1152]{1,0:T(8,128)S(1)}) custom-call(s32[2]{0:T(128)S(1)} %pad_add_fusion.1.place, f32[2]{0:T(128)S(1)} %pad_maximum_fusion.factors, bf16[128,1152]{1,0:T(8,128)(2,1)S(1)} %copy-done.2, ...), custom_call_target="tpu_custom_call" | custom-call | tf_op jit(solution)/shard_map/near/pallas_call | solution.py:64
  36.8 0.0 collective-permute-done.6.far_other
  36.8 0.0 collective-permute-done.4.above_other
  36.8 0.0 collective-permute-done.2.below_other
  36.8 8.7 %far.1 = (bf16[288,1152]{1,0:T(8,128)(2,1)S(1)}, bf16[144,1152]{1,0:T(8,128)(2,1)S(1)}, bf16[144,1152]{1,0:T(8,128)(2,1)S(1)}, bf16[144,1152]{1,0:T(8,128)(2,1)S...) custom-call(s32[2]{0:T(128)S(1)} %pad_add_fusion.1.place, ...), custom_call_target="tpu_custom_call" | custom-call | tf_op jit(solution)/shard_map/far/pallas_call | solution.py:64
  45.5 0.1 collective-permute-start.9
  45.6 2.7 collective-permute-start.10
  48.3 0.0 collective-permute-start.12
  48.3 2.7 collective-permute-start.13
  51.0 2.1 collective-permute-done.9.b
  53.1 0.0 collective-permute-done.10.d
  53.1 0.2 sum_first.2
  53.3 0.1 collective-permute-start.11
  53.4 2.8 collective-permute-start.14
  56.1 0.5 collective-permute-done.12.a_bottom
  56.7 3.9 %collective-permute-done.11.a_top = bf16[144,1152]{1,0:T(8,128)(2,1)S(1)} collective-permute-done((bf16[144,1152]{1,0:T(8,128)(2,1)S(1)}, bf16[144,1152]{1,0:T(8,128)(2,1)S(1)}, u32[]{:S(2)}, u32[]{:S(2)}) %collective-permute-start.11) | collective-permute-done | bytes 331808 | tf_op jit(solution)/shard_map/sum_first/ppermute | solution.py:53
  60.5 0.0 collective-permute-done.14.b_bottom
  60.5 0.3 sum_first.3
  60.8 10.1 %all_to_all.20 = bf16[4,72,1152]{2,1,0:T(8,128)(2,1)S(1)} all-to-all(bf16[4,72,1152]{2,1,0:T(8,128)(2,1)S(1)} %bitcast.17), channel_id=1, replica_groups={{0,64,128,192},{1,17,33,49},{2,66,130,194},{3,19,35,51},{4,68,132,196},..., dimensions={0} | all-to-all | bytes 1327104 | tf_op jit(solution)/shard_map/sum_second/all_to_all | solution.py:57
  70.9 0.1 reduce_sum.24
  71.0 12.7 %all_to_all.21 = bf16[88,8,128]{2,1,0:T(8,128)(2,1)S(1)} all-to-all(bf16[88,8,128]{2,1,0:T(8,128)(2,1)S(1)} %concatenate.11), channel_id=1, replica_groups={{0,2,4,6,8,10,12,14},{1,3,5,7,9,11,13,15},{16,18,20,22,24,26,28,30},{17..., dimensions={0} | all-to-all | bytes 360448 | tf_op jit(solution)/shard_map/sum_lines/all_to_all | solution.py:57
  83.8 10.8 %all_to_all.22 = bf16[88,8,128]{2,1,0:T(8,128)(2,1)S(1)} all-to-all(bf16[88,8,128]{2,1,0:T(8,128)(2,1)S(1)} %bitcast.23), channel_id=1, replica_groups={{0,2,4,6,8,10,12,14},{1,3,5,7,9,11,13,15},{16,18,20,22,24,26,28,30},{17..., dimensions={0} | all-to-all | bytes 360448 | tf_op jit(solution)/shard_map/share_lines/all_to_all | solution.py:57
  94.7 10.1 %all_to_all.23 = bf16[4,72,1152]{2,1,0:T(8,128)(2,1)S(1)} all-to-all(bf16[4,72,1152]{2,1,0:T(8,128)(2,1)S(1)} %tile.20), channel_id=1, replica_groups={{0,64,128,192},{1,17,33,49},{2,66,130,194},{3,19,35,51},{4,68,132,196},..., dimensions={0} | all-to-all | bytes 1327104 | tf_op jit(solution)/shard_map/share_second/all_to_all | solution.py:57
  104.8 2.4 collective-permute-start.16
  107.2 0.0 collective-permute-start.15
  107.2 14.5 %collective-permute-start.19 = (bf16[288,1152]{1,0:T(8,128)(2,1)S(1)}, bf16[288,1152]{1,0:T(8,128)(2,1)S(1)}, u32[]{:S(2)}, u32[]{:S(2)}) collective-permute-start(bf16[288,1152]{1,0:T(8,128)(2,1)S(1)} %bitcast.20), channel_id=1, source_target_pairs={{0,1},{1,0},{2,3},{3,2},{4,5},{5,4},{6,7},{7,6},{8,9},{9,8},{10,11... | collective-permute-start | bytes 1990664 | tf_op jit(solution)/shard_map/share_first/ppermute | solution.py:53
  121.7 0.0 collective-permute-done.16.refs_2_
  121.7 0.9 collective-permute-start.18
  122.6 0.0 collective-permute-done.15.refs_1_
  122.7 0.7 collective-permute-start.17
  123.4 10.5 %collective-permute-start.21 = (bf16[288,1152]{1,0:T(8,128)(2,1)S(1)}, bf16[288,1152]{1,0:T(8,128)(2,1)S(1)}, u32[]{:S(2)}, u32[]{:S(2)}) collective-permute-start(bf16[288,1152]{1,0:T(8,128)(2,1)S(1)} %collective-permute-done.16.refs_2_), channel_id=1, source_target_pairs={{0,1},{1,0},{2,3},{3,2},{4,5},{5,4},{6,7},{7,6},{8,9},{9,8},{10,11... | collective-permute-start | bytes 1990664 | tf_op jit(solution)/shard_map/share_first/ppermute | solution.py:53
  133.9 0.1 collective-permute-start.20
  134.0 4.3 %collective-permute-start.23 = (bf16[144,1152]{1,0:T(8,128)(2,1)S(1)}, bf16[144,1152]{1,0:T(8,128)(2,1)S(1)}, u32[]{:S(2)}, u32[]{:S(2)}) collective-permute-start(bf16[144,1152]{1,0:T(8,128)(2,1)S(1)} %collective-permute-done.18.refs_4_), channel_id=1, source_target_pairs={{0,1},{1,0},{2,3},{3,2},{4,5},{5,4},{6,7},{7,6},{8,9},{9,8},{10,11... | collective-permute-start | bytes 995336 | tf_op jit(solution)/shard_map/share_first/ppermute | solution.py:53
  138.3 0.0 collective-permute-done.17.refs_3_
  138.3 3.8 %collective-permute-start.22 = (bf16[144,1152]{1,0:T(8,128)(2,1)S(1)}, bf16[144,1152]{1,0:T(8,128)(2,1)S(1)}, u32[]{:S(2)}, u32[]{:S(2)}) collective-permute-start(bf16[144,1152]{1,0:T(8,128)(2,1)S(1)} %collective-permute-done.17.refs_3_), channel_id=1, source_target_pairs={{0,1},{1,0},{2,3},{3,2},{4,5},{5,4},{6,7},{7,6},{8,9},{9,8},{10,11... | collective-permute-start | bytes 995336 | tf_op jit(solution)/shard_map/share_first/ppermute | solution.py:53
  142.1 0.0 collective-permute-done.19.refs_5_
  142.1 0.0 collective-permute-done.23.refs_9_
  142.2 1.2 collective-permute-done.22.refs_8_
  143.4 0.7 copy-done.12
  144.2 162.1 %write.1 = (bf16[1152,1152]{1,0:T(8,128)(2,1)}, bf16[1152,1152]{1,0:T(8,128)(2,1)}) custom-call(bf16[288,1152]{1,0:T(8,128)(2,1)} %bitcast.21, bf16[288,1152]{1,0:T(8,128)(2,1)} %copy-done.6, bf16[288,1152]{1,0:T(8,128)(2,1)} %copy-done.5, bf16[144,1152]{1,0:T(8,128)(2,1)} %copy-done.10, bf16[144,1152]{1,0:T(8,128)(2,1)} %copy-done.9, ...), custom_call_target="tpu_custom_call" | custom-call | tf_op jit(solution)/shard_map/write/pallas_call | solution.py:341
  (32 shorter events, 0.2 us)
Async XLA Ops:
  0.6 16.0 %collective-permute-start.5 = (bf16[128,1152]{1,0:T(8,128)(2,1)}, bf16[128,1152]{1,0:T(8,128)(2,1)S(1)}, u32[]{:S(2)}, u32[]{:S(2)}) collective-permute-start(bf16[128,1152]{1,0:T(8,128)(2,1)} %text_own.3), channel_id=1, source_target_pairs={{0,253},{1,4},{2,255},{3,6},{4,1},{5,8},{6,3},{7,10},{8,5},{9,12},... | collective-permute-start | bytes 884744 | tf_op jit(solution)/shard_map/band_exchange/ppermute | solution.py:53
  5.1 17.5 %collective-permute-start.3 = (bf16[128,1152]{1,0:T(8,128)(2,1)}, bf16[128,1152]{1,0:T(8,128)(2,1)S(1)}, u32[]{:S(2)}, u32[]{:S(2)}) collective-permute-start(bf16[128,1152]{1,0:T(8,128)(2,1)} %text_own.3), channel_id=1, source_target_pairs={{0,254},{1,255},{2,0},{3,1},{4,2},{5,3},{6,4},{7,5},{8,6},{9,7},{1... | collective-permute-start | bytes 884744 | tf_op jit(solution)/shard_map/band_exchange/ppermute | solution.py:53
  11.9 13.9 %collective-permute-start.1 = (bf16[128,1152]{1,0:T(8,128)(2,1)}, bf16[128,1152]{1,0:T(8,128)(2,1)S(1)}, u32[]{:S(2)}, u32[]{:S(2)}) collective-permute-start(bf16[128,1152]{1,0:T(8,128)(2,1)} %text_own.3), channel_id=1, source_target_pairs={{0,2},{1,3},{2,4},{3,5},{4,6},{5,7},{6,8},{7,9},{8,10},{9,11},{10,... | collective-permute-start | bytes 884744 | tf_op jit(solution)/shard_map/band_exchange/ppermute | solution.py:53
  11.9 15.9 %collective-permute-start = (bf16[128,1152]{1,0:T(8,128)(2,1)}, bf16[128,1152]{1,0:T(8,128)(2,1)S(1)}, u32[]{:S(2)}, u32[]{:S(2)}) collective-permute-start(bf16[128,1152]{1,0:T(8,128)(2,1)} %text_own.3), channel_id=1, source_target_pairs={{0,1},{1,0},{2,3},{3,2},{4,5},{5,4},{6,7},{7,6},{8,9},{9,8},{10,11... | collective-permute-start | bytes 884744 | tf_op jit(solution)/shard_map/band_exchange/ppermute | solution.py:53
  14.6 1.5 collective-permute-start.8
  16.1 11.6 %collective-permute-start.7 = (bf16[128,1152]{1,0:T(8,128)(2,1)}, bf16[128,1152]{1,0:T(8,128)(2,1)S(1)}, u32[]{:S(2)}, u32[]{:S(2)}) collective-permute-start(bf16[128,1152]{1,0:T(8,128)(2,1)} %image_own.3), channel_id=1, source_target_pairs={{0,1},{1,0},{2,3},{3,2},{4,5},{5,4},{6,7},{7,6},{8,9},{9,8},{10,11... | collective-permute-start | bytes 884744 | tf_op jit(solution)/shard_map/band_exchange/ppermute | solution.py:53
  16.7 20.2 %collective-permute-start.6 = (bf16[128,1152]{1,0:T(8,128)(2,1)S(1)}, bf16[128,1152]{1,0:T(8,128)(2,1)S(1)}, u32[]{:S(2)}, u32[]{:S(2)}) collective-permute-start(bf16[128,1152]{1,0:T(8,128)(2,1)S(1)} %collective-permute-done.5.far), channel_id=1, source_target_pairs={{0,1},{1,0},{2,3},{3,2},{4,5},{5,4},{6,7},{7,6},{8,9},{9,8},{10,11... | collective-permute-start | bytes 884744 | tf_op jit(solution)/shard_map/band_exchange/ppermute | solution.py:53
  22.6 14.3 %collective-permute-start.4 = (bf16[128,1152]{1,0:T(8,128)(2,1)S(1)}, bf16[128,1152]{1,0:T(8,128)(2,1)S(1)}, u32[]{:S(2)}, u32[]{:S(2)}) collective-permute-start(bf16[128,1152]{1,0:T(8,128)(2,1)S(1)} %collective-permute-done.3.above), channel_id=1, source_target_pairs={{0,1},{1,0},{2,3},{3,2},{4,5},{5,4},{6,7},{7,6},{8,9},{9,8},{10,11... | collective-permute-start | bytes 884744 | tf_op jit(solution)/shard_map/band_exchange/ppermute | solution.py:53
  25.7 11.1 %collective-permute-start.2 = (bf16[128,1152]{1,0:T(8,128)(2,1)S(1)}, bf16[128,1152]{1,0:T(8,128)(2,1)S(1)}, u32[]{:S(2)}, u32[]{:S(2)}) collective-permute-start(bf16[128,1152]{1,0:T(8,128)(2,1)S(1)} %collective-permute-done.1.below), channel_id=1, source_target_pairs={{0,1},{1,0},{2,3},{3,2},{4,5},{5,4},{6,7},{7,6},{8,9},{9,8},{10,11... | collective-permute-start | bytes 884744 | tf_op jit(solution)/shard_map/band_exchange/ppermute | solution.py:53
  27.8 1.8 copy-start
  29.5 1.7 copy-start.1
  31.3 1.0 copy-start.2
  32.2 1.0 copy-start.3
  45.5 7.6 %collective-permute-start.9 = (bf16[144,1152]{1,0:T(8,128)(2,1)S(1)}, bf16[144,1152]{1,0:T(8,128)(2,1)S(1)}, u32[]{:S(2)}, u32[]{:S(2)}) collective-permute-start(bf16[144,1152]{1,0:T(8,128)(2,1)S(1)} %get-tuple-element.23), channel_id=1, source_target_pairs={{0,16},{1,65},{2,18},{3,67},{4,20},{5,69},{6,22},{7,71},{8,24},{9,... | collective-permute-start | bytes 995336 | tf_op jit(solution)/shard_map/sum_first/ppermute | solution.py:53
  45.6 7.5 %collective-permute-start.10 = (bf16[144,1152]{1,0:T(8,128)(2,1)S(1)}, bf16[144,1152]{1,0:T(8,128)(2,1)S(1)}, u32[]{:S(2)}, u32[]{:S(2)}) collective-permute-start(bf16[144,1152]{1,0:T(8,128)(2,1)S(1)} %get-tuple-element.25), channel_id=1, source_target_pairs={{0,48},{1,193},{2,50},{3,195},{4,52},{5,197},{6,54},{7,199},{8,56}... | collective-permute-start | bytes 995336 | tf_op jit(solution)/shard_map/sum_first/ppermute | solution.py:53
  48.3 8.4 %collective-permute-start.12 = (bf16[144,1152]{1,0:T(8,128)(2,1)S(1)}, bf16[144,1152]{1,0:T(8,128)(2,1)S(1)}, u32[]{:S(2)}, u32[]{:S(2)}) collective-permute-start(bf16[144,1152]{1,0:T(8,128)(2,1)S(1)} %get-tuple-element.27), channel_id=1, source_target_pairs={{0,16},{1,65},{2,18},{3,67},{4,20},{5,69},{6,22},{7,71},{8,24},{9,... | collective-permute-start | bytes 995336 | tf_op jit(solution)/shard_map/sum_first/ppermute | solution.py:53
  48.3 8.4 %collective-permute-start.13 = (bf16[144,1152]{1,0:T(8,128)(2,1)S(1)}, bf16[144,1152]{1,0:T(8,128)(2,1)S(1)}, u32[]{:S(2)}, u32[]{:S(2)}) collective-permute-start(bf16[144,1152]{1,0:T(8,128)(2,1)S(1)} %get-tuple-element.28), channel_id=1, source_target_pairs={{0,48},{1,193},{2,50},{3,195},{4,52},{5,197},{6,54},{7,199},{8,56}... | collective-permute-start | bytes 995336 | tf_op jit(solution)/shard_map/sum_first/ppermute | solution.py:53
  53.3 7.3 %collective-permute-start.11 = (bf16[144,1152]{1,0:T(8,128)(2,1)S(1)}, bf16[144,1152]{1,0:T(8,128)(2,1)S(1)}, u32[]{:S(2)}, u32[]{:S(2)}) collective-permute-start(bf16[144,1152]{1,0:T(8,128)(2,1)S(1)} %get-tuple-element.26), channel_id=1, source_target_pairs={{0,16},{1,65},{2,18},{3,67},{4,20},{5,69},{6,22},{7,71},{8,24},{9,... | collective-permute-start | bytes 995336 | tf_op jit(solution)/shard_map/sum_first/ppermute | solution.py:53
  53.4 7.2 %collective-permute-start.14 = (bf16[144,1152]{1,0:T(8,128)(2,1)S(1)}, bf16[144,1152]{1,0:T(8,128)(2,1)S(1)}, u32[]{:S(2)}, u32[]{:S(2)}) collective-permute-start(bf16[144,1152]{1,0:T(8,128)(2,1)S(1)} %get-tuple-element.29), channel_id=1, source_target_pairs={{0,48},{1,193},{2,50},{3,195},{4,52},{5,197},{6,54},{7,199},{8,56}... | collective-permute-start | bytes 995336 | tf_op jit(solution)/shard_map/sum_first/ppermute | solution.py:53
  104.8 39.3 %copy-start.4 = (bf16[4,72,1152]{2,1,0:T(8,128)(2,1)}, bf16[4,72,1152]{2,1,0:T(8,128)(2,1)S(1)}, u32[]{:S(2)}) copy-start(bf16[4,72,1152]{2,1,0:T(8,128)(2,1)S(1)} %all_to_all.23) | copy-start | bytes 1990660
  104.8 16.9 %collective-permute-start.16 = (bf16[288,1152]{1,0:T(8,128)(2,1)S(1)}, bf16[288,1152]{1,0:T(8,128)(2,1)S(1)}, u32[]{:S(2)}, u32[]{:S(2)}) collective-permute-start(bf16[288,1152]{1,0:T(8,128)(2,1)S(1)} %bitcast.18), channel_id=1, source_target_pairs={{0,48},{1,193},{2,50},{3,195},{4,52},{5,197},{6,54},{7,199},{8,56}... | collective-permute-start | bytes 1990664 | tf_op jit(solution)/shard_map/share_first/ppermute | solution.py:53
  107.2 15.5 %collective-permute-start.15 = (bf16[288,1152]{1,0:T(8,128)(2,1)S(1)}, bf16[288,1152]{1,0:T(8,128)(2,1)S(1)}, u32[]{:S(2)}, u32[]{:S(2)}) collective-permute-start(bf16[288,1152]{1,0:T(8,128)(2,1)S(1)} %bitcast.19), channel_id=1, source_target_pairs={{0,16},{1,65},{2,18},{3,67},{4,20},{5,69},{6,22},{7,71},{8,24},{9,... | collective-permute-start | bytes 1990664 | tf_op jit(solution)/shard_map/share_first/ppermute | solution.py:53
  107.2 35.0 %collective-permute-start.19 = (bf16[288,1152]{1,0:T(8,128)(2,1)S(1)}, bf16[288,1152]{1,0:T(8,128)(2,1)S(1)}, u32[]{:S(2)}, u32[]{:S(2)}) collective-permute-start(bf16[288,1152]{1,0:T(8,128)(2,1)S(1)} %bitcast.20), channel_id=1, source_target_pairs={{0,1},{1,0},{2,3},{3,2},{4,5},{5,4},{6,7},{7,6},{8,9},{9,8},{10,11... | collective-permute-start | bytes 1990664 | tf_op jit(solution)/shard_map/share_first/ppermute | solution.py:53
  121.7 22.4 %copy-start.5 = (bf16[288,1152]{1,0:T(8,128)(2,1)}, bf16[288,1152]{1,0:T(8,128)(2,1)S(1)}, u32[]{:S(2)}) copy-start(bf16[288,1152]{1,0:T(8,128)(2,1)S(1)} %collective-permute-done.16.refs_2_) | copy-start | bytes 1990660
  121.7 12.3 %collective-permute-start.18 = (bf16[144,1152]{1,0:T(8,128)(2,1)S(1)}, bf16[144,1152]{1,0:T(8,128)(2,1)S(1)}, u32[]{:S(2)}, u32[]{:S(2)}) collective-permute-start(bf16[144,1152]{1,0:T(8,128)(2,1)S(1)} %slice.14), channel_id=1, source_target_pairs={{0,48},{1,193},{2,50},{3,195},{4,52},{5,197},{6,54},{7,199},{8,56}... | collective-permute-start | bytes 995336 | tf_op jit(solution)/shard_map/share_first/ppermute | solution.py:53
  122.6 21.5 %copy-start.6 = (bf16[288,1152]{1,0:T(8,128)(2,1)}, bf16[288,1152]{1,0:T(8,128)(2,1)S(1)}, u32[]{:S(2)}) copy-start(bf16[288,1152]{1,0:T(8,128)(2,1)S(1)} %collective-permute-done.15.refs_1_) | copy-start | bytes 1990660
  122.7 15.7 %collective-permute-start.17 = (bf16[144,1152]{1,0:T(8,128)(2,1)S(1)}, bf16[144,1152]{1,0:T(8,128)(2,1)S(1)}, u32[]{:S(2)}, u32[]{:S(2)}) collective-permute-start(bf16[144,1152]{1,0:T(8,128)(2,1)S(1)} %slice.13), channel_id=1, source_target_pairs={{0,16},{1,65},{2,18},{3,67},{4,20},{5,69},{6,22},{7,71},{8,24},{9,... | collective-permute-start | bytes 995336 | tf_op jit(solution)/shard_map/share_first/ppermute | solution.py:53
  123.4 18.8 %collective-permute-start.21 = (bf16[288,1152]{1,0:T(8,128)(2,1)S(1)}, bf16[288,1152]{1,0:T(8,128)(2,1)S(1)}, u32[]{:S(2)}, u32[]{:S(2)}) collective-permute-start(bf16[288,1152]{1,0:T(8,128)(2,1)S(1)} %collective-permute-done.16.refs_2_), channel_id=1, source_target_pairs={{0,1},{1,0},{2,3},{3,2},{4,5},{5,4},{6,7},{7,6},{8,9},{9,8},{10,11... | collective-permute-start | bytes 1990664 | tf_op jit(solution)/shard_map/share_first/ppermute | solution.py:53
  133.9 10.2 %collective-permute-start.20 = (bf16[288,1152]{1,0:T(8,128)(2,1)S(1)}, bf16[288,1152]{1,0:T(8,128)(2,1)}, u32[]{:S(2)}, u32[]{:S(2)}) collective-permute-start(bf16[288,1152]{1,0:T(8,128)(2,1)S(1)} %collective-permute-done.15.refs_1_), channel_id=1, source_target_pairs={{0,1},{1,0},{2,3},{3,2},{4,5},{5,4},{6,7},{7,6},{8,9},{9,8},{10,11... | collective-permute-start | bytes 1990664 | tf_op jit(solution)/shard_map/share_first/ppermute | solution.py:53
  134.0 8.2 %copy-start.9 = (bf16[144,1152]{1,0:T(8,128)(2,1)}, bf16[144,1152]{1,0:T(8,128)(2,1)S(1)}, u32[]{:S(2)}) copy-start(bf16[144,1152]{1,0:T(8,128)(2,1)S(1)} %collective-permute-done.18.refs_4_) | copy-start | bytes 995332
  134.0 8.1 %collective-permute-start.23 = (bf16[144,1152]{1,0:T(8,128)(2,1)S(1)}, bf16[144,1152]{1,0:T(8,128)(2,1)S(1)}, u32[]{:S(2)}, u32[]{:S(2)}) collective-permute-start(bf16[144,1152]{1,0:T(8,128)(2,1)S(1)} %collective-permute-done.18.refs_4_), channel_id=1, source_target_pairs={{0,1},{1,0},{2,3},{3,2},{4,5},{5,4},{6,7},{7,6},{8,9},{9,8},{10,11... | collective-permute-start | bytes 995336 | tf_op jit(solution)/shard_map/share_first/ppermute | solution.py:53
  138.3 5.1 %copy-start.10 = (bf16[144,1152]{1,0:T(8,128)(2,1)}, bf16[144,1152]{1,0:T(8,128)(2,1)S(1)}, u32[]{:S(2)}) copy-start(bf16[144,1152]{1,0:T(8,128)(2,1)S(1)} %collective-permute-done.17.refs_3_) | copy-start | bytes 995332
  138.3 5.1 %collective-permute-start.22 = (bf16[144,1152]{1,0:T(8,128)(2,1)S(1)}, bf16[144,1152]{1,0:T(8,128)(2,1)S(1)}, u32[]{:S(2)}, u32[]{:S(2)}) collective-permute-start(bf16[144,1152]{1,0:T(8,128)(2,1)S(1)} %collective-permute-done.17.refs_3_), channel_id=1, source_target_pairs={{0,1},{1,0},{2,3},{3,2},{4,5},{5,4},{6,7},{7,6},{8,9},{9,8},{10,11... | collective-permute-start | bytes 995336 | tf_op jit(solution)/shard_map/share_first/ppermute | solution.py:53
  142.1 2.0 copy-start.7
  142.2 1.3 copy-start.11
  142.2 2.0 copy-start.8
  143.4 0.7 copy-start.12

commit v3 on v2

v3 whole, which is shorter than its diff:
```python
import functools

import jax
import jax.numpy as jnp
from jax import lax
from jax.experimental import pallas as pl
from jax.experimental.pallas import tpu as pltpu
from jax.sharding import PartitionSpec as P

NY, NX, NZ, CORES = 4, 4, 8, 2
N = NY * NX * NZ * CORES
epsilon = 1e-06
bf16, f32 = jnp.bfloat16, jnp.float32
MIB = 1 << 20


def index(y, x, z, c):
    return ((y % NY * NX + x % NX) * NZ + z % NZ) * CORES + c


PLACES = [
    (y, x, z, c) for y in range(NY) for x in range(NX) for z in range(NZ) for c in range(CORES)
]


def route(move):
    return [(index(*place), index(*move(*place))) for place in PLACES]


def groups(key):
    found = {}
    for place in PLACES:
        found.setdefault(key(*place), []).append(index(*place))
    return list(found.values())


def along_first(step):
    return route(lambda y, x, z, c: (y, x + step, z, c) if c == 0 else (y + step, x, z, c))


SWAP = route(lambda y, x, z, c: (y, x, z, 1 - c))
RIGHT, LEFT = along_first(1), along_first(-1)
SECOND = groups(lambda y, x, z, c: (c, z, x if c == 0 else y))
LINES = groups(lambda y, x, z, c: (c, x, y))
FAR = [(i, (i + 3) % N if i % 2 else (i - 3) % N) for i in range(N)]


def shifted(distance):
    return [(i, (i + distance) % N) for i in range(N)]


def send(block, pairs):
    return lax.ppermute(block, "dp", pairs)


def exchange(parts, members):
    return lax.all_to_all(parts, "dp", 0, 0, axis_index_groups=members, tiled=True)


def call(body, outs, scratch=(), limit=32, flops=0, aliases=()):
    def run(scalars, outside, *arrays):
        specs = (
            [pl.BlockSpec(memory_space=pltpu.SMEM)] * len(scalars)
            + [pl.BlockSpec(memory_space=pltpu.HBM)] * len(outside)
            + [pl.BlockSpec(memory_space=pltpu.VMEM)] * len(arrays)
        )
        held = [pltpu.with_memory_space_constraint(a, pltpu.VMEM) for a in arrays]
        outside = [pltpu.with_memory_space_constraint(a, pltpu.HBM) for a in outside]
        return pl.pallas_call(
            body,
            out_shape=[jax.ShapeDtypeStruct(s, d) for s, d in outs],
            in_specs=specs,
            out_specs=[pl.BlockSpec(memory_space=pltpu.VMEM)] * len(outs),
            scratch_shapes=list(scratch),
            input_output_aliases=dict(aliases),
            cost_estimate=pl.CostEstimate(flops=flops, bytes_accessed=0, transcendentals=0),
            compiler_params=pltpu.CompilerParams(vmem_limit_bytes=limit * MIB),
        )(*scalars, *outside, *held)

    return run


def embed(features, weight):
    projected = jnp.dot(features, weight, preferred_element_type=f32)
    length = jnp.sqrt(jnp.sum(projected * projected, axis=-1, keepdims=True) + epsilon)
    inverse = 1.0 / length
    return projected * inverse, inverse


def pull_back(gradient, unit_rows, inverse):
    radial = jnp.sum(gradient * unit_rows, axis=-1, keepdims=True)
    return ((gradient - unit_rows * radial) * inverse).astype(bf16)


def contract(a, b, da, db):
    return lax.dot_general(a, b, (((da,), (db,)), ((), ())), preferred_element_type=f32)


def add_head(head, x, back, before):
    step = head.shape[0] // 3
    for k in range(3):
        at = pl.ds(k * step, step)
        new = contract(x[:, at], back[...], 0, 0)
        head[at, :] = new if before is None else before[at, :] + new


def near_kernel(
    place, factors, text_hbm, image_hbm, text_w_hbm, image_w_hbm, text_other, image_other, target,
    image_near, text_w, image_emb, image_unit, image_norm, grad, head,
    text_near, image_w, back, sems,
):
    scale, bias = factors[0], factors[1]
    rows = text_other.shape[0]
    first = pl.ds(0, rows)
    moves = [
        pltpu.make_async_copy(image_hbm, image_near.at[first, :], sems.at[0]),
        pltpu.make_async_copy(image_w_hbm, image_w, sems.at[1]),
        pltpu.make_async_copy(text_hbm, text_near.at[first, :], sems.at[2]),
        pltpu.make_async_copy(text_w_hbm, text_w, sems.at[3]),
    ]
    for move in moves:
        move.start()
    image_near[pl.ds(rows, rows), :] = image_other[...]
    text_near[pl.ds(rows, rows), :] = text_other[...]
    moves[0].wait()
    moves[1].wait()
    unit, norm = embed(image_near[...], image_w[...])
    emb = unit.astype(bf16)
    image_emb[...] = emb
    image_unit[...] = unit
    image_norm[...] = norm
    moves[2].wait()
    moves[3].wait()
    unit, norm = embed(text_near[...], text_w[...])
    text_emb = unit.astype(bf16)
    logits = scale * contract(text_emb, emb, 1, 1) + bias
    labels = (lax.broadcasted_iota(jnp.int32, logits.shape, 1) == target[...]).astype(f32)
    coefficient = (jax.nn.sigmoid(logits) - labels).astype(bf16)

    @pl.when(place[0] == 0)
    def _():
        gradient = scale * jnp.dot(coefficient, emb, preferred_element_type=f32)
        back[...] = pull_back(gradient, unit, norm)
        add_head(head, text_near, back, None)

    @pl.when(place[0] != 0)
    def _():
        grad[...] = contract(coefficient, text_emb, 0, 0)


def gate_kernel(*refs):
    pass


def visit(place, factors, blocks, text_w, image_emb, mine, xs, backs, grad_before, grad):
    scale, bias = factors[0], factors[1]
    rows = blocks[0].shape[0]
    for k, block in enumerate(blocks):
        xs[pl.ds(rows * k, rows), :] = block[...]
    unit, norm = embed(xs[...], text_w[...])
    emb = unit.astype(bf16)
    logits = scale * contract(emb, image_emb[...], 1, 1) + bias
    row = lax.broadcasted_iota(jnp.int32, logits.shape, 0)
    column = lax.broadcasted_iota(jnp.int32, logits.shape, 1)
    inside = jnp.logical_or(row < 2 * rows, (column < rows) == mine)
    coefficient = jnp.where(inside, jax.nn.sigmoid(logits), 0.0).astype(bf16)

    @pl.when(place[0] == 0)
    def _():
        gradient = scale * jnp.dot(coefficient, image_emb[...], preferred_element_type=f32)
        backs[...] = pull_back(gradient, unit, norm)

    @pl.when(place[0] != 0)
    def _():
        grad[...] = grad_before[...] + contract(coefficient, emb, 0, 0)


def received_kernel(
    place, factors, below, above, far, text_w, image_emb, grad_before, head_before,
    grad, head, xs, backs,
):
    visit(
        place, factors, (below, above, far), text_w, image_emb, True, xs, backs, grad_before, grad
    )

    @pl.when(place[0] == 0)
    def _():
        add_head(head, xs, backs, head_before)


def last_kernel(
    place, factors, below, above, far, text_w, image_emb, grad_before, head_before,
    image_near, image_unit, image_norm,
    own, right, left, far_right, far_left, grad, head, xs, backs,
):
    visit(
        place, factors, (below, above, far), text_w, image_emb, False, xs, backs, grad_before, grad
    )

    @pl.when(place[0] == 0)
    def _():
        add_head(head, xs, backs, head_before)

    @pl.when(place[0] != 0)
    def _():
        back = pull_back(factors[0] * grad[...], image_unit[...], image_norm[...])
        add_head(head, image_near, back, None)

    slab = head.shape[0] // 4
    half = slab // 2

    def part(turn, upper, size):
        start = lax.rem(place[1] + turn, 4) * slab + upper
        return head[pl.ds(pl.multiple_of(start, 16), size), :].astype(bf16)

    far_right[...] = part(2, 0, half)
    far_left[...] = part(2, half, half)
    right[...] = part(1, 0, slab)
    left[...] = part(3, 0, slab)
    own[...] = part(0, 0, slab)


def add_kernel(right, upper, left, lower, right_sum, left_sum):
    half = upper.shape[0]
    first, second = pl.ds(0, half), pl.ds(half, half)
    right_sum[first, :] = (right[first, :].astype(f32) + upper[...].astype(f32)).astype(bf16)
    right_sum[second, :] = right[second, :]
    left_sum[first, :] = left[first, :]
    left_sum[second, :] = (left[second, :].astype(f32) + lower[...].astype(f32)).astype(bf16)


def join_kernel(own, a, b, out):
    out[...] = (own[...].astype(f32) + a[...].astype(f32) + b[...].astype(f32)).astype(bf16)


def pack_kernel(own, left_top, right_bottom, to_right, to_left):
    half = left_top.shape[0]
    first, second = pl.ds(0, half), pl.ds(half, half)
    to_right[first, :] = own[second, :]
    to_right[second, :] = left_top[...]
    to_left[first, :] = own[first, :]
    to_left[second, :] = right_bottom[...]


def write_kernel(place, *refs):
    mine, theirs, (text, image, sems) = refs[:5], refs[5:10], refs[10:]
    slab = mine[0].shape[0]
    half = slab // 2

    def copies(pieces, position, out, first):
        own, left_top, right_bottom, from_left, from_right = pieces
        upper, lower = pl.ds(0, half), pl.ds(half, half)
        placed = [
            (own, 0, 0),
            (left_top, 3, 0),
            (right_bottom, 1, 1),
            (from_left.at[upper, :], 3, 1),
            (from_left.at[lower, :], 2, 0),
            (from_right.at[upper, :], 1, 0),
            (from_right.at[lower, :], 2, 1),
        ]
        moves = []
        for k, (piece, turn, part) in enumerate(placed):
            start = lax.rem(position + turn, 4) * slab + part * half
            target = out.at[pl.ds(pl.multiple_of(start, 16), piece.shape[0]), :]
            moves.append(pltpu.make_async_copy(piece, target, sems.at[first + k]))
        return moves

    def go(moves):
        for move in moves:
            move.start()
        for move in moves:
            move.wait()

    @pl.when(place[0] == 0)
    def _():
        go(copies(mine, place[1], text, 0) + copies(theirs, place[2], image, 7))

    @pl.when(place[0] != 0)
    def _():
        go(copies(mine, place[1], image, 0) + copies(theirs, place[2], text, 7))


def on_device(text_x, image_x, text_w, image_w, position, log_scale, shift):
    rows, width = text_x.shape
    depth = text_w.shape[0]
    slab = depth // 4
    half = slab // 2
    me = lax.axis_index("dp")
    core = lax.rem(me, CORES)
    x = lax.rem(me // (NZ * CORES), NX)
    y = me // (NX * NZ * CORES)
    place = jnp.stack([core, jnp.where(core == 0, x, y), jnp.where(core == 0, y, x)])
    place = place.astype(jnp.int32)
    factors = jnp.concatenate([jnp.exp(log_scale), shift])
    with jax.named_scope("band_exchange"):
        below = send(text_x, shifted(2))
        above = send(text_x, shifted(-2))
        far = send(text_x, FAR)
        text_other = send(text_x, SWAP)
        image_other = send(image_x, SWAP)
        target = jnp.concatenate([position, send(position, SWAP) + rows])[:, None]
    pair = ((2 * rows, width), bf16)
    pair_f32 = ((2 * rows, width), f32)
    total = ((depth, width), f32)
    matrix = pltpu.VMEM((depth, width), bf16)
    blocks = pltpu.VMEM((3 * rows, width), bf16)
    piece = ((slab, width), bf16)
    near = call(
        near_kernel,
        [pair, ((depth, width), bf16), pair, pair_f32, ((2 * rows, 1), f32), pair_f32, total],
        [pltpu.VMEM(*pair), matrix, pltpu.VMEM(*pair), pltpu.SemaphoreType.DMA((4,))],
        flops=4 * 10**9,
    )
    with jax.named_scope("near"):
        image_near, weight, image_emb, image_unit, image_norm, grad, head = near(
            (place, factors), (text_x, image_x, text_w, image_w), text_other, image_other, target
        )
    with jax.named_scope("between"):
        block = ((rows, width), bf16)
        below, above, far = call(gate_kernel, [block] * 3, aliases=[(0, 0), (1, 1), (2, 2)])(
            (), (), below, above, far, image_norm
        )
        below_other = send(below, SWAP)
        above_other = send(above, SWAP)
        far_other = send(far, SWAP)
    with jax.named_scope("received"):
        grad, head = call(received_kernel, [pair_f32, total], [blocks, blocks], flops=4 * 10**9)(
            (place, factors), (), below, above, far, weight, image_emb, grad, head
        )
    with jax.named_scope("last"):
        own, right, left, far_right, far_left = call(
            last_kernel,
            [piece, piece, piece, ((half, width), bf16), ((half, width), bf16)],
            [pltpu.VMEM(*pair_f32), pltpu.VMEM(*total), blocks, blocks],
            flops=4 * 10**9,
        )(
            (place, factors), (), below_other, above_other, far_other, weight, image_emb, grad,
            head, image_near, image_unit, image_norm,
        )
    with jax.named_scope("sum_first"):
        from_left = send(far_right, RIGHT)
        from_right = send(far_left, LEFT)
        right, left = call(add_kernel, [piece, piece])((), (), right, from_left, left, from_right)
        from_left = send(right, RIGHT)
        from_right = send(left, LEFT)
        [part] = call(join_kernel, [piece])((), (), own, from_left, from_right)
    with jax.named_scope("sum_second"):
        part = exchange(part.reshape(4, slab // 4, width), SECOND)
        part = jnp.sum(part.astype(f32), axis=0).astype(bf16)
    with jax.named_scope("sum_lines"):
        tiles = (
            part.reshape(slab // 32, 8, width // 128, 128).transpose(0, 2, 1, 3).reshape(-1, 8, 128)
        )
        count = tiles.shape[0]
        each = -(-count // NZ)
        tiles = jnp.concatenate([tiles, jnp.zeros((each * NZ - count, 8, 128), bf16)])
        tiles = exchange(tiles, LINES).reshape(NZ, each, 8, 128)
        tiles = jnp.sum(tiles.astype(f32), axis=0).astype(bf16)
    with jax.named_scope("share_lines"):
        tiles = exchange(jnp.tile(tiles, (NZ, 1, 1)), LINES)[:count]
        part = (
            tiles.reshape(slab // 32, width // 128, 8, 128).transpose(0, 2, 1, 3).reshape(-1, width)
        )
    with jax.named_scope("share_second"):
        whole = exchange(jnp.tile(part[None], (4, 1, 1)), SECOND)
        own = whole.reshape(slab, width)
    with jax.named_scope("share_first"):
        left_top = send(own[:half], RIGHT)
        right_bottom = send(own[half:], LEFT)
        to_right, to_left = call(pack_kernel, [piece, piece])(
            (), (), own, left_top, right_bottom
        )
        mine = [own, left_top, right_bottom, send(to_right, RIGHT), send(to_left, LEFT)]
        theirs = [send(one, SWAP) for one in mine]
    with jax.named_scope("write"):
        pieces = mine + theirs
        return pl.pallas_call(
            write_kernel,
            out_shape=[jax.ShapeDtypeStruct((depth, width), bf16)] * 2,
            in_specs=[pl.BlockSpec(memory_space=pltpu.SMEM)]
            + [pl.BlockSpec(memory_space=pltpu.VMEM)] * len(pieces),
            out_specs=[pl.BlockSpec(memory_space=pl.ANY)] * 2,
            scratch_shapes=[pltpu.SemaphoreType.DMA((14,))],
            compiler_params=pltpu.CompilerParams(vmem_limit_bytes=32 * MIB),
        )(place, *[pltpu.with_memory_space_constraint(a, pltpu.VMEM) for a in pieces])


def solution(mesh):
    return jax.shard_map(
        on_device,
        mesh=mesh,
        in_specs=(P("dp", None), P("dp", None), P(), P(), P("dp"), P(), P()),
        out_specs=(P(), P()),
        check_vma=False,
    )
```

time: 307 us -> 140 us (0.46)
  Pallas kernels: 175 us -> 18 us
  starting transfers between devices: 70.3 us -> 48.9 us
  waiting for transfers between devices: 7.8 us -> 25.4 us
  local copies, waits for them, and re-layouts: 6.46 us -> 0.29 us
    pallas_call x1, Pallas kernels: 162 us -> 3.03 us  [on_device(): pl.pallas_call(write_kernel, out_shape=[jax.ShapeDtypeStruct((depth, widt...]
    ppermute x24 -> x22, starting transfers between devices: 70.3 us -> 48.9 us  [send(): return lax.ppermute(block, 'dp', pairs)]
    ppermute x24 -> x22, waiting for transfers between devices: 7.8 us -> 25.4 us  [send(): return lax.ppermute(block, 'dp', pairs)]
    unnamed x26 -> x0, local copies, waits for them, and re-layouts: 6.18 us -> none
    pallas_call x4 -> x7, Pallas kernels: 12.8 us -> 15 us  [run(): pl.pallas_call(body, out_shape=[jax.ShapeDtypeStruct(s, d) for s, d in ou...]
  transfers between devices with their start and end apart: 24 -> 22, of which waited for: 4 -> 7; matrix products, arithmetic and copies ran while one was open for 0% -> 1% of each run, Pallas kernels for 1% -> 7%
where the time goes in v3:
time: 140 us; the launch traced here: 139 us
  starting transfers between devices  48.9 us (35%)
  blocking collectives  43.5 us (31%)
  waiting for transfers between devices  25.4 us (18%)
  Pallas kernels  18 us (13%)
  between operations  2.32 us (2%)
    ppermute x22, starting transfers between devices, send(): return lax.ppermute(block, 'dp', pairs)  48.9 us
    all_to_all x4, blocking collectives, exchange(): lax.all_to_all(parts, 'dp', 0, 0, axis_index_groups=members, tiled=True)  43.5 us
    ppermute x22, waiting for transfers between devices, send(): return lax.ppermute(block, 'dp', pairs)  25.4 us
    pallas_call x7, Pallas kernels, run(): pl.pallas_call(body, out_shape=[jax.ShapeDtypeStruct(s, d) for s, d in ou...  15 us
    pallas_call x1, Pallas kernels, on_device(): pl.pallas_call(write_kernel, out_shape=[jax.ShapeDtypeStruct((depth, widt...  3.03 us
  transfers between devices with their start and end apart: 22, of which 7 were waited for; matrix products, arithmetic and copies ran while one was open for 1% of the time, Pallas kernels for 7%

profile of v3, /device:TPU:1, one launch (start us, length us, event | category | flops | bytes accessed | tf_op | source)
XLA Modules:
  0.0 139.4 jit_solution(16625850348133402044)
XLA Ops:
  0.6 4.5 %collective-permute-start.2 = (bf16[128,1152]{1,0:T(8,128)(2,1)}, bf16[128,1152]{1,0:T(8,128)(2,1)S(1)}, u32[]{:S(2)}, u32[]{:S(2)}) collective-permute-start(bf16[128,1152]{1,0:T(8,128)(2,1)} %text_hbm.1), channel_id=1, source_target_pairs={{0,253},{1,4},{2,255},{3,6},{4,1},{5,8},{6,3},{7,10},{8,5},{9,12},... | collective-permute-start | bytes 884744 | tf_op jit(solution)/shard_map/band_exchange/ppermute | solution.py:53
  5.1 6.8 %collective-permute-start.1 = (bf16[128,1152]{1,0:T(8,128)(2,1)}, bf16[128,1152]{1,0:T(8,128)(2,1)S(1)}, u32[]{:S(2)}, u32[]{:S(2)}) collective-permute-start(bf16[128,1152]{1,0:T(8,128)(2,1)} %text_hbm.1), channel_id=1, source_target_pairs={{0,254},{1,255},{2,0},{3,1},{4,2},{5,3},{6,4},{7,5},{8,6},{9,7},{1... | collective-permute-start | bytes 884744 | tf_op jit(solution)/shard_map/band_exchange/ppermute | solution.py:53
  11.9 0.0 collective-permute-start
  11.9 2.8 %collective-permute-start.3 = (bf16[128,1152]{1,0:T(8,128)(2,1)}, bf16[128,1152]{1,0:T(8,128)(2,1)S(1)}, u32[]{:S(2)}, u32[]{:S(2)}) collective-permute-start(bf16[128,1152]{1,0:T(8,128)(2,1)} %text_hbm.1), channel_id=1, source_target_pairs={{0,1},{1,0},{2,3},{3,2},{4,5},{5,4},{6,7},{7,6},{8,9},{9,8},{10,11... | collective-permute-start | bytes 884744 | tf_op jit(solution)/shard_map/band_exchange/ppermute | solution.py:53
  14.6 0.0 collective-permute-start.5
  16.0 0.1 pad_maximum_fusion.factors
  16.1 0.1 pad_add_fusion.1.place
  16.1 0.0 collective-permute-done.5
  16.1 0.5 collective-permute-start.4
  16.7 0.7 pad_add_fusion
  17.3 0.1 copy.13.target
  17.5 0.6 collective-permute-done.4.image_other
  18.1 0.0 collective-permute-done.3.text_other
  18.1 5.8 %near.1 = (bf16[256,1152]{1,0:T(8,128)(2,1)S(1)}, bf16[1152,1152]{1,0:T(8,128)(2,1)S(1)}, bf16[256,1152]{1,0:T(8,128)(2,1)S(1)}, f32[256,1152]{1,0:T(8,128)S(1)}...) custom-call(s32[3]{0:T(128)S(1)} %pad_add_fusion.1.place, ...), custom_call_target="tpu_custom_call" | custom-call | flops 4000000000 | tf_op jit(solution)/shard_map/near/pallas_call | solution.py:69
  23.9 0.0 collective-permute-done.2.refs_2_
  23.9 0.0 collective-permute-done.1.refs_1_
  23.9 0.3 collective-permute-done.refs_0_
  24.2 2.7 %collective-permute-start.6 = (bf16[128,1152]{1,0:T(8,128)(2,1)S(1)}, bf16[128,1152]{1,0:T(8,128)(2,1)S(1)}, u32[]{:S(2)}, u32[]{:S(2)}) collective-permute-start(bf16[128,1152]{1,0:T(8,128)(2,1)S(1)} %get-tuple-element.24.below), channel_id=1, source_target_pairs={{0,1},{1,0},{2,3},{3,2},{4,5},{5,4},{6,7},{7,6},{8,9},{9,8},{10,11... | collective-permute-start | bytes 884744 | tf_op jit(solution)/shard_map/between/ppermute | solution.py:53
  26.9 0.0 collective-permute-start.7
  26.9 0.5 collective-permute-start.8
  27.4 3.6 %received.1 = (f32[256,1152]{1,0:T(8,128)S(1)}, f32[1152,1152]{1,0:T(8,128)S(1)}) custom-call(s32[3]{0:T(128)S(1)} %pad_add_fusion.1.place, f32[2]{0:T(128)S(1)} %pad_maximum_fusion.factors, bf16[128,1152]{1,0:T(8,128)(2,1)S(1)} %get-tuple-element.24.below, bf16[128,1152]{1,0:T(8,128)(2,1)S(1)} %get-tuple-element.25.above, ...), custom_call_target="tpu_custom_call" | custom-call | flops 4000000000 | tf_op jit(solution)/shard_map/received/pallas_call | solution.py:69
  31.1 0.0 collective-permute-done.6.below
  31.1 0.0 collective-permute-done.7.above
  31.1 0.0 collective-permute-done.8.far
  31.1 5.0 %last.1 = (bf16[288,1152]{1,0:T(8,128)(2,1)S(1)}, bf16[288,1152]{1,0:T(8,128)(2,1)S(1)}, bf16[288,1152]{1,0:T(8,128)(2,1)S(1)}, bf16[144,1152]{1,0:T(8,128)(2,1)S(1)}, bf16[144,1152]{1,0:T(8,128)(2,1)S(1)}) custom-call(s32[3]{0:T(128)S(1)} %pad_add_fusion.1.place, f32[2]{0:T(128)S(1)} %pad_maximum_fusion.factors, ...), custom_call_target="tpu_custom_call" | custom-call | flops 4000000000 | tf_op jit(solution)/shard_map/last/pallas_call | solution.py:69
  36.1 0.1 collective-permute-start.9
  36.2 2.7 %collective-permute-start.10 = (bf16[144,1152]{1,0:T(8,128)(2,1)S(1)}, bf16[144,1152]{1,0:T(8,128)(2,1)S(1)}, u32[]{:S(2)}, u32[]{:S(2)}) collective-permute-start(bf16[144,1152]{1,0:T(8,128)(2,1)S(1)} %get-tuple-element.39), channel_id=1, source_target_pairs={{0,48},{1,193},{2,50},{3,195},{4,52},{5,197},{6,54},{7,199},{8,56}... | collective-permute-start | bytes 995336 | tf_op jit(solution)/shard_map/sum_first/ppermute | solution.py:53
  38.9 4.8 %collective-permute-done.9.upper = bf16[144,1152]{1,0:T(8,128)(2,1)S(1)} collective-permute-done((bf16[144,1152]{1,0:T(8,128)(2,1)S(1)}, bf16[144,1152]{1,0:T(8,128)(2,1)S(1)}, u32[]{:S(2)}, u32[]{:S(2)}) %collective-permute-start.9) | collective-permute-done | bytes 331808 | tf_op jit(solution)/shard_map/sum_first/ppermute | solution.py:53
  43.7 0.0 collective-permute-done.10.lower
  43.7 0.2 sum_first.2
  43.9 0.1 collective-permute-start.11
  44.0 2.8 %collective-permute-start.12 = (bf16[288,1152]{1,0:T(8,128)(2,1)S(1)}, bf16[288,1152]{1,0:T(8,128)(2,1)S(1)}, u32[]{:S(2)}, u32[]{:S(2)}) collective-permute-start(bf16[288,1152]{1,0:T(8,128)(2,1)S(1)} %get-tuple-element.41), channel_id=1, source_target_pairs={{0,48},{1,193},{2,50},{3,195},{4,52},{5,197},{6,54},{7,199},{8,56}... | collective-permute-start | bytes 1990664 | tf_op jit(solution)/shard_map/sum_first/ppermute | solution.py:53
  46.7 8.3 %collective-permute-done.11.a = bf16[288,1152]{1,0:T(8,128)(2,1)S(1)} collective-permute-done((bf16[288,1152]{1,0:T(8,128)(2,1)S(1)}, bf16[288,1152]{1,0:T(8,128)(2,1)S(1)}, u32[]{:S(2)}, u32[]{:S(2)}) %collective-permute-start.11) | collective-permute-done | bytes 663584 | tf_op jit(solution)/shard_map/sum_first/ppermute | solution.py:53
  55.0 0.0 collective-permute-done.12.b
  55.0 0.2 sum_first.3
  55.2 10.1 %all_to_all.20 = bf16[4,72,1152]{2,1,0:T(8,128)(2,1)S(1)} all-to-all(bf16[4,72,1152]{2,1,0:T(8,128)(2,1)S(1)} %bitcast.23), channel_id=1, replica_groups={{0,64,128,192},{1,17,33,49},{2,66,130,194},{3,19,35,51},{4,68,132,196},..., dimensions={0} | all-to-all | bytes 1327104 | tf_op jit(solution)/shard_map/sum_second/all_to_all | solution.py:57
  65.3 0.1 reduce_sum.24
  65.4 12.5 %all_to_all.21 = bf16[88,8,128]{2,1,0:T(8,128)(2,1)S(1)} all-to-all(bf16[88,8,128]{2,1,0:T(8,128)(2,1)S(1)} %concatenate.11), channel_id=1, replica_groups={{0,2,4,6,8,10,12,14},{1,3,5,7,9,11,13,15},{16,18,20,22,24,26,28,30},{17..., dimensions={0} | all-to-all | bytes 360448 | tf_op jit(solution)/shard_map/sum_lines/all_to_all | solution.py:57
  78.0 10.8 %all_to_all.22 = bf16[88,8,128]{2,1,0:T(8,128)(2,1)S(1)} all-to-all(bf16[88,8,128]{2,1,0:T(8,128)(2,1)S(1)} %bitcast.25), channel_id=1, replica_groups={{0,2,4,6,8,10,12,14},{1,3,5,7,9,11,13,15},{16,18,20,22,24,26,28,30},{17..., dimensions={0} | all-to-all | bytes 360448 | tf_op jit(solution)/shard_map/share_lines/all_to_all | solution.py:57
  88.9 10.1 %all_to_all.23 = bf16[4,72,1152]{2,1,0:T(8,128)(2,1)S(1)} all-to-all(bf16[4,72,1152]{2,1,0:T(8,128)(2,1)S(1)} %tile.20), channel_id=1, replica_groups={{0,64,128,192},{1,17,33,49},{2,66,130,194},{3,19,35,51},{4,68,132,196},..., dimensions={0} | all-to-all | bytes 1327104 | tf_op jit(solution)/shard_map/share_second/all_to_all | solution.py:57
  99.0 0.1 fusion
  99.1 1.3 collective-permute-start.13
  100.4 2.2 %collective-permute-start.14 = (bf16[144,1152]{1,0:T(8,128)(2,1)S(1)}, bf16[144,1152]{1,0:T(8,128)(2,1)S(1)}, u32[]{:S(2)}, u32[]{:S(2)}) collective-permute-start(bf16[144,1152]{1,0:T(8,128)(2,1)S(1)} %bitcast.28), channel_id=1, source_target_pairs={{0,48},{1,193},{2,50},{3,195},{4,52},{5,197},{6,54},{7,199},{8,56}... | collective-permute-start | bytes 995336 | tf_op jit(solution)/shard_map/share_first/ppermute | solution.py:53
  102.6 8.2 %collective-permute-done.13.left_top.refs_1_ = bf16[144,1152]{1,0:T(8,128)(2,1)S(1)} collective-permute-done((bf16[144,1152]{1,0:T(8,128)(2,1)S(1)}, bf16[144,1152]{1,0:T(8,128)(2,1)S(1)}, u32[]{:S(2)}, u32[]{:S(2)}) %collective-permute-start.13) | collective-permute-done | bytes 331808 | tf_op jit(solution)/shard_map/share_first/ppermute | solution.py:53
  110.8 0.0 collective-permute-done.14.right_bottom.refs_2_
  110.8 0.1 share_first.1
  110.9 0.1 collective-permute-start.15
  111.0 2.7 %collective-permute-start.16 = (bf16[288,1152]{1,0:T(8,128)(2,1)S(1)}, bf16[288,1152]{1,0:T(8,128)(2,1)S(1)}, u32[]{:S(2)}, u32[]{:S(2)}) collective-permute-start(bf16[288,1152]{1,0:T(8,128)(2,1)S(1)} %get-tuple-element.43), channel_id=1, source_target_pairs={{0,48},{1,193},{2,50},{3,195},{4,52},{5,197},{6,54},{7,199},{8,56}... | collective-permute-start | bytes 1990664 | tf_op jit(solution)/shard_map/share_first/ppermute | solution.py:53
  113.7 10.2 %collective-permute-start.17 = (bf16[288,1152]{1,0:T(8,128)(2,1)S(1)}, bf16[288,1152]{1,0:T(8,128)(2,1)S(1)}, u32[]{:S(2)}, u32[]{:S(2)}) collective-permute-start(bf16[288,1152]{1,0:T(8,128)(2,1)S(1)} %bitcast.21), channel_id=1, source_target_pairs={{0,1},{1,0},{2,3},{3,2},{4,5},{5,4},{6,7},{7,6},{8,9},{9,8},{10,11... | collective-permute-start | bytes 1990664 | tf_op jit(solution)/shard_map/share_first/ppermute | solution.py:53
  123.9 0.0 collective-permute-done.15.refs_3_
  123.9 8.6 %collective-permute-start.20 = (bf16[288,1152]{1,0:T(8,128)(2,1)S(1)}, bf16[288,1152]{1,0:T(8,128)(2,1)S(1)}, u32[]{:S(2)}, u32[]{:S(2)}) collective-permute-start(bf16[288,1152]{1,0:T(8,128)(2,1)S(1)} %collective-permute-done.15.refs_3_), channel_id=1, source_target_pairs={{0,1},{1,0},{2,3},{3,2},{4,5},{5,4},{6,7},{7,6},{8,9},{9,8},{10,11... | collective-permute-start | bytes 1990664 | tf_op jit(solution)/shard_map/share_first/ppermute | solution.py:53
  132.5 0.0 collective-permute-done.16.refs_4_
  132.5 0.0 collective-permute-start.21
  132.5 0.5 collective-permute-start.18
  133.1 0.0 collective-permute-start.19
  133.1 2.6 %collective-permute-done.18.refs_6_ = bf16[144,1152]{1,0:T(8,128)(2,1)S(1)} collective-permute-done((bf16[144,1152]{1,0:T(8,128)(2,1)S(1)}, bf16[144,1152]{1,0:T(8,128)(2,1)S(1)}, u32[]{:S(2)}, u32[]{:S(2)}) %collective-permute-start.18) | collective-permute-done | bytes 331808 | tf_op jit(solution)/shard_map/share_first/ppermute | solution.py:53
  135.7 0.5 collective-permute-done.19.refs_7_
  136.2 0.0 collective-permute-done.17.refs_5_
  136.2 0.0 collective-permute-done.20.refs_8_
  136.2 0.0 collective-permute-done.21.refs_9_
  136.2 3.0 %write.1 = (bf16[1152,1152]{1,0:T(8,128)(2,1)}, bf16[1152,1152]{1,0:T(8,128)(2,1)}) custom-call(s32[3]{0:T(128)S(1)} %pad_add_fusion.1.place, bf16[288,1152]{1,0:T(8,128)(2,1)S(1)} %bitcast.22, bf16[144,1152]{1,0:T(8,128)(2,1)S(1)} %collective-permute-done.13.left_top.refs_1_, bf16[144,1152]{1,0:T(8,128)(2,1)S(1)} %collective-permute-done.14.right_bottom.refs_2_, ...), custom_call_target="tpu_custom_call" | custom-call | tf_op jit(solution)/shard_map/write/pallas_call | solution.py:378
  (7 shorter events, 0.1 us)
Async XLA Ops:
  0.6 23.3 %collective-permute-start.2 = (bf16[128,1152]{1,0:T(8,128)(2,1)}, bf16[128,1152]{1,0:T(8,128)(2,1)S(1)}, u32[]{:S(2)}, u32[]{:S(2)}) collective-permute-start(bf16[128,1152]{1,0:T(8,128)(2,1)} %text_hbm.1), channel_id=1, source_target_pairs={{0,253},{1,4},{2,255},{3,6},{4,1},{5,8},{6,3},{7,10},{8,5},{9,12},... | collective-permute-start | bytes 884744 | tf_op jit(solution)/shard_map/band_exchange/ppermute | solution.py:53
  5.1 18.8 %collective-permute-start.1 = (bf16[128,1152]{1,0:T(8,128)(2,1)}, bf16[128,1152]{1,0:T(8,128)(2,1)S(1)}, u32[]{:S(2)}, u32[]{:S(2)}) collective-permute-start(bf16[128,1152]{1,0:T(8,128)(2,1)} %text_hbm.1), channel_id=1, source_target_pairs={{0,254},{1,255},{2,0},{3,1},{4,2},{5,3},{6,4},{7,5},{8,6},{9,7},{1... | collective-permute-start | bytes 884744 | tf_op jit(solution)/shard_map/band_exchange/ppermute | solution.py:53
  11.9 12.4 %collective-permute-start = (bf16[128,1152]{1,0:T(8,128)(2,1)}, bf16[128,1152]{1,0:T(8,128)(2,1)S(1)}, u32[]{:S(2)}, u32[]{:S(2)}) collective-permute-start(bf16[128,1152]{1,0:T(8,128)(2,1)} %text_hbm.1), channel_id=1, source_target_pairs={{0,2},{1,3},{2,4},{3,5},{4,6},{5,7},{6,8},{7,9},{8,10},{9,11},{10,... | collective-permute-start | bytes 884744 | tf_op jit(solution)/shard_map/band_exchange/ppermute | solution.py:53
  11.9 6.2 %collective-permute-start.3 = (bf16[128,1152]{1,0:T(8,128)(2,1)}, bf16[128,1152]{1,0:T(8,128)(2,1)S(1)}, u32[]{:S(2)}, u32[]{:S(2)}) collective-permute-start(bf16[128,1152]{1,0:T(8,128)(2,1)} %text_hbm.1), channel_id=1, source_target_pairs={{0,1},{1,0},{2,3},{3,2},{4,5},{5,4},{6,7},{7,6},{8,9},{9,8},{10,11... | collective-permute-start | bytes 884744 | tf_op jit(solution)/shard_map/band_exchange/ppermute | solution.py:53
  14.6 1.5 %collective-permute-start.5 = (s32[128]{0:T(128)}, s32[128]{0:T(128)S(1)}, u32[]{:S(2)}, u32[]{:S(2)}) collective-permute-start(s32[128]{0:T(128)} %param.11), channel_id=1, source_target_pairs={{0,1},{1,0},{2,3},{3,2},{4,5},{5,4},{6,7},{7,6},{8,9},{9,8},{10,11... | collective-permute-start | bytes 1544 | tf_op jit(solution)/shard_map/band_exchange/ppermute | solution.py:53
  16.1 2.0 %collective-permute-start.4 = (bf16[128,1152]{1,0:T(8,128)(2,1)}, bf16[128,1152]{1,0:T(8,128)(2,1)S(1)}, u32[]{:S(2)}, u32[]{:S(2)}) collective-permute-start(bf16[128,1152]{1,0:T(8,128)(2,1)} %image_hbm.1), channel_id=1, source_target_pairs={{0,1},{1,0},{2,3},{3,2},{4,5},{5,4},{6,7},{7,6},{8,9},{9,8},{10,11... | collective-permute-start | bytes 884744 | tf_op jit(solution)/shard_map/band_exchange/ppermute | solution.py:53
  24.2 6.8 %collective-permute-start.6 = (bf16[128,1152]{1,0:T(8,128)(2,1)S(1)}, bf16[128,1152]{1,0:T(8,128)(2,1)S(1)}, u32[]{:S(2)}, u32[]{:S(2)}) collective-permute-start(bf16[128,1152]{1,0:T(8,128)(2,1)S(1)} %get-tuple-element.24.below), channel_id=1, source_target_pairs={{0,1},{1,0},{2,3},{3,2},{4,5},{5,4},{6,7},{7,6},{8,9},{9,8},{10,11... | collective-permute-start | bytes 884744 | tf_op jit(solution)/shard_map/between/ppermute | solution.py:53
  26.9 4.1 %collective-permute-start.7 = (bf16[128,1152]{1,0:T(8,128)(2,1)S(1)}, bf16[128,1152]{1,0:T(8,128)(2,1)S(1)}, u32[]{:S(2)}, u32[]{:S(2)}) collective-permute-start(bf16[128,1152]{1,0:T(8,128)(2,1)S(1)} %get-tuple-element.25.above), channel_id=1, source_target_pairs={{0,1},{1,0},{2,3},{3,2},{4,5},{5,4},{6,7},{7,6},{8,9},{9,8},{10,11... | collective-permute-start | bytes 884744 | tf_op jit(solution)/shard_map/between/ppermute | solution.py:53
  26.9 4.2 %collective-permute-start.8 = (bf16[128,1152]{1,0:T(8,128)(2,1)S(1)}, bf16[128,1152]{1,0:T(8,128)(2,1)S(1)}, u32[]{:S(2)}, u32[]{:S(2)}) collective-permute-start(bf16[128,1152]{1,0:T(8,128)(2,1)S(1)} %get-tuple-element.26.far), channel_id=1, source_target_pairs={{0,1},{1,0},{2,3},{3,2},{4,5},{5,4},{6,7},{7,6},{8,9},{9,8},{10,11... | collective-permute-start | bytes 884744 | tf_op jit(solution)/shard_map/between/ppermute | solution.py:53
  36.1 7.6 %collective-permute-start.9 = (bf16[144,1152]{1,0:T(8,128)(2,1)S(1)}, bf16[144,1152]{1,0:T(8,128)(2,1)S(1)}, u32[]{:S(2)}, u32[]{:S(2)}) collective-permute-start(bf16[144,1152]{1,0:T(8,128)(2,1)S(1)} %get-tuple-element.37), channel_id=1, source_target_pairs={{0,16},{1,65},{2,18},{3,67},{4,20},{5,69},{6,22},{7,71},{8,24},{9,... | collective-permute-start | bytes 995336 | tf_op jit(solution)/shard_map/sum_first/ppermute | solution.py:53
  36.2 7.5 %collective-permute-start.10 = (bf16[144,1152]{1,0:T(8,128)(2,1)S(1)}, bf16[144,1152]{1,0:T(8,128)(2,1)S(1)}, u32[]{:S(2)}, u32[]{:S(2)}) collective-permute-start(bf16[144,1152]{1,0:T(8,128)(2,1)S(1)} %get-tuple-element.39), channel_id=1, source_target_pairs={{0,48},{1,193},{2,50},{3,195},{4,52},{5,197},{6,54},{7,199},{8,56}... | collective-permute-start | bytes 995336 | tf_op jit(solution)/shard_map/sum_first/ppermute | solution.py:53
  43.9 11.1 %collective-permute-start.11 = (bf16[288,1152]{1,0:T(8,128)(2,1)S(1)}, bf16[288,1152]{1,0:T(8,128)(2,1)S(1)}, u32[]{:S(2)}, u32[]{:S(2)}) collective-permute-start(bf16[288,1152]{1,0:T(8,128)(2,1)S(1)} %get-tuple-element.40), channel_id=1, source_target_pairs={{0,16},{1,65},{2,18},{3,67},{4,20},{5,69},{6,22},{7,71},{8,24},{9,... | collective-permute-start | bytes 1990664 | tf_op jit(solution)/shard_map/sum_first/ppermute | solution.py:53
  44.0 11.0 %collective-permute-start.12 = (bf16[288,1152]{1,0:T(8,128)(2,1)S(1)}, bf16[288,1152]{1,0:T(8,128)(2,1)S(1)}, u32[]{:S(2)}, u32[]{:S(2)}) collective-permute-start(bf16[288,1152]{1,0:T(8,128)(2,1)S(1)} %get-tuple-element.41), channel_id=1, source_target_pairs={{0,48},{1,193},{2,50},{3,195},{4,52},{5,197},{6,54},{7,199},{8,56}... | collective-permute-start | bytes 1990664 | tf_op jit(solution)/shard_map/sum_first/ppermute | solution.py:53
  99.1 11.8 %collective-permute-start.13 = (bf16[144,1152]{1,0:T(8,128)(2,1)S(1)}, bf16[144,1152]{1,0:T(8,128)(2,1)S(1)}, u32[]{:S(2)}, u32[]{:S(2)}) collective-permute-start(bf16[144,1152]{1,0:T(8,128)(2,1)S(1)} %bitcast.29), channel_id=1, source_target_pairs={{0,16},{1,65},{2,18},{3,67},{4,20},{5,69},{6,22},{7,71},{8,24},{9,... | collective-permute-start | bytes 995336 | tf_op jit(solution)/shard_map/share_first/ppermute | solution.py:53
  100.4 10.5 %collective-permute-start.14 = (bf16[144,1152]{1,0:T(8,128)(2,1)S(1)}, bf16[144,1152]{1,0:T(8,128)(2,1)S(1)}, u32[]{:S(2)}, u32[]{:S(2)}) collective-permute-start(bf16[144,1152]{1,0:T(8,128)(2,1)S(1)} %bitcast.28), channel_id=1, source_target_pairs={{0,48},{1,193},{2,50},{3,195},{4,52},{5,197},{6,54},{7,199},{8,56}... | collective-permute-start | bytes 995336 | tf_op jit(solution)/shard_map/share_first/ppermute | solution.py:53
  110.9 13.0 %collective-permute-start.15 = (bf16[288,1152]{1,0:T(8,128)(2,1)S(1)}, bf16[288,1152]{1,0:T(8,128)(2,1)S(1)}, u32[]{:S(2)}, u32[]{:S(2)}) collective-permute-start(bf16[288,1152]{1,0:T(8,128)(2,1)S(1)} %get-tuple-element.42), channel_id=1, source_target_pairs={{0,16},{1,65},{2,18},{3,67},{4,20},{5,69},{6,22},{7,71},{8,24},{9,... | collective-permute-start | bytes 1990664 | tf_op jit(solution)/shard_map/share_first/ppermute | solution.py:53
  111.0 21.5 %collective-permute-start.16 = (bf16[288,1152]{1,0:T(8,128)(2,1)S(1)}, bf16[288,1152]{1,0:T(8,128)(2,1)S(1)}, u32[]{:S(2)}, u32[]{:S(2)}) collective-permute-start(bf16[288,1152]{1,0:T(8,128)(2,1)S(1)} %get-tuple-element.43), channel_id=1, source_target_pairs={{0,48},{1,193},{2,50},{3,195},{4,52},{5,197},{6,54},{7,199},{8,56}... | collective-permute-start | bytes 1990664 | tf_op jit(solution)/shard_map/share_first/ppermute | solution.py:53
  113.7 22.5 %collective-permute-start.17 = (bf16[288,1152]{1,0:T(8,128)(2,1)S(1)}, bf16[288,1152]{1,0:T(8,128)(2,1)S(1)}, u32[]{:S(2)}, u32[]{:S(2)}) collective-permute-start(bf16[288,1152]{1,0:T(8,128)(2,1)S(1)} %bitcast.21), channel_id=1, source_target_pairs={{0,1},{1,0},{2,3},{3,2},{4,5},{5,4},{6,7},{7,6},{8,9},{9,8},{10,11... | collective-permute-start | bytes 1990664 | tf_op jit(solution)/shard_map/share_first/ppermute | solution.py:53
  123.9 12.3 %collective-permute-start.20 = (bf16[288,1152]{1,0:T(8,128)(2,1)S(1)}, bf16[288,1152]{1,0:T(8,128)(2,1)S(1)}, u32[]{:S(2)}, u32[]{:S(2)}) collective-permute-start(bf16[288,1152]{1,0:T(8,128)(2,1)S(1)} %collective-permute-done.15.refs_3_), channel_id=1, source_target_pairs={{0,1},{1,0},{2,3},{3,2},{4,5},{5,4},{6,7},{7,6},{8,9},{9,8},{10,11... | collective-permute-start | bytes 1990664 | tf_op jit(solution)/shard_map/share_first/ppermute | solution.py:53
  132.5 3.6 %collective-permute-start.21 = (bf16[288,1152]{1,0:T(8,128)(2,1)S(1)}, bf16[288,1152]{1,0:T(8,128)(2,1)S(1)}, u32[]{:S(2)}, u32[]{:S(2)}) collective-permute-start(bf16[288,1152]{1,0:T(8,128)(2,1)S(1)} %collective-permute-done.16.refs_4_), channel_id=1, source_target_pairs={{0,1},{1,0},{2,3},{3,2},{4,5},{5,4},{6,7},{7,6},{8,9},{9,8},{10,11... | collective-permute-start | bytes 1990664 | tf_op jit(solution)/shard_map/share_first/ppermute | solution.py:53
  132.5 3.2 %collective-permute-start.18 = (bf16[144,1152]{1,0:T(8,128)(2,1)S(1)}, bf16[144,1152]{1,0:T(8,128)(2,1)S(1)}, u32[]{:S(2)}, u32[]{:S(2)}) collective-permute-start(bf16[144,1152]{1,0:T(8,128)(2,1)S(1)} %collective-permute-done.13.left_top.refs_1_), channel_id=1, source_target_pairs={{0,1},{1,0},{2,3},{3,2},{4,5},{5,4},{6,7},{7,6},{8,9},{9,8},{10,11... | collective-permute-start | bytes 995336 | tf_op jit(solution)/shard_map/share_first/ppermute | solution.py:53
  133.1 3.1 %collective-permute-start.19 = (bf16[144,1152]{1,0:T(8,128)(2,1)S(1)}, bf16[144,1152]{1,0:T(8,128)(2,1)S(1)}, u32[]{:S(2)}, u32[]{:S(2)}) collective-permute-start(bf16[144,1152]{1,0:T(8,128)(2,1)S(1)} %collective-permute-done.14.right_bottom.refs_2_), channel_id=1, source_target_pairs={{0,1},{1,0},{2,3},{3,2},{4,5},{5,4},{6,7},{7,6},{8,9},{9,8},{10,11... | collective-permute-start | bytes 995336 | tf_op jit(solution)/shard_map/share_first/ppermute | solution.py:53

commit v4 on v3

v4 whole, which is shorter than its diff:
```python
import jax
import jax.numpy as jnp
from jax import lax
from jax.experimental import pallas as pl
from jax.experimental.pallas import tpu as pltpu
from jax.sharding import PartitionSpec as P

NY, NX, NZ, CORES = 4, 4, 8, 2
N = NY * NX * NZ * CORES
epsilon = 1e-06
bf16, f32 = jnp.bfloat16, jnp.float32
MIB = 1 << 20


def index(y, x, z, c):
    return ((y % NY * NX + x % NX) * NZ + z % NZ) * CORES + c


PLACES = [
    (y, x, z, c) for y in range(NY) for x in range(NX) for z in range(NZ) for c in range(CORES)
]


def route(move):
    return [(index(*place), index(*move(*place))) for place in PLACES]


def groups(key):
    found = {}
    for place in PLACES:
        found.setdefault(key(*place), []).append(index(*place))
    return list(found.values())


def along_first(step):
    return route(lambda y, x, z, c: (y, x + step, z, c) if c == 0 else (y + step, x, z, c))


SWAP = route(lambda y, x, z, c: (y, x, z, 1 - c))
RIGHT, LEFT = along_first(1), along_first(-1)
SECOND = groups(lambda y, x, z, c: (c, z, x if c == 0 else y))
LINES = groups(lambda y, x, z, c: (c, x, y))
FORWARD = [(i, (i + 1) % N if i % 2 else (i - 1) % N) for i in range(N)]
TEXT = 1


def shifted(distance):
    return [(i, (i + distance) % N) for i in range(N)]


def send(block, pairs):
    return lax.ppermute(block, "dp", pairs)


def exchange(parts, members):
    return lax.all_to_all(parts, "dp", 0, 0, axis_index_groups=members, tiled=True)


def call(body, outs, scratch=(), flops=0, result=pltpu.VMEM):
    def run(smem, outside, *arrays):
        specs = (
            [pl.BlockSpec(memory_space=pltpu.SMEM)] * len(smem)
            + [pl.BlockSpec(memory_space=pltpu.HBM)] * len(outside)
            + [pl.BlockSpec(memory_space=pltpu.VMEM)] * len(arrays)
        )
        held = [pltpu.with_memory_space_constraint(a, pltpu.VMEM) for a in arrays]
        outside = [pltpu.with_memory_space_constraint(a, pltpu.HBM) for a in outside]
        return pl.pallas_call(
            body,
            out_shape=[jax.ShapeDtypeStruct(s, d) for s, d in outs],
            in_specs=specs,
            out_specs=[pl.BlockSpec(memory_space=result)] * len(outs),
            scratch_shapes=list(scratch),
            cost_estimate=pl.CostEstimate(flops=flops, bytes_accessed=0, transcendentals=0),
            compiler_params=pltpu.CompilerParams(vmem_limit_bytes=32 * MIB),
        )(*smem, *outside, *held)

    return run


def contract(a, b, da, db):
    return lax.dot_general(a, b, (((da,), (db,)), ((), ())), preferred_element_type=f32)


def core_place():
    me = lax.axis_index("dp")
    core = lax.rem(me, CORES)
    x = lax.rem(me // (NZ * CORES), NX)
    y = me // (NX * NZ * CORES)
    return core, jnp.where(core == 0, x, y), jnp.where(core == 0, y, x)


def on_text():
    return core_place()[0] == TEXT


def factor(log_scale):
    return jnp.exp(jnp.full((1, 1), log_scale[0], f32))


def embed(features, weight):
    projected = jnp.dot(features, weight, preferred_element_type=f32)
    square = jnp.sum(projected * projected, axis=-1, keepdims=True)
    inverse = 1.0 / jnp.sqrt(square + epsilon)
    return projected, inverse


def add_head(head, x, back, before):
    step = head.shape[0] // 3
    for k in range(3):
        at = pl.ds(k * step, step)
        new = contract(x[:, at], back[...], 0, 0)
        head[at, :] = new if before is None else before[at, :] + new


def visit(log_scale, shift, x, text_w, image_emb, finish, back, grad, grad_before):
    scale = factor(log_scale)
    projected, inverse = embed(x[...], text_w[...])
    emb = (projected * inverse).astype(bf16)
    similarity = contract(emb, image_emb[...], 1, 1)
    coefficient = finish(jax.nn.sigmoid(scale * similarity + shift[0])).astype(bf16)

    @pl.when(on_text())
    def _():
        radial = jnp.sum(coefficient.astype(f32) * similarity, axis=-1, keepdims=True)
        gradient = jnp.dot(coefficient, image_emb[...], preferred_element_type=f32)
        outer = scale * inverse
        back[...] = (gradient * outer - projected * (outer * inverse * radial)).astype(bf16)

    @pl.when(jnp.logical_not(on_text()))
    def _():
        share = contract(coefficient, emb, 0, 0)
        grad[...] = share if grad_before is None else grad_before[...] + share


def near_kernel(
    log_scale, shift, text_hbm, image_hbm, text_w_hbm, image_w_hbm, text_other, image_other,
    position, position_other,
    image_near, text_w, image_emb, image_projected, image_inverse, grad, head,
    text_near, image_w, back, sems,
):
    rows = text_other.shape[0]
    first, second = pl.ds(0, rows), pl.ds(rows, rows)
    moves = [
        pltpu.make_async_copy(image_hbm, image_near.at[first, :], sems.at[0]),
        pltpu.make_async_copy(image_w_hbm, image_w, sems.at[1]),
        pltpu.make_async_copy(text_hbm, text_near.at[first, :], sems.at[2]),
        pltpu.make_async_copy(text_w_hbm, text_w, sems.at[3]),
    ]
    for move in moves:
        move.start()
    image_near[second, :] = image_other[...]
    text_near[second, :] = text_other[...]
    moves[0].wait()
    moves[1].wait()
    projected, inverse = embed(image_near[...], image_w[...])
    image_emb[...] = (projected * inverse).astype(bf16)
    image_projected[...] = projected
    image_inverse[...] = inverse
    moves[2].wait()
    moves[3].wait()

    def with_labels(sigmoid):
        column = lax.broadcasted_iota(jnp.int32, (2 * rows, rows), 0)
        own = (column == position[...]).astype(f32)
        other = (column == position_other[...] + rows).astype(f32)
        return sigmoid - jnp.concatenate([own, other], axis=1).T

    visit(log_scale, shift, text_near, text_w, image_emb, with_labels, back, grad, None)

    @pl.when(on_text())
    def _():
        add_head(head, text_near, back, None)


def choose_kernel(below, above, done_first, out):
    core = core_place()[0]

    @pl.when(core == 1)
    def _():
        out[...] = below[...]

    @pl.when(core == 0)
    def _():
        out[...] = above[...]


def pair_kernel(
    log_scale, shift, below, above, text_w, image_emb, grad_before, head_before,
    grad, head, x, back,
):
    rows = below.shape[0]
    x[pl.ds(0, rows), :] = below[...]
    x[pl.ds(rows, rows), :] = above[...]
    visit(log_scale, shift, x, text_w, image_emb, lambda c: c, back, grad, grad_before)

    @pl.when(on_text())
    def _():
        add_head(head, x, back, head_before)


def far_kernel(
    log_scale, shift, far, far_other, text_w, image_emb, grad_before, head_before,
    image_near, image_projected, image_inverse,
    own, right_top, right_bottom, left_top, left_bottom, far_right, far_left,
    grad, head, x, back,
):
    rows = far.shape[0]
    x[pl.ds(0, rows), :] = far[...]
    x[pl.ds(rows, rows), :] = far_other[...]

    def inside(sigmoid):
        row = lax.broadcasted_iota(jnp.int32, sigmoid.shape, 0) < rows
        column = lax.broadcasted_iota(jnp.int32, sigmoid.shape, 1) < rows
        return jnp.where(row == column, sigmoid, 0.0)

    visit(log_scale, shift, x, text_w, image_emb, inside, back, grad, grad_before)

    @pl.when(on_text())
    def _():
        add_head(head, x, back, head_before)

    @pl.when(jnp.logical_not(on_text()))
    def _():
        gradient = factor(log_scale) * grad[...]
        inverse = image_inverse[...]
        unit = image_projected[...] * inverse
        radial = jnp.sum(gradient * unit, axis=-1, keepdims=True)
        back[...] = ((gradient - unit * radial) * inverse).astype(bf16)
        add_head(head, image_near, back, None)

    slab = head.shape[0] // 4
    half = slab // 2
    place = core_place()[1]

    def part(turn, upper, size):
        start = lax.rem(place + turn, 4) * slab + upper
        return head[pl.ds(pl.multiple_of(start, 16), size), :].astype(bf16)

    far_right[...] = part(2, 0, half)
    far_left[...] = part(2, half, half)
    right_top[...] = part(1, 0, half)
    right_bottom[...] = part(1, half, half)
    left_top[...] = part(3, 0, half)
    left_bottom[...] = part(3, half, half)
    own[...] = part(0, 0, slab)


def add_kernel(a, b, c, d, ab, cd):
    ab[...] = (a[...].astype(f32) + b[...].astype(f32)).astype(bf16)
    cd[...] = (c[...].astype(f32) + d[...].astype(f32)).astype(bf16)


def join_kernel(own, a_top, a_bottom, b_top, b_bottom, out):
    half = a_top.shape[0]
    upper, lower = pl.ds(0, half), pl.ds(half, half)
    out[upper, :] = (
        own[upper, :].astype(f32) + a_top[...].astype(f32) + b_top[...].astype(f32)
    ).astype(bf16)
    out[lower, :] = (
        own[lower, :].astype(f32) + a_bottom[...].astype(f32) + b_bottom[...].astype(f32)
    ).astype(bf16)


PIECES = [(0, 0), (3, 0), (1, 1), (3, 1), (1, 0), (2, 0), (2, 1)]


def write_kernel(*refs):
    count = len(PIECES)
    mine, theirs, (text, image, sems) = refs[:count], refs[count : 2 * count], refs[2 * count :]
    core, place, other_place = core_place()
    slab = mine[0].shape[0]

    def copies(pieces, position, out, first):
        moves = []
        for k, (piece, (turn, part)) in enumerate(zip(pieces, PIECES)):
            start = lax.rem(position + turn, 4) * slab + part * (slab // 2)
            target = out.at[pl.ds(pl.multiple_of(start, 16), piece.shape[0]), :]
            moves.append(pltpu.make_async_copy(piece, target, sems.at[first + k]))
        return moves

    def go(moves):
        for move in moves:
            move.start()
        for move in moves:
            move.wait()

    @pl.when(core == TEXT)
    def _():
        go(copies(mine, place, text, 0) + copies(theirs, other_place, image, count))

    @pl.when(core != TEXT)
    def _():
        go(copies(mine, place, image, 0) + copies(theirs, other_place, text, count))


def on_device(text_x, image_x, text_w, image_w, position, log_scale, shift):
    rows, width = text_x.shape
    depth = text_w.shape[0]
    slab = depth // 4
    half = slab // 2
    scalars = (log_scale, shift)
    block = ((rows, width), bf16)
    pair, pair_f32 = ((2 * rows, width), bf16), ((2 * rows, width), f32)
    total = ((depth, width), f32)
    matrix = ((depth, width), bf16)
    piece, half_piece = ((slab, width), bf16), ((half, width), bf16)
    with jax.named_scope("band_exchange"):
        text_other = send(text_x, SWAP)
        image_other = send(image_x, SWAP)
        position_other = send(position, SWAP)
        below = send(text_x, shifted(2))
        above = send(text_x, shifted(-2))
    with jax.named_scope("near"):
        image_near, weight, image_emb, image_projected, image_inverse, grad, head = call(
            near_kernel,
            [pair, matrix, pair, pair_f32, ((2 * rows, 1), f32), pair_f32, total],
            [
                pltpu.VMEM(*pair),
                pltpu.VMEM(*matrix),
                pltpu.VMEM(*pair),
                pltpu.SemaphoreType.DMA((4,)),
            ],
            flops=4 * 10**9,
        )(
            scalars, (text_x, image_x, text_w, image_w), text_other, image_other,
            position[None], position_other[None],
        )
    with jax.named_scope("forward"):
        [onward] = call(choose_kernel, [block])((), (), below, above, image_inverse)
        far = send(onward, FORWARD)
        below_other = send(below, SWAP)
        above_other = send(above, SWAP)
    visits = call(
        pair_kernel, [pair_f32, total], [pltpu.VMEM(*pair), pltpu.VMEM(*pair)], flops=4 * 10**9
    )
    with jax.named_scope("received"):
        grad, head = visits(scalars, (), below, above, weight, image_emb, grad, head)
    with jax.named_scope("partners"):
        grad, head = visits(scalars, (), below_other, above_other, weight, image_emb, grad, head)
    with jax.named_scope("far"):
        far_other = send(far, SWAP)
        own, right_top, right_bottom, left_top, left_bottom, far_right, far_left = call(
            far_kernel,
            [piece] + [half_piece] * 6,
            [pltpu.VMEM(*pair_f32), pltpu.VMEM(*total), pltpu.VMEM(*pair), pltpu.VMEM(*pair)],
            flops=4 * 10**9,
        )(
            scalars, (), far, far_other, weight, image_emb, grad, head, image_near,
            image_projected, image_inverse,
        )
    with jax.named_scope("sum_first"):
        from_left = send(far_right, RIGHT)
        from_right = send(far_left, LEFT)
        a_bottom = send(right_bottom, RIGHT)
        b_top = send(left_top, LEFT)
        right_top, left_bottom = call(add_kernel, [half_piece] * 2)(
            (), (), right_top, from_left, left_bottom, from_right
        )
        a_top = send(right_top, RIGHT)
        b_bottom = send(left_bottom, LEFT)
        [part] = call(join_kernel, [piece])((), (), own, a_top, a_bottom, b_top, b_bottom)
    with jax.named_scope("sum_second"):
        part = exchange(part.reshape(4, slab // 4, width), SECOND)
        part = jnp.sum(part.astype(f32), axis=0).astype(bf16)
    with jax.named_scope("sum_lines"):
        tiles = (
            part.reshape(slab // 32, 8, width // 128, 128).transpose(0, 2, 1, 3).reshape(-1, 8, 128)
        )
        count = tiles.shape[0]
        each = -(-count // NZ)
        tiles = jnp.concatenate([tiles, jnp.zeros((each * NZ - count, 8, 128), bf16)])
        tiles = exchange(tiles, LINES).reshape(NZ, each, 8, 128)
        tiles = jnp.sum(tiles.astype(f32), axis=0).astype(bf16)
    with jax.named_scope("share_lines"):
        tiles = exchange(jnp.tile(tiles, (NZ, 1, 1)), LINES)[:count]
        part = (
            tiles.reshape(slab // 32, width // 128, 8, 128).transpose(0, 2, 1, 3).reshape(-1, width)
        )
    with jax.named_scope("share_second"):
        own = exchange(jnp.tile(part[None], (4, 1, 1)), SECOND).reshape(slab, width)
    with jax.named_scope("share_first"):
        top, bottom = own[:half], own[half:]
        left_top = send(top, RIGHT)
        right_bottom = send(bottom, LEFT)
        left_bottom = send(bottom, RIGHT)
        right_top = send(top, LEFT)
        across_top = send(left_top, RIGHT)
        across_bottom = send(right_bottom, LEFT)
        mine = [own, left_top, right_bottom, left_bottom, right_top, across_top, across_bottom]
        theirs = [send(one, SWAP) for one in mine]
    with jax.named_scope("write"):
        return call(
            write_kernel,
            [matrix, matrix],
            [pltpu.SemaphoreType.DMA((2 * len(PIECES),))],
            result=pltpu.HBM,
        )((), (), *mine, *theirs)


def solution(mesh):
    return jax.shard_map(
        on_device,
        mesh=mesh,
        in_specs=(P("dp", None), P("dp", None), P(), P(), P("dp"), P(), P()),
        out_specs=(P(), P()),
        check_vma=False,
    )
```

time: 140 us -> 139 us (level)
  starting transfers between devices: 48.9 us -> 58.7 us
  waiting for transfers between devices: 25.4 us -> 16.2 us
    ppermute x22 -> x28, starting transfers between devices: 48.9 us -> 58.7 us  [send(): return lax.ppermute(block, 'dp', pairs)]
    ppermute x22 -> x28, waiting for transfers between devices: 25.4 us -> 16.2 us  [send(): return lax.ppermute(block, 'dp', pairs)]
    pallas_call x7 -> x8, Pallas kernels: 15 us -> 18.5 us  [run(): pl.pallas_call(body, out_shape=[jax.ShapeDtypeStruct(s, d) for s, d in ou...]
    pallas_call x1 -> x0, Pallas kernels: 3.03 us -> none  [on_device(): pl.pallas_call(write_kernel, out_shape=[jax.ShapeDtypeStruct((depth, widt...]
  transfers between devices with their start and end apart: 22 -> 28, of which waited for: 7 -> 8; matrix products, arithmetic and copies ran while one was open for 1% -> 0% of each run, Pallas kernels for 7% -> 9%
where the time goes in v4:
time: 139 us
  starting transfers between devices  58.7 us (42%)
  blocking collectives  42.4 us (31%)
  Pallas kernels  18.5 us (13%)
  waiting for transfers between devices  16.2 us (12%)
  between operations  2.3 us (2%)
    ppermute x28, starting transfers between devices, send(): return lax.ppermute(block, 'dp', pairs)  58.7 us
    all_to_all x4, blocking collectives, exchange(): lax.all_to_all(parts, 'dp', 0, 0, axis_index_groups=members, tiled=True)  42.4 us
    pallas_call x8, Pallas kernels, run(): pl.pallas_call(body, out_shape=[jax.ShapeDtypeStruct(s, d) for s, d in ou...  18.5 us
    ppermute x28, waiting for transfers between devices, send(): return lax.ppermute(block, 'dp', pairs)  16.2 us
  transfers between devices with their start and end apart: 28, of which 8 were waited for; matrix products, arithmetic and copies ran while one was open for 0% of the time, Pallas kernels for 9%

profile of v4, /device:TPU:1, one launch (start us, length us, event | category | flops | bytes accessed | tf_op | source)
XLA Modules:
  0.0 139.0 jit_solution(6000991652330151848)
XLA Ops:
  0.6 3.3 %collective-permute-start.3 = (bf16[128,1152]{1,0:T(8,128)(2,1)}, bf16[128,1152]{1,0:T(8,128)(2,1)S(1)}, u32[]{:S(2)}, u32[]{:S(2)}) collective-permute-start(bf16[128,1152]{1,0:T(8,128)(2,1)} %image_hbm.1), channel_id=1, source_target_pairs={{0,1},{1,0},{2,3},{3,2},{4,5},{5,4},{6,7},{7,6},{8,9},{9,8},{10,11... | collective-permute-start | bytes 884744 | tf_op jit(solution)/shard_map/band_exchange/ppermute | solution.py:52
  4.0 0.1 collective-permute-start.2
  4.1 0.4 collective-permute-start.4
  4.5 8.5 %collective-permute-start.1 = (bf16[128,1152]{1,0:T(8,128)(2,1)}, bf16[128,1152]{1,0:T(8,128)(2,1)S(1)}, u32[]{:S(2)}, u32[]{:S(2)}) collective-permute-start(bf16[128,1152]{1,0:T(8,128)(2,1)} %text_hbm.1), channel_id=1, source_target_pairs={{0,254},{1,255},{2,0},{3,1},{4,2},{5,3},{6,4},{7,5},{8,6},{9,7},{1... | collective-permute-start | bytes 884744 | tf_op jit(solution)/shard_map/band_exchange/ppermute | solution.py:52
  13.0 0.0 collective-permute-start
  14.3 0.0 collective-permute-done.4
  14.3 0.0 collective-permute-done.3.image_other
  14.3 0.0 collective-permute-done.2.text_other
  14.3 0.6 copy-done
  15.0 6.1 %near.1 = (bf16[256,1152]{1,0:T(8,128)(2,1)S(1)}, bf16[1152,1152]{1,0:T(8,128)(2,1)S(1)}, bf16[256,1152]{1,0:T(8,128)(2,1)S(1)}, f32[256,1152]{1,0:T(8,128)S(1)}...) custom-call(f32[1]{0:T(128)S(6)} %copy.9.log_scale, f32[1]{0:T(128)S(6)} %copy.10.shift, ...), custom_call_target="tpu_custom_call" | custom-call | flops 4000000000 | tf_op jit(solution)/shard_map/near/pallas_call | solution.py:68
  21.1 0.0 collective-permute-done.1.above
  21.1 5.7 %collective-permute-done.below = bf16[128,1152]{1,0:T(8,128)(2,1)S(1)} collective-permute-done((bf16[128,1152]{1,0:T(8,128)(2,1)}, bf16[128,1152]{1,0:T(8,128)(2,1)S(1)}, u32[]{:S(2)}, u32[]{:S(2)}) %collective-permute-start) | collective-permute-done | bytes 294944 | tf_op jit(solution)/shard_map/band_exchange/ppermute | solution.py:52
  26.9 0.1 collective-permute-start.5
  27.0 1.6 %collective-permute-start.8 = (bf16[128,1152]{1,0:T(8,128)(2,1)S(1)}, bf16[128,1152]{1,0:T(8,128)(2,1)S(1)}, u32[]{:S(2)}, u32[]{:S(2)}) collective-permute-start(bf16[128,1152]{1,0:T(8,128)(2,1)S(1)} %collective-permute-done.1.above), channel_id=1, source_target_pairs={{0,1},{1,0},{2,3},{3,2},{4,5},{5,4},{6,7},{7,6},{8,9},{9,8},{10,11... | collective-permute-start | bytes 884744 | tf_op jit(solution)/shard_map/forward/ppermute | solution.py:52
  28.5 0.0 collective-permute-start.7
  28.5 3.1 %received.1 = (f32[256,1152]{1,0:T(8,128)S(1)}, f32[1152,1152]{1,0:T(8,128)S(1)}) custom-call(f32[1]{0:T(128)S(6)} %copy.9.log_scale, f32[1]{0:T(128)S(6)} %copy.10.shift, bf16[128,1152]{1,0:T(8,128)(2,1)S(1)} %collective-permute-done.below, bf16[128,1152]{1,0:T(8,128)(2,1)S(1)} %collective-permute-done.1.above, ...), custom_call_target="tpu_custom_call" | custom-call | flops 4000000000 | tf_op jit(solution)/shard_map/received/pallas_call | solution.py:68
  31.6 1.5 %collective-permute-done.5.far = bf16[128,1152]{1,0:T(8,128)(2,1)S(1)} collective-permute-done((bf16[128,1152]{1,0:T(8,128)(2,1)S(1)}, bf16[128,1152]{1,0:T(8,128)(2,1)S(1)}, u32[]{:S(2)}, u32[]{:S(2)}) %collective-permute-start.5) | collective-permute-done | bytes 294944 | tf_op jit(solution)/shard_map/forward/ppermute | solution.py:52
  33.1 6.6 %collective-permute-start.6 = (bf16[128,1152]{1,0:T(8,128)(2,1)S(1)}, bf16[128,1152]{1,0:T(8,128)(2,1)S(1)}, u32[]{:S(2)}, u32[]{:S(2)}) collective-permute-start(bf16[128,1152]{1,0:T(8,128)(2,1)S(1)} %collective-permute-done.5.far), channel_id=1, source_target_pairs={{0,1},{1,0},{2,3},{3,2},{4,5},{5,4},{6,7},{7,6},{8,9},{9,8},{10,11... | collective-permute-start | bytes 884744 | tf_op jit(solution)/shard_map/far/ppermute | solution.py:52
  39.7 0.0 collective-permute-done.8.above
  39.7 0.0 collective-permute-done.7.below
  39.7 3.1 %partners.1 = (f32[256,1152]{1,0:T(8,128)S(1)}, f32[1152,1152]{1,0:T(8,128)S(1)}) custom-call(f32[1]{0:T(128)S(6)} %copy.9.log_scale, f32[1]{0:T(128)S(6)} %copy.10.shift, bf16[128,1152]{1,0:T(8,128)(2,1)S(1)} %collective-permute-done.7.below, bf16[128,1152]{1,0:T(8,128)(2,1)S(1)} %collective-permute-done.8.above, ...), custom_call_target="tpu_custom_call" | custom-call | flops 4000000000 | tf_op jit(solution)/shard_map/partners/pallas_call | solution.py:68
  42.8 0.0 collective-permute-done.6.far_other
  42.8 3.3 %far.1 = (bf16[288,1152]{1,0:T(8,128)(2,1)S(1)}, bf16[144,1152]{1,0:T(8,128)(2,1)S(1)}, bf16[144,1152]{1,0:T(8,128)(2,1)S(1)}, bf16[144,1152]{1,0:T(8,128)(2,1)S...) custom-call(f32[1]{0:T(128)S(6)} %copy.9.log_scale, ...), custom_call_target="tpu_custom_call" | custom-call | flops 4000000000 | tf_op jit(solution)/shard_map/far/pallas_call | solution.py:68
  46.2 0.1 collective-permute-start.9
  46.2 2.7 %collective-permute-start.10 = (bf16[144,1152]{1,0:T(8,128)(2,1)S(1)}, bf16[144,1152]{1,0:T(8,128)(2,1)S(1)}, u32[]{:S(2)}, u32[]{:S(2)}) collective-permute-start(bf16[144,1152]{1,0:T(8,128)(2,1)S(1)} %get-tuple-element.37), channel_id=1, source_target_pairs={{0,48},{1,193},{2,50},{3,195},{4,52},{5,197},{6,54},{7,199},{8,56}... | collective-permute-start | bytes 995336 | tf_op jit(solution)/shard_map/sum_first/ppermute | solution.py:52
  48.9 0.0 collective-permute-start.12
  48.9 2.7 %collective-permute-start.13 = (bf16[144,1152]{1,0:T(8,128)(2,1)S(1)}, bf16[144,1152]{1,0:T(8,128)(2,1)S(1)}, u32[]{:S(2)}, u32[]{:S(2)}) collective-permute-start(bf16[144,1152]{1,0:T(8,128)(2,1)S(1)} %get-tuple-element.40), channel_id=1, source_target_pairs={{0,48},{1,193},{2,50},{3,195},{4,52},{5,197},{6,54},{7,199},{8,56}... | collective-permute-start | bytes 995336 | tf_op jit(solution)/shard_map/sum_first/ppermute | solution.py:52
  51.6 2.1 %collective-permute-done.9.b = bf16[144,1152]{1,0:T(8,128)(2,1)S(1)} collective-permute-done((bf16[144,1152]{1,0:T(8,128)(2,1)S(1)}, bf16[144,1152]{1,0:T(8,128)(2,1)S(1)}, u32[]{:S(2)}, u32[]{:S(2)}) %collective-permute-start.9) | collective-permute-done | bytes 331808 | tf_op jit(solution)/shard_map/sum_first/ppermute | solution.py:52
  53.7 0.0 collective-permute-done.10.d
  53.7 0.2 sum_first.2
  53.9 0.1 collective-permute-start.11
  54.0 2.7 %collective-permute-start.14 = (bf16[144,1152]{1,0:T(8,128)(2,1)S(1)}, bf16[144,1152]{1,0:T(8,128)(2,1)S(1)}, u32[]{:S(2)}, u32[]{:S(2)}) collective-permute-start(bf16[144,1152]{1,0:T(8,128)(2,1)S(1)} %get-tuple-element.41), channel_id=1, source_target_pairs={{0,48},{1,193},{2,50},{3,195},{4,52},{5,197},{6,54},{7,199},{8,56}... | collective-permute-start | bytes 995336 | tf_op jit(solution)/shard_map/sum_first/ppermute | solution.py:52
  56.6 0.5 collective-permute-done.12.a_bottom
  57.1 0.0 collective-permute-done.13.b_top
  57.1 4.3 %collective-permute-done.11.a_top = bf16[144,1152]{1,0:T(8,128)(2,1)S(1)} collective-permute-done((bf16[144,1152]{1,0:T(8,128)(2,1)S(1)}, bf16[144,1152]{1,0:T(8,128)(2,1)S(1)}, u32[]{:S(2)}, u32[]{:S(2)}) %collective-permute-start.11) | collective-permute-done | bytes 331808 | tf_op jit(solution)/shard_map/sum_first/ppermute | solution.py:52
  61.4 0.0 collective-permute-done.14.b_bottom
  61.4 0.3 sum_first.3
  61.7 10.6 %all_to_all.20 = bf16[4,72,1152]{2,1,0:T(8,128)(2,1)S(1)} all-to-all(bf16[4,72,1152]{2,1,0:T(8,128)(2,1)S(1)} %bitcast.20), channel_id=1, replica_groups={{0,64,128,192},{1,17,33,49},{2,66,130,194},{3,19,35,51},{4,68,132,196},..., dimensions={0} | all-to-all | bytes 1327104 | tf_op jit(solution)/shard_map/sum_second/all_to_all | solution.py:56
  72.3 0.1 reduce_sum.24
  72.4 10.9 %all_to_all.21 = bf16[88,8,128]{2,1,0:T(8,128)(2,1)S(1)} all-to-all(bf16[88,8,128]{2,1,0:T(8,128)(2,1)S(1)} %concatenate.3), channel_id=1, replica_groups={{0,2,4,6,8,10,12,14},{1,3,5,7,9,11,13,15},{16,18,20,22,24,26,28,30},{17..., dimensions={0} | all-to-all | bytes 360448 | tf_op jit(solution)/shard_map/sum_lines/all_to_all | solution.py:56
  83.4 10.9 %all_to_all.22 = bf16[88,8,128]{2,1,0:T(8,128)(2,1)S(1)} all-to-all(bf16[88,8,128]{2,1,0:T(8,128)(2,1)S(1)} %bitcast.24), channel_id=1, replica_groups={{0,2,4,6,8,10,12,14},{1,3,5,7,9,11,13,15},{16,18,20,22,24,26,28,30},{17..., dimensions={0} | all-to-all | bytes 360448 | tf_op jit(solution)/shard_map/share_lines/all_to_all | solution.py:56
  94.3 10.1 %all_to_all.23 = bf16[4,72,1152]{2,1,0:T(8,128)(2,1)S(1)} all-to-all(bf16[4,72,1152]{2,1,0:T(8,128)(2,1)S(1)} %tile.20), channel_id=1, replica_groups={{0,64,128,192},{1,17,33,49},{2,66,130,194},{3,19,35,51},{4,68,132,196},..., dimensions={0} | all-to-all | bytes 1327104 | tf_op jit(solution)/shard_map/share_second/all_to_all | solution.py:56
  104.4 0.1 fusion
  104.4 3.7 %collective-permute-start.18 = (bf16[144,1152]{1,0:T(8,128)(2,1)S(1)}, bf16[144,1152]{1,0:T(8,128)(2,1)S(1)}, u32[]{:S(2)}, u32[]{:S(2)}) collective-permute-start(bf16[144,1152]{1,0:T(8,128)(2,1)S(1)} %bitcast.29), channel_id=1, source_target_pairs={{0,48},{1,193},{2,50},{3,195},{4,52},{5,197},{6,54},{7,199},{8,56}... | collective-permute-start | bytes 995336 | tf_op jit(solution)/shard_map/share_first/ppermute | solution.py:52
  108.1 0.0 collective-permute-start.15
  108.2 2.7 %collective-permute-start.16 = (bf16[144,1152]{1,0:T(8,128)(2,1)S(1)}, bf16[144,1152]{1,0:T(8,128)(2,1)S(1)}, u32[]{:S(2)}, u32[]{:S(2)}) collective-permute-start(bf16[144,1152]{1,0:T(8,128)(2,1)S(1)} %bitcast.28), channel_id=1, source_target_pairs={{0,48},{1,193},{2,50},{3,195},{4,52},{5,197},{6,54},{7,199},{8,56}... | collective-permute-start | bytes 995336 | tf_op jit(solution)/shard_map/share_first/ppermute | solution.py:52
  110.9 6.8 %collective-permute-start.21 = (bf16[288,1152]{1,0:T(8,128)(2,1)S(1)}, bf16[288,1152]{1,0:T(8,128)(2,1)S(1)}, u32[]{:S(2)}, u32[]{:S(2)}) collective-permute-start(bf16[288,1152]{1,0:T(8,128)(2,1)S(1)} %bitcast.18), channel_id=1, source_target_pairs={{0,1},{1,0},{2,3},{3,2},{4,5},{5,4},{6,7},{7,6},{8,9},{9,8},{10,11... | collective-permute-start | bytes 1990664 | tf_op jit(solution)/shard_map/share_first/ppermute | solution.py:52
  117.7 1.4 collective-permute-start.25
  119.1 0.0 collective-permute-done.15.refs_1_
  119.1 3.7 %collective-permute-start.22 = (bf16[144,1152]{1,0:T(8,128)(2,1)S(1)}, bf16[144,1152]{1,0:T(8,128)(2,1)S(1)}, u32[]{:S(2)}, u32[]{:S(2)}) collective-permute-start(bf16[144,1152]{1,0:T(8,128)(2,1)S(1)} %collective-permute-done.15.refs_1_), channel_id=1, source_target_pairs={{0,1},{1,0},{2,3},{3,2},{4,5},{5,4},{6,7},{7,6},{8,9},{9,8},{10,11... | collective-permute-start | bytes 995336 | tf_op jit(solution)/shard_map/share_first/ppermute | solution.py:52
  122.8 1.1 collective-permute-start.19
  123.8 1.6 %collective-permute-start.20 = (bf16[144,1152]{1,0:T(8,128)(2,1)S(1)}, bf16[144,1152]{1,0:T(8,128)(2,1)S(1)}, u32[]{:S(2)}, u32[]{:S(2)}) collective-permute-start(bf16[144,1152]{1,0:T(8,128)(2,1)S(1)} %collective-permute-done.16.refs_2_), channel_id=1, source_target_pairs={{0,48},{1,193},{2,50},{3,195},{4,52},{5,197},{6,54},{7,199},{8,56}... | collective-permute-start | bytes 995336 | tf_op jit(solution)/shard_map/share_first/ppermute | solution.py:52
  125.4 0.0 collective-permute-done.25.refs_11_
  125.4 4.1 %collective-permute-start.23 = (bf16[144,1152]{1,0:T(8,128)(2,1)S(1)}, bf16[144,1152]{1,0:T(8,128)(2,1)S(1)}, u32[]{:S(2)}, u32[]{:S(2)}) collective-permute-start(bf16[144,1152]{1,0:T(8,128)(2,1)S(1)} %collective-permute-done.16.refs_2_), channel_id=1, source_target_pairs={{0,1},{1,0},{2,3},{3,2},{4,5},{5,4},{6,7},{7,6},{8,9},{9,8},{10,11... | collective-permute-start | bytes 995336 | tf_op jit(solution)/shard_map/share_first/ppermute | solution.py:52
  129.6 0.0 collective-permute-done.22.refs_8_
  129.6 0.1 collective-permute-start.24
  129.7 0.3 collective-permute-done.19.refs_5_
  129.9 4.7 %collective-permute-start.26 = (bf16[144,1152]{1,0:T(8,128)(2,1)S(1)}, bf16[144,1152]{1,0:T(8,128)(2,1)S(1)}, u32[]{:S(2)}, u32[]{:S(2)}) collective-permute-start(bf16[144,1152]{1,0:T(8,128)(2,1)S(1)} %collective-permute-done.19.refs_5_), channel_id=1, source_target_pairs={{0,1},{1,0},{2,3},{3,2},{4,5},{5,4},{6,7},{7,6},{8,9},{9,8},{10,11... | collective-permute-start | bytes 995336 | tf_op jit(solution)/shard_map/share_first/ppermute | solution.py:52
  134.6 0.0 collective-permute-done.20.refs_6_
  134.6 0.0 collective-permute-start.27
  134.7 0.0 collective-permute-done.23.refs_9_
  134.7 1.2 collective-permute-done.26.refs_12_
  135.9 0.5 collective-permute-done.27.refs_13_
  136.4 2.5 %write.1 = (bf16[1152,1152]{1,0:T(8,128)(2,1)}, bf16[1152,1152]{1,0:T(8,128)(2,1)}) custom-call(bf16[288,1152]{1,0:T(8,128)(2,1)S(1)} %bitcast.19, bf16[144,1152]{1,0:T(8,128)(2,1)S(1)} %collective-permute-done.15.refs_1_, bf16[144,1152]{1,0:T(8,128)(2,1)S(1)} %collective-permute-done.16.refs_2_, bf16[144,1152]{1,0:T(8,128)(2,1)S(1)} %collective-permute-done.17.refs_3_, ...), custom_call_target="tpu_custom_call" | custom-call | tf_op jit(solution)/shard_map/write/pallas_call | solution.py:68
  (13 shorter events, 0.2 us)
Async XLA Ops:
  0.6 13.7 %collective-permute-start.3 = (bf16[128,1152]{1,0:T(8,128)(2,1)}, bf16[128,1152]{1,0:T(8,128)(2,1)S(1)}, u32[]{:S(2)}, u32[]{:S(2)}) collective-permute-start(bf16[128,1152]{1,0:T(8,128)(2,1)} %image_hbm.1), channel_id=1, source_target_pairs={{0,1},{1,0},{2,3},{3,2},{4,5},{5,4},{6,7},{7,6},{8,9},{9,8},{10,11... | collective-permute-start | bytes 884744 | tf_op jit(solution)/shard_map/band_exchange/ppermute | solution.py:52
  4.0 10.3 %collective-permute-start.2 = (bf16[128,1152]{1,0:T(8,128)(2,1)}, bf16[128,1152]{1,0:T(8,128)(2,1)S(1)}, u32[]{:S(2)}, u32[]{:S(2)}) collective-permute-start(bf16[128,1152]{1,0:T(8,128)(2,1)} %text_hbm.1), channel_id=1, source_target_pairs={{0,1},{1,0},{2,3},{3,2},{4,5},{5,4},{6,7},{7,6},{8,9},{9,8},{10,11... | collective-permute-start | bytes 884744 | tf_op jit(solution)/shard_map/band_exchange/ppermute | solution.py:52
  4.1 10.2 %collective-permute-start.4 = (s32[128]{0:T(128)}, s32[128]{0:T(128)S(1)}, u32[]{:S(2)}, u32[]{:S(2)}) collective-permute-start(s32[128]{0:T(128)} %param.11), channel_id=1, source_target_pairs={{0,1},{1,0},{2,3},{3,2},{4,5},{5,4},{6,7},{7,6},{8,9},{9,8},{10,11... | collective-permute-start | bytes 1544 | tf_op jit(solution)/shard_map/band_exchange/ppermute | solution.py:52
  4.5 16.6 %collective-permute-start.1 = (bf16[128,1152]{1,0:T(8,128)(2,1)}, bf16[128,1152]{1,0:T(8,128)(2,1)S(1)}, u32[]{:S(2)}, u32[]{:S(2)}) collective-permute-start(bf16[128,1152]{1,0:T(8,128)(2,1)} %text_hbm.1), channel_id=1, source_target_pairs={{0,254},{1,255},{2,0},{3,1},{4,2},{5,3},{6,4},{7,5},{8,6},{9,7},{1... | collective-permute-start | bytes 884744 | tf_op jit(solution)/shard_map/band_exchange/ppermute | solution.py:52
  13.0 13.9 %collective-permute-start = (bf16[128,1152]{1,0:T(8,128)(2,1)}, bf16[128,1152]{1,0:T(8,128)(2,1)S(1)}, u32[]{:S(2)}, u32[]{:S(2)}) collective-permute-start(bf16[128,1152]{1,0:T(8,128)(2,1)} %text_hbm.1), channel_id=1, source_target_pairs={{0,2},{1,3},{2,4},{3,5},{4,6},{5,7},{6,8},{7,9},{8,10},{9,11},{10,... | collective-permute-start | bytes 884744 | tf_op jit(solution)/shard_map/band_exchange/ppermute | solution.py:52
  14.3 0.7 copy-start
  26.9 6.2 %collective-permute-start.5 = (bf16[128,1152]{1,0:T(8,128)(2,1)S(1)}, bf16[128,1152]{1,0:T(8,128)(2,1)S(1)}, u32[]{:S(2)}, u32[]{:S(2)}) collective-permute-start(bf16[128,1152]{1,0:T(8,128)(2,1)S(1)} %forward.1), channel_id=1, source_target_pairs={{0,255},{1,2},{2,1},{3,4},{4,3},{5,6},{6,5},{7,8},{8,7},{9,10},{10... | collective-permute-start | bytes 884744 | tf_op jit(solution)/shard_map/forward/ppermute | solution.py:52
  27.0 12.8 %collective-permute-start.8 = (bf16[128,1152]{1,0:T(8,128)(2,1)S(1)}, bf16[128,1152]{1,0:T(8,128)(2,1)S(1)}, u32[]{:S(2)}, u32[]{:S(2)}) collective-permute-start(bf16[128,1152]{1,0:T(8,128)(2,1)S(1)} %collective-permute-done.1.above), channel_id=1, source_target_pairs={{0,1},{1,0},{2,3},{3,2},{4,5},{5,4},{6,7},{7,6},{8,9},{9,8},{10,11... | collective-permute-start | bytes 884744 | tf_op jit(solution)/shard_map/forward/ppermute | solution.py:52
  28.5 11.2 %collective-permute-start.7 = (bf16[128,1152]{1,0:T(8,128)(2,1)S(1)}, bf16[128,1152]{1,0:T(8,128)(2,1)S(1)}, u32[]{:S(2)}, u32[]{:S(2)}) collective-permute-start(bf16[128,1152]{1,0:T(8,128)(2,1)S(1)} %collective-permute-done.below), channel_id=1, source_target_pairs={{0,1},{1,0},{2,3},{3,2},{4,5},{5,4},{6,7},{7,6},{8,9},{9,8},{10,11... | collective-permute-start | bytes 884744 | tf_op jit(solution)/shard_map/forward/ppermute | solution.py:52
  33.1 9.7 %collective-permute-start.6 = (bf16[128,1152]{1,0:T(8,128)(2,1)S(1)}, bf16[128,1152]{1,0:T(8,128)(2,1)S(1)}, u32[]{:S(2)}, u32[]{:S(2)}) collective-permute-start(bf16[128,1152]{1,0:T(8,128)(2,1)S(1)} %collective-permute-done.5.far), channel_id=1, source_target_pairs={{0,1},{1,0},{2,3},{3,2},{4,5},{5,4},{6,7},{7,6},{8,9},{9,8},{10,11... | collective-permute-start | bytes 884744 | tf_op jit(solution)/shard_map/far/ppermute | solution.py:52
  46.2 7.6 %collective-permute-start.9 = (bf16[144,1152]{1,0:T(8,128)(2,1)S(1)}, bf16[144,1152]{1,0:T(8,128)(2,1)S(1)}, u32[]{:S(2)}, u32[]{:S(2)}) collective-permute-start(bf16[144,1152]{1,0:T(8,128)(2,1)S(1)} %get-tuple-element.35), channel_id=1, source_target_pairs={{0,16},{1,65},{2,18},{3,67},{4,20},{5,69},{6,22},{7,71},{8,24},{9,... | collective-permute-start | bytes 995336 | tf_op jit(solution)/shard_map/sum_first/ppermute | solution.py:52
  46.2 7.5 %collective-permute-start.10 = (bf16[144,1152]{1,0:T(8,128)(2,1)S(1)}, bf16[144,1152]{1,0:T(8,128)(2,1)S(1)}, u32[]{:S(2)}, u32[]{:S(2)}) collective-permute-start(bf16[144,1152]{1,0:T(8,128)(2,1)S(1)} %get-tuple-element.37), channel_id=1, source_target_pairs={{0,48},{1,193},{2,50},{3,195},{4,52},{5,197},{6,54},{7,199},{8,56}... | collective-permute-start | bytes 995336 | tf_op jit(solution)/shard_map/sum_first/ppermute | solution.py:52
  48.9 8.2 %collective-permute-start.12 = (bf16[144,1152]{1,0:T(8,128)(2,1)S(1)}, bf16[144,1152]{1,0:T(8,128)(2,1)S(1)}, u32[]{:S(2)}, u32[]{:S(2)}) collective-permute-start(bf16[144,1152]{1,0:T(8,128)(2,1)S(1)} %get-tuple-element.39), channel_id=1, source_target_pairs={{0,16},{1,65},{2,18},{3,67},{4,20},{5,69},{6,22},{7,71},{8,24},{9,... | collective-permute-start | bytes 995336 | tf_op jit(solution)/shard_map/sum_first/ppermute | solution.py:52
  48.9 8.2 %collective-permute-start.13 = (bf16[144,1152]{1,0:T(8,128)(2,1)S(1)}, bf16[144,1152]{1,0:T(8,128)(2,1)S(1)}, u32[]{:S(2)}, u32[]{:S(2)}) collective-permute-start(bf16[144,1152]{1,0:T(8,128)(2,1)S(1)} %get-tuple-element.40), channel_id=1, source_target_pairs={{0,48},{1,193},{2,50},{3,195},{4,52},{5,197},{6,54},{7,199},{8,56}... | collective-permute-start | bytes 995336 | tf_op jit(solution)/shard_map/sum_first/ppermute | solution.py:52
  53.9 7.6 %collective-permute-start.11 = (bf16[144,1152]{1,0:T(8,128)(2,1)S(1)}, bf16[144,1152]{1,0:T(8,128)(2,1)S(1)}, u32[]{:S(2)}, u32[]{:S(2)}) collective-permute-start(bf16[144,1152]{1,0:T(8,128)(2,1)S(1)} %get-tuple-element.38), channel_id=1, source_target_pairs={{0,16},{1,65},{2,18},{3,67},{4,20},{5,69},{6,22},{7,71},{8,24},{9,... | collective-permute-start | bytes 995336 | tf_op jit(solution)/shard_map/sum_first/ppermute | solution.py:52
  54.0 7.5 %collective-permute-start.14 = (bf16[144,1152]{1,0:T(8,128)(2,1)S(1)}, bf16[144,1152]{1,0:T(8,128)(2,1)S(1)}, u32[]{:S(2)}, u32[]{:S(2)}) collective-permute-start(bf16[144,1152]{1,0:T(8,128)(2,1)S(1)} %get-tuple-element.41), channel_id=1, source_target_pairs={{0,48},{1,193},{2,50},{3,195},{4,52},{5,197},{6,54},{7,199},{8,56}... | collective-permute-start | bytes 995336 | tf_op jit(solution)/shard_map/sum_first/ppermute | solution.py:52
  104.4 13.3 %collective-permute-start.18 = (bf16[144,1152]{1,0:T(8,128)(2,1)S(1)}, bf16[144,1152]{1,0:T(8,128)(2,1)S(1)}, u32[]{:S(2)}, u32[]{:S(2)}) collective-permute-start(bf16[144,1152]{1,0:T(8,128)(2,1)S(1)} %bitcast.29), channel_id=1, source_target_pairs={{0,48},{1,193},{2,50},{3,195},{4,52},{5,197},{6,54},{7,199},{8,56}... | collective-permute-start | bytes 995336 | tf_op jit(solution)/shard_map/share_first/ppermute | solution.py:52
  108.1 10.9 %collective-permute-start.15 = (bf16[144,1152]{1,0:T(8,128)(2,1)S(1)}, bf16[144,1152]{1,0:T(8,128)(2,1)S(1)}, u32[]{:S(2)}, u32[]{:S(2)}) collective-permute-start(bf16[144,1152]{1,0:T(8,128)(2,1)S(1)} %bitcast.30), channel_id=1, source_target_pairs={{0,16},{1,65},{2,18},{3,67},{4,20},{5,69},{6,22},{7,71},{8,24},{9,... | collective-permute-start | bytes 995336 | tf_op jit(solution)/shard_map/share_first/ppermute | solution.py:52
  108.1 14.6 %collective-permute-start.17 = (bf16[144,1152]{1,0:T(8,128)(2,1)S(1)}, bf16[144,1152]{1,0:T(8,128)(2,1)S(1)}, u32[]{:S(2)}, u32[]{:S(2)}) collective-permute-start(bf16[144,1152]{1,0:T(8,128)(2,1)S(1)} %bitcast.27), channel_id=1, source_target_pairs={{0,16},{1,65},{2,18},{3,67},{4,20},{5,69},{6,22},{7,71},{8,24},{9,... | collective-permute-start | bytes 995336 | tf_op jit(solution)/shard_map/share_first/ppermute | solution.py:52
  108.2 15.7 %collective-permute-start.16 = (bf16[144,1152]{1,0:T(8,128)(2,1)S(1)}, bf16[144,1152]{1,0:T(8,128)(2,1)S(1)}, u32[]{:S(2)}, u32[]{:S(2)}) collective-permute-start(bf16[144,1152]{1,0:T(8,128)(2,1)S(1)} %bitcast.28), channel_id=1, source_target_pairs={{0,48},{1,193},{2,50},{3,195},{4,52},{5,197},{6,54},{7,199},{8,56}... | collective-permute-start | bytes 995336 | tf_op jit(solution)/shard_map/share_first/ppermute | solution.py:52
  110.9 23.8 %collective-permute-start.21 = (bf16[288,1152]{1,0:T(8,128)(2,1)S(1)}, bf16[288,1152]{1,0:T(8,128)(2,1)S(1)}, u32[]{:S(2)}, u32[]{:S(2)}) collective-permute-start(bf16[288,1152]{1,0:T(8,128)(2,1)S(1)} %bitcast.18), channel_id=1, source_target_pairs={{0,1},{1,0},{2,3},{3,2},{4,5},{5,4},{6,7},{7,6},{8,9},{9,8},{10,11... | collective-permute-start | bytes 1990664 | tf_op jit(solution)/shard_map/share_first/ppermute | solution.py:52
  117.7 7.7 %collective-permute-start.25 = (bf16[144,1152]{1,0:T(8,128)(2,1)S(1)}, bf16[144,1152]{1,0:T(8,128)(2,1)S(1)}, u32[]{:S(2)}, u32[]{:S(2)}) collective-permute-start(bf16[144,1152]{1,0:T(8,128)(2,1)S(1)} %collective-permute-done.18.refs_4_), channel_id=1, source_target_pairs={{0,1},{1,0},{2,3},{3,2},{4,5},{5,4},{6,7},{7,6},{8,9},{9,8},{10,11... | collective-permute-start | bytes 995336 | tf_op jit(solution)/shard_map/share_first/ppermute | solution.py:52
  119.1 10.5 %collective-permute-start.22 = (bf16[144,1152]{1,0:T(8,128)(2,1)S(1)}, bf16[144,1152]{1,0:T(8,128)(2,1)S(1)}, u32[]{:S(2)}, u32[]{:S(2)}) collective-permute-start(bf16[144,1152]{1,0:T(8,128)(2,1)S(1)} %collective-permute-done.15.refs_1_), channel_id=1, source_target_pairs={{0,1},{1,0},{2,3},{3,2},{4,5},{5,4},{6,7},{7,6},{8,9},{9,8},{10,11... | collective-permute-start | bytes 995336 | tf_op jit(solution)/shard_map/share_first/ppermute | solution.py:52
  122.8 7.2 %collective-permute-start.19 = (bf16[144,1152]{1,0:T(8,128)(2,1)S(1)}, bf16[144,1152]{1,0:T(8,128)(2,1)S(1)}, u32[]{:S(2)}, u32[]{:S(2)}) collective-permute-start(bf16[144,1152]{1,0:T(8,128)(2,1)S(1)} %collective-permute-done.15.refs_1_), channel_id=1, source_target_pairs={{0,16},{1,65},{2,18},{3,67},{4,20},{5,69},{6,22},{7,71},{8,24},{9,... | collective-permute-start | bytes 995336 | tf_op jit(solution)/shard_map/share_first/ppermute | solution.py:52
  123.8 10.8 %collective-permute-start.20 = (bf16[144,1152]{1,0:T(8,128)(2,1)S(1)}, bf16[144,1152]{1,0:T(8,128)(2,1)S(1)}, u32[]{:S(2)}, u32[]{:S(2)}) collective-permute-start(bf16[144,1152]{1,0:T(8,128)(2,1)S(1)} %collective-permute-done.16.refs_2_), channel_id=1, source_target_pairs={{0,48},{1,193},{2,50},{3,195},{4,52},{5,197},{6,54},{7,199},{8,56}... | collective-permute-start | bytes 995336 | tf_op jit(solution)/shard_map/share_first/ppermute | solution.py:52
  125.4 9.2 %collective-permute-start.23 = (bf16[144,1152]{1,0:T(8,128)(2,1)S(1)}, bf16[144,1152]{1,0:T(8,128)(2,1)S(1)}, u32[]{:S(2)}, u32[]{:S(2)}) collective-permute-start(bf16[144,1152]{1,0:T(8,128)(2,1)S(1)} %collective-permute-done.16.refs_2_), channel_id=1, source_target_pairs={{0,1},{1,0},{2,3},{3,2},{4,5},{5,4},{6,7},{7,6},{8,9},{9,8},{10,11... | collective-permute-start | bytes 995336 | tf_op jit(solution)/shard_map/share_first/ppermute | solution.py:52
  129.6 5.1 %collective-permute-start.24 = (bf16[144,1152]{1,0:T(8,128)(2,1)S(1)}, bf16[144,1152]{1,0:T(8,128)(2,1)S(1)}, u32[]{:S(2)}, u32[]{:S(2)}) collective-permute-start(bf16[144,1152]{1,0:T(8,128)(2,1)S(1)} %collective-permute-done.17.refs_3_), channel_id=1, source_target_pairs={{0,1},{1,0},{2,3},{3,2},{4,5},{5,4},{6,7},{7,6},{8,9},{9,8},{10,11... | collective-permute-start | bytes 995336 | tf_op jit(solution)/shard_map/share_first/ppermute | solution.py:52
  129.9 6.0 %collective-permute-start.26 = (bf16[144,1152]{1,0:T(8,128)(2,1)S(1)}, bf16[144,1152]{1,0:T(8,128)(2,1)S(1)}, u32[]{:S(2)}, u32[]{:S(2)}) collective-permute-start(bf16[144,1152]{1,0:T(8,128)(2,1)S(1)} %collective-permute-done.19.refs_5_), channel_id=1, source_target_pairs={{0,1},{1,0},{2,3},{3,2},{4,5},{5,4},{6,7},{7,6},{8,9},{9,8},{10,11... | collective-permute-start | bytes 995336 | tf_op jit(solution)/shard_map/share_first/ppermute | solution.py:52
  134.6 1.7 %collective-permute-start.27 = (bf16[144,1152]{1,0:T(8,128)(2,1)S(1)}, bf16[144,1152]{1,0:T(8,128)(2,1)S(1)}, u32[]{:S(2)}, u32[]{:S(2)}) collective-permute-start(bf16[144,1152]{1,0:T(8,128)(2,1)S(1)} %collective-permute-done.20.refs_6_), channel_id=1, source_target_pairs={{0,1},{1,0},{2,3},{3,2},{4,5},{5,4},{6,7},{7,6},{8,9},{9,8},{10,11... | collective-permute-start | bytes 995336 | tf_op jit(solution)/shard_map/share_first/ppermute | solution.py:52

commit v5 on v4

--- a/solution.py
+++ b/solution.py
@@ -40,7 +40,7 @@
 RIGHT, LEFT = along_first(1), along_first(-1)
 SECOND = groups(lambda y, x, z, c: (c, z, x if c == 0 else y))
 LINES = groups(lambda y, x, z, c: (c, x, y))
-FORWARD = [(i, (i + 1) % N if i % 2 else (i - 1) % N) for i in range(N)]
+FAR = [(i, (i + 3) % N if i % 2 else (i - 3) % N) for i in range(N)]
 TEXT = 1
 
 
@@ -56,7 +56,7 @@
     return lax.all_to_all(parts, "dp", 0, 0, axis_index_groups=members, tiled=True)
 
 
-def call(body, outs, scratch=(), flops=0, result=pltpu.VMEM):
+def call(body, outs, scratch=(), flops=0, result=pltpu.VMEM, aliases=()):
     def run(smem, outside, *arrays):
         specs = (
             [pl.BlockSpec(memory_space=pltpu.SMEM)] * len(smem)
@@ -71,6 +71,7 @@
             in_specs=specs,
             out_specs=[pl.BlockSpec(memory_space=result)] * len(outs),
             scratch_shapes=list(scratch),
+            input_output_aliases=dict(aliases),
             cost_estimate=pl.CostEstimate(flops=flops, bytes_accessed=0, transcendentals=0),
             compiler_params=pltpu.CompilerParams(vmem_limit_bytes=32 * MIB),
         )(*smem, *outside, *held)
@@ -173,16 +174,15 @@
         add_head(head, text_near, back, None)
 
 
-def choose_kernel(below, above, done_first, out):
-    core = core_place()[0]
-
-    @pl.when(core == 1)
-    def _():
-        out[...] = below[...]
-
-    @pl.when(core == 0)
-    def _():
-        out[...] = above[...]
+def gate_kernel(*refs):
+    pass
+
+
+def after(token, *arrays):
+    outs = [(a.shape, a.dtype) for a in arrays]
+    return call(gate_kernel, outs, aliases=[(k, k) for k in range(len(arrays))])(
+        (), (), *arrays, token
+    )
 
 
 def pair_kernel(
@@ -300,7 +300,6 @@
     slab = depth // 4
     half = slab // 2
     scalars = (log_scale, shift)
-    block = ((rows, width), bf16)
     pair, pair_f32 = ((2 * rows, width), bf16), ((2 * rows, width), f32)
     total = ((depth, width), f32)
     matrix = ((depth, width), bf16)
@@ -311,6 +310,7 @@
         position_other = send(position, SWAP)
         below = send(text_x, shifted(2))
         above = send(text_x, shifted(-2))
+        far = send(text_x, FAR)
     with jax.named_scope("near"):
         image_near, weight, image_emb, image_projected, image_inverse, grad, head = call(
             near_kernel,
@@ -326,9 +326,8 @@
             scalars, (text_x, image_x, text_w, image_w), text_other, image_other,
             position[None], position_other[None],
         )
-    with jax.named_scope("forward"):
-        [onward] = call(choose_kernel, [block])((), (), below, above, image_inverse)
-        far = send(onward, FORWARD)
+    with jax.named_scope("swap_neighbours"):
+        below, above = after(image_inverse, below, above)
         below_other = send(below, SWAP)
         above_other = send(above, SWAP)
     visits = call(
@@ -382,13 +381,15 @@
     with jax.named_scope("share_first"):
         top, bottom = own[:half], own[half:]
         left_top = send(top, RIGHT)
+        right_top = send(top, LEFT)
+        left_bottom = send(bottom, RIGHT)
         right_bottom = send(bottom, LEFT)
-        left_bottom = send(bottom, RIGHT)
-        right_top = send(top, LEFT)
+        own_other = send(own, SWAP)
         across_top = send(left_top, RIGHT)
         across_bottom = send(right_bottom, LEFT)
-        mine = [own, left_top, right_bottom, left_bottom, right_top, across_top, across_bottom]
-        theirs = [send(one, SWAP) for one in mine]
+        mine = [left_top, right_bottom, left_bottom, right_top, across_top, across_bottom]
+        theirs = [own_other] + [send(one, SWAP) for one in mine]
+        mine = [own] + mine
     with jax.named_scope("write"):
         return call(
             write_kernel,

time: 139 us -> 130 us (0.935)
  starting transfers between devices: 58.7 us -> 49.4 us
  blocking collectives: 42.4 us -> 44.5 us
  waiting for transfers between devices: 16.2 us -> 14.1 us
    ppermute x28, starting transfers between devices: 58.7 us -> 49.4 us  [send(): return lax.ppermute(block, 'dp', pairs)]
    ppermute x28, waiting for transfers between devices: 16.2 us -> 14.1 us  [send(): return lax.ppermute(block, 'dp', pairs)]
    all_to_all x4, blocking collectives: 42.4 us -> 44.5 us  [exchange(): lax.all_to_all(parts, 'dp', 0, 0, axis_index_groups=members, tiled=True)]
  transfers between devices with their start and end apart: 28 -> 28, of which waited for: 8 -> 11; matrix products, arithmetic and copies ran while one was open for 0% -> 0% of each run, Pallas kernels for 9% -> 10%
where the time goes in v5:
time: 130 us
  starting transfers between devices  49.4 us (38%)
  blocking collectives  44.5 us (34%)
  Pallas kernels  18.6 us (14%)
  waiting for transfers between devices  14.1 us (11%)
  between operations  2.3 us (2%)
    ppermute x28, starting transfers between devices, send(): return lax.ppermute(block, 'dp', pairs)  49.4 us
    all_to_all x4, blocking collectives, exchange(): lax.all_to_all(parts, 'dp', 0, 0, axis_index_groups=members, tiled=True)  44.5 us
    pallas_call x8, Pallas kernels, run(): pl.pallas_call(body, out_shape=[jax.ShapeDtypeStruct(s, d) for s, d in ou...  18.6 us
    ppermute x28, waiting for transfers between devices, send(): return lax.ppermute(block, 'dp', pairs)  14.1 us
  transfers between devices with their start and end apart: 28, of which 11 were waited for; matrix products, arithmetic and copies ran while one was open for 0% of the time, Pallas kernels for 10%

profile of v5, /device:TPU:1, one launch (start us, length us, event | category | flops | bytes accessed | tf_op | source)
XLA Modules:
  0.0 129.8 jit_solution(18114759066458148478)
XLA Ops:
  0.6 3.3 %collective-permute-start.2 = (bf16[128,1152]{1,0:T(8,128)(2,1)}, bf16[128,1152]{1,0:T(8,128)(2,1)S(1)}, u32[]{:S(2)}, u32[]{:S(2)}) collective-permute-start(bf16[128,1152]{1,0:T(8,128)(2,1)} %text_hbm.1), channel_id=1, source_target_pairs={{0,1},{1,0},{2,3},{3,2},{4,5},{5,4},{6,7},{7,6},{8,9},{9,8},{10,11... | collective-permute-start | bytes 884744 | tf_op jit(solution)/shard_map/band_exchange/ppermute | solution.py:52
  4.0 0.1 collective-permute-start.3
  4.1 0.4 collective-permute-start.4
  4.5 0.0 collective-permute-start.5
  4.5 8.5 %collective-permute-start.6 = (bf16[128,1152]{1,0:T(8,128)(2,1)}, bf16[128,1152]{1,0:T(8,128)(2,1)S(1)}, u32[]{:S(2)}, u32[]{:S(2)}) collective-permute-start(bf16[128,1152]{1,0:T(8,128)(2,1)} %text_hbm.1), channel_id=1, source_target_pairs={{0,254},{1,255},{2,0},{3,1},{4,2},{5,3},{6,4},{7,5},{8,6},{9,7},{1... | collective-permute-start | bytes 884744 | tf_op jit(solution)/shard_map/band_exchange/ppermute | solution.py:52
  14.3 0.0 collective-permute-done.4
  14.3 0.1 collective-permute-start
  14.4 0.0 collective-permute-done.3.image_other
  14.4 0.6 copy-done
  15.1 6.1 %near.1 = (bf16[256,1152]{1,0:T(8,128)(2,1)S(1)}, bf16[1152,1152]{1,0:T(8,128)(2,1)S(1)}, bf16[256,1152]{1,0:T(8,128)(2,1)S(1)}, f32[256,1152]{1,0:T(8,128)S(1)}...) custom-call(f32[1]{0:T(128)S(6)} %copy.13.log_scale, f32[1]{0:T(128)S(6)} %copy.14.shift, ...), custom_call_target="tpu_custom_call" | custom-call | flops 4000000000 | tf_op jit(solution)/shard_map/near/pallas_call | solution.py:68
  21.2 0.0 collective-permute-done.5.refs_0_
  21.2 0.5 collective-permute-done.6.refs_1_
  21.6 1.0 collective-permute-start.7
  22.6 0.1 collective-permute-start.8
  22.7 1.4 %collective-permute-done.far = bf16[128,1152]{1,0:T(8,128)(2,1)S(1)} collective-permute-done((bf16[128,1152]{1,0:T(8,128)(2,1)}, bf16[128,1152]{1,0:T(8,128)(2,1)S(1)}, u32[]{:S(2)}, u32[]{:S(2)}) %collective-permute-start) | collective-permute-done | bytes 294944 | tf_op jit(solution)/shard_map/band_exchange/ppermute | solution.py:52
  24.1 5.9 %collective-permute-start.1 = (bf16[128,1152]{1,0:T(8,128)(2,1)S(1)}, bf16[128,1152]{1,0:T(8,128)(2,1)S(1)}, u32[]{:S(2)}, u32[]{:S(2)}) collective-permute-start(bf16[128,1152]{1,0:T(8,128)(2,1)S(1)} %collective-permute-done.far), channel_id=1, source_target_pairs={{0,1},{1,0},{2,3},{3,2},{4,5},{5,4},{6,7},{7,6},{8,9},{9,8},{10,11... | collective-permute-start | bytes 884744 | tf_op jit(solution)/shard_map/far/ppermute | solution.py:52
  30.0 3.2 %received.1 = (f32[256,1152]{1,0:T(8,128)S(1)}, f32[1152,1152]{1,0:T(8,128)S(1)}) custom-call(f32[1]{0:T(128)S(6)} %copy.13.log_scale, f32[1]{0:T(128)S(6)} %copy.14.shift, bf16[128,1152]{1,0:T(8,128)(2,1)S(1)} %get-tuple-element.27.below, bf16[128,1152]{1,0:T(8,128)(2,1)S(1)} %get-tuple-element.28.above, bf16[1152,1152]{1,0:T(8,128)(2,1)S(1)} %get-tuple-element.24.text_w, ...), custom_call_target="tpu_custom_call" | custom-call | flops 4000000000 | tf_op jit(solution)/shard_map/received/pallas_call | solution.py:68
  33.3 0.0 collective-permute-done.7.below
  33.3 0.0 collective-permute-done.8.above
  33.3 3.0 %partners.1 = (f32[256,1152]{1,0:T(8,128)S(1)}, f32[1152,1152]{1,0:T(8,128)S(1)}) custom-call(f32[1]{0:T(128)S(6)} %copy.13.log_scale, f32[1]{0:T(128)S(6)} %copy.14.shift, bf16[128,1152]{1,0:T(8,128)(2,1)S(1)} %collective-permute-done.7.below, bf16[128,1152]{1,0:T(8,128)(2,1)S(1)} %collective-permute-done.8.above, ...), custom_call_target="tpu_custom_call" | custom-call | flops 4000000000 | tf_op jit(solution)/shard_map/partners/pallas_call | solution.py:68
  36.4 3.3 %far.1 = (bf16[288,1152]{1,0:T(8,128)(2,1)S(1)}, bf16[144,1152]{1,0:T(8,128)(2,1)S(1)}, bf16[144,1152]{1,0:T(8,128)(2,1)S(1)}, bf16[144,1152]{1,0:T(8,128)(2,1)S...) custom-call(f32[1]{0:T(128)S(6)} %copy.13.log_scale, ...), custom_call_target="tpu_custom_call" | custom-call | flops 4000000000 | tf_op jit(solution)/shard_map/far/pallas_call | solution.py:68
  39.7 0.1 collective-permute-start.10
  39.8 1.5 %collective-permute-start.9 = (bf16[144,1152]{1,0:T(8,128)(2,1)S(1)}, bf16[144,1152]{1,0:T(8,128)(2,1)S(1)}, u32[]{:S(2)}, u32[]{:S(2)}) collective-permute-start(bf16[144,1152]{1,0:T(8,128)(2,1)S(1)} %get-tuple-element.39), channel_id=1, source_target_pairs={{0,16},{1,65},{2,18},{3,67},{4,20},{5,69},{6,22},{7,71},{8,24},{9,... | collective-permute-start | bytes 995336 | tf_op jit(solution)/shard_map/sum_first/ppermute | solution.py:52
  41.3 0.0 collective-permute-start.12
  41.3 2.6 %collective-permute-start.13 = (bf16[144,1152]{1,0:T(8,128)(2,1)S(1)}, bf16[144,1152]{1,0:T(8,128)(2,1)S(1)}, u32[]{:S(2)}, u32[]{:S(2)}) collective-permute-start(bf16[144,1152]{1,0:T(8,128)(2,1)S(1)} %get-tuple-element.44), channel_id=1, source_target_pairs={{0,48},{1,193},{2,50},{3,195},{4,52},{5,197},{6,54},{7,199},{8,56}... | collective-permute-start | bytes 995336 | tf_op jit(solution)/shard_map/sum_first/ppermute | solution.py:52
  43.9 2.1 %collective-permute-done.10.d = bf16[144,1152]{1,0:T(8,128)(2,1)S(1)} collective-permute-done((bf16[144,1152]{1,0:T(8,128)(2,1)S(1)}, bf16[144,1152]{1,0:T(8,128)(2,1)S(1)}, u32[]{:S(2)}, u32[]{:S(2)}) %collective-permute-start.10) | collective-permute-done | bytes 331808 | tf_op jit(solution)/shard_map/sum_first/ppermute | solution.py:52
  46.1 1.3 %collective-permute-done.9.b = bf16[144,1152]{1,0:T(8,128)(2,1)S(1)} collective-permute-done((bf16[144,1152]{1,0:T(8,128)(2,1)S(1)}, bf16[144,1152]{1,0:T(8,128)(2,1)S(1)}, u32[]{:S(2)}, u32[]{:S(2)}) %collective-permute-start.9) | collective-permute-done | bytes 331808 | tf_op jit(solution)/shard_map/sum_first/ppermute | solution.py:52
  47.4 0.2 sum_first.2
  47.5 0.2 collective-permute-start.11
  47.8 2.5 %collective-permute-start.14 = (bf16[144,1152]{1,0:T(8,128)(2,1)S(1)}, bf16[144,1152]{1,0:T(8,128)(2,1)S(1)}, u32[]{:S(2)}, u32[]{:S(2)}) collective-permute-start(bf16[144,1152]{1,0:T(8,128)(2,1)S(1)} %get-tuple-element.45), channel_id=1, source_target_pairs={{0,48},{1,193},{2,50},{3,195},{4,52},{5,197},{6,54},{7,199},{8,56}... | collective-permute-start | bytes 995336 | tf_op jit(solution)/shard_map/sum_first/ppermute | solution.py:52
  50.3 0.3 collective-permute-done.12.a_bottom
  50.6 0.0 collective-permute-done.13.b_top
  50.6 4.2 %collective-permute-done.11.a_top = bf16[144,1152]{1,0:T(8,128)(2,1)S(1)} collective-permute-done((bf16[144,1152]{1,0:T(8,128)(2,1)S(1)}, bf16[144,1152]{1,0:T(8,128)(2,1)S(1)}, u32[]{:S(2)}, u32[]{:S(2)}) %collective-permute-start.11) | collective-permute-done | bytes 331808 | tf_op jit(solution)/shard_map/sum_first/ppermute | solution.py:52
  54.8 0.0 collective-permute-done.14.b_bottom
  54.8 0.3 sum_first.3
  55.0 10.6 %all_to_all.20 = bf16[4,72,1152]{2,1,0:T(8,128)(2,1)S(1)} all-to-all(bf16[4,72,1152]{2,1,0:T(8,128)(2,1)S(1)} %bitcast.20), channel_id=1, replica_groups={{0,64,128,192},{1,17,33,49},{2,66,130,194},{3,19,35,51},{4,68,132,196},..., dimensions={0} | all-to-all | bytes 1327104 | tf_op jit(solution)/shard_map/sum_second/all_to_all | solution.py:56
  65.6 0.1 reduce_sum.24
  65.8 12.9 %all_to_all.21 = bf16[88,8,128]{2,1,0:T(8,128)(2,1)S(1)} all-to-all(bf16[88,8,128]{2,1,0:T(8,128)(2,1)S(1)} %concatenate.3), channel_id=1, replica_groups={{0,2,4,6,8,10,12,14},{1,3,5,7,9,11,13,15},{16,18,20,22,24,26,28,30},{17..., dimensions={0} | all-to-all | bytes 360448 | tf_op jit(solution)/shard_map/sum_lines/all_to_all | solution.py:56
  78.7 10.9 %all_to_all.22 = bf16[88,8,128]{2,1,0:T(8,128)(2,1)S(1)} all-to-all(bf16[88,8,128]{2,1,0:T(8,128)(2,1)S(1)} %bitcast.24), channel_id=1, replica_groups={{0,2,4,6,8,10,12,14},{1,3,5,7,9,11,13,15},{16,18,20,22,24,26,28,30},{17..., dimensions={0} | all-to-all | bytes 360448 | tf_op jit(solution)/shard_map/share_lines/all_to_all | solution.py:56
  89.7 10.1 %all_to_all.23 = bf16[4,72,1152]{2,1,0:T(8,128)(2,1)S(1)} all-to-all(bf16[4,72,1152]{2,1,0:T(8,128)(2,1)S(1)} %tile.20), channel_id=1, replica_groups={{0,64,128,192},{1,17,33,49},{2,66,130,194},{3,19,35,51},{4,68,132,196},..., dimensions={0} | all-to-all | bytes 1327104 | tf_op jit(solution)/shard_map/share_second/all_to_all | solution.py:56
  99.8 0.1 fusion
  99.9 0.1 collective-permute-start.15
  99.9 4.8 %collective-permute-start.16 = (bf16[144,1152]{1,0:T(8,128)(2,1)S(1)}, bf16[144,1152]{1,0:T(8,128)(2,1)S(1)}, u32[]{:S(2)}, u32[]{:S(2)}) collective-permute-start(bf16[144,1152]{1,0:T(8,128)(2,1)S(1)} %bitcast.29), channel_id=1, source_target_pairs={{0,48},{1,193},{2,50},{3,195},{4,52},{5,197},{6,54},{7,199},{8,56}... | collective-permute-start | bytes 995336 | tf_op jit(solution)/shard_map/share_first/ppermute | solution.py:52
  104.8 0.0 collective-permute-start.17
  104.8 2.7 %collective-permute-start.18 = (bf16[144,1152]{1,0:T(8,128)(2,1)S(1)}, bf16[144,1152]{1,0:T(8,128)(2,1)S(1)}, u32[]{:S(2)}, u32[]{:S(2)}) collective-permute-start(bf16[144,1152]{1,0:T(8,128)(2,1)S(1)} %bitcast.28), channel_id=1, source_target_pairs={{0,48},{1,193},{2,50},{3,195},{4,52},{5,197},{6,54},{7,199},{8,56}... | collective-permute-start | bytes 995336 | tf_op jit(solution)/shard_map/share_first/ppermute | solution.py:52
  107.4 6.9 %collective-permute-start.21 = (bf16[288,1152]{1,0:T(8,128)(2,1)S(1)}, bf16[288,1152]{1,0:T(8,128)(2,1)S(1)}, u32[]{:S(2)}, u32[]{:S(2)}) collective-permute-start(bf16[288,1152]{1,0:T(8,128)(2,1)S(1)} %bitcast.18), channel_id=1, source_target_pairs={{0,1},{1,0},{2,3},{3,2},{4,5},{5,4},{6,7},{7,6},{8,9},{9,8},{10,11... | collective-permute-start | bytes 1990664 | tf_op jit(solution)/shard_map/share_first/ppermute | solution.py:52
  114.3 0.0 collective-permute-done.15.refs_1_
  114.3 0.0 collective-permute-start.19
  114.3 0.0 collective-permute-done.16.refs_2_
  114.3 2.7 %collective-permute-start.20 = (bf16[144,1152]{1,0:T(8,128)(2,1)S(1)}, bf16[144,1152]{1,0:T(8,128)(2,1)S(1)}, u32[]{:S(2)}, u32[]{:S(2)}) collective-permute-start(bf16[144,1152]{1,0:T(8,128)(2,1)S(1)} %collective-permute-done.16.refs_2_), channel_id=1, source_target_pairs={{0,48},{1,193},{2,50},{3,195},{4,52},{5,197},{6,54},{7,199},{8,56}... | collective-permute-start | bytes 995336 | tf_op jit(solution)/shard_map/share_first/ppermute | solution.py:52
  117.0 0.0 collective-permute-done.17.refs_3_
  117.0 2.6 %collective-permute-start.22 = (bf16[144,1152]{1,0:T(8,128)(2,1)S(1)}, bf16[144,1152]{1,0:T(8,128)(2,1)S(1)}, u32[]{:S(2)}, u32[]{:S(2)}) collective-permute-start(bf16[144,1152]{1,0:T(8,128)(2,1)S(1)} %collective-permute-done.15.refs_1_), channel_id=1, source_target_pairs={{0,1},{1,0},{2,3},{3,2},{4,5},{5,4},{6,7},{7,6},{8,9},{9,8},{10,11... | collective-permute-start | bytes 995336 | tf_op jit(solution)/shard_map/share_first/ppermute | solution.py:52
  119.7 0.0 collective-permute-done.18.refs_4_
  119.7 0.0 collective-permute-start.23
  119.7 2.1 %collective-permute-done.19.refs_5_ = bf16[144,1152]{1,0:T(8,128)(2,1)S(1)} collective-permute-done((bf16[144,1152]{1,0:T(8,128)(2,1)S(1)}, bf16[144,1152]{1,0:T(8,128)(2,1)S(1)}, u32[]{:S(2)}, u32[]{:S(2)}) %collective-permute-start.19) | collective-permute-done | bytes 331808 | tf_op jit(solution)/shard_map/share_first/ppermute | solution.py:52
  121.8 2.6 %collective-permute-start.24 = (bf16[144,1152]{1,0:T(8,128)(2,1)S(1)}, bf16[144,1152]{1,0:T(8,128)(2,1)S(1)}, u32[]{:S(2)}, u32[]{:S(2)}) collective-permute-start(bf16[144,1152]{1,0:T(8,128)(2,1)S(1)} %collective-permute-done.17.refs_3_), channel_id=1, source_target_pairs={{0,1},{1,0},{2,3},{3,2},{4,5},{5,4},{6,7},{7,6},{8,9},{9,8},{10,11... | collective-permute-start | bytes 995336 | tf_op jit(solution)/shard_map/share_first/ppermute | solution.py:52
  124.4 0.0 collective-permute-start.25
  124.4 0.5 collective-permute-start.26
  125.0 0.1 collective-permute-start.27
  125.0 0.6 collective-permute-done.24.refs_10_
  125.7 0.5 collective-permute-done.25.refs_11_
  126.2 0.5 collective-permute-done.26.refs_12_
  126.6 0.5 collective-permute-done.27.refs_13_
  127.1 2.5 %write.1 = (bf16[1152,1152]{1,0:T(8,128)(2,1)}, bf16[1152,1152]{1,0:T(8,128)(2,1)}) custom-call(bf16[288,1152]{1,0:T(8,128)(2,1)S(1)} %bitcast.19, bf16[144,1152]{1,0:T(8,128)(2,1)S(1)} %collective-permute-done.15.refs_1_, bf16[144,1152]{1,0:T(8,128)(2,1)S(1)} %collective-permute-done.16.refs_2_, bf16[144,1152]{1,0:T(8,128)(2,1)S(1)} %collective-permute-done.17.refs_3_, ...), custom_call_target="tpu_custom_call" | custom-call | tf_op jit(solution)/shard_map/write/pallas_call | solution.py:68
  (13 shorter events, 0.2 us)
Async XLA Ops:
  0.6 13.8 %collective-permute-start.2 = (bf16[128,1152]{1,0:T(8,128)(2,1)}, bf16[128,1152]{1,0:T(8,128)(2,1)S(1)}, u32[]{:S(2)}, u32[]{:S(2)}) collective-permute-start(bf16[128,1152]{1,0:T(8,128)(2,1)} %text_hbm.1), channel_id=1, source_target_pairs={{0,1},{1,0},{2,3},{3,2},{4,5},{5,4},{6,7},{7,6},{8,9},{9,8},{10,11... | collective-permute-start | bytes 884744 | tf_op jit(solution)/shard_map/band_exchange/ppermute | solution.py:52
  4.0 10.4 %collective-permute-start.3 = (bf16[128,1152]{1,0:T(8,128)(2,1)}, bf16[128,1152]{1,0:T(8,128)(2,1)S(1)}, u32[]{:S(2)}, u32[]{:S(2)}) collective-permute-start(bf16[128,1152]{1,0:T(8,128)(2,1)} %image_hbm.1), channel_id=1, source_target_pairs={{0,1},{1,0},{2,3},{3,2},{4,5},{5,4},{6,7},{7,6},{8,9},{9,8},{10,11... | collective-permute-start | bytes 884744 | tf_op jit(solution)/shard_map/band_exchange/ppermute | solution.py:52
  4.1 10.2 %collective-permute-start.4 = (s32[128]{0:T(128)}, s32[128]{0:T(128)S(1)}, u32[]{:S(2)}, u32[]{:S(2)}) collective-permute-start(s32[128]{0:T(128)} %param.11), channel_id=1, source_target_pairs={{0,1},{1,0},{2,3},{3,2},{4,5},{5,4},{6,7},{7,6},{8,9},{9,8},{10,11... | collective-permute-start | bytes 1544 | tf_op jit(solution)/shard_map/band_exchange/ppermute | solution.py:52
  4.5 16.7 %collective-permute-start.5 = (bf16[128,1152]{1,0:T(8,128)(2,1)}, bf16[128,1152]{1,0:T(8,128)(2,1)S(1)}, u32[]{:S(2)}, u32[]{:S(2)}) collective-permute-start(bf16[128,1152]{1,0:T(8,128)(2,1)} %text_hbm.1), channel_id=1, source_target_pairs={{0,2},{1,3},{2,4},{3,5},{4,6},{5,7},{6,8},{7,9},{8,10},{9,11},{10,... | collective-permute-start | bytes 884744 | tf_op jit(solution)/shard_map/band_exchange/ppermute | solution.py:52
  4.5 17.2 %collective-permute-start.6 = (bf16[128,1152]{1,0:T(8,128)(2,1)}, bf16[128,1152]{1,0:T(8,128)(2,1)S(1)}, u32[]{:S(2)}, u32[]{:S(2)}) collective-permute-start(bf16[128,1152]{1,0:T(8,128)(2,1)} %text_hbm.1), channel_id=1, source_target_pairs={{0,254},{1,255},{2,0},{3,1},{4,2},{5,3},{6,4},{7,5},{8,6},{9,7},{1... | collective-permute-start | bytes 884744 | tf_op jit(solution)/shard_map/band_exchange/ppermute | solution.py:52
  14.3 9.8 %collective-permute-start = (bf16[128,1152]{1,0:T(8,128)(2,1)}, bf16[128,1152]{1,0:T(8,128)(2,1)S(1)}, u32[]{:S(2)}, u32[]{:S(2)}) collective-permute-start(bf16[128,1152]{1,0:T(8,128)(2,1)} %text_hbm.1), channel_id=1, source_target_pairs={{0,253},{1,4},{2,255},{3,6},{4,1},{5,8},{6,3},{7,10},{8,5},{9,12},... | collective-permute-start | bytes 884744 | tf_op jit(solution)/shard_map/band_exchange/ppermute | solution.py:52
  14.4 0.7 copy-start
  21.6 11.6 %collective-permute-start.7 = (bf16[128,1152]{1,0:T(8,128)(2,1)S(1)}, bf16[128,1152]{1,0:T(8,128)(2,1)S(1)}, u32[]{:S(2)}, u32[]{:S(2)}) collective-permute-start(bf16[128,1152]{1,0:T(8,128)(2,1)S(1)} %get-tuple-element.27.below), channel_id=1, source_target_pairs={{0,1},{1,0},{2,3},{3,2},{4,5},{5,4},{6,7},{7,6},{8,9},{9,8},{10,11... | collective-permute-start | bytes 884744 | tf_op jit(solution)/shard_map/swap_neighbours/ppermute | solution.py:52
  22.6 10.7 %collective-permute-start.8 = (bf16[128,1152]{1,0:T(8,128)(2,1)S(1)}, bf16[128,1152]{1,0:T(8,128)(2,1)S(1)}, u32[]{:S(2)}, u32[]{:S(2)}) collective-permute-start(bf16[128,1152]{1,0:T(8,128)(2,1)S(1)} %get-tuple-element.28.above), channel_id=1, source_target_pairs={{0,1},{1,0},{2,3},{3,2},{4,5},{5,4},{6,7},{7,6},{8,9},{9,8},{10,11... | collective-permute-start | bytes 884744 | tf_op jit(solution)/shard_map/swap_neighbours/ppermute | solution.py:52
  24.1 12.2 %collective-permute-start.1 = (bf16[128,1152]{1,0:T(8,128)(2,1)S(1)}, bf16[128,1152]{1,0:T(8,128)(2,1)S(1)}, u32[]{:S(2)}, u32[]{:S(2)}) collective-permute-start(bf16[128,1152]{1,0:T(8,128)(2,1)S(1)} %collective-permute-done.far), channel_id=1, source_target_pairs={{0,1},{1,0},{2,3},{3,2},{4,5},{5,4},{6,7},{7,6},{8,9},{9,8},{10,11... | collective-permute-start | bytes 884744 | tf_op jit(solution)/shard_map/far/ppermute | solution.py:52
  39.7 6.3 %collective-permute-start.10 = (bf16[144,1152]{1,0:T(8,128)(2,1)S(1)}, bf16[144,1152]{1,0:T(8,128)(2,1)S(1)}, u32[]{:S(2)}, u32[]{:S(2)}) collective-permute-start(bf16[144,1152]{1,0:T(8,128)(2,1)S(1)} %get-tuple-element.41), channel_id=1, source_target_pairs={{0,48},{1,193},{2,50},{3,195},{4,52},{5,197},{6,54},{7,199},{8,56}... | collective-permute-start | bytes 995336 | tf_op jit(solution)/shard_map/sum_first/ppermute | solution.py:52
  39.8 7.6 %collective-permute-start.9 = (bf16[144,1152]{1,0:T(8,128)(2,1)S(1)}, bf16[144,1152]{1,0:T(8,128)(2,1)S(1)}, u32[]{:S(2)}, u32[]{:S(2)}) collective-permute-start(bf16[144,1152]{1,0:T(8,128)(2,1)S(1)} %get-tuple-element.39), channel_id=1, source_target_pairs={{0,16},{1,65},{2,18},{3,67},{4,20},{5,69},{6,22},{7,71},{8,24},{9,... | collective-permute-start | bytes 995336 | tf_op jit(solution)/shard_map/sum_first/ppermute | solution.py:52
  41.3 9.4 %collective-permute-start.12 = (bf16[144,1152]{1,0:T(8,128)(2,1)S(1)}, bf16[144,1152]{1,0:T(8,128)(2,1)S(1)}, u32[]{:S(2)}, u32[]{:S(2)}) collective-permute-start(bf16[144,1152]{1,0:T(8,128)(2,1)S(1)} %get-tuple-element.43), channel_id=1, source_target_pairs={{0,16},{1,65},{2,18},{3,67},{4,20},{5,69},{6,22},{7,71},{8,24},{9,... | collective-permute-start | bytes 995336 | tf_op jit(solution)/shard_map/sum_first/ppermute | solution.py:52
  41.3 9.3 %collective-permute-start.13 = (bf16[144,1152]{1,0:T(8,128)(2,1)S(1)}, bf16[144,1152]{1,0:T(8,128)(2,1)S(1)}, u32[]{:S(2)}, u32[]{:S(2)}) collective-permute-start(bf16[144,1152]{1,0:T(8,128)(2,1)S(1)} %get-tuple-element.44), channel_id=1, source_target_pairs={{0,48},{1,193},{2,50},{3,195},{4,52},{5,197},{6,54},{7,199},{8,56}... | collective-permute-start | bytes 995336 | tf_op jit(solution)/shard_map/sum_first/ppermute | solution.py:52
  47.5 7.3 %collective-permute-start.11 = (bf16[144,1152]{1,0:T(8,128)(2,1)S(1)}, bf16[144,1152]{1,0:T(8,128)(2,1)S(1)}, u32[]{:S(2)}, u32[]{:S(2)}) collective-permute-start(bf16[144,1152]{1,0:T(8,128)(2,1)S(1)} %get-tuple-element.42), channel_id=1, source_target_pairs={{0,16},{1,65},{2,18},{3,67},{4,20},{5,69},{6,22},{7,71},{8,24},{9,... | collective-permute-start | bytes 995336 | tf_op jit(solution)/shard_map/sum_first/ppermute | solution.py:52
  47.8 7.0 %collective-permute-start.14 = (bf16[144,1152]{1,0:T(8,128)(2,1)S(1)}, bf16[144,1152]{1,0:T(8,128)(2,1)S(1)}, u32[]{:S(2)}, u32[]{:S(2)}) collective-permute-start(bf16[144,1152]{1,0:T(8,128)(2,1)S(1)} %get-tuple-element.45), channel_id=1, source_target_pairs={{0,48},{1,193},{2,50},{3,195},{4,52},{5,197},{6,54},{7,199},{8,56}... | collective-permute-start | bytes 995336 | tf_op jit(solution)/shard_map/sum_first/ppermute | solution.py:52
  99.9 14.5 %collective-permute-start.15 = (bf16[144,1152]{1,0:T(8,128)(2,1)S(1)}, bf16[144,1152]{1,0:T(8,128)(2,1)S(1)}, u32[]{:S(2)}, u32[]{:S(2)}) collective-permute-start(bf16[144,1152]{1,0:T(8,128)(2,1)S(1)} %bitcast.27), channel_id=1, source_target_pairs={{0,16},{1,65},{2,18},{3,67},{4,20},{5,69},{6,22},{7,71},{8,24},{9,... | collective-permute-start | bytes 995336 | tf_op jit(solution)/shard_map/share_first/ppermute | solution.py:52
  99.9 14.4 %collective-permute-start.16 = (bf16[144,1152]{1,0:T(8,128)(2,1)S(1)}, bf16[144,1152]{1,0:T(8,128)(2,1)S(1)}, u32[]{:S(2)}, u32[]{:S(2)}) collective-permute-start(bf16[144,1152]{1,0:T(8,128)(2,1)S(1)} %bitcast.29), channel_id=1, source_target_pairs={{0,48},{1,193},{2,50},{3,195},{4,52},{5,197},{6,54},{7,199},{8,56}... | collective-permute-start | bytes 995336 | tf_op jit(solution)/shard_map/share_first/ppermute | solution.py:52
  104.8 12.3 %collective-permute-start.17 = (bf16[144,1152]{1,0:T(8,128)(2,1)S(1)}, bf16[144,1152]{1,0:T(8,128)(2,1)S(1)}, u32[]{:S(2)}, u32[]{:S(2)}) collective-permute-start(bf16[144,1152]{1,0:T(8,128)(2,1)S(1)} %bitcast.30), channel_id=1, source_target_pairs={{0,16},{1,65},{2,18},{3,67},{4,20},{5,69},{6,22},{7,71},{8,24},{9,... | collective-permute-start | bytes 995336 | tf_op jit(solution)/shard_map/share_first/ppermute | solution.py:52
  104.8 14.9 %collective-permute-start.18 = (bf16[144,1152]{1,0:T(8,128)(2,1)S(1)}, bf16[144,1152]{1,0:T(8,128)(2,1)S(1)}, u32[]{:S(2)}, u32[]{:S(2)}) collective-permute-start(bf16[144,1152]{1,0:T(8,128)(2,1)S(1)} %bitcast.28), channel_id=1, source_target_pairs={{0,48},{1,193},{2,50},{3,195},{4,52},{5,197},{6,54},{7,199},{8,56}... | collective-permute-start | bytes 995336 | tf_op jit(solution)/shard_map/share_first/ppermute | solution.py:52
  107.4 18.7 %collective-permute-start.21 = (bf16[288,1152]{1,0:T(8,128)(2,1)S(1)}, bf16[288,1152]{1,0:T(8,128)(2,1)S(1)}, u32[]{:S(2)}, u32[]{:S(2)}) collective-permute-start(bf16[288,1152]{1,0:T(8,128)(2,1)S(1)} %bitcast.18), channel_id=1, source_target_pairs={{0,1},{1,0},{2,3},{3,2},{4,5},{5,4},{6,7},{7,6},{8,9},{9,8},{10,11... | collective-permute-start | bytes 1990664 | tf_op jit(solution)/shard_map/share_first/ppermute | solution.py:52
  114.3 7.5 %collective-permute-start.19 = (bf16[144,1152]{1,0:T(8,128)(2,1)S(1)}, bf16[144,1152]{1,0:T(8,128)(2,1)S(1)}, u32[]{:S(2)}, u32[]{:S(2)}) collective-permute-start(bf16[144,1152]{1,0:T(8,128)(2,1)S(1)} %collective-permute-done.15.refs_1_), channel_id=1, source_target_pairs={{0,16},{1,65},{2,18},{3,67},{4,20},{5,69},{6,22},{7,71},{8,24},{9,... | collective-permute-start | bytes 995336 | tf_op jit(solution)/shard_map/share_first/ppermute | solution.py:52
  114.3 10.1 %collective-permute-start.20 = (bf16[144,1152]{1,0:T(8,128)(2,1)S(1)}, bf16[144,1152]{1,0:T(8,128)(2,1)S(1)}, u32[]{:S(2)}, u32[]{:S(2)}) collective-permute-start(bf16[144,1152]{1,0:T(8,128)(2,1)S(1)} %collective-permute-done.16.refs_2_), channel_id=1, source_target_pairs={{0,48},{1,193},{2,50},{3,195},{4,52},{5,197},{6,54},{7,199},{8,56}... | collective-permute-start | bytes 995336 | tf_op jit(solution)/shard_map/share_first/ppermute | solution.py:52
  117.0 7.4 %collective-permute-start.22 = (bf16[144,1152]{1,0:T(8,128)(2,1)S(1)}, bf16[144,1152]{1,0:T(8,128)(2,1)S(1)}, u32[]{:S(2)}, u32[]{:S(2)}) collective-permute-start(bf16[144,1152]{1,0:T(8,128)(2,1)S(1)} %collective-permute-done.15.refs_1_), channel_id=1, source_target_pairs={{0,1},{1,0},{2,3},{3,2},{4,5},{5,4},{6,7},{7,6},{8,9},{9,8},{10,11... | collective-permute-start | bytes 995336 | tf_op jit(solution)/shard_map/share_first/ppermute | solution.py:52
  119.7 5.3 %collective-permute-start.23 = (bf16[144,1152]{1,0:T(8,128)(2,1)S(1)}, bf16[144,1152]{1,0:T(8,128)(2,1)S(1)}, u32[]{:S(2)}, u32[]{:S(2)}) collective-permute-start(bf16[144,1152]{1,0:T(8,128)(2,1)S(1)} %collective-permute-done.16.refs_2_), channel_id=1, source_target_pairs={{0,1},{1,0},{2,3},{3,2},{4,5},{5,4},{6,7},{7,6},{8,9},{9,8},{10,11... | collective-permute-start | bytes 995336 | tf_op jit(solution)/shard_map/share_first/ppermute | solution.py:52
  121.8 3.9 %collective-permute-start.24 = (bf16[144,1152]{1,0:T(8,128)(2,1)S(1)}, bf16[144,1152]{1,0:T(8,128)(2,1)S(1)}, u32[]{:S(2)}, u32[]{:S(2)}) collective-permute-start(bf16[144,1152]{1,0:T(8,128)(2,1)S(1)} %collective-permute-done.17.refs_3_), channel_id=1, source_target_pairs={{0,1},{1,0},{2,3},{3,2},{4,5},{5,4},{6,7},{7,6},{8,9},{9,8},{10,11... | collective-permute-start | bytes 995336 | tf_op jit(solution)/shard_map/share_first/ppermute | solution.py:52
  124.4 1.7 %collective-permute-start.25 = (bf16[144,1152]{1,0:T(8,128)(2,1)S(1)}, bf16[144,1152]{1,0:T(8,128)(2,1)S(1)}, u32[]{:S(2)}, u32[]{:S(2)}) collective-permute-start(bf16[144,1152]{1,0:T(8,128)(2,1)S(1)} %collective-permute-done.18.refs_4_), channel_id=1, source_target_pairs={{0,1},{1,0},{2,3},{3,2},{4,5},{5,4},{6,7},{7,6},{8,9},{9,8},{10,11... | collective-permute-start | bytes 995336 | tf_op jit(solution)/shard_map/share_first/ppermute | solution.py:52
  124.4 2.2 %collective-permute-start.26 = (bf16[144,1152]{1,0:T(8,128)(2,1)S(1)}, bf16[144,1152]{1,0:T(8,128)(2,1)S(1)}, u32[]{:S(2)}, u32[]{:S(2)}) collective-permute-start(bf16[144,1152]{1,0:T(8,128)(2,1)S(1)} %collective-permute-done.19.refs_5_), channel_id=1, source_target_pairs={{0,1},{1,0},{2,3},{3,2},{4,5},{5,4},{6,7},{7,6},{8,9},{9,8},{10,11... | collective-permute-start | bytes 995336 | tf_op jit(solution)/shard_map/share_first/ppermute | solution.py:52
  125.0 2.2 %collective-permute-start.27 = (bf16[144,1152]{1,0:T(8,128)(2,1)S(1)}, bf16[144,1152]{1,0:T(8,128)(2,1)S(1)}, u32[]{:S(2)}, u32[]{:S(2)}) collective-permute-start(bf16[144,1152]{1,0:T(8,128)(2,1)S(1)} %collective-permute-done.20.refs_6_), channel_id=1, source_target_pairs={{0,1},{1,0},{2,3},{3,2},{4,5},{5,4},{6,7},{7,6},{8,9},{9,8},{10,11... | collective-permute-start | bytes 995336 | tf_op jit(solution)/shard_map/share_first/ppermute | solution.py:52

commit v6 on v5

--- a/solution.py
+++ b/solution.py
@@ -178,11 +178,11 @@
     pass
 
 
-def after(token, *arrays):
+def after(token, *arrays, in_hbm=False):
     outs = [(a.shape, a.dtype) for a in arrays]
-    return call(gate_kernel, outs, aliases=[(k, k) for k in range(len(arrays))])(
-        (), (), *arrays, token
-    )
+    first = 1 if in_hbm else 0
+    gate = call(gate_kernel, outs, aliases=[(first + k, k) for k in range(len(arrays))])
+    return gate((), (token,), *arrays) if in_hbm else gate((), (), *arrays, token)
 
 
 def pair_kernel(
@@ -262,36 +262,51 @@
     ).astype(bf16)
 
 
-PIECES = [(0, 0), (3, 0), (1, 1), (3, 1), (1, 0), (2, 0), (2, 1)]
-
-
-def write_kernel(*refs):
-    count = len(PIECES)
-    mine, theirs, (text, image, sems) = refs[:count], refs[count : 2 * count], refs[2 * count :]
-    core, place, other_place = core_place()
-    slab = mine[0].shape[0]
-
-    def copies(pieces, position, out, first):
-        moves = []
-        for k, (piece, (turn, part)) in enumerate(zip(pieces, PIECES)):
-            start = lax.rem(position + turn, 4) * slab + part * (slab // 2)
-            target = out.at[pl.ds(pl.multiple_of(start, 16), piece.shape[0]), :]
-            moves.append(pltpu.make_async_copy(piece, target, sems.at[first + k]))
-        return moves
-
-    def go(moves):
-        for move in moves:
-            move.start()
-        for move in moves:
-            move.wait()
-
-    @pl.when(core == TEXT)
-    def _():
-        go(copies(mine, place, text, 0) + copies(theirs, other_place, image, count))
-
-    @pl.when(core != TEXT)
-    def _():
-        go(copies(mine, place, image, 0) + copies(theirs, other_place, text, count))
+OWN, LEFT_TOP, RIGHT_BOTTOM, LEFT_BOTTOM, RIGHT_TOP, ACROSS_TOP, ACROSS_BOTTOM = PIECES = (
+    (0, 0), (3, 0), (1, 1), (3, 1), (1, 0), (2, 0), (2, 1)
+)
+
+
+def write(outs, mine, theirs):
+    places = [*mine, *theirs]
+
+    def body(*refs):
+        pieces, (text, image, sems) = refs[len(outs) : len(outs) + len(places)], refs[-3:]
+        core, place, other_place = core_place()
+
+        def copies(first, other):
+            moves = []
+            for k, (piece, (turn, part)) in enumerate(zip(pieces, places)):
+                own = k < len(mine)
+                slab = piece.shape[0] * (1 if (turn, part) == OWN else 2)
+                start = lax.rem((place if own else other_place) + turn, 4) * slab + part * slab // 2
+                at = pl.ds(pl.multiple_of(start, 16), piece.shape[0])
+                moves.append(
+                    pltpu.make_async_copy(piece, (first if own else other).at[at, :], sems.at[k])
+                )
+            for move in moves:
+                move.start()
+            for move in moves:
+                move.wait()
+
+        @pl.when(core == TEXT)
+        def _():
+            copies(text, image)
+
+        @pl.when(core != TEXT)
+        def _():
+            copies(image, text)
+
+    def run(*arrays, shape):
+        return call(
+            body,
+            [shape, shape],
+            [pltpu.SemaphoreType.DMA((len(places),))],
+            result=pltpu.HBM,
+            aliases=[(k, k) for k in range(len(outs))],
+        )((), outs, *arrays)
+
+    return run
 
 
 def on_device(text_x, image_x, text_w, image_w, position, log_scale, shift):
@@ -335,10 +350,11 @@
     )
     with jax.named_scope("received"):
         grad, head = visits(scalars, (), below, above, weight, image_emb, grad, head)
+        [far] = after(grad, far)
+        far_other = send(far, SWAP)
     with jax.named_scope("partners"):
         grad, head = visits(scalars, (), below_other, above_other, weight, image_emb, grad, head)
     with jax.named_scope("far"):
-        far_other = send(far, SWAP)
         own, right_top, right_bottom, left_top, left_bottom, far_right, far_left = call(
             far_kernel,
             [piece] + [half_piece] * 6,
@@ -387,16 +403,16 @@
         own_other = send(own, SWAP)
         across_top = send(left_top, RIGHT)
         across_bottom = send(right_bottom, LEFT)
-        mine = [left_top, right_bottom, left_bottom, right_top, across_top, across_bottom]
-        theirs = [own_other] + [send(one, SWAP) for one in mine]
-        mine = [own] + mine
+        others = [send(piece, SWAP) for piece in (left_top, right_bottom, left_bottom, right_top)]
     with jax.named_scope("write"):
-        return call(
-            write_kernel,
-            [matrix, matrix],
-            [pltpu.SemaphoreType.DMA((2 * len(PIECES),))],
-            result=pltpu.HBM,
-        )((), (), *mine, *theirs)
+        outs = write((), [OWN, LEFT_TOP, RIGHT_BOTTOM, LEFT_BOTTOM, RIGHT_TOP], [OWN])(
+            own, left_top, right_bottom, left_bottom, right_top, own_other, shape=matrix
+        )
+        across_top, across_bottom = after(outs[0], across_top, across_bottom, in_hbm=True)
+        others += [send(across_top, SWAP), send(across_bottom, SWAP)]
+        return write(tuple(outs), [ACROSS_TOP, ACROSS_BOTTOM], PIECES[1:])(
+            across_top, across_bottom, *others, shape=matrix
+        )
 
 
 def solution(mesh):

time: 130 us -> 125 us (0.962)
  starting transfers between devices: 49.4 us -> 43.3 us
    ppermute x28, starting transfers between devices: 49.4 us -> 43.3 us  [send(): return lax.ppermute(block, 'dp', pairs)]
    pallas_call x8 -> x11, Pallas kernels: 18.6 us -> 19.1 us  [run(): pl.pallas_call(body, out_shape=[jax.ShapeDtypeStruct(s, d) for s, d in ou...]
  transfers between devices with their start and end apart: 28 -> 28, of which waited for: 11 -> 11; matrix products, arithmetic and copies ran while one was open for 0% -> 0% of each run, Pallas kernels for 10% -> 11%
where the time goes in v6:
time: 125 us; the launch traced here: 124 us
  blocking collectives  44.4 us (36%)
  starting transfers between devices  43.3 us (35%)
  Pallas kernels  19.1 us (15%)
  waiting for transfers between devices  14.4 us (12%)
  between operations  2.3 us (2%)
    all_to_all x4, blocking collectives, exchange(): lax.all_to_all(parts, 'dp', 0, 0, axis_index_groups=members, tiled=True)  44.4 us
    ppermute x28, starting transfers between devices, send(): return lax.ppermute(block, 'dp', pairs)  43.3 us
    pallas_call x11, Pallas kernels, run(): pl.pallas_call(body, out_shape=[jax.ShapeDtypeStruct(s, d) for s, d in ou...  19.1 us
    ppermute x28, waiting for transfers between devices, send(): return lax.ppermute(block, 'dp', pairs)  14.4 us
  transfers between devices with their start and end apart: 28, of which 11 were waited for; matrix products, arithmetic and copies ran while one was open for 0% of the time, Pallas kernels for 11%

profile of v6, /device:TPU:1, one launch (start us, length us, event | category | flops | bytes accessed | tf_op | source)
XLA Modules:
  0.0 124.3 jit_solution(13362337663022392361)
XLA Ops:
  0.6 3.3 %collective-permute-start.3 = (bf16[128,1152]{1,0:T(8,128)(2,1)}, bf16[128,1152]{1,0:T(8,128)(2,1)S(1)}, u32[]{:S(2)}, u32[]{:S(2)}) collective-permute-start(bf16[128,1152]{1,0:T(8,128)(2,1)} %text_hbm.1), channel_id=1, source_target_pairs={{0,1},{1,0},{2,3},{3,2},{4,5},{5,4},{6,7},{7,6},{8,9},{9,8},{10,11... | collective-permute-start | bytes 884744 | tf_op jit(solution)/shard_map/band_exchange/ppermute | solution.py:52
  4.0 0.1 collective-permute-start.4
  4.1 0.4 collective-permute-start.5
  4.5 0.0 collective-permute-start.1
  4.5 8.5 %collective-permute-start.2 = (bf16[128,1152]{1,0:T(8,128)(2,1)}, bf16[128,1152]{1,0:T(8,128)(2,1)S(1)}, u32[]{:S(2)}, u32[]{:S(2)}) collective-permute-start(bf16[128,1152]{1,0:T(8,128)(2,1)} %text_hbm.1), channel_id=1, source_target_pairs={{0,254},{1,255},{2,0},{3,1},{4,2},{5,3},{6,4},{7,5},{8,6},{9,7},{1... | collective-permute-start | bytes 884744 | tf_op jit(solution)/shard_map/band_exchange/ppermute | solution.py:52
  14.3 0.0 collective-permute-done.5
  14.3 0.1 collective-permute-start
  14.4 0.0 collective-permute-done.3.text_other
  14.4 0.0 collective-permute-done.4.image_other
  14.4 0.6 copy-done
  15.1 6.1 %near.1 = (bf16[256,1152]{1,0:T(8,128)(2,1)S(1)}, bf16[1152,1152]{1,0:T(8,128)(2,1)S(1)}, bf16[256,1152]{1,0:T(8,128)(2,1)S(1)}, f32[256,1152]{1,0:T(8,128)S(1)}...) custom-call(f32[1]{0:T(128)S(6)} %copy.23.log_scale, f32[1]{0:T(128)S(6)} %copy.24.shift, ...), custom_call_target="tpu_custom_call" | custom-call | flops 4000000000 | tf_op jit(solution)/shard_map/near/pallas_call | solution.py:68
  21.2 0.0 collective-permute-done.1.refs_0_
  21.2 0.5 collective-permute-done.2.refs_1_
  21.6 1.0 collective-permute-start.7
  22.6 0.1 collective-permute-start.8
  22.7 3.0 %received.2 = (f32[256,1152]{1,0:T(8,128)S(1)}, f32[1152,1152]{1,0:T(8,128)S(1)}) custom-call(f32[1]{0:T(128)S(6)} %copy.23.log_scale, f32[1]{0:T(128)S(6)} %copy.24.shift, bf16[128,1152]{1,0:T(8,128)(2,1)S(1)} %get-tuple-element.29.below, bf16[128,1152]{1,0:T(8,128)(2,1)S(1)} %get-tuple-element.30.above, bf16[1152,1152]{1,0:T(8,128)(2,1)S(1)} %get-tuple-element.31.text_w, ...), custom_call_target="tpu_custom_call" | custom-call | flops 4000000000 | tf_op jit(solution)/shard_map/received/pallas_call | solution.py:68
  25.8 0.0 collective-permute-done.refs_0_
  25.8 4.3 %collective-permute-start.6 = (bf16[128,1152]{1,0:T(8,128)(2,1)S(1)}, bf16[128,1152]{1,0:T(8,128)(2,1)S(1)}, u32[]{:S(2)}, u32[]{:S(2)}) collective-permute-start(bf16[128,1152]{1,0:T(8,128)(2,1)S(1)} %received.3.far), channel_id=1, source_target_pairs={{0,1},{1,0},{2,3},{3,2},{4,5},{5,4},{6,7},{7,6},{8,9},{9,8},{10,11... | collective-permute-start | bytes 884744 | tf_op jit(solution)/shard_map/received/ppermute | solution.py:52
  30.0 0.0 collective-permute-done.7.below
  30.0 0.0 collective-permute-done.8.above
  30.0 3.1 %partners.1 = (f32[256,1152]{1,0:T(8,128)S(1)}, f32[1152,1152]{1,0:T(8,128)S(1)}) custom-call(f32[1]{0:T(128)S(6)} %copy.23.log_scale, f32[1]{0:T(128)S(6)} %copy.24.shift, bf16[128,1152]{1,0:T(8,128)(2,1)S(1)} %collective-permute-done.7.below, bf16[128,1152]{1,0:T(8,128)(2,1)S(1)} %collective-permute-done.8.above, ...), custom_call_target="tpu_custom_call" | custom-call | flops 4000000000 | tf_op jit(solution)/shard_map/partners/pallas_call | solution.py:68
  33.1 3.4 %far.1 = (bf16[288,1152]{1,0:T(8,128)(2,1)S(1)}, bf16[144,1152]{1,0:T(8,128)(2,1)S(1)}, bf16[144,1152]{1,0:T(8,128)(2,1)S(1)}, bf16[144,1152]{1,0:T(8,128)(2,1)S...) custom-call(f32[1]{0:T(128)S(6)} %copy.23.log_scale, ...), custom_call_target="tpu_custom_call" | custom-call | flops 4000000000 | tf_op jit(solution)/shard_map/far/pallas_call | solution.py:68
  36.5 0.1 collective-permute-start.10
  36.6 1.5 %collective-permute-start.9 = (bf16[144,1152]{1,0:T(8,128)(2,1)S(1)}, bf16[144,1152]{1,0:T(8,128)(2,1)S(1)}, u32[]{:S(2)}, u32[]{:S(2)}) collective-permute-start(bf16[144,1152]{1,0:T(8,128)(2,1)S(1)} %get-tuple-element.43), channel_id=1, source_target_pairs={{0,16},{1,65},{2,18},{3,67},{4,20},{5,69},{6,22},{7,71},{8,24},{9,... | collective-permute-start | bytes 995336 | tf_op jit(solution)/shard_map/sum_first/ppermute | solution.py:52
  38.0 0.0 collective-permute-start.12
  38.0 2.6 %collective-permute-start.13 = (bf16[144,1152]{1,0:T(8,128)(2,1)S(1)}, bf16[144,1152]{1,0:T(8,128)(2,1)S(1)}, u32[]{:S(2)}, u32[]{:S(2)}) collective-permute-start(bf16[144,1152]{1,0:T(8,128)(2,1)S(1)} %get-tuple-element.48), channel_id=1, source_target_pairs={{0,48},{1,193},{2,50},{3,195},{4,52},{5,197},{6,54},{7,199},{8,56}... | collective-permute-start | bytes 995336 | tf_op jit(solution)/shard_map/sum_first/ppermute | solution.py:52
  40.7 2.1 %collective-permute-done.10.d = bf16[144,1152]{1,0:T(8,128)(2,1)S(1)} collective-permute-done((bf16[144,1152]{1,0:T(8,128)(2,1)S(1)}, bf16[144,1152]{1,0:T(8,128)(2,1)S(1)}, u32[]{:S(2)}, u32[]{:S(2)}) %collective-permute-start.10) | collective-permute-done | bytes 331808 | tf_op jit(solution)/shard_map/sum_first/ppermute | solution.py:52
  42.8 1.3 %collective-permute-done.9.b = bf16[144,1152]{1,0:T(8,128)(2,1)S(1)} collective-permute-done((bf16[144,1152]{1,0:T(8,128)(2,1)S(1)}, bf16[144,1152]{1,0:T(8,128)(2,1)S(1)}, u32[]{:S(2)}, u32[]{:S(2)}) %collective-permute-start.9) | collective-permute-done | bytes 331808 | tf_op jit(solution)/shard_map/sum_first/ppermute | solution.py:52
  44.1 0.2 sum_first.2
  44.3 0.1 collective-permute-start.11
  44.4 2.7 %collective-permute-start.14 = (bf16[144,1152]{1,0:T(8,128)(2,1)S(1)}, bf16[144,1152]{1,0:T(8,128)(2,1)S(1)}, u32[]{:S(2)}, u32[]{:S(2)}) collective-permute-start(bf16[144,1152]{1,0:T(8,128)(2,1)S(1)} %get-tuple-element.49), channel_id=1, source_target_pairs={{0,48},{1,193},{2,50},{3,195},{4,52},{5,197},{6,54},{7,199},{8,56}... | collective-permute-start | bytes 995336 | tf_op jit(solution)/shard_map/sum_first/ppermute | solution.py:52
  47.0 0.5 collective-permute-done.12.a_bottom
  47.5 4.3 %collective-permute-done.11.a_top = bf16[144,1152]{1,0:T(8,128)(2,1)S(1)} collective-permute-done((bf16[144,1152]{1,0:T(8,128)(2,1)S(1)}, bf16[144,1152]{1,0:T(8,128)(2,1)S(1)}, u32[]{:S(2)}, u32[]{:S(2)}) %collective-permute-start.11) | collective-permute-done | bytes 331808 | tf_op jit(solution)/shard_map/sum_first/ppermute | solution.py:52
  51.8 0.0 collective-permute-done.14.b_bottom
  51.8 0.3 sum_first.3
  52.1 10.6 %all_to_all.20 = bf16[4,72,1152]{2,1,0:T(8,128)(2,1)S(1)} all-to-all(bf16[4,72,1152]{2,1,0:T(8,128)(2,1)S(1)} %bitcast.20), channel_id=1, replica_groups={{0,64,128,192},{1,17,33,49},{2,66,130,194},{3,19,35,51},{4,68,132,196},..., dimensions={0} | all-to-all | bytes 1327104 | tf_op jit(solution)/shard_map/sum_second/all_to_all | solution.py:56
  62.7 0.1 reduce_sum.24
  62.8 12.8 %all_to_all.21 = bf16[88,8,128]{2,1,0:T(8,128)(2,1)S(1)} all-to-all(bf16[88,8,128]{2,1,0:T(8,128)(2,1)S(1)} %concatenate.3), channel_id=1, replica_groups={{0,2,4,6,8,10,12,14},{1,3,5,7,9,11,13,15},{16,18,20,22,24,26,28,30},{17..., dimensions={0} | all-to-all | bytes 360448 | tf_op jit(solution)/shard_map/sum_lines/all_to_all | solution.py:56
  75.7 10.8 %all_to_all.22 = bf16[88,8,128]{2,1,0:T(8,128)(2,1)S(1)} all-to-all(bf16[88,8,128]{2,1,0:T(8,128)(2,1)S(1)} %bitcast.24), channel_id=1, replica_groups={{0,2,4,6,8,10,12,14},{1,3,5,7,9,11,13,15},{16,18,20,22,24,26,28,30},{17..., dimensions={0} | all-to-all | bytes 360448 | tf_op jit(solution)/shard_map/share_lines/all_to_all | solution.py:56
  86.6 10.1 %all_to_all.23 = bf16[4,72,1152]{2,1,0:T(8,128)(2,1)S(1)} all-to-all(bf16[4,72,1152]{2,1,0:T(8,128)(2,1)S(1)} %tile.20), channel_id=1, replica_groups={{0,64,128,192},{1,17,33,49},{2,66,130,194},{3,19,35,51},{4,68,132,196},..., dimensions={0} | all-to-all | bytes 1327104 | tf_op jit(solution)/shard_map/share_second/all_to_all | solution.py:56
  96.7 6.9 %collective-permute-start.19 = (bf16[288,1152]{1,0:T(8,128)(2,1)S(1)}, bf16[288,1152]{1,0:T(8,128)(2,1)S(1)}, u32[]{:S(2)}, u32[]{:S(2)}) collective-permute-start(bf16[288,1152]{1,0:T(8,128)(2,1)S(1)} %bitcast.18), channel_id=1, source_target_pairs={{0,1},{1,0},{2,3},{3,2},{4,5},{5,4},{6,7},{7,6},{8,9},{9,8},{10,11... | collective-permute-start | bytes 1990664 | tf_op jit(solution)/shard_map/share_first/ppermute | solution.py:52
  103.6 0.1 fusion
  103.6 0.4 collective-permute-start.15
  104.0 2.4 %collective-permute-start.16 = (bf16[144,1152]{1,0:T(8,128)(2,1)S(1)}, bf16[144,1152]{1,0:T(8,128)(2,1)S(1)}, u32[]{:S(2)}, u32[]{:S(2)}) collective-permute-start(bf16[144,1152]{1,0:T(8,128)(2,1)S(1)} %bitcast.29), channel_id=1, source_target_pairs={{0,48},{1,193},{2,50},{3,195},{4,52},{5,197},{6,54},{7,199},{8,56}... | collective-permute-start | bytes 995336 | tf_op jit(solution)/shard_map/share_first/ppermute | solution.py:52
  106.4 0.0 collective-permute-start.17
  106.4 2.7 %collective-permute-start.18 = (bf16[144,1152]{1,0:T(8,128)(2,1)S(1)}, bf16[144,1152]{1,0:T(8,128)(2,1)S(1)}, u32[]{:S(2)}, u32[]{:S(2)}) collective-permute-start(bf16[144,1152]{1,0:T(8,128)(2,1)S(1)} %bitcast.28), channel_id=1, source_target_pairs={{0,48},{1,193},{2,50},{3,195},{4,52},{5,197},{6,54},{7,199},{8,56}... | collective-permute-start | bytes 995336 | tf_op jit(solution)/shard_map/share_first/ppermute | solution.py:52
  109.1 2.1 %collective-permute-done.15.refs_1_ = bf16[144,1152]{1,0:T(8,128)(2,1)S(1)} collective-permute-done((bf16[144,1152]{1,0:T(8,128)(2,1)S(1)}, bf16[144,1152]{1,0:T(8,128)(2,1)S(1)}, u32[]{:S(2)}, u32[]{:S(2)}) %collective-permute-start.15) | collective-permute-done | bytes 331808 | tf_op jit(solution)/shard_map/share_first/ppermute | solution.py:52
  111.2 2.7 %collective-permute-start.21 = (bf16[144,1152]{1,0:T(8,128)(2,1)S(1)}, bf16[144,1152]{1,0:T(8,128)(2,1)S(1)}, u32[]{:S(2)}, u32[]{:S(2)}) collective-permute-start(bf16[144,1152]{1,0:T(8,128)(2,1)S(1)} %collective-permute-done.16.refs_2_), channel_id=1, source_target_pairs={{0,48},{1,193},{2,50},{3,195},{4,52},{5,197},{6,54},{7,199},{8,56}... | collective-permute-start | bytes 995336 | tf_op jit(solution)/shard_map/share_first/ppermute | solution.py:52
  113.9 0.9 collective-permute-done.17.refs_3_
  114.8 0.9 collective-permute-start.22
  115.6 0.0 collective-permute-start.23
  115.6 0.5 collective-permute-start.24
  116.1 1.5 %write.3 = (bf16[1152,1152]{1,0:T(8,128)(2,1)}, bf16[1152,1152]{1,0:T(8,128)(2,1)}) custom-call(bf16[288,1152]{1,0:T(8,128)(2,1)S(1)} %bitcast.19, bf16[144,1152]{1,0:T(8,128)(2,1)S(1)} %collective-permute-done.15.refs_1_, bf16[144,1152]{1,0:T(8,128)(2,1)S(1)} %collective-permute-done.16.refs_2_, bf16[144,1152]{1,0:T(8,128)(2,1)S(1)} %collective-permute-done.17.refs_3_, ...), custom_call_target="tpu_custom_call" | custom-call | tf_op jit(solution)/shard_map/write/pallas_call | solution.py:68
  117.7 1.0 collective-permute-done.20.refs_1_
  118.7 1.7 %collective-permute-start.25 = (bf16[144,1152]{1,0:T(8,128)(2,1)S(1)}, bf16[144,1152]{1,0:T(8,128)(2,1)S(1)}, u32[]{:S(2)}, u32[]{:S(2)}) collective-permute-start(bf16[144,1152]{1,0:T(8,128)(2,1)S(1)} %collective-permute-done.18.refs_4_), channel_id=1, source_target_pairs={{0,1},{1,0},{2,3},{3,2},{4,5},{5,4},{6,7},{7,6},{8,9},{9,8},{10,11... | collective-permute-start | bytes 995336 | tf_op jit(solution)/shard_map/share_first/ppermute | solution.py:52
  120.4 0.1 collective-permute-start.26
  120.5 0.0 collective-permute-done.22.refs_4_
  120.5 0.4 collective-permute-start.27
  120.9 0.0 collective-permute-done.23.refs_5_
  120.9 0.0 collective-permute-done.24.refs_6_
  120.9 0.7 collective-permute-done.25.refs_7_
  121.7 0.5 collective-permute-done.26.refs_8_
  122.1 0.5 collective-permute-done.27.refs_9_
  122.6 1.6 %write.5 = (bf16[1152,1152]{1,0:T(8,128)(2,1)}, bf16[1152,1152]{1,0:T(8,128)(2,1)}) custom-call(bf16[1152,1152]{1,0:T(8,128)(2,1)} %get-tuple-element.50.refs_0_, bf16[1152,1152]{1,0:T(8,128)(2,1)} %get-tuple-element.51.refs_1_, bf16[144,1152]{1,0:T(8,128)(2,1)S(1)} %get-tuple-element.52.refs_2_, ...), custom_call_target="tpu_custom_call", output_to_operand_aliasing={{0}: (0, {}), {1}: (1, {})} | custom-call | tf_op jit(solution)/shard_map/write/pallas_call | solution.py:68
  (16 shorter events, 0.2 us)
Async XLA Ops:
  0.6 13.8 %collective-permute-start.3 = (bf16[128,1152]{1,0:T(8,128)(2,1)}, bf16[128,1152]{1,0:T(8,128)(2,1)S(1)}, u32[]{:S(2)}, u32[]{:S(2)}) collective-permute-start(bf16[128,1152]{1,0:T(8,128)(2,1)} %text_hbm.1), channel_id=1, source_target_pairs={{0,1},{1,0},{2,3},{3,2},{4,5},{5,4},{6,7},{7,6},{8,9},{9,8},{10,11... | collective-permute-start | bytes 884744 | tf_op jit(solution)/shard_map/band_exchange/ppermute | solution.py:52
  4.0 10.4 %collective-permute-start.4 = (bf16[128,1152]{1,0:T(8,128)(2,1)}, bf16[128,1152]{1,0:T(8,128)(2,1)S(1)}, u32[]{:S(2)}, u32[]{:S(2)}) collective-permute-start(bf16[128,1152]{1,0:T(8,128)(2,1)} %image_hbm.1), channel_id=1, source_target_pairs={{0,1},{1,0},{2,3},{3,2},{4,5},{5,4},{6,7},{7,6},{8,9},{9,8},{10,11... | collective-permute-start | bytes 884744 | tf_op jit(solution)/shard_map/band_exchange/ppermute | solution.py:52
  4.1 10.2 %collective-permute-start.5 = (s32[128]{0:T(128)}, s32[128]{0:T(128)S(1)}, u32[]{:S(2)}, u32[]{:S(2)}) collective-permute-start(s32[128]{0:T(128)} %param.11), channel_id=1, source_target_pairs={{0,1},{1,0},{2,3},{3,2},{4,5},{5,4},{6,7},{7,6},{8,9},{9,8},{10,11... | collective-permute-start | bytes 1544 | tf_op jit(solution)/shard_map/band_exchange/ppermute | solution.py:52
  4.5 16.7 %collective-permute-start.1 = (bf16[128,1152]{1,0:T(8,128)(2,1)}, bf16[128,1152]{1,0:T(8,128)(2,1)S(1)}, u32[]{:S(2)}, u32[]{:S(2)}) collective-permute-start(bf16[128,1152]{1,0:T(8,128)(2,1)} %text_hbm.1), channel_id=1, source_target_pairs={{0,2},{1,3},{2,4},{3,5},{4,6},{5,7},{6,8},{7,9},{8,10},{9,11},{10,... | collective-permute-start | bytes 884744 | tf_op jit(solution)/shard_map/band_exchange/ppermute | solution.py:52
  4.5 17.2 %collective-permute-start.2 = (bf16[128,1152]{1,0:T(8,128)(2,1)}, bf16[128,1152]{1,0:T(8,128)(2,1)S(1)}, u32[]{:S(2)}, u32[]{:S(2)}) collective-permute-start(bf16[128,1152]{1,0:T(8,128)(2,1)} %text_hbm.1), channel_id=1, source_target_pairs={{0,254},{1,255},{2,0},{3,1},{4,2},{5,3},{6,4},{7,5},{8,6},{9,7},{1... | collective-permute-start | bytes 884744 | tf_op jit(solution)/shard_map/band_exchange/ppermute | solution.py:52
  14.3 11.5 %collective-permute-start = (bf16[128,1152]{1,0:T(8,128)(2,1)}, bf16[128,1152]{1,0:T(8,128)(2,1)S(1)}, u32[]{:S(2)}, u32[]{:S(2)}) collective-permute-start(bf16[128,1152]{1,0:T(8,128)(2,1)} %text_hbm.1), channel_id=1, source_target_pairs={{0,253},{1,4},{2,255},{3,6},{4,1},{5,8},{6,3},{7,10},{8,5},{9,12},... | collective-permute-start | bytes 884744 | tf_op jit(solution)/shard_map/band_exchange/ppermute | solution.py:52
  14.4 0.7 copy-start
  21.6 8.4 %collective-permute-start.7 = (bf16[128,1152]{1,0:T(8,128)(2,1)S(1)}, bf16[128,1152]{1,0:T(8,128)(2,1)S(1)}, u32[]{:S(2)}, u32[]{:S(2)}) collective-permute-start(bf16[128,1152]{1,0:T(8,128)(2,1)S(1)} %get-tuple-element.29.below), channel_id=1, source_target_pairs={{0,1},{1,0},{2,3},{3,2},{4,5},{5,4},{6,7},{7,6},{8,9},{9,8},{10,11... | collective-permute-start | bytes 884744 | tf_op jit(solution)/shard_map/swap_neighbours/ppermute | solution.py:52
  22.6 7.4 %collective-permute-start.8 = (bf16[128,1152]{1,0:T(8,128)(2,1)S(1)}, bf16[128,1152]{1,0:T(8,128)(2,1)S(1)}, u32[]{:S(2)}, u32[]{:S(2)}) collective-permute-start(bf16[128,1152]{1,0:T(8,128)(2,1)S(1)} %get-tuple-element.30.above), channel_id=1, source_target_pairs={{0,1},{1,0},{2,3},{3,2},{4,5},{5,4},{6,7},{7,6},{8,9},{9,8},{10,11... | collective-permute-start | bytes 884744 | tf_op jit(solution)/shard_map/swap_neighbours/ppermute | solution.py:52
  25.8 7.3 %collective-permute-start.6 = (bf16[128,1152]{1,0:T(8,128)(2,1)S(1)}, bf16[128,1152]{1,0:T(8,128)(2,1)S(1)}, u32[]{:S(2)}, u32[]{:S(2)}) collective-permute-start(bf16[128,1152]{1,0:T(8,128)(2,1)S(1)} %received.3.far), channel_id=1, source_target_pairs={{0,1},{1,0},{2,3},{3,2},{4,5},{5,4},{6,7},{7,6},{8,9},{9,8},{10,11... | collective-permute-start | bytes 884744 | tf_op jit(solution)/shard_map/received/ppermute | solution.py:52
  36.5 6.3 %collective-permute-start.10 = (bf16[144,1152]{1,0:T(8,128)(2,1)S(1)}, bf16[144,1152]{1,0:T(8,128)(2,1)S(1)}, u32[]{:S(2)}, u32[]{:S(2)}) collective-permute-start(bf16[144,1152]{1,0:T(8,128)(2,1)S(1)} %get-tuple-element.45), channel_id=1, source_target_pairs={{0,48},{1,193},{2,50},{3,195},{4,52},{5,197},{6,54},{7,199},{8,56}... | collective-permute-start | bytes 995336 | tf_op jit(solution)/shard_map/sum_first/ppermute | solution.py:52
  36.6 7.6 %collective-permute-start.9 = (bf16[144,1152]{1,0:T(8,128)(2,1)S(1)}, bf16[144,1152]{1,0:T(8,128)(2,1)S(1)}, u32[]{:S(2)}, u32[]{:S(2)}) collective-permute-start(bf16[144,1152]{1,0:T(8,128)(2,1)S(1)} %get-tuple-element.43), channel_id=1, source_target_pairs={{0,16},{1,65},{2,18},{3,67},{4,20},{5,69},{6,22},{7,71},{8,24},{9,... | collective-permute-start | bytes 995336 | tf_op jit(solution)/shard_map/sum_first/ppermute | solution.py:52
  38.0 9.5 %collective-permute-start.12 = (bf16[144,1152]{1,0:T(8,128)(2,1)S(1)}, bf16[144,1152]{1,0:T(8,128)(2,1)S(1)}, u32[]{:S(2)}, u32[]{:S(2)}) collective-permute-start(bf16[144,1152]{1,0:T(8,128)(2,1)S(1)} %get-tuple-element.47), channel_id=1, source_target_pairs={{0,16},{1,65},{2,18},{3,67},{4,20},{5,69},{6,22},{7,71},{8,24},{9,... | collective-permute-start | bytes 995336 | tf_op jit(solution)/shard_map/sum_first/ppermute | solution.py:52
  38.0 9.4 %collective-permute-start.13 = (bf16[144,1152]{1,0:T(8,128)(2,1)S(1)}, bf16[144,1152]{1,0:T(8,128)(2,1)S(1)}, u32[]{:S(2)}, u32[]{:S(2)}) collective-permute-start(bf16[144,1152]{1,0:T(8,128)(2,1)S(1)} %get-tuple-element.48), channel_id=1, source_target_pairs={{0,48},{1,193},{2,50},{3,195},{4,52},{5,197},{6,54},{7,199},{8,56}... | collective-permute-start | bytes 995336 | tf_op jit(solution)/shard_map/sum_first/ppermute | solution.py:52
  44.3 7.6 %collective-permute-start.11 = (bf16[144,1152]{1,0:T(8,128)(2,1)S(1)}, bf16[144,1152]{1,0:T(8,128)(2,1)S(1)}, u32[]{:S(2)}, u32[]{:S(2)}) collective-permute-start(bf16[144,1152]{1,0:T(8,128)(2,1)S(1)} %get-tuple-element.46), channel_id=1, source_target_pairs={{0,16},{1,65},{2,18},{3,67},{4,20},{5,69},{6,22},{7,71},{8,24},{9,... | collective-permute-start | bytes 995336 | tf_op jit(solution)/shard_map/sum_first/ppermute | solution.py:52
  44.4 7.5 %collective-permute-start.14 = (bf16[144,1152]{1,0:T(8,128)(2,1)S(1)}, bf16[144,1152]{1,0:T(8,128)(2,1)S(1)}, u32[]{:S(2)}, u32[]{:S(2)}) collective-permute-start(bf16[144,1152]{1,0:T(8,128)(2,1)S(1)} %get-tuple-element.49), channel_id=1, source_target_pairs={{0,48},{1,193},{2,50},{3,195},{4,52},{5,197},{6,54},{7,199},{8,56}... | collective-permute-start | bytes 995336 | tf_op jit(solution)/shard_map/sum_first/ppermute | solution.py:52
  96.7 18.9 %collective-permute-start.19 = (bf16[288,1152]{1,0:T(8,128)(2,1)S(1)}, bf16[288,1152]{1,0:T(8,128)(2,1)S(1)}, u32[]{:S(2)}, u32[]{:S(2)}) collective-permute-start(bf16[288,1152]{1,0:T(8,128)(2,1)S(1)} %bitcast.18), channel_id=1, source_target_pairs={{0,1},{1,0},{2,3},{3,2},{4,5},{5,4},{6,7},{7,6},{8,9},{9,8},{10,11... | collective-permute-start | bytes 1990664 | tf_op jit(solution)/shard_map/share_first/ppermute | solution.py:52
  103.6 7.6 %collective-permute-start.15 = (bf16[144,1152]{1,0:T(8,128)(2,1)S(1)}, bf16[144,1152]{1,0:T(8,128)(2,1)S(1)}, u32[]{:S(2)}, u32[]{:S(2)}) collective-permute-start(bf16[144,1152]{1,0:T(8,128)(2,1)S(1)} %bitcast.27), channel_id=1, source_target_pairs={{0,16},{1,65},{2,18},{3,67},{4,20},{5,69},{6,22},{7,71},{8,24},{9,... | collective-permute-start | bytes 995336 | tf_op jit(solution)/shard_map/share_first/ppermute | solution.py:52
  104.0 7.2 %collective-permute-start.16 = (bf16[144,1152]{1,0:T(8,128)(2,1)S(1)}, bf16[144,1152]{1,0:T(8,128)(2,1)S(1)}, u32[]{:S(2)}, u32[]{:S(2)}) collective-permute-start(bf16[144,1152]{1,0:T(8,128)(2,1)S(1)} %bitcast.29), channel_id=1, source_target_pairs={{0,48},{1,193},{2,50},{3,195},{4,52},{5,197},{6,54},{7,199},{8,56}... | collective-permute-start | bytes 995336 | tf_op jit(solution)/shard_map/share_first/ppermute | solution.py:52
  106.4 8.4 %collective-permute-start.17 = (bf16[144,1152]{1,0:T(8,128)(2,1)S(1)}, bf16[144,1152]{1,0:T(8,128)(2,1)S(1)}, u32[]{:S(2)}, u32[]{:S(2)}) collective-permute-start(bf16[144,1152]{1,0:T(8,128)(2,1)S(1)} %bitcast.30), channel_id=1, source_target_pairs={{0,16},{1,65},{2,18},{3,67},{4,20},{5,69},{6,22},{7,71},{8,24},{9,... | collective-permute-start | bytes 995336 | tf_op jit(solution)/shard_map/share_first/ppermute | solution.py:52
  106.4 9.2 %collective-permute-start.18 = (bf16[144,1152]{1,0:T(8,128)(2,1)S(1)}, bf16[144,1152]{1,0:T(8,128)(2,1)S(1)}, u32[]{:S(2)}, u32[]{:S(2)}) collective-permute-start(bf16[144,1152]{1,0:T(8,128)(2,1)S(1)} %bitcast.28), channel_id=1, source_target_pairs={{0,48},{1,193},{2,50},{3,195},{4,52},{5,197},{6,54},{7,199},{8,56}... | collective-permute-start | bytes 995336 | tf_op jit(solution)/shard_map/share_first/ppermute | solution.py:52
  111.2 7.5 %collective-permute-start.20 = (bf16[144,1152]{1,0:T(8,128)(2,1)S(1)}, bf16[144,1152]{1,0:T(8,128)(2,1)S(1)}, u32[]{:S(2)}, u32[]{:S(2)}) collective-permute-start(bf16[144,1152]{1,0:T(8,128)(2,1)S(1)} %collective-permute-done.15.refs_1_), channel_id=1, source_target_pairs={{0,16},{1,65},{2,18},{3,67},{4,20},{5,69},{6,22},{7,71},{8,24},{9,... | collective-permute-start | bytes 995336 | tf_op jit(solution)/shard_map/share_first/ppermute | solution.py:52
  111.2 9.2 %collective-permute-start.21 = (bf16[144,1152]{1,0:T(8,128)(2,1)S(1)}, bf16[144,1152]{1,0:T(8,128)(2,1)S(1)}, u32[]{:S(2)}, u32[]{:S(2)}) collective-permute-start(bf16[144,1152]{1,0:T(8,128)(2,1)S(1)} %collective-permute-done.16.refs_2_), channel_id=1, source_target_pairs={{0,48},{1,193},{2,50},{3,195},{4,52},{5,197},{6,54},{7,199},{8,56}... | collective-permute-start | bytes 995336 | tf_op jit(solution)/shard_map/share_first/ppermute | solution.py:52
  114.8 5.7 %collective-permute-start.22 = (bf16[144,1152]{1,0:T(8,128)(2,1)S(1)}, bf16[144,1152]{1,0:T(8,128)(2,1)S(1)}, u32[]{:S(2)}, u32[]{:S(2)}) collective-permute-start(bf16[144,1152]{1,0:T(8,128)(2,1)S(1)} %collective-permute-done.15.refs_1_), channel_id=1, source_target_pairs={{0,1},{1,0},{2,3},{3,2},{4,5},{5,4},{6,7},{7,6},{8,9},{9,8},{10,11... | collective-permute-start | bytes 995336 | tf_op jit(solution)/shard_map/share_first/ppermute | solution.py:52
  115.6 5.3 %collective-permute-start.23 = (bf16[144,1152]{1,0:T(8,128)(2,1)S(1)}, bf16[144,1152]{1,0:T(8,128)(2,1)S(1)}, u32[]{:S(2)}, u32[]{:S(2)}) collective-permute-start(bf16[144,1152]{1,0:T(8,128)(2,1)S(1)} %collective-permute-done.16.refs_2_), channel_id=1, source_target_pairs={{0,1},{1,0},{2,3},{3,2},{4,5},{5,4},{6,7},{7,6},{8,9},{9,8},{10,11... | collective-permute-start | bytes 995336 | tf_op jit(solution)/shard_map/share_first/ppermute | solution.py:52
  115.6 5.3 %collective-permute-start.24 = (bf16[144,1152]{1,0:T(8,128)(2,1)S(1)}, bf16[144,1152]{1,0:T(8,128)(2,1)S(1)}, u32[]{:S(2)}, u32[]{:S(2)}) collective-permute-start(bf16[144,1152]{1,0:T(8,128)(2,1)S(1)} %collective-permute-done.17.refs_3_), channel_id=1, source_target_pairs={{0,1},{1,0},{2,3},{3,2},{4,5},{5,4},{6,7},{7,6},{8,9},{9,8},{10,11... | collective-permute-start | bytes 995336 | tf_op jit(solution)/shard_map/share_first/ppermute | solution.py:52
  118.7 3.0 %collective-permute-start.25 = (bf16[144,1152]{1,0:T(8,128)(2,1)S(1)}, bf16[144,1152]{1,0:T(8,128)(2,1)S(1)}, u32[]{:S(2)}, u32[]{:S(2)}) collective-permute-start(bf16[144,1152]{1,0:T(8,128)(2,1)S(1)} %collective-permute-done.18.refs_4_), channel_id=1, source_target_pairs={{0,1},{1,0},{2,3},{3,2},{4,5},{5,4},{6,7},{7,6},{8,9},{9,8},{10,11... | collective-permute-start | bytes 995336 | tf_op jit(solution)/shard_map/share_first/ppermute | solution.py:52
  120.4 1.7 %collective-permute-start.26 = (bf16[144,1152]{1,0:T(8,128)(2,1)S(1)}, bf16[144,1152]{1,0:T(8,128)(2,1)S(1)}, u32[]{:S(2)}, u32[]{:S(2)}) collective-permute-start(bf16[144,1152]{1,0:T(8,128)(2,1)S(1)} %get-tuple-element.52.refs_2_), channel_id=1, source_target_pairs={{0,1},{1,0},{2,3},{3,2},{4,5},{5,4},{6,7},{7,6},{8,9},{9,8},{10,11... | collective-permute-start | bytes 995336 | tf_op jit(solution)/shard_map/write/ppermute | solution.py:52
  120.5 2.1 %collective-permute-start.27 = (bf16[144,1152]{1,0:T(8,128)(2,1)S(1)}, bf16[144,1152]{1,0:T(8,128)(2,1)S(1)}, u32[]{:S(2)}, u32[]{:S(2)}) collective-permute-start(bf16[144,1152]{1,0:T(8,128)(2,1)S(1)} %get-tuple-element.53.refs_3_), channel_id=1, source_target_pairs={{0,1},{1,0},{2,3},{3,2},{4,5},{5,4},{6,7},{7,6},{8,9},{9,8},{10,11... | collective-permute-start | bytes 995336 | tf_op jit(solution)/shard_map/write/ppermute | solution.py:52

commit v7 on v6

--- a/solution.py
+++ b/solution.py
@@ -41,6 +41,7 @@
 SECOND = groups(lambda y, x, z, c: (c, z, x if c == 0 else y))
 LINES = groups(lambda y, x, z, c: (c, x, y))
 FAR = [(i, (i + 3) % N if i % 2 else (i - 3) % N) for i in range(N)]
+TAIL = 16
 TEXT = 1
 
 
@@ -135,36 +136,39 @@
 
 
 def near_kernel(
-    log_scale, shift, text_hbm, image_hbm, text_w_hbm, image_w_hbm, text_other, image_other,
-    position, position_other,
+    log_scale, shift, text_hbm, text_w_hbm, image_w_hbm, text_other, image_own, image_other,
     image_near, text_w, image_emb, image_projected, image_inverse, grad, head,
     text_near, image_w, back, sems,
 ):
     rows = text_other.shape[0]
     first, second = pl.ds(0, rows), pl.ds(rows, rows)
     moves = [
-        pltpu.make_async_copy(image_hbm, image_near.at[first, :], sems.at[0]),
-        pltpu.make_async_copy(image_w_hbm, image_w, sems.at[1]),
-        pltpu.make_async_copy(text_hbm, text_near.at[first, :], sems.at[2]),
-        pltpu.make_async_copy(text_w_hbm, text_w, sems.at[3]),
+        pltpu.make_async_copy(image_w_hbm, image_w, sems.at[0]),
+        pltpu.make_async_copy(text_hbm, text_near.at[first, :], sems.at[1]),
+        pltpu.make_async_copy(text_w_hbm, text_w, sems.at[2]),
     ]
     for move in moves:
         move.start()
-    image_near[second, :] = image_other[...]
+    image_near[first, :] = image_own[first, :]
+    image_near[second, :] = image_other[first, :]
     text_near[second, :] = text_other[...]
     moves[0].wait()
-    moves[1].wait()
     projected, inverse = embed(image_near[...], image_w[...])
     image_emb[...] = (projected * inverse).astype(bf16)
     image_projected[...] = projected
     image_inverse[...] = inverse
+    moves[1].wait()
     moves[2].wait()
-    moves[3].wait()
 
     def with_labels(sigmoid):
         column = lax.broadcasted_iota(jnp.int32, (2 * rows, rows), 0)
-        own = (column == position[...]).astype(f32)
-        other = (column == position_other[...] + rows).astype(f32)
+
+        def positions(block):
+            tail = block[pl.ds(rows, TAIL), pl.ds(0, rows)]
+            return tail.astype(f32)[:1].astype(jnp.int32)
+
+        own = (column == positions(image_own)).astype(f32)
+        other = (column == positions(image_other) + rows).astype(f32)
         return sigmoid - jnp.concatenate([own, other], axis=1).T
 
     visit(log_scale, shift, text_near, text_w, image_emb, with_labels, back, grad, None)
@@ -321,8 +325,9 @@
     piece, half_piece = ((slab, width), bf16), ((half, width), bf16)
     with jax.named_scope("band_exchange"):
         text_other = send(text_x, SWAP)
-        image_other = send(image_x, SWAP)
-        position_other = send(position, SWAP)
+        tail = jnp.pad(position.astype(bf16)[None], ((0, TAIL - 1), (0, width - rows)))
+        image_own = jnp.concatenate([image_x, tail])
+        image_other = send(image_own, SWAP)
         below = send(text_x, shifted(2))
         above = send(text_x, shifted(-2))
         far = send(text_x, FAR)
@@ -334,12 +339,11 @@
                 pltpu.VMEM(*pair),
                 pltpu.VMEM(*matrix),
                 pltpu.VMEM(*pair),
-                pltpu.SemaphoreType.DMA((4,)),
+                pltpu.SemaphoreType.DMA((3,)),
             ],
             flops=4 * 10**9,
         )(
-            scalars, (text_x, image_x, text_w, image_w), text_other, image_other,
-            position[None], position_other[None],
+            scalars, (text_x, text_w, image_w), text_other, image_own, image_other
         )
     with jax.named_scope("swap_neighbours"):
         below, above = after(image_inverse, below, above)
@@ -409,10 +413,13 @@
             own, left_top, right_bottom, left_bottom, right_top, own_other, shape=matrix
         )
         across_top, across_bottom = after(outs[0], across_top, across_bottom, in_hbm=True)
-        others += [send(across_top, SWAP), send(across_bottom, SWAP)]
-        return write(tuple(outs), [ACROSS_TOP, ACROSS_BOTTOM], PIECES[1:])(
-            across_top, across_bottom, *others, shape=matrix
-        )
+        across_others = [send(across_top, SWAP), send(across_bottom, SWAP)]
+        outs = write(
+            tuple(outs),
+            [ACROSS_TOP, ACROSS_BOTTOM],
+            [LEFT_TOP, RIGHT_BOTTOM, LEFT_BOTTOM, RIGHT_TOP],
+        )(across_top, across_bottom, *others, shape=matrix)
+        return write(tuple(outs), [], [ACROSS_TOP, ACROSS_BOTTOM])(*across_others, shape=matrix)
 
 
 def solution(mesh):

time: 125 us -> 123 us (0.984)
  starting transfers between devices: 43.3 us -> 39.8 us
  other arithmetic: 0.13 us -> 1.78 us
    ppermute x28 -> x27, starting transfers between devices: 43.3 us -> 39.8 us  [send(): return lax.ppermute(block, 'dp', pairs)]
    ppermute x28 -> x27, waiting for transfers between devices: 14.4 us -> 13.7 us  [send(): return lax.ppermute(block, 'dp', pairs)]
    pallas_call x11 -> x12, Pallas kernels: 19.1 us -> 19.6 us  [run(): pl.pallas_call(body, out_shape=[jax.ShapeDtypeStruct(s, d) for s, d in ou...]
  transfers between devices with their start and end apart: 28 -> 27, of which waited for: 11 -> 8; matrix products, arithmetic and copies ran while one was open for 0% -> 0% of each run, Pallas kernels for 11% -> 12%
where the time goes in v7:
time: 123 us
  blocking collectives  45.2 us (37%)
  starting transfers between devices  39.8 us (32%)
  Pallas kernels  19.6 us (16%)
  waiting for transfers between devices  13.7 us (11%)
  between operations  2.33 us (2%)
  other arithmetic  1.78 us (1%)
    all_to_all x4, blocking collectives, exchange(): lax.all_to_all(parts, 'dp', 0, 0, axis_index_groups=members, tiled=True)  45.2 us
    ppermute x27, starting transfers between devices, send(): return lax.ppermute(block, 'dp', pairs)  39.8 us
    pallas_call x12, Pallas kernels, run(): pl.pallas_call(body, out_shape=[jax.ShapeDtypeStruct(s, d) for s, d in ou...  19.6 us
    ppermute x27, waiting for transfers between devices, send(): return lax.ppermute(block, 'dp', pairs)  13.7 us
  transfers between devices with their start and end apart: 27, of which 8 were waited for; matrix products, arithmetic and copies ran while one was open for 0% of the time, Pallas kernels for 12%

profile of v7, /device:TPU:1, one launch (start us, length us, event | category | flops | bytes accessed | tf_op | source)
XLA Modules:
  0.0 122.6 jit_solution(17282369561324086165)
XLA Ops:
  0.6 0.7 convert_bitcast_fusion
  1.3 1.0 fusion.1.image_own
  2.3 3.3 %collective-permute-start.4 = (bf16[144,1152]{1,0:T(8,128)(2,1)S(1)}, bf16[144,1152]{1,0:T(8,128)(2,1)S(1)}, u32[]{:S(2)}, u32[]{:S(2)}) collective-permute-start(bf16[144,1152]{1,0:T(8,128)(2,1)S(1)} %fusion.1.image_own), channel_id=1, source_target_pairs={{0,1},{1,0},{2,3},{3,2},{4,5},{5,4},{6,7},{7,6},{8,9},{9,8},{10,11... | collective-permute-start | bytes 995336 | tf_op jit(solution)/shard_map/band_exchange/ppermute | solution.py:53
  5.6 0.1 collective-permute-start.3
  5.7 0.0 collective-permute-start.1
  5.7 8.5 %collective-permute-start.2 = (bf16[128,1152]{1,0:T(8,128)(2,1)}, bf16[128,1152]{1,0:T(8,128)(2,1)S(1)}, u32[]{:S(2)}, u32[]{:S(2)}) collective-permute-start(bf16[128,1152]{1,0:T(8,128)(2,1)} %text_hbm.1), channel_id=1, source_target_pairs={{0,254},{1,255},{2,0},{3,1},{4,2},{5,3},{6,4},{7,5},{8,6},{9,7},{1... | collective-permute-start | bytes 884744 | tf_op jit(solution)/shard_map/band_exchange/ppermute | solution.py:53
  14.2 0.0 collective-permute-start
  15.5 0.0 collective-permute-done.3.text_other
  15.5 0.0 collective-permute-done.4.image_other
  15.5 6.0 %near.1 = (bf16[256,1152]{1,0:T(8,128)(2,1)S(1)}, bf16[1152,1152]{1,0:T(8,128)(2,1)S(1)}, bf16[256,1152]{1,0:T(8,128)(2,1)S(1)}, f32[256,1152]{1,0:T(8,128)S(1)}...) custom-call(f32[1]{0:T(128)S(6)} %copy.27.log_scale, f32[1]{0:T(128)S(6)} %copy.28.shift, ...), custom_call_target="tpu_custom_call" | custom-call | flops 4000000000 | tf_op jit(solution)/shard_map/near/pallas_call | solution.py:69
  21.5 0.0 collective-permute-done.1.refs_0_
  21.5 2.1 %collective-permute-done.2.refs_1_ = bf16[128,1152]{1,0:T(8,128)(2,1)S(1)} collective-permute-done((bf16[128,1152]{1,0:T(8,128)(2,1)}, bf16[128,1152]{1,0:T(8,128)(2,1)S(1)}, u32[]{:S(2)}, u32[]{:S(2)}) %collective-permute-start.2) | collective-permute-done | bytes 294944 | tf_op jit(solution)/shard_map/band_exchange/ppermute | solution.py:53
  23.6 1.2 %collective-permute-start.6 = (bf16[128,1152]{1,0:T(8,128)(2,1)S(1)}, bf16[128,1152]{1,0:T(8,128)(2,1)S(1)}, u32[]{:S(2)}, u32[]{:S(2)}) collective-permute-start(bf16[128,1152]{1,0:T(8,128)(2,1)S(1)} %get-tuple-element.31.below), channel_id=1, source_target_pairs={{0,1},{1,0},{2,3},{3,2},{4,5},{5,4},{6,7},{7,6},{8,9},{9,8},{10,11... | collective-permute-start | bytes 884744 | tf_op jit(solution)/shard_map/swap_neighbours/ppermute | solution.py:53
  24.9 0.0 collective-permute-start.7
  24.9 3.1 %received.2 = (f32[256,1152]{1,0:T(8,128)S(1)}, f32[1152,1152]{1,0:T(8,128)S(1)}) custom-call(f32[1]{0:T(128)S(6)} %copy.27.log_scale, f32[1]{0:T(128)S(6)} %copy.28.shift, bf16[128,1152]{1,0:T(8,128)(2,1)S(1)} %get-tuple-element.31.below, bf16[128,1152]{1,0:T(8,128)(2,1)S(1)} %get-tuple-element.32.above, bf16[1152,1152]{1,0:T(8,128)(2,1)S(1)} %get-tuple-element.33.text_w, ...), custom_call_target="tpu_custom_call" | custom-call | flops 4000000000 | tf_op jit(solution)/shard_map/received/pallas_call | solution.py:69
  28.0 0.0 collective-permute-done.refs_0_
  28.0 0.3 collective-permute-start.5
  28.3 0.0 collective-permute-done.6.below
  28.3 0.0 collective-permute-done.7.above
  28.3 3.1 %partners.1 = (f32[256,1152]{1,0:T(8,128)S(1)}, f32[1152,1152]{1,0:T(8,128)S(1)}) custom-call(f32[1]{0:T(128)S(6)} %copy.27.log_scale, f32[1]{0:T(128)S(6)} %copy.28.shift, bf16[128,1152]{1,0:T(8,128)(2,1)S(1)} %collective-permute-done.6.below, bf16[128,1152]{1,0:T(8,128)(2,1)S(1)} %collective-permute-done.7.above, ...), custom_call_target="tpu_custom_call" | custom-call | flops 4000000000 | tf_op jit(solution)/shard_map/partners/pallas_call | solution.py:69
  31.4 0.0 collective-permute-done.5.far_other
  31.4 3.4 %far.1 = (bf16[288,1152]{1,0:T(8,128)(2,1)S(1)}, bf16[144,1152]{1,0:T(8,128)(2,1)S(1)}, bf16[144,1152]{1,0:T(8,128)(2,1)S(1)}, bf16[144,1152]{1,0:T(8,128)(2,1)S...) custom-call(f32[1]{0:T(128)S(6)} %copy.27.log_scale, ...), custom_call_target="tpu_custom_call" | custom-call | flops 4000000000 | tf_op jit(solution)/shard_map/far/pallas_call | solution.py:69
  34.7 0.1 collective-permute-start.8
  34.8 2.7 %collective-permute-start.9 = (bf16[144,1152]{1,0:T(8,128)(2,1)S(1)}, bf16[144,1152]{1,0:T(8,128)(2,1)S(1)}, u32[]{:S(2)}, u32[]{:S(2)}) collective-permute-start(bf16[144,1152]{1,0:T(8,128)(2,1)S(1)} %get-tuple-element.47), channel_id=1, source_target_pairs={{0,48},{1,193},{2,50},{3,195},{4,52},{5,197},{6,54},{7,199},{8,56}... | collective-permute-start | bytes 995336 | tf_op jit(solution)/shard_map/sum_first/ppermute | solution.py:53
  37.5 2.7 %collective-permute-start.12 = (bf16[144,1152]{1,0:T(8,128)(2,1)S(1)}, bf16[144,1152]{1,0:T(8,128)(2,1)S(1)}, u32[]{:S(2)}, u32[]{:S(2)}) collective-permute-start(bf16[144,1152]{1,0:T(8,128)(2,1)S(1)} %get-tuple-element.50), channel_id=1, source_target_pairs={{0,48},{1,193},{2,50},{3,195},{4,52},{5,197},{6,54},{7,199},{8,56}... | collective-permute-start | bytes 995336 | tf_op jit(solution)/shard_map/sum_first/ppermute | solution.py:53
  40.2 2.1 %collective-permute-done.8.b = bf16[144,1152]{1,0:T(8,128)(2,1)S(1)} collective-permute-done((bf16[144,1152]{1,0:T(8,128)(2,1)S(1)}, bf16[144,1152]{1,0:T(8,128)(2,1)S(1)}, u32[]{:S(2)}, u32[]{:S(2)}) %collective-permute-start.8) | collective-permute-done | bytes 331808 | tf_op jit(solution)/shard_map/sum_first/ppermute | solution.py:53
  42.3 0.0 collective-permute-done.9.d
  42.3 0.2 sum_first.2
  42.4 0.1 collective-permute-start.10
  42.5 2.8 %collective-permute-start.13 = (bf16[144,1152]{1,0:T(8,128)(2,1)S(1)}, bf16[144,1152]{1,0:T(8,128)(2,1)S(1)}, u32[]{:S(2)}, u32[]{:S(2)}) collective-permute-start(bf16[144,1152]{1,0:T(8,128)(2,1)S(1)} %get-tuple-element.51), channel_id=1, source_target_pairs={{0,48},{1,193},{2,50},{3,195},{4,52},{5,197},{6,54},{7,199},{8,56}... | collective-permute-start | bytes 995336 | tf_op jit(solution)/shard_map/sum_first/ppermute | solution.py:53
  45.3 0.5 collective-permute-done.11.a_bottom
  45.8 0.0 collective-permute-done.12.b_top
  45.8 4.2 %collective-permute-done.10.a_top = bf16[144,1152]{1,0:T(8,128)(2,1)S(1)} collective-permute-done((bf16[144,1152]{1,0:T(8,128)(2,1)S(1)}, bf16[144,1152]{1,0:T(8,128)(2,1)S(1)}, u32[]{:S(2)}, u32[]{:S(2)}) %collective-permute-start.10) | collective-permute-done | bytes 331808 | tf_op jit(solution)/shard_map/sum_first/ppermute | solution.py:53
  50.0 0.3 sum_first.3
  50.3 10.4 %all_to_all.20 = bf16[4,72,1152]{2,1,0:T(8,128)(2,1)S(1)} all-to-all(bf16[4,72,1152]{2,1,0:T(8,128)(2,1)S(1)} %bitcast.20), channel_id=1, replica_groups={{0,64,128,192},{1,17,33,49},{2,66,130,194},{3,19,35,51},{4,68,132,196},..., dimensions={0} | all-to-all | bytes 1327104 | tf_op jit(solution)/shard_map/sum_second/all_to_all | solution.py:57
  60.7 0.1 reduce_sum.24
  60.8 13.7 %all_to_all.21 = bf16[88,8,128]{2,1,0:T(8,128)(2,1)S(1)} all-to-all(bf16[88,8,128]{2,1,0:T(8,128)(2,1)S(1)} %concatenate.7), channel_id=1, replica_groups={{0,2,4,6,8,10,12,14},{1,3,5,7,9,11,13,15},{16,18,20,22,24,26,28,30},{17..., dimensions={0} | all-to-all | bytes 360448 | tf_op jit(solution)/shard_map/sum_lines/all_to_all | solution.py:57
  74.6 10.9 %all_to_all.22 = bf16[88,8,128]{2,1,0:T(8,128)(2,1)S(1)} all-to-all(bf16[88,8,128]{2,1,0:T(8,128)(2,1)S(1)} %bitcast.22), channel_id=1, replica_groups={{0,2,4,6,8,10,12,14},{1,3,5,7,9,11,13,15},{16,18,20,22,24,26,28,30},{17..., dimensions={0} | all-to-all | bytes 360448 | tf_op jit(solution)/shard_map/share_lines/all_to_all | solution.py:57
  85.6 10.1 %all_to_all.23 = bf16[4,72,1152]{2,1,0:T(8,128)(2,1)S(1)} all-to-all(bf16[4,72,1152]{2,1,0:T(8,128)(2,1)S(1)} %tile.20), channel_id=1, replica_groups={{0,64,128,192},{1,17,33,49},{2,66,130,194},{3,19,35,51},{4,68,132,196},..., dimensions={0} | all-to-all | bytes 1327104 | tf_op jit(solution)/shard_map/share_second/all_to_all | solution.py:57
  95.7 6.5 %collective-permute-start.18 = (bf16[288,1152]{1,0:T(8,128)(2,1)S(1)}, bf16[288,1152]{1,0:T(8,128)(2,1)S(1)}, u32[]{:S(2)}, u32[]{:S(2)}) collective-permute-start(bf16[288,1152]{1,0:T(8,128)(2,1)S(1)} %bitcast.18), channel_id=1, source_target_pairs={{0,1},{1,0},{2,3},{3,2},{4,5},{5,4},{6,7},{7,6},{8,9},{9,8},{10,11... | collective-permute-start | bytes 1990664 | tf_op jit(solution)/shard_map/share_first/ppermute | solution.py:53
  102.2 0.1 fusion.2
  102.2 0.4 collective-permute-start.14
  102.6 2.4 %collective-permute-start.15 = (bf16[144,1152]{1,0:T(8,128)(2,1)S(1)}, bf16[144,1152]{1,0:T(8,128)(2,1)S(1)}, u32[]{:S(2)}, u32[]{:S(2)}) collective-permute-start(bf16[144,1152]{1,0:T(8,128)(2,1)S(1)} %bitcast.27), channel_id=1, source_target_pairs={{0,48},{1,193},{2,50},{3,195},{4,52},{5,197},{6,54},{7,199},{8,56}... | collective-permute-start | bytes 995336 | tf_op jit(solution)/shard_map/share_first/ppermute | solution.py:53
  105.0 0.0 collective-permute-start.16
  105.0 2.7 %collective-permute-start.17 = (bf16[144,1152]{1,0:T(8,128)(2,1)S(1)}, bf16[144,1152]{1,0:T(8,128)(2,1)S(1)}, u32[]{:S(2)}, u32[]{:S(2)}) collective-permute-start(bf16[144,1152]{1,0:T(8,128)(2,1)S(1)} %bitcast.26), channel_id=1, source_target_pairs={{0,48},{1,193},{2,50},{3,195},{4,52},{5,197},{6,54},{7,199},{8,56}... | collective-permute-start | bytes 995336 | tf_op jit(solution)/shard_map/share_first/ppermute | solution.py:53
  107.7 2.1 %collective-permute-done.14.refs_1_ = bf16[144,1152]{1,0:T(8,128)(2,1)S(1)} collective-permute-done((bf16[144,1152]{1,0:T(8,128)(2,1)S(1)}, bf16[144,1152]{1,0:T(8,128)(2,1)S(1)}, u32[]{:S(2)}, u32[]{:S(2)}) %collective-permute-start.14) | collective-permute-done | bytes 331808 | tf_op jit(solution)/shard_map/share_first/ppermute | solution.py:53
  109.8 2.7 %collective-permute-start.20 = (bf16[144,1152]{1,0:T(8,128)(2,1)S(1)}, bf16[144,1152]{1,0:T(8,128)(2,1)S(1)}, u32[]{:S(2)}, u32[]{:S(2)}) collective-permute-start(bf16[144,1152]{1,0:T(8,128)(2,1)S(1)} %collective-permute-done.15.refs_2_), channel_id=1, source_target_pairs={{0,48},{1,193},{2,50},{3,195},{4,52},{5,197},{6,54},{7,199},{8,56}... | collective-permute-start | bytes 995336 | tf_op jit(solution)/shard_map/share_first/ppermute | solution.py:53
  112.5 0.9 collective-permute-done.16.refs_3_
  113.3 0.9 collective-permute-start.21
  114.2 0.4 collective-permute-start.22
  114.6 0.1 collective-permute-start.23
  114.7 1.5 %write.4 = (bf16[1152,1152]{1,0:T(8,128)(2,1)}, bf16[1152,1152]{1,0:T(8,128)(2,1)}) custom-call(bf16[288,1152]{1,0:T(8,128)(2,1)S(1)} %bitcast.19, bf16[144,1152]{1,0:T(8,128)(2,1)S(1)} %collective-permute-done.14.refs_1_, bf16[144,1152]{1,0:T(8,128)(2,1)S(1)} %collective-permute-done.15.refs_2_, bf16[144,1152]{1,0:T(8,128)(2,1)S(1)} %collective-permute-done.16.refs_3_, ...), custom_call_target="tpu_custom_call" | custom-call | tf_op jit(solution)/shard_map/write/pallas_call | solution.py:69
  116.3 1.0 collective-permute-done.19.refs_1_
  117.2 1.7 %collective-permute-start.24 = (bf16[144,1152]{1,0:T(8,128)(2,1)S(1)}, bf16[144,1152]{1,0:T(8,128)(2,1)S(1)}, u32[]{:S(2)}, u32[]{:S(2)}) collective-permute-start(bf16[144,1152]{1,0:T(8,128)(2,1)S(1)} %collective-permute-done.17.refs_4_), channel_id=1, source_target_pairs={{0,1},{1,0},{2,3},{3,2},{4,5},{5,4},{6,7},{7,6},{8,9},{9,8},{10,11... | collective-permute-start | bytes 995336 | tf_op jit(solution)/shard_map/share_first/ppermute | solution.py:53
  119.0 0.1 collective-permute-start.25
  119.0 0.0 collective-permute-done.21.refs_4_
  119.1 0.4 collective-permute-start.26
  119.5 0.0 collective-permute-done.22.refs_5_
  119.5 0.0 collective-permute-done.23.refs_6_
  119.5 0.7 collective-permute-done.24.refs_7_
  120.2 1.3 %write.6 = (bf16[1152,1152]{1,0:T(8,128)(2,1)}, bf16[1152,1152]{1,0:T(8,128)(2,1)}) custom-call(bf16[1152,1152]{1,0:T(8,128)(2,1)} %get-tuple-element.52.refs_0_, bf16[1152,1152]{1,0:T(8,128)(2,1)} %get-tuple-element.53.refs_1_, bf16[144,1152]{1,0:T(8,128)(2,1)S(1)} %get-tuple-element.54.refs_2_, ...), custom_call_target="tpu_custom_call", output_to_operand_aliasing={{0}: (0, {}), {1}: (1, {})} | custom-call | tf_op jit(solution)/shard_map/write/pallas_call | solution.py:69
  121.6 0.0 collective-permute-done.25.refs_2_
  121.6 0.0 collective-permute-done.26.refs_3_
  121.6 0.9 write.7
  (15 shorter events, 0.2 us)
Async XLA Ops:
  2.3 13.2 %collective-permute-start.4 = (bf16[144,1152]{1,0:T(8,128)(2,1)S(1)}, bf16[144,1152]{1,0:T(8,128)(2,1)S(1)}, u32[]{:S(2)}, u32[]{:S(2)}) collective-permute-start(bf16[144,1152]{1,0:T(8,128)(2,1)S(1)} %fusion.1.image_own), channel_id=1, source_target_pairs={{0,1},{1,0},{2,3},{3,2},{4,5},{5,4},{6,7},{7,6},{8,9},{9,8},{10,11... | collective-permute-start | bytes 995336 | tf_op jit(solution)/shard_map/band_exchange/ppermute | solution.py:53
  5.6 9.9 %collective-permute-start.3 = (bf16[128,1152]{1,0:T(8,128)(2,1)}, bf16[128,1152]{1,0:T(8,128)(2,1)S(1)}, u32[]{:S(2)}, u32[]{:S(2)}) collective-permute-start(bf16[128,1152]{1,0:T(8,128)(2,1)} %text_hbm.1), channel_id=1, source_target_pairs={{0,1},{1,0},{2,3},{3,2},{4,5},{5,4},{6,7},{7,6},{8,9},{9,8},{10,11... | collective-permute-start | bytes 884744 | tf_op jit(solution)/shard_map/band_exchange/ppermute | solution.py:53
  5.7 15.8 %collective-permute-start.1 = (bf16[128,1152]{1,0:T(8,128)(2,1)}, bf16[128,1152]{1,0:T(8,128)(2,1)S(1)}, u32[]{:S(2)}, u32[]{:S(2)}) collective-permute-start(bf16[128,1152]{1,0:T(8,128)(2,1)} %text_hbm.1), channel_id=1, source_target_pairs={{0,2},{1,3},{2,4},{3,5},{4,6},{5,7},{6,8},{7,9},{8,10},{9,11},{10,... | collective-permute-start | bytes 884744 | tf_op jit(solution)/shard_map/band_exchange/ppermute | solution.py:53
  5.7 17.9 %collective-permute-start.2 = (bf16[128,1152]{1,0:T(8,128)(2,1)}, bf16[128,1152]{1,0:T(8,128)(2,1)S(1)}, u32[]{:S(2)}, u32[]{:S(2)}) collective-permute-start(bf16[128,1152]{1,0:T(8,128)(2,1)} %text_hbm.1), channel_id=1, source_target_pairs={{0,254},{1,255},{2,0},{3,1},{4,2},{5,3},{6,4},{7,5},{8,6},{9,7},{1... | collective-permute-start | bytes 884744 | tf_op jit(solution)/shard_map/band_exchange/ppermute | solution.py:53
  14.2 13.8 %collective-permute-start = (bf16[128,1152]{1,0:T(8,128)(2,1)}, bf16[128,1152]{1,0:T(8,128)(2,1)S(1)}, u32[]{:S(2)}, u32[]{:S(2)}) collective-permute-start(bf16[128,1152]{1,0:T(8,128)(2,1)} %text_hbm.1), channel_id=1, source_target_pairs={{0,253},{1,4},{2,255},{3,6},{4,1},{5,8},{6,3},{7,10},{8,5},{9,12},... | collective-permute-start | bytes 884744 | tf_op jit(solution)/shard_map/band_exchange/ppermute | solution.py:53
  23.6 4.6 %collective-permute-start.6 = (bf16[128,1152]{1,0:T(8,128)(2,1)S(1)}, bf16[128,1152]{1,0:T(8,128)(2,1)S(1)}, u32[]{:S(2)}, u32[]{:S(2)}) collective-permute-start(bf16[128,1152]{1,0:T(8,128)(2,1)S(1)} %get-tuple-element.31.below), channel_id=1, source_target_pairs={{0,1},{1,0},{2,3},{3,2},{4,5},{5,4},{6,7},{7,6},{8,9},{9,8},{10,11... | collective-permute-start | bytes 884744 | tf_op jit(solution)/shard_map/swap_neighbours/ppermute | solution.py:53
  24.9 3.4 %collective-permute-start.7 = (bf16[128,1152]{1,0:T(8,128)(2,1)S(1)}, bf16[128,1152]{1,0:T(8,128)(2,1)S(1)}, u32[]{:S(2)}, u32[]{:S(2)}) collective-permute-start(bf16[128,1152]{1,0:T(8,128)(2,1)S(1)} %get-tuple-element.32.above), channel_id=1, source_target_pairs={{0,1},{1,0},{2,3},{3,2},{4,5},{5,4},{6,7},{7,6},{8,9},{9,8},{10,11... | collective-permute-start | bytes 884744 | tf_op jit(solution)/shard_map/swap_neighbours/ppermute | solution.py:53
  28.0 3.4 %collective-permute-start.5 = (bf16[128,1152]{1,0:T(8,128)(2,1)S(1)}, bf16[128,1152]{1,0:T(8,128)(2,1)S(1)}, u32[]{:S(2)}, u32[]{:S(2)}) collective-permute-start(bf16[128,1152]{1,0:T(8,128)(2,1)S(1)} %received.3.far), channel_id=1, source_target_pairs={{0,1},{1,0},{2,3},{3,2},{4,5},{5,4},{6,7},{7,6},{8,9},{9,8},{10,11... | collective-permute-start | bytes 884744 | tf_op jit(solution)/shard_map/received/ppermute | solution.py:53
  34.7 7.6 %collective-permute-start.8 = (bf16[144,1152]{1,0:T(8,128)(2,1)S(1)}, bf16[144,1152]{1,0:T(8,128)(2,1)S(1)}, u32[]{:S(2)}, u32[]{:S(2)}) collective-permute-start(bf16[144,1152]{1,0:T(8,128)(2,1)S(1)} %get-tuple-element.45), channel_id=1, source_target_pairs={{0,16},{1,65},{2,18},{3,67},{4,20},{5,69},{6,22},{7,71},{8,24},{9,... | collective-permute-start | bytes 995336 | tf_op jit(solution)/shard_map/sum_first/ppermute | solution.py:53
  34.8 7.5 %collective-permute-start.9 = (bf16[144,1152]{1,0:T(8,128)(2,1)S(1)}, bf16[144,1152]{1,0:T(8,128)(2,1)S(1)}, u32[]{:S(2)}, u32[]{:S(2)}) collective-permute-start(bf16[144,1152]{1,0:T(8,128)(2,1)S(1)} %get-tuple-element.47), channel_id=1, source_target_pairs={{0,48},{1,193},{2,50},{3,195},{4,52},{5,197},{6,54},{7,199},{8,56}... | collective-permute-start | bytes 995336 | tf_op jit(solution)/shard_map/sum_first/ppermute | solution.py:53
  37.5 8.4 %collective-permute-start.11 = (bf16[144,1152]{1,0:T(8,128)(2,1)S(1)}, bf16[144,1152]{1,0:T(8,128)(2,1)S(1)}, u32[]{:S(2)}, u32[]{:S(2)}) collective-permute-start(bf16[144,1152]{1,0:T(8,128)(2,1)S(1)} %get-tuple-element.49), channel_id=1, source_target_pairs={{0,16},{1,65},{2,18},{3,67},{4,20},{5,69},{6,22},{7,71},{8,24},{9,... | collective-permute-start | bytes 995336 | tf_op jit(solution)/shard_map/sum_first/ppermute | solution.py:53
  37.5 8.4 %collective-permute-start.12 = (bf16[144,1152]{1,0:T(8,128)(2,1)S(1)}, bf16[144,1152]{1,0:T(8,128)(2,1)S(1)}, u32[]{:S(2)}, u32[]{:S(2)}) collective-permute-start(bf16[144,1152]{1,0:T(8,128)(2,1)S(1)} %get-tuple-element.50), channel_id=1, source_target_pairs={{0,48},{1,193},{2,50},{3,195},{4,52},{5,197},{6,54},{7,199},{8,56}... | collective-permute-start | bytes 995336 | tf_op jit(solution)/shard_map/sum_first/ppermute | solution.py:53
  42.4 7.6 %collective-permute-start.10 = (bf16[144,1152]{1,0:T(8,128)(2,1)S(1)}, bf16[144,1152]{1,0:T(8,128)(2,1)S(1)}, u32[]{:S(2)}, u32[]{:S(2)}) collective-permute-start(bf16[144,1152]{1,0:T(8,128)(2,1)S(1)} %get-tuple-element.48), channel_id=1, source_target_pairs={{0,16},{1,65},{2,18},{3,67},{4,20},{5,69},{6,22},{7,71},{8,24},{9,... | collective-permute-start | bytes 995336 | tf_op jit(solution)/shard_map/sum_first/ppermute | solution.py:53
  42.5 7.5 %collective-permute-start.13 = (bf16[144,1152]{1,0:T(8,128)(2,1)S(1)}, bf16[144,1152]{1,0:T(8,128)(2,1)S(1)}, u32[]{:S(2)}, u32[]{:S(2)}) collective-permute-start(bf16[144,1152]{1,0:T(8,128)(2,1)S(1)} %get-tuple-element.51), channel_id=1, source_target_pairs={{0,48},{1,193},{2,50},{3,195},{4,52},{5,197},{6,54},{7,199},{8,56}... | collective-permute-start | bytes 995336 | tf_op jit(solution)/shard_map/sum_first/ppermute | solution.py:53
  95.7 18.9 %collective-permute-start.18 = (bf16[288,1152]{1,0:T(8,128)(2,1)S(1)}, bf16[288,1152]{1,0:T(8,128)(2,1)S(1)}, u32[]{:S(2)}, u32[]{:S(2)}) collective-permute-start(bf16[288,1152]{1,0:T(8,128)(2,1)S(1)} %bitcast.18), channel_id=1, source_target_pairs={{0,1},{1,0},{2,3},{3,2},{4,5},{5,4},{6,7},{7,6},{8,9},{9,8},{10,11... | collective-permute-start | bytes 1990664 | tf_op jit(solution)/shard_map/share_first/ppermute | solution.py:53
  102.2 7.6 %collective-permute-start.14 = (bf16[144,1152]{1,0:T(8,128)(2,1)S(1)}, bf16[144,1152]{1,0:T(8,128)(2,1)S(1)}, u32[]{:S(2)}, u32[]{:S(2)}) collective-permute-start(bf16[144,1152]{1,0:T(8,128)(2,1)S(1)} %bitcast.25), channel_id=1, source_target_pairs={{0,16},{1,65},{2,18},{3,67},{4,20},{5,69},{6,22},{7,71},{8,24},{9,... | collective-permute-start | bytes 995336 | tf_op jit(solution)/shard_map/share_first/ppermute | solution.py:53
  102.6 7.2 %collective-permute-start.15 = (bf16[144,1152]{1,0:T(8,128)(2,1)S(1)}, bf16[144,1152]{1,0:T(8,128)(2,1)S(1)}, u32[]{:S(2)}, u32[]{:S(2)}) collective-permute-start(bf16[144,1152]{1,0:T(8,128)(2,1)S(1)} %bitcast.27), channel_id=1, source_target_pairs={{0,48},{1,193},{2,50},{3,195},{4,52},{5,197},{6,54},{7,199},{8,56}... | collective-permute-start | bytes 995336 | tf_op jit(solution)/shard_map/share_first/ppermute | solution.py:53
  105.0 8.4 %collective-permute-start.16 = (bf16[144,1152]{1,0:T(8,128)(2,1)S(1)}, bf16[144,1152]{1,0:T(8,128)(2,1)S(1)}, u32[]{:S(2)}, u32[]{:S(2)}) collective-permute-start(bf16[144,1152]{1,0:T(8,128)(2,1)S(1)} %bitcast.28), channel_id=1, source_target_pairs={{0,16},{1,65},{2,18},{3,67},{4,20},{5,69},{6,22},{7,71},{8,24},{9,... | collective-permute-start | bytes 995336 | tf_op jit(solution)/shard_map/share_first/ppermute | solution.py:53
  105.0 9.2 %collective-permute-start.17 = (bf16[144,1152]{1,0:T(8,128)(2,1)S(1)}, bf16[144,1152]{1,0:T(8,128)(2,1)S(1)}, u32[]{:S(2)}, u32[]{:S(2)}) collective-permute-start(bf16[144,1152]{1,0:T(8,128)(2,1)S(1)} %bitcast.26), channel_id=1, source_target_pairs={{0,48},{1,193},{2,50},{3,195},{4,52},{5,197},{6,54},{7,199},{8,56}... | collective-permute-start | bytes 995336 | tf_op jit(solution)/shard_map/share_first/ppermute | solution.py:53
  109.8 7.5 %collective-permute-start.19 = (bf16[144,1152]{1,0:T(8,128)(2,1)S(1)}, bf16[144,1152]{1,0:T(8,128)(2,1)S(1)}, u32[]{:S(2)}, u32[]{:S(2)}) collective-permute-start(bf16[144,1152]{1,0:T(8,128)(2,1)S(1)} %collective-permute-done.14.refs_1_), channel_id=1, source_target_pairs={{0,16},{1,65},{2,18},{3,67},{4,20},{5,69},{6,22},{7,71},{8,24},{9,... | collective-permute-start | bytes 995336 | tf_op jit(solution)/shard_map/share_first/ppermute | solution.py:53
  109.8 9.2 %collective-permute-start.20 = (bf16[144,1152]{1,0:T(8,128)(2,1)S(1)}, bf16[144,1152]{1,0:T(8,128)(2,1)S(1)}, u32[]{:S(2)}, u32[]{:S(2)}) collective-permute-start(bf16[144,1152]{1,0:T(8,128)(2,1)S(1)} %collective-permute-done.15.refs_2_), channel_id=1, source_target_pairs={{0,48},{1,193},{2,50},{3,195},{4,52},{5,197},{6,54},{7,199},{8,56}... | collective-permute-start | bytes 995336 | tf_op jit(solution)/shard_map/share_first/ppermute | solution.py:53
  113.3 5.7 %collective-permute-start.21 = (bf16[144,1152]{1,0:T(8,128)(2,1)S(1)}, bf16[144,1152]{1,0:T(8,128)(2,1)S(1)}, u32[]{:S(2)}, u32[]{:S(2)}) collective-permute-start(bf16[144,1152]{1,0:T(8,128)(2,1)S(1)} %collective-permute-done.14.refs_1_), channel_id=1, source_target_pairs={{0,1},{1,0},{2,3},{3,2},{4,5},{5,4},{6,7},{7,6},{8,9},{9,8},{10,11... | collective-permute-start | bytes 995336 | tf_op jit(solution)/shard_map/share_first/ppermute | solution.py:53
  114.2 5.3 %collective-permute-start.22 = (bf16[144,1152]{1,0:T(8,128)(2,1)S(1)}, bf16[144,1152]{1,0:T(8,128)(2,1)S(1)}, u32[]{:S(2)}, u32[]{:S(2)}) collective-permute-start(bf16[144,1152]{1,0:T(8,128)(2,1)S(1)} %collective-permute-done.15.refs_2_), channel_id=1, source_target_pairs={{0,1},{1,0},{2,3},{3,2},{4,5},{5,4},{6,7},{7,6},{8,9},{9,8},{10,11... | collective-permute-start | bytes 995336 | tf_op jit(solution)/shard_map/share_first/ppermute | solution.py:53
  114.6 4.9 %collective-permute-start.23 = (bf16[144,1152]{1,0:T(8,128)(2,1)S(1)}, bf16[144,1152]{1,0:T(8,128)(2,1)S(1)}, u32[]{:S(2)}, u32[]{:S(2)}) collective-permute-start(bf16[144,1152]{1,0:T(8,128)(2,1)S(1)} %collective-permute-done.16.refs_3_), channel_id=1, source_target_pairs={{0,1},{1,0},{2,3},{3,2},{4,5},{5,4},{6,7},{7,6},{8,9},{9,8},{10,11... | collective-permute-start | bytes 995336 | tf_op jit(solution)/shard_map/share_first/ppermute | solution.py:53
  117.2 3.0 %collective-permute-start.24 = (bf16[144,1152]{1,0:T(8,128)(2,1)S(1)}, bf16[144,1152]{1,0:T(8,128)(2,1)S(1)}, u32[]{:S(2)}, u32[]{:S(2)}) collective-permute-start(bf16[144,1152]{1,0:T(8,128)(2,1)S(1)} %collective-permute-done.17.refs_4_), channel_id=1, source_target_pairs={{0,1},{1,0},{2,3},{3,2},{4,5},{5,4},{6,7},{7,6},{8,9},{9,8},{10,11... | collective-permute-start | bytes 995336 | tf_op jit(solution)/shard_map/share_first/ppermute | solution.py:53
  119.0 2.6 %collective-permute-start.25 = (bf16[144,1152]{1,0:T(8,128)(2,1)S(1)}, bf16[144,1152]{1,0:T(8,128)(2,1)S(1)}, u32[]{:S(2)}, u32[]{:S(2)}) collective-permute-start(bf16[144,1152]{1,0:T(8,128)(2,1)S(1)} %get-tuple-element.54.refs_2_), channel_id=1, source_target_pairs={{0,1},{1,0},{2,3},{3,2},{4,5},{5,4},{6,7},{7,6},{8,9},{9,8},{10,11... | collective-permute-start | bytes 995336 | tf_op jit(solution)/shard_map/write/ppermute | solution.py:53
  119.1 2.5 %collective-permute-start.26 = (bf16[144,1152]{1,0:T(8,128)(2,1)S(1)}, bf16[144,1152]{1,0:T(8,128)(2,1)S(1)}, u32[]{:S(2)}, u32[]{:S(2)}) collective-permute-start(bf16[144,1152]{1,0:T(8,128)(2,1)S(1)} %get-tuple-element.55.refs_3_), channel_id=1, source_target_pairs={{0,1},{1,0},{2,3},{3,2},{4,5},{5,4},{6,7},{7,6},{8,9},{9,8},{10,11... | collective-permute-start | bytes 995336 | tf_op jit(solution)/shard_map/write/ppermute | solution.py:53

commit v8 on v7

--- a/solution.py
+++ b/solution.py
@@ -107,12 +107,27 @@
     return projected, inverse
 
 
-def add_head(head, x, back, before):
-    step = head.shape[0] // 3
-    for k in range(3):
+def make_head(head, pairs):
+    step = 128
+    for k in range(head.shape[0] // step):
         at = pl.ds(k * step, step)
-        new = contract(x[:, at], back[...], 0, 0)
-        head[at, :] = new if before is None else before[at, :] + new
+        head[at, :] = sum(contract(x[:, at], back[...], 0, 0) for x, back in pairs)
+
+
+def join_positions(image_hbm, position_hbm, out, position, sems):
+    rows = position.shape[0]
+    moves = [
+        pltpu.make_async_copy(position_hbm, position, sems.at[0]),
+        pltpu.make_async_copy(image_hbm, out.at[pl.ds(0, rows), :], sems.at[1]),
+    ]
+    for move in moves:
+        move.start()
+    tail = pl.ds(rows, TAIL)
+    out[tail, :] = jnp.zeros((TAIL, out.shape[1]), bf16)
+    moves[0].wait()
+    row = position[...].reshape(1, rows).astype(f32)
+    out[tail, pl.ds(0, rows)] = jnp.broadcast_to(row, (TAIL, rows)).astype(bf16)
+    moves[1].wait()
 
 
 def visit(log_scale, shift, x, text_w, image_emb, finish, back, grad, grad_before):
@@ -137,8 +152,8 @@
 
 def near_kernel(
     log_scale, shift, text_hbm, text_w_hbm, image_w_hbm, text_other, image_own, image_other,
-    image_near, text_w, image_emb, image_projected, image_inverse, grad, head,
-    text_near, image_w, back, sems,
+    image_near, text_w, image_emb, image_projected, image_inverse, grad, text_near, back,
+    image_w, sems,
 ):
     rows = text_other.shape[0]
     first, second = pl.ds(0, rows), pl.ds(rows, rows)
@@ -173,10 +188,6 @@
 
     visit(log_scale, shift, text_near, text_w, image_emb, with_labels, back, grad, None)
 
-    @pl.when(on_text())
-    def _():
-        add_head(head, text_near, back, None)
-
 
 def gate_kernel(*refs):
     pass
@@ -189,23 +200,16 @@
     return gate((), (token,), *arrays) if in_hbm else gate((), (), *arrays, token)
 
 
-def pair_kernel(
-    log_scale, shift, below, above, text_w, image_emb, grad_before, head_before,
-    grad, head, x, back,
-):
+def pair_kernel(log_scale, shift, below, above, text_w, image_emb, grad_before, grad, x, back):
     rows = below.shape[0]
     x[pl.ds(0, rows), :] = below[...]
     x[pl.ds(rows, rows), :] = above[...]
     visit(log_scale, shift, x, text_w, image_emb, lambda c: c, back, grad, grad_before)
 
-    @pl.when(on_text())
-    def _():
-        add_head(head, x, back, head_before)
-
 
 def far_kernel(
-    log_scale, shift, far, far_other, text_w, image_emb, grad_before, head_before,
-    image_near, image_projected, image_inverse,
+    log_scale, shift, far, far_other, text_w, image_emb, grad_before,
+    image_near, image_projected, image_inverse, x_1, back_1, x_2, back_2, x_3, back_3,
     own, right_top, right_bottom, left_top, left_bottom, far_right, far_left,
     grad, head, x, back,
 ):
@@ -222,7 +226,7 @@
 
     @pl.when(on_text())
     def _():
-        add_head(head, x, back, head_before)
+        make_head(head, [(x_1, back_1), (x_2, back_2), (x_3, back_3), (x, back)])
 
     @pl.when(jnp.logical_not(on_text()))
     def _():
@@ -231,7 +235,7 @@
         unit = image_projected[...] * inverse
         radial = jnp.sum(gradient * unit, axis=-1, keepdims=True)
         back[...] = ((gradient - unit * radial) * inverse).astype(bf16)
-        add_head(head, image_near, back, None)
+        make_head(head, [(image_near, back)])
 
     slab = head.shape[0] // 4
     half = slab // 2
@@ -325,22 +329,20 @@
     piece, half_piece = ((slab, width), bf16), ((half, width), bf16)
     with jax.named_scope("band_exchange"):
         text_other = send(text_x, SWAP)
-        tail = jnp.pad(position.astype(bf16)[None], ((0, TAIL - 1), (0, width - rows)))
-        image_own = jnp.concatenate([image_x, tail])
+        [image_own] = call(
+            join_positions,
+            [((rows + TAIL, width), bf16)],
+            [pltpu.VMEM((rows,), jnp.int32), pltpu.SemaphoreType.DMA((2,))],
+        )((), (image_x, position))
         image_other = send(image_own, SWAP)
         below = send(text_x, shifted(2))
         above = send(text_x, shifted(-2))
         far = send(text_x, FAR)
     with jax.named_scope("near"):
-        image_near, weight, image_emb, image_projected, image_inverse, grad, head = call(
+        image_near, weight, image_emb, image_projected, image_inverse, grad, *near = call(
             near_kernel,
-            [pair, matrix, pair, pair_f32, ((2 * rows, 1), f32), pair_f32, total],
-            [
-                pltpu.VMEM(*pair),
-                pltpu.VMEM(*matrix),
-                pltpu.VMEM(*pair),
-                pltpu.SemaphoreType.DMA((3,)),
-            ],
+            [pair, matrix, pair, pair_f32, ((2 * rows, 1), f32), pair_f32, pair, pair],
+            [pltpu.VMEM(*matrix), pltpu.SemaphoreType.DMA((3,))],
             flops=4 * 10**9,
         )(
             scalars, (text_x, text_w, image_w), text_other, image_own, image_other
@@ -349,15 +351,13 @@
         below, above = after(image_inverse, below, above)
         below_other = send(below, SWAP)
         above_other = send(above, SWAP)
-    visits = call(
-        pair_kernel, [pair_f32, total], [pltpu.VMEM(*pair), pltpu.VMEM(*pair)], flops=4 * 10**9
-    )
+    visits = call(pair_kernel, [pair_f32, pair, pair], flops=4 * 10**9)
     with jax.named_scope("received"):
-        grad, head = visits(scalars, (), below, above, weight, image_emb, grad, head)
+        grad, *first = visits(scalars, (), below, above, weight, image_emb, grad)
         [far] = after(grad, far)
         far_other = send(far, SWAP)
     with jax.named_scope("partners"):
-        grad, head = visits(scalars, (), below_other, above_other, weight, image_emb, grad, head)
+        grad, *second = visits(scalars, (), below_other, above_other, weight, image_emb, grad)
     with jax.named_scope("far"):
         own, right_top, right_bottom, left_top, left_bottom, far_right, far_left = call(
             far_kernel,
@@ -365,8 +365,8 @@
             [pltpu.VMEM(*pair_f32), pltpu.VMEM(*total), pltpu.VMEM(*pair), pltpu.VMEM(*pair)],
             flops=4 * 10**9,
         )(
-            scalars, (), far, far_other, weight, image_emb, grad, head, image_near,
-            image_projected, image_inverse,
+            scalars, (), far, far_other, weight, image_emb, grad, image_near, image_projected,
+            image_inverse, *near, *first, *second,
         )
     with jax.named_scope("sum_first"):
         from_left = send(far_right, RIGHT)

time: 123 us -> 129 us (1.049)
  waiting for transfers between devices: 13.7 us -> 22.5 us
  blocking collectives: 45.2 us -> 42.5 us
  other arithmetic: 1.78 us -> 0.13 us
  starting transfers between devices: 39.8 us -> 41.2 us
    ppermute x27, waiting for transfers between devices: 13.7 us -> 22.5 us  [send(): return lax.ppermute(block, 'dp', pairs)]
    all_to_all x4, blocking collectives: 45.2 us -> 42.5 us  [exchange(): lax.all_to_all(parts, 'dp', 0, 0, axis_index_groups=members, tiled=True)]
    ppermute x27, starting transfers between devices: 39.8 us -> 41.2 us  [send(): return lax.ppermute(block, 'dp', pairs)]
    pallas_call x12 -> x13, Pallas kernels: 19.6 us -> 20.2 us  [run(): pl.pallas_call(body, out_shape=[jax.ShapeDtypeStruct(s, d) for s, d in ou...]
  transfers between devices with their start and end apart: 27 -> 27, of which waited for: 8 -> 8; matrix products, arithmetic and copies ran while one was open for 0% -> 0% of each run, Pallas kernels for 12% -> 10%
where the time goes in v8:
time: 129 us
  blocking collectives  42.5 us (33%)
  starting transfers between devices  41.2 us (32%)
  waiting for transfers between devices  22.5 us (17%)
  Pallas kernels  20.2 us (16%)
  between operations  2.31 us (2%)
    all_to_all x4, blocking collectives, exchange(): lax.all_to_all(parts, 'dp', 0, 0, axis_index_groups=members, tiled=True)  42.5 us
    ppermute x27, starting transfers between devices, send(): return lax.ppermute(block, 'dp', pairs)  41.2 us
    ppermute x27, waiting for transfers between devices, send(): return lax.ppermute(block, 'dp', pairs)  22.5 us
    pallas_call x13, Pallas kernels, run(): pl.pallas_call(body, out_shape=[jax.ShapeDtypeStruct(s, d) for s, d in ou...  20.2 us
  transfers between devices with their start and end apart: 27, of which 8 were waited for; matrix products, arithmetic and copies ran while one was open for 0% of the time, Pallas kernels for 10%

profile of v8, /device:TPU:1, one launch (start us, length us, event | category | flops | bytes accessed | tf_op | source)
XLA Modules:
  0.0 129.0 jit_solution(13669622497716392643)
XLA Ops:
  0.6 1.0 band_exchange.1.image_own
  1.6 3.3 %collective-permute-start.4 = (bf16[144,1152]{1,0:T(8,128)(2,1)S(1)}, bf16[144,1152]{1,0:T(8,128)(2,1)S(1)}, u32[]{:S(2)}, u32[]{:S(2)}) collective-permute-start(bf16[144,1152]{1,0:T(8,128)(2,1)S(1)} %band_exchange.1.image_own), channel_id=1, source_target_pairs={{0,1},{1,0},{2,3},{3,2},{4,5},{5,4},{6,7},{7,6},{8,9},{9,8},{10,11... | collective-permute-start | bytes 995336 | tf_op jit(solution)/shard_map/band_exchange/ppermute | solution.py:53
  5.0 0.1 collective-permute-start.3
  5.1 8.5 %collective-permute-start.2 = (bf16[128,1152]{1,0:T(8,128)(2,1)}, bf16[128,1152]{1,0:T(8,128)(2,1)S(1)}, u32[]{:S(2)}, u32[]{:S(2)}) collective-permute-start(bf16[128,1152]{1,0:T(8,128)(2,1)} %text_hbm.1), channel_id=1, source_target_pairs={{0,254},{1,255},{2,0},{3,1},{4,2},{5,3},{6,4},{7,5},{8,6},{9,7},{1... | collective-permute-start | bytes 884744 | tf_op jit(solution)/shard_map/band_exchange/ppermute | solution.py:53
  13.5 0.0 collective-permute-start.1
  13.6 0.0 collective-permute-start
  14.9 0.0 collective-permute-done.3.text_other
  14.9 0.0 collective-permute-done.4.image_other
  14.9 5.0 %near.1 = (bf16[256,1152]{1,0:T(8,128)(2,1)S(1)}, bf16[1152,1152]{1,0:T(8,128)(2,1)S(1)}, bf16[256,1152]{1,0:T(8,128)(2,1)S(1)}, f32[256,1152]{1,0:T(8,128)S(1)}...) custom-call(f32[1]{0:T(128)S(6)} %copy.27.log_scale, ...), custom_call_target="tpu_custom_call" | custom-call | flops 4000000000 | tf_op jit(solution)/shard_map/near/pallas_call | solution.py:69
  19.9 0.0 collective-permute-done.2.refs_1_
  19.9 10.3 %collective-permute-done.1.refs_0_ = bf16[128,1152]{1,0:T(8,128)(2,1)S(1)} collective-permute-done((bf16[128,1152]{1,0:T(8,128)(2,1)}, bf16[128,1152]{1,0:T(8,128)(2,1)S(1)}, u32[]{:S(2)}, u32[]{:S(2)}) %collective-permute-start.1) | collective-permute-done | bytes 294944 | tf_op jit(solution)/shard_map/band_exchange/ppermute | solution.py:53
  30.2 2.7 %collective-permute-start.6 = (bf16[128,1152]{1,0:T(8,128)(2,1)S(1)}, bf16[128,1152]{1,0:T(8,128)(2,1)S(1)}, u32[]{:S(2)}, u32[]{:S(2)}) collective-permute-start(bf16[128,1152]{1,0:T(8,128)(2,1)S(1)} %get-tuple-element.34.below), channel_id=1, source_target_pairs={{0,1},{1,0},{2,3},{3,2},{4,5},{5,4},{6,7},{7,6},{8,9},{9,8},{10,11... | collective-permute-start | bytes 884744 | tf_op jit(solution)/shard_map/swap_neighbours/ppermute | solution.py:53
  32.9 0.0 collective-permute-start.7
  32.9 2.1 %received.2 = (f32[256,1152]{1,0:T(8,128)S(1)}, bf16[256,1152]{1,0:T(8,128)(2,1)S(1)}, bf16[256,1152]{1,0:T(8,128)(2,1)S(1)}) custom-call(f32[1]{0:T(128)S(6)} %copy.27.log_scale, f32[1]{0:T(128)S(6)} %copy.28.shift, bf16[128,1152]{1,0:T(8,128)(2,1)S(1)} %get-tuple-element.34.below, bf16[128,1152]{1,0:T(8,128)(2,1)S(1)} %get-tuple-element.35.above, ...), custom_call_target="tpu_custom_call" | custom-call | flops 4000000000 | tf_op jit(solution)/shard_map/received/pallas_call | solution.py:69
  35.0 0.0 collective-permute-done.refs_0_
  35.1 0.6 collective-permute-start.5
  35.7 0.0 collective-permute-done.6.below
  35.7 2.3 %partners.1 = (f32[256,1152]{1,0:T(8,128)S(1)}, bf16[256,1152]{1,0:T(8,128)(2,1)S(1)}, bf16[256,1152]{1,0:T(8,128)(2,1)S(1)}) custom-call(f32[1]{0:T(128)S(6)} %copy.27.log_scale, f32[1]{0:T(128)S(6)} %copy.28.shift, bf16[128,1152]{1,0:T(8,128)(2,1)S(1)} %collective-permute-done.6.below, bf16[128,1152]{1,0:T(8,128)(2,1)S(1)} %collective-permute-done.7.above, ...), custom_call_target="tpu_custom_call" | custom-call | flops 4000000000 | tf_op jit(solution)/shard_map/partners/pallas_call | solution.py:69
  37.9 0.0 collective-permute-done.5.far_other
  38.0 5.6 %far.1 = (bf16[288,1152]{1,0:T(8,128)(2,1)S(1)}, bf16[144,1152]{1,0:T(8,128)(2,1)S(1)}, bf16[144,1152]{1,0:T(8,128)(2,1)S(1)}, bf16[144,1152]{1,0:T(8,128)(2,1)S...) custom-call(f32[1]{0:T(128)S(6)} %copy.27.log_scale, ...), custom_call_target="tpu_custom_call" | custom-call | flops 4000000000 | tf_op jit(solution)/shard_map/far/pallas_call | solution.py:69
  43.6 0.1 collective-permute-start.8
  43.7 2.7 %collective-permute-start.9 = (bf16[144,1152]{1,0:T(8,128)(2,1)S(1)}, bf16[144,1152]{1,0:T(8,128)(2,1)S(1)}, u32[]{:S(2)}, u32[]{:S(2)}) collective-permute-start(bf16[144,1152]{1,0:T(8,128)(2,1)S(1)} %get-tuple-element.53), channel_id=1, source_target_pairs={{0,48},{1,193},{2,50},{3,195},{4,52},{5,197},{6,54},{7,199},{8,56}... | collective-permute-start | bytes 995336 | tf_op jit(solution)/shard_map/sum_first/ppermute | solution.py:53
  46.4 2.7 %collective-permute-start.12 = (bf16[144,1152]{1,0:T(8,128)(2,1)S(1)}, bf16[144,1152]{1,0:T(8,128)(2,1)S(1)}, u32[]{:S(2)}, u32[]{:S(2)}) collective-permute-start(bf16[144,1152]{1,0:T(8,128)(2,1)S(1)} %get-tuple-element.56), channel_id=1, source_target_pairs={{0,48},{1,193},{2,50},{3,195},{4,52},{5,197},{6,54},{7,199},{8,56}... | collective-permute-start | bytes 995336 | tf_op jit(solution)/shard_map/sum_first/ppermute | solution.py:53
  49.0 2.1 %collective-permute-done.8.b = bf16[144,1152]{1,0:T(8,128)(2,1)S(1)} collective-permute-done((bf16[144,1152]{1,0:T(8,128)(2,1)S(1)}, bf16[144,1152]{1,0:T(8,128)(2,1)S(1)}, u32[]{:S(2)}, u32[]{:S(2)}) %collective-permute-start.8) | collective-permute-done | bytes 331808 | tf_op jit(solution)/shard_map/sum_first/ppermute | solution.py:53
  51.2 0.0 collective-permute-done.9.d
  51.2 0.2 sum_first.2
  51.3 0.1 collective-permute-start.10
  51.4 2.7 %collective-permute-start.13 = (bf16[144,1152]{1,0:T(8,128)(2,1)S(1)}, bf16[144,1152]{1,0:T(8,128)(2,1)S(1)}, u32[]{:S(2)}, u32[]{:S(2)}) collective-permute-start(bf16[144,1152]{1,0:T(8,128)(2,1)S(1)} %get-tuple-element.57), channel_id=1, source_target_pairs={{0,48},{1,193},{2,50},{3,195},{4,52},{5,197},{6,54},{7,199},{8,56}... | collective-permute-start | bytes 995336 | tf_op jit(solution)/shard_map/sum_first/ppermute | solution.py:53
  54.1 0.3 collective-permute-done.11.a_bottom
  54.4 0.0 collective-permute-done.12.b_top
  54.4 4.2 %collective-permute-done.10.a_top = bf16[144,1152]{1,0:T(8,128)(2,1)S(1)} collective-permute-done((bf16[144,1152]{1,0:T(8,128)(2,1)S(1)}, bf16[144,1152]{1,0:T(8,128)(2,1)S(1)}, u32[]{:S(2)}, u32[]{:S(2)}) %collective-permute-start.10) | collective-permute-done | bytes 331808 | tf_op jit(solution)/shard_map/sum_first/ppermute | solution.py:53
  58.6 0.0 collective-permute-done.13.b_bottom
  58.6 0.3 sum_first.3
  58.8 10.2 %all_to_all.20 = bf16[4,72,1152]{2,1,0:T(8,128)(2,1)S(1)} all-to-all(bf16[4,72,1152]{2,1,0:T(8,128)(2,1)S(1)} %bitcast.18), channel_id=1, replica_groups={{0,64,128,192},{1,17,33,49},{2,66,130,194},{3,19,35,51},{4,68,132,196},..., dimensions={0} | all-to-all | bytes 1327104 | tf_op jit(solution)/shard_map/sum_second/all_to_all | solution.py:57
  69.0 0.1 reduce_sum.24
  69.2 10.8 %all_to_all.21 = bf16[88,8,128]{2,1,0:T(8,128)(2,1)S(1)} all-to-all(bf16[88,8,128]{2,1,0:T(8,128)(2,1)S(1)} %concatenate.3), channel_id=1, replica_groups={{0,2,4,6,8,10,12,14},{1,3,5,7,9,11,13,15},{16,18,20,22,24,26,28,30},{17..., dimensions={0} | all-to-all | bytes 360448 | tf_op jit(solution)/shard_map/sum_lines/all_to_all | solution.py:57
  80.0 11.4 %all_to_all.22 = bf16[88,8,128]{2,1,0:T(8,128)(2,1)S(1)} all-to-all(bf16[88,8,128]{2,1,0:T(8,128)(2,1)S(1)} %bitcast.20), channel_id=1, replica_groups={{0,2,4,6,8,10,12,14},{1,3,5,7,9,11,13,15},{16,18,20,22,24,26,28,30},{17..., dimensions={0} | all-to-all | bytes 360448 | tf_op jit(solution)/shard_map/share_lines/all_to_all | solution.py:57
  91.5 10.1 %all_to_all.23 = bf16[4,72,1152]{2,1,0:T(8,128)(2,1)S(1)} all-to-all(bf16[4,72,1152]{2,1,0:T(8,128)(2,1)S(1)} %tile.20), channel_id=1, replica_groups={{0,64,128,192},{1,17,33,49},{2,66,130,194},{3,19,35,51},{4,68,132,196},..., dimensions={0} | all-to-all | bytes 1327104 | tf_op jit(solution)/shard_map/share_second/all_to_all | solution.py:57
  101.6 6.9 %collective-permute-start.18 = (bf16[288,1152]{1,0:T(8,128)(2,1)S(1)}, bf16[288,1152]{1,0:T(8,128)(2,1)S(1)}, u32[]{:S(2)}, u32[]{:S(2)}) collective-permute-start(bf16[288,1152]{1,0:T(8,128)(2,1)S(1)} %bitcast.16), channel_id=1, source_target_pairs={{0,1},{1,0},{2,3},{3,2},{4,5},{5,4},{6,7},{7,6},{8,9},{9,8},{10,11... | collective-permute-start | bytes 1990664 | tf_op jit(solution)/shard_map/share_first/ppermute | solution.py:53
  108.5 0.1 fusion
  108.5 0.4 collective-permute-start.14
  108.9 2.4 %collective-permute-start.15 = (bf16[144,1152]{1,0:T(8,128)(2,1)S(1)}, bf16[144,1152]{1,0:T(8,128)(2,1)S(1)}, u32[]{:S(2)}, u32[]{:S(2)}) collective-permute-start(bf16[144,1152]{1,0:T(8,128)(2,1)S(1)} %bitcast.23), channel_id=1, source_target_pairs={{0,48},{1,193},{2,50},{3,195},{4,52},{5,197},{6,54},{7,199},{8,56}... | collective-permute-start | bytes 995336 | tf_op jit(solution)/shard_map/share_first/ppermute | solution.py:53
  111.3 0.0 collective-permute-start.17
  111.3 1.4 %collective-permute-start.16 = (bf16[144,1152]{1,0:T(8,128)(2,1)S(1)}, bf16[144,1152]{1,0:T(8,128)(2,1)S(1)}, u32[]{:S(2)}, u32[]{:S(2)}) collective-permute-start(bf16[144,1152]{1,0:T(8,128)(2,1)S(1)} %bitcast.24), channel_id=1, source_target_pairs={{0,16},{1,65},{2,18},{3,67},{4,20},{5,69},{6,22},{7,71},{8,24},{9,... | collective-permute-start | bytes 995336 | tf_op jit(solution)/shard_map/share_first/ppermute | solution.py:53
  112.8 3.3 %collective-permute-done.14.refs_1_ = bf16[144,1152]{1,0:T(8,128)(2,1)S(1)} collective-permute-done((bf16[144,1152]{1,0:T(8,128)(2,1)S(1)}, bf16[144,1152]{1,0:T(8,128)(2,1)S(1)}, u32[]{:S(2)}, u32[]{:S(2)}) %collective-permute-start.14) | collective-permute-done | bytes 331808 | tf_op jit(solution)/shard_map/share_first/ppermute | solution.py:53
  116.1 0.0 collective-permute-start.19
  116.1 0.0 collective-permute-done.15.refs_2_
  116.1 2.7 %collective-permute-start.20 = (bf16[144,1152]{1,0:T(8,128)(2,1)S(1)}, bf16[144,1152]{1,0:T(8,128)(2,1)S(1)}, u32[]{:S(2)}, u32[]{:S(2)}) collective-permute-start(bf16[144,1152]{1,0:T(8,128)(2,1)S(1)} %collective-permute-done.15.refs_2_), channel_id=1, source_target_pairs={{0,48},{1,193},{2,50},{3,195},{4,52},{5,197},{6,54},{7,199},{8,56}... | collective-permute-start | bytes 995336 | tf_op jit(solution)/shard_map/share_first/ppermute | solution.py:53
  118.8 0.1 collective-permute-done.17.refs_4_
  118.9 1.3 collective-permute-start.24
  120.2 0.0 collective-permute-done.16.refs_3_
  120.2 0.3 collective-permute-start.21
  120.5 0.0 collective-permute-done.18.refs_5_
  120.5 0.2 collective-permute-start.23
  120.7 1.5 %write.4 = (bf16[1152,1152]{1,0:T(8,128)(2,1)}, bf16[1152,1152]{1,0:T(8,128)(2,1)}) custom-call(bf16[288,1152]{1,0:T(8,128)(2,1)S(1)} %bitcast.17, bf16[144,1152]{1,0:T(8,128)(2,1)S(1)} %collective-permute-done.14.refs_1_, bf16[144,1152]{1,0:T(8,128)(2,1)S(1)} %collective-permute-done.15.refs_2_, bf16[144,1152]{1,0:T(8,128)(2,1)S(1)} %collective-permute-done.16.refs_3_, ...), custom_call_target="tpu_custom_call" | custom-call | tf_op jit(solution)/shard_map/write/pallas_call | solution.py:69
  122.3 1.3 %collective-permute-done.19.refs_1_ = bf16[144,1152]{1,0:T(8,128)(2,1)S(1)} collective-permute-done((bf16[144,1152]{1,0:T(8,128)(2,1)S(1)}, bf16[144,1152]{1,0:T(8,128)(2,1)S(1)}, u32[]{:S(2)}, u32[]{:S(2)}) %collective-permute-start.19) | collective-permute-done | bytes 331808 | tf_op jit(solution)/shard_map/share_first/ppermute | solution.py:53
  123.6 1.7 %collective-permute-start.22 = (bf16[144,1152]{1,0:T(8,128)(2,1)S(1)}, bf16[144,1152]{1,0:T(8,128)(2,1)S(1)}, u32[]{:S(2)}, u32[]{:S(2)}) collective-permute-start(bf16[144,1152]{1,0:T(8,128)(2,1)S(1)} %collective-permute-done.15.refs_2_), channel_id=1, source_target_pairs={{0,1},{1,0},{2,3},{3,2},{4,5},{5,4},{6,7},{7,6},{8,9},{9,8},{10,11... | collective-permute-start | bytes 995336 | tf_op jit(solution)/shard_map/share_first/ppermute | solution.py:53
  125.3 0.0 collective-permute-done.20.refs_2_
  125.3 0.1 collective-permute-start.25
  125.4 0.4 collective-permute-start.26
  125.8 0.7 collective-permute-done.22.refs_5_
  126.5 1.3 %write.6 = (bf16[1152,1152]{1,0:T(8,128)(2,1)}, bf16[1152,1152]{1,0:T(8,128)(2,1)}) custom-call(bf16[1152,1152]{1,0:T(8,128)(2,1)} %get-tuple-element.58.refs_0_, bf16[1152,1152]{1,0:T(8,128)(2,1)} %get-tuple-element.59.refs_1_, bf16[144,1152]{1,0:T(8,128)(2,1)S(1)} %get-tuple-element.60.refs_2_, ...), custom_call_target="tpu_custom_call", output_to_operand_aliasing={{0}: (0, {}), {1}: (1, {})} | custom-call | tf_op jit(solution)/shard_map/write/pallas_call | solution.py:69
  127.9 0.0 collective-permute-done.25.refs_2_
  127.9 0.9 write.7
  (14 shorter events, 0.2 us)
Async XLA Ops:
  1.6 13.2 %collective-permute-start.4 = (bf16[144,1152]{1,0:T(8,128)(2,1)S(1)}, bf16[144,1152]{1,0:T(8,128)(2,1)S(1)}, u32[]{:S(2)}, u32[]{:S(2)}) collective-permute-start(bf16[144,1152]{1,0:T(8,128)(2,1)S(1)} %band_exchange.1.image_own), channel_id=1, source_target_pairs={{0,1},{1,0},{2,3},{3,2},{4,5},{5,4},{6,7},{7,6},{8,9},{9,8},{10,11... | collective-permute-start | bytes 995336 | tf_op jit(solution)/shard_map/band_exchange/ppermute | solution.py:53
  5.0 9.9 %collective-permute-start.3 = (bf16[128,1152]{1,0:T(8,128)(2,1)}, bf16[128,1152]{1,0:T(8,128)(2,1)S(1)}, u32[]{:S(2)}, u32[]{:S(2)}) collective-permute-start(bf16[128,1152]{1,0:T(8,128)(2,1)} %text_hbm.1), channel_id=1, source_target_pairs={{0,1},{1,0},{2,3},{3,2},{4,5},{5,4},{6,7},{7,6},{8,9},{9,8},{10,11... | collective-permute-start | bytes 884744 | tf_op jit(solution)/shard_map/band_exchange/ppermute | solution.py:53
  5.1 14.9 %collective-permute-start.2 = (bf16[128,1152]{1,0:T(8,128)(2,1)}, bf16[128,1152]{1,0:T(8,128)(2,1)S(1)}, u32[]{:S(2)}, u32[]{:S(2)}) collective-permute-start(bf16[128,1152]{1,0:T(8,128)(2,1)} %text_hbm.1), channel_id=1, source_target_pairs={{0,254},{1,255},{2,0},{3,1},{4,2},{5,3},{6,4},{7,5},{8,6},{9,7},{1... | collective-permute-start | bytes 884744 | tf_op jit(solution)/shard_map/band_exchange/ppermute | solution.py:53
  13.5 16.7 %collective-permute-start.1 = (bf16[128,1152]{1,0:T(8,128)(2,1)}, bf16[128,1152]{1,0:T(8,128)(2,1)S(1)}, u32[]{:S(2)}, u32[]{:S(2)}) collective-permute-start(bf16[128,1152]{1,0:T(8,128)(2,1)} %text_hbm.1), channel_id=1, source_target_pairs={{0,2},{1,3},{2,4},{3,5},{4,6},{5,7},{6,8},{7,9},{8,10},{9,11},{10,... | collective-permute-start | bytes 884744 | tf_op jit(solution)/shard_map/band_exchange/ppermute | solution.py:53
  13.6 21.5 %collective-permute-start = (bf16[128,1152]{1,0:T(8,128)(2,1)}, bf16[128,1152]{1,0:T(8,128)(2,1)S(1)}, u32[]{:S(2)}, u32[]{:S(2)}) collective-permute-start(bf16[128,1152]{1,0:T(8,128)(2,1)} %text_hbm.1), channel_id=1, source_target_pairs={{0,253},{1,4},{2,255},{3,6},{4,1},{5,8},{6,3},{7,10},{8,5},{9,12},... | collective-permute-start | bytes 884744 | tf_op jit(solution)/shard_map/band_exchange/ppermute | solution.py:53
  30.2 5.5 %collective-permute-start.6 = (bf16[128,1152]{1,0:T(8,128)(2,1)S(1)}, bf16[128,1152]{1,0:T(8,128)(2,1)S(1)}, u32[]{:S(2)}, u32[]{:S(2)}) collective-permute-start(bf16[128,1152]{1,0:T(8,128)(2,1)S(1)} %get-tuple-element.34.below), channel_id=1, source_target_pairs={{0,1},{1,0},{2,3},{3,2},{4,5},{5,4},{6,7},{7,6},{8,9},{9,8},{10,11... | collective-permute-start | bytes 884744 | tf_op jit(solution)/shard_map/swap_neighbours/ppermute | solution.py:53
  32.9 2.7 %collective-permute-start.7 = (bf16[128,1152]{1,0:T(8,128)(2,1)S(1)}, bf16[128,1152]{1,0:T(8,128)(2,1)S(1)}, u32[]{:S(2)}, u32[]{:S(2)}) collective-permute-start(bf16[128,1152]{1,0:T(8,128)(2,1)S(1)} %get-tuple-element.35.above), channel_id=1, source_target_pairs={{0,1},{1,0},{2,3},{3,2},{4,5},{5,4},{6,7},{7,6},{8,9},{9,8},{10,11... | collective-permute-start | bytes 884744 | tf_op jit(solution)/shard_map/swap_neighbours/ppermute | solution.py:53
  35.1 2.9 %collective-permute-start.5 = (bf16[128,1152]{1,0:T(8,128)(2,1)S(1)}, bf16[128,1152]{1,0:T(8,128)(2,1)S(1)}, u32[]{:S(2)}, u32[]{:S(2)}) collective-permute-start(bf16[128,1152]{1,0:T(8,128)(2,1)S(1)} %received.3.far), channel_id=1, source_target_pairs={{0,1},{1,0},{2,3},{3,2},{4,5},{5,4},{6,7},{7,6},{8,9},{9,8},{10,11... | collective-permute-start | bytes 884744 | tf_op jit(solution)/shard_map/received/ppermute | solution.py:53
  43.6 7.6 %collective-permute-start.8 = (bf16[144,1152]{1,0:T(8,128)(2,1)S(1)}, bf16[144,1152]{1,0:T(8,128)(2,1)S(1)}, u32[]{:S(2)}, u32[]{:S(2)}) collective-permute-start(bf16[144,1152]{1,0:T(8,128)(2,1)S(1)} %get-tuple-element.51), channel_id=1, source_target_pairs={{0,16},{1,65},{2,18},{3,67},{4,20},{5,69},{6,22},{7,71},{8,24},{9,... | collective-permute-start | bytes 995336 | tf_op jit(solution)/shard_map/sum_first/ppermute | solution.py:53
  43.7 7.5 %collective-permute-start.9 = (bf16[144,1152]{1,0:T(8,128)(2,1)S(1)}, bf16[144,1152]{1,0:T(8,128)(2,1)S(1)}, u32[]{:S(2)}, u32[]{:S(2)}) collective-permute-start(bf16[144,1152]{1,0:T(8,128)(2,1)S(1)} %get-tuple-element.53), channel_id=1, source_target_pairs={{0,48},{1,193},{2,50},{3,195},{4,52},{5,197},{6,54},{7,199},{8,56}... | collective-permute-start | bytes 995336 | tf_op jit(solution)/shard_map/sum_first/ppermute | solution.py:53
  46.4 8.1 %collective-permute-start.11 = (bf16[144,1152]{1,0:T(8,128)(2,1)S(1)}, bf16[144,1152]{1,0:T(8,128)(2,1)S(1)}, u32[]{:S(2)}, u32[]{:S(2)}) collective-permute-start(bf16[144,1152]{1,0:T(8,128)(2,1)S(1)} %get-tuple-element.55), channel_id=1, source_target_pairs={{0,16},{1,65},{2,18},{3,67},{4,20},{5,69},{6,22},{7,71},{8,24},{9,... | collective-permute-start | bytes 995336 | tf_op jit(solution)/shard_map/sum_first/ppermute | solution.py:53
  46.4 8.1 %collective-permute-start.12 = (bf16[144,1152]{1,0:T(8,128)(2,1)S(1)}, bf16[144,1152]{1,0:T(8,128)(2,1)S(1)}, u32[]{:S(2)}, u32[]{:S(2)}) collective-permute-start(bf16[144,1152]{1,0:T(8,128)(2,1)S(1)} %get-tuple-element.56), channel_id=1, source_target_pairs={{0,48},{1,193},{2,50},{3,195},{4,52},{5,197},{6,54},{7,199},{8,56}... | collective-permute-start | bytes 995336 | tf_op jit(solution)/shard_map/sum_first/ppermute | solution.py:53
  51.3 7.3 %collective-permute-start.10 = (bf16[144,1152]{1,0:T(8,128)(2,1)S(1)}, bf16[144,1152]{1,0:T(8,128)(2,1)S(1)}, u32[]{:S(2)}, u32[]{:S(2)}) collective-permute-start(bf16[144,1152]{1,0:T(8,128)(2,1)S(1)} %get-tuple-element.54), channel_id=1, source_target_pairs={{0,16},{1,65},{2,18},{3,67},{4,20},{5,69},{6,22},{7,71},{8,24},{9,... | collective-permute-start | bytes 995336 | tf_op jit(solution)/shard_map/sum_first/ppermute | solution.py:53
  51.4 7.2 %collective-permute-start.13 = (bf16[144,1152]{1,0:T(8,128)(2,1)S(1)}, bf16[144,1152]{1,0:T(8,128)(2,1)S(1)}, u32[]{:S(2)}, u32[]{:S(2)}) collective-permute-start(bf16[144,1152]{1,0:T(8,128)(2,1)S(1)} %get-tuple-element.57), channel_id=1, source_target_pairs={{0,48},{1,193},{2,50},{3,195},{4,52},{5,197},{6,54},{7,199},{8,56}... | collective-permute-start | bytes 995336 | tf_op jit(solution)/shard_map/sum_first/ppermute | solution.py:53
  101.6 18.9 %collective-permute-start.18 = (bf16[288,1152]{1,0:T(8,128)(2,1)S(1)}, bf16[288,1152]{1,0:T(8,128)(2,1)S(1)}, u32[]{:S(2)}, u32[]{:S(2)}) collective-permute-start(bf16[288,1152]{1,0:T(8,128)(2,1)S(1)} %bitcast.16), channel_id=1, source_target_pairs={{0,1},{1,0},{2,3},{3,2},{4,5},{5,4},{6,7},{7,6},{8,9},{9,8},{10,11... | collective-permute-start | bytes 1990664 | tf_op jit(solution)/shard_map/share_first/ppermute | solution.py:53
  108.5 7.6 %collective-permute-start.14 = (bf16[144,1152]{1,0:T(8,128)(2,1)S(1)}, bf16[144,1152]{1,0:T(8,128)(2,1)S(1)}, u32[]{:S(2)}, u32[]{:S(2)}) collective-permute-start(bf16[144,1152]{1,0:T(8,128)(2,1)S(1)} %bitcast.25), channel_id=1, source_target_pairs={{0,16},{1,65},{2,18},{3,67},{4,20},{5,69},{6,22},{7,71},{8,24},{9,... | collective-permute-start | bytes 995336 | tf_op jit(solution)/shard_map/share_first/ppermute | solution.py:53
  108.9 7.2 %collective-permute-start.15 = (bf16[144,1152]{1,0:T(8,128)(2,1)S(1)}, bf16[144,1152]{1,0:T(8,128)(2,1)S(1)}, u32[]{:S(2)}, u32[]{:S(2)}) collective-permute-start(bf16[144,1152]{1,0:T(8,128)(2,1)S(1)} %bitcast.23), channel_id=1, source_target_pairs={{0,48},{1,193},{2,50},{3,195},{4,52},{5,197},{6,54},{7,199},{8,56}... | collective-permute-start | bytes 995336 | tf_op jit(solution)/shard_map/share_first/ppermute | solution.py:53
  111.3 7.6 %collective-permute-start.17 = (bf16[144,1152]{1,0:T(8,128)(2,1)S(1)}, bf16[144,1152]{1,0:T(8,128)(2,1)S(1)}, u32[]{:S(2)}, u32[]{:S(2)}) collective-permute-start(bf16[144,1152]{1,0:T(8,128)(2,1)S(1)} %bitcast.26), channel_id=1, source_target_pairs={{0,48},{1,193},{2,50},{3,195},{4,52},{5,197},{6,54},{7,199},{8,56}... | collective-permute-start | bytes 995336 | tf_op jit(solution)/shard_map/share_first/ppermute | solution.py:53
  111.3 8.9 %collective-permute-start.16 = (bf16[144,1152]{1,0:T(8,128)(2,1)S(1)}, bf16[144,1152]{1,0:T(8,128)(2,1)S(1)}, u32[]{:S(2)}, u32[]{:S(2)}) collective-permute-start(bf16[144,1152]{1,0:T(8,128)(2,1)S(1)} %bitcast.24), channel_id=1, source_target_pairs={{0,16},{1,65},{2,18},{3,67},{4,20},{5,69},{6,22},{7,71},{8,24},{9,... | collective-permute-start | bytes 995336 | tf_op jit(solution)/shard_map/share_first/ppermute | solution.py:53
  116.1 7.5 %collective-permute-start.19 = (bf16[144,1152]{1,0:T(8,128)(2,1)S(1)}, bf16[144,1152]{1,0:T(8,128)(2,1)S(1)}, u32[]{:S(2)}, u32[]{:S(2)}) collective-permute-start(bf16[144,1152]{1,0:T(8,128)(2,1)S(1)} %collective-permute-done.14.refs_1_), channel_id=1, source_target_pairs={{0,16},{1,65},{2,18},{3,67},{4,20},{5,69},{6,22},{7,71},{8,24},{9,... | collective-permute-start | bytes 995336 | tf_op jit(solution)/shard_map/share_first/ppermute | solution.py:53
  116.1 9.2 %collective-permute-start.20 = (bf16[144,1152]{1,0:T(8,128)(2,1)S(1)}, bf16[144,1152]{1,0:T(8,128)(2,1)S(1)}, u32[]{:S(2)}, u32[]{:S(2)}) collective-permute-start(bf16[144,1152]{1,0:T(8,128)(2,1)S(1)} %collective-permute-done.15.refs_2_), channel_id=1, source_target_pairs={{0,48},{1,193},{2,50},{3,195},{4,52},{5,197},{6,54},{7,199},{8,56}... | collective-permute-start | bytes 995336 | tf_op jit(solution)/shard_map/share_first/ppermute | solution.py:53
  118.9 6.5 %collective-permute-start.24 = (bf16[144,1152]{1,0:T(8,128)(2,1)S(1)}, bf16[144,1152]{1,0:T(8,128)(2,1)S(1)}, u32[]{:S(2)}, u32[]{:S(2)}) collective-permute-start(bf16[144,1152]{1,0:T(8,128)(2,1)S(1)} %collective-permute-done.17.refs_4_), channel_id=1, source_target_pairs={{0,1},{1,0},{2,3},{3,2},{4,5},{5,4},{6,7},{7,6},{8,9},{9,8},{10,11... | collective-permute-start | bytes 995336 | tf_op jit(solution)/shard_map/share_first/ppermute | solution.py:53
  120.2 5.6 %collective-permute-start.21 = (bf16[144,1152]{1,0:T(8,128)(2,1)S(1)}, bf16[144,1152]{1,0:T(8,128)(2,1)S(1)}, u32[]{:S(2)}, u32[]{:S(2)}) collective-permute-start(bf16[144,1152]{1,0:T(8,128)(2,1)S(1)} %collective-permute-done.14.refs_1_), channel_id=1, source_target_pairs={{0,1},{1,0},{2,3},{3,2},{4,5},{5,4},{6,7},{7,6},{8,9},{9,8},{10,11... | collective-permute-start | bytes 995336 | tf_op jit(solution)/shard_map/share_first/ppermute | solution.py:53
  120.5 5.3 %collective-permute-start.23 = (bf16[144,1152]{1,0:T(8,128)(2,1)S(1)}, bf16[144,1152]{1,0:T(8,128)(2,1)S(1)}, u32[]{:S(2)}, u32[]{:S(2)}) collective-permute-start(bf16[144,1152]{1,0:T(8,128)(2,1)S(1)} %collective-permute-done.16.refs_3_), channel_id=1, source_target_pairs={{0,1},{1,0},{2,3},{3,2},{4,5},{5,4},{6,7},{7,6},{8,9},{9,8},{10,11... | collective-permute-start | bytes 995336 | tf_op jit(solution)/shard_map/share_first/ppermute | solution.py:53
  123.6 3.0 %collective-permute-start.22 = (bf16[144,1152]{1,0:T(8,128)(2,1)S(1)}, bf16[144,1152]{1,0:T(8,128)(2,1)S(1)}, u32[]{:S(2)}, u32[]{:S(2)}) collective-permute-start(bf16[144,1152]{1,0:T(8,128)(2,1)S(1)} %collective-permute-done.15.refs_2_), channel_id=1, source_target_pairs={{0,1},{1,0},{2,3},{3,2},{4,5},{5,4},{6,7},{7,6},{8,9},{9,8},{10,11... | collective-permute-start | bytes 995336 | tf_op jit(solution)/shard_map/share_first/ppermute | solution.py:53
  125.3 2.6 %collective-permute-start.25 = (bf16[144,1152]{1,0:T(8,128)(2,1)S(1)}, bf16[144,1152]{1,0:T(8,128)(2,1)S(1)}, u32[]{:S(2)}, u32[]{:S(2)}) collective-permute-start(bf16[144,1152]{1,0:T(8,128)(2,1)S(1)} %get-tuple-element.60.refs_2_), channel_id=1, source_target_pairs={{0,1},{1,0},{2,3},{3,2},{4,5},{5,4},{6,7},{7,6},{8,9},{9,8},{10,11... | collective-permute-start | bytes 995336 | tf_op jit(solution)/shard_map/write/ppermute | solution.py:53
  125.4 2.5 %collective-permute-start.26 = (bf16[144,1152]{1,0:T(8,128)(2,1)S(1)}, bf16[144,1152]{1,0:T(8,128)(2,1)S(1)}, u32[]{:S(2)}, u32[]{:S(2)}) collective-permute-start(bf16[144,1152]{1,0:T(8,128)(2,1)S(1)} %get-tuple-element.61.refs_3_), channel_id=1, source_target_pairs={{0,1},{1,0},{2,3},{3,2},{4,5},{5,4},{6,7},{7,6},{8,9},{9,8},{10,11... | collective-permute-start | bytes 995336 | tf_op jit(solution)/shard_map/write/ppermute | solution.py:53

commit v9 on v8

--- a/solution.py
+++ b/solution.py
@@ -348,7 +348,7 @@
             scalars, (text_x, text_w, image_w), text_other, image_own, image_other
         )
     with jax.named_scope("swap_neighbours"):
-        below, above = after(image_inverse, below, above)
+        above, below = after(image_inverse, above, below)
         below_other = send(below, SWAP)
         above_other = send(above, SWAP)
     visits = call(pair_kernel, [pair_f32, pair, pair], flops=4 * 10**9)

time: 129 us -> 124 us (0.961)
  waiting for transfers between devices: 22.5 us -> 15.3 us
  blocking collectives: 42.5 us -> 45 us
    ppermute x27, waiting for transfers between devices: 22.5 us -> 15.3 us  [send(): return lax.ppermute(block, 'dp', pairs)]
    all_to_all x4, blocking collectives: 42.5 us -> 45 us  [exchange(): lax.all_to_all(parts, 'dp', 0, 0, axis_index_groups=members, tiled=True)]
  transfers between devices with their start and end apart: 27 -> 27, of which waited for: 8 -> 9; matrix products, arithmetic and copies ran while one was open for 0% -> 0% of each run, Pallas kernels for 10% -> 10%
where the time goes in v9:
time: 124 us
  blocking collectives  45 us (36%)
  starting transfers between devices  41 us (33%)
  Pallas kernels  20.2 us (16%)
  waiting for transfers between devices  15.3 us (12%)
  between operations  2.3 us (2%)
    all_to_all x4, blocking collectives, exchange(): lax.all_to_all(parts, 'dp', 0, 0, axis_index_groups=members, tiled=True)  45 us
    ppermute x27, starting transfers between devices, send(): return lax.ppermute(block, 'dp', pairs)  41 us
    pallas_call x13, Pallas kernels, run(): pl.pallas_call(body, out_shape=[jax.ShapeDtypeStruct(s, d) for s, d in ou...  20.2 us
    ppermute x27, waiting for transfers between devices, send(): return lax.ppermute(block, 'dp', pairs)  15.3 us
  transfers between devices with their start and end apart: 27, of which 9 were waited for; matrix products, arithmetic and copies ran while one was open for 0% of the time, Pallas kernels for 10%

profile of v9, /device:TPU:1, one launch (start us, length us, event | category | flops | bytes accessed | tf_op | source)
XLA Modules:
  0.0 124.1 jit_solution(6187364372326951041)
XLA Ops:
  0.6 1.0 band_exchange.1.image_own
  1.6 3.3 %collective-permute-start.4 = (bf16[144,1152]{1,0:T(8,128)(2,1)S(1)}, bf16[144,1152]{1,0:T(8,128)(2,1)S(1)}, u32[]{:S(2)}, u32[]{:S(2)}) collective-permute-start(bf16[144,1152]{1,0:T(8,128)(2,1)S(1)} %band_exchange.1.image_own), channel_id=1, source_target_pairs={{0,1},{1,0},{2,3},{3,2},{4,5},{5,4},{6,7},{7,6},{8,9},{9,8},{10,11... | collective-permute-start | bytes 995336 | tf_op jit(solution)/shard_map/band_exchange/ppermute | solution.py:53
  5.0 0.1 collective-permute-start.3
  5.1 0.0 collective-permute-start.2
  5.1 8.5 %collective-permute-start.1 = (bf16[128,1152]{1,0:T(8,128)(2,1)}, bf16[128,1152]{1,0:T(8,128)(2,1)S(1)}, u32[]{:S(2)}, u32[]{:S(2)}) collective-permute-start(bf16[128,1152]{1,0:T(8,128)(2,1)} %text_hbm.1), channel_id=1, source_target_pairs={{0,254},{1,255},{2,0},{3,1},{4,2},{5,3},{6,4},{7,5},{8,6},{9,7},{1... | collective-permute-start | bytes 884744 | tf_op jit(solution)/shard_map/band_exchange/ppermute | solution.py:53
  13.6 0.0 collective-permute-start
  14.9 0.0 collective-permute-done.3.text_other
  14.9 0.0 collective-permute-done.4.image_other
  14.9 5.0 %near.1 = (bf16[256,1152]{1,0:T(8,128)(2,1)S(1)}, bf16[1152,1152]{1,0:T(8,128)(2,1)S(1)}, bf16[256,1152]{1,0:T(8,128)(2,1)S(1)}, f32[256,1152]{1,0:T(8,128)S(1)}...) custom-call(f32[1]{0:T(128)S(6)} %copy.27.log_scale, ...), custom_call_target="tpu_custom_call" | custom-call | flops 4000000000 | tf_op jit(solution)/shard_map/near/pallas_call | solution.py:69
  19.9 0.9 collective-permute-done.2.refs_1_
  20.8 2.2 %collective-permute-done.1.refs_0_ = bf16[128,1152]{1,0:T(8,128)(2,1)S(1)} collective-permute-done((bf16[128,1152]{1,0:T(8,128)(2,1)}, bf16[128,1152]{1,0:T(8,128)(2,1)S(1)}, u32[]{:S(2)}, u32[]{:S(2)}) %collective-permute-start.1) | collective-permute-done | bytes 294944 | tf_op jit(solution)/shard_map/band_exchange/ppermute | solution.py:53
  23.0 1.2 %collective-permute-start.6 = (bf16[128,1152]{1,0:T(8,128)(2,1)S(1)}, bf16[128,1152]{1,0:T(8,128)(2,1)S(1)}, u32[]{:S(2)}, u32[]{:S(2)}) collective-permute-start(bf16[128,1152]{1,0:T(8,128)(2,1)S(1)} %get-tuple-element.34.below), channel_id=1, source_target_pairs={{0,1},{1,0},{2,3},{3,2},{4,5},{5,4},{6,7},{7,6},{8,9},{9,8},{10,11... | collective-permute-start | bytes 884744 | tf_op jit(solution)/shard_map/swap_neighbours/ppermute | solution.py:53
  24.2 0.0 collective-permute-start.7
  24.3 2.1 %received.2 = (f32[256,1152]{1,0:T(8,128)S(1)}, bf16[256,1152]{1,0:T(8,128)(2,1)S(1)}, bf16[256,1152]{1,0:T(8,128)(2,1)S(1)}) custom-call(f32[1]{0:T(128)S(6)} %copy.27.log_scale, f32[1]{0:T(128)S(6)} %copy.28.shift, bf16[128,1152]{1,0:T(8,128)(2,1)S(1)} %get-tuple-element.34.below, bf16[128,1152]{1,0:T(8,128)(2,1)S(1)} %get-tuple-element.35.above, ...), custom_call_target="tpu_custom_call" | custom-call | flops 4000000000 | tf_op jit(solution)/shard_map/received/pallas_call | solution.py:69
  26.3 0.0 collective-permute-done.refs_0_
  26.4 1.0 collective-permute-start.5
  27.4 0.0 collective-permute-done.6.below
  27.4 0.0 collective-permute-done.7.above
  27.4 2.3 %partners.1 = (f32[256,1152]{1,0:T(8,128)S(1)}, bf16[256,1152]{1,0:T(8,128)(2,1)S(1)}, bf16[256,1152]{1,0:T(8,128)(2,1)S(1)}) custom-call(f32[1]{0:T(128)S(6)} %copy.27.log_scale, f32[1]{0:T(128)S(6)} %copy.28.shift, bf16[128,1152]{1,0:T(8,128)(2,1)S(1)} %collective-permute-done.6.below, bf16[128,1152]{1,0:T(8,128)(2,1)S(1)} %collective-permute-done.7.above, ...), custom_call_target="tpu_custom_call" | custom-call | flops 4000000000 | tf_op jit(solution)/shard_map/partners/pallas_call | solution.py:69
  29.7 0.0 collective-permute-done.5.far_other
  29.7 5.6 %far.1 = (bf16[288,1152]{1,0:T(8,128)(2,1)S(1)}, bf16[144,1152]{1,0:T(8,128)(2,1)S(1)}, bf16[144,1152]{1,0:T(8,128)(2,1)S(1)}, bf16[144,1152]{1,0:T(8,128)(2,1)S...) custom-call(f32[1]{0:T(128)S(6)} %copy.27.log_scale, ...), custom_call_target="tpu_custom_call" | custom-call | flops 4000000000 | tf_op jit(solution)/shard_map/far/pallas_call | solution.py:69
  35.3 0.1 collective-permute-start.8
  35.4 2.7 %collective-permute-start.9 = (bf16[144,1152]{1,0:T(8,128)(2,1)S(1)}, bf16[144,1152]{1,0:T(8,128)(2,1)S(1)}, u32[]{:S(2)}, u32[]{:S(2)}) collective-permute-start(bf16[144,1152]{1,0:T(8,128)(2,1)S(1)} %get-tuple-element.53), channel_id=1, source_target_pairs={{0,48},{1,193},{2,50},{3,195},{4,52},{5,197},{6,54},{7,199},{8,56}... | collective-permute-start | bytes 995336 | tf_op jit(solution)/shard_map/sum_first/ppermute | solution.py:53
  38.1 0.0 collective-permute-start.11
  38.1 2.7 %collective-permute-start.12 = (bf16[144,1152]{1,0:T(8,128)(2,1)S(1)}, bf16[144,1152]{1,0:T(8,128)(2,1)S(1)}, u32[]{:S(2)}, u32[]{:S(2)}) collective-permute-start(bf16[144,1152]{1,0:T(8,128)(2,1)S(1)} %get-tuple-element.56), channel_id=1, source_target_pairs={{0,48},{1,193},{2,50},{3,195},{4,52},{5,197},{6,54},{7,199},{8,56}... | collective-permute-start | bytes 995336 | tf_op jit(solution)/shard_map/sum_first/ppermute | solution.py:53
  40.8 2.1 %collective-permute-done.8.b = bf16[144,1152]{1,0:T(8,128)(2,1)S(1)} collective-permute-done((bf16[144,1152]{1,0:T(8,128)(2,1)S(1)}, bf16[144,1152]{1,0:T(8,128)(2,1)S(1)}, u32[]{:S(2)}, u32[]{:S(2)}) %collective-permute-start.8) | collective-permute-done | bytes 331808 | tf_op jit(solution)/shard_map/sum_first/ppermute | solution.py:53
  42.9 0.0 collective-permute-done.9.d
  42.9 0.2 sum_first.2
  43.1 0.1 collective-permute-start.10
  43.2 2.7 %collective-permute-start.13 = (bf16[144,1152]{1,0:T(8,128)(2,1)S(1)}, bf16[144,1152]{1,0:T(8,128)(2,1)S(1)}, u32[]{:S(2)}, u32[]{:S(2)}) collective-permute-start(bf16[144,1152]{1,0:T(8,128)(2,1)S(1)} %get-tuple-element.57), channel_id=1, source_target_pairs={{0,48},{1,193},{2,50},{3,195},{4,52},{5,197},{6,54},{7,199},{8,56}... | collective-permute-start | bytes 995336 | tf_op jit(solution)/shard_map/sum_first/ppermute | solution.py:53
  45.8 0.6 collective-permute-done.11.a_bottom
  46.5 0.0 collective-permute-done.12.b_top
  46.5 3.9 %collective-permute-done.10.a_top = bf16[144,1152]{1,0:T(8,128)(2,1)S(1)} collective-permute-done((bf16[144,1152]{1,0:T(8,128)(2,1)S(1)}, bf16[144,1152]{1,0:T(8,128)(2,1)S(1)}, u32[]{:S(2)}, u32[]{:S(2)}) %collective-permute-start.10) | collective-permute-done | bytes 331808 | tf_op jit(solution)/shard_map/sum_first/ppermute | solution.py:53
  50.3 0.3 sum_first.3
  50.6 10.2 %all_to_all.20 = bf16[4,72,1152]{2,1,0:T(8,128)(2,1)S(1)} all-to-all(bf16[4,72,1152]{2,1,0:T(8,128)(2,1)S(1)} %bitcast.18), channel_id=1, replica_groups={{0,64,128,192},{1,17,33,49},{2,66,130,194},{3,19,35,51},{4,68,132,196},..., dimensions={0} | all-to-all | bytes 1327104 | tf_op jit(solution)/shard_map/sum_second/all_to_all | solution.py:57
  60.8 0.1 reduce_sum.24
  60.9 13.9 %all_to_all.21 = bf16[88,8,128]{2,1,0:T(8,128)(2,1)S(1)} all-to-all(bf16[88,8,128]{2,1,0:T(8,128)(2,1)S(1)} %concatenate.3), channel_id=1, replica_groups={{0,2,4,6,8,10,12,14},{1,3,5,7,9,11,13,15},{16,18,20,22,24,26,28,30},{17..., dimensions={0} | all-to-all | bytes 360448 | tf_op jit(solution)/shard_map/sum_lines/all_to_all | solution.py:57
  74.9 10.8 %all_to_all.22 = bf16[88,8,128]{2,1,0:T(8,128)(2,1)S(1)} all-to-all(bf16[88,8,128]{2,1,0:T(8,128)(2,1)S(1)} %bitcast.20), channel_id=1, replica_groups={{0,2,4,6,8,10,12,14},{1,3,5,7,9,11,13,15},{16,18,20,22,24,26,28,30},{17..., dimensions={0} | all-to-all | bytes 360448 | tf_op jit(solution)/shard_map/share_lines/all_to_all | solution.py:57
  85.8 10.1 %all_to_all.23 = bf16[4,72,1152]{2,1,0:T(8,128)(2,1)S(1)} all-to-all(bf16[4,72,1152]{2,1,0:T(8,128)(2,1)S(1)} %tile.20), channel_id=1, replica_groups={{0,64,128,192},{1,17,33,49},{2,66,130,194},{3,19,35,51},{4,68,132,196},..., dimensions={0} | all-to-all | bytes 1327104 | tf_op jit(solution)/shard_map/share_second/all_to_all | solution.py:57
  95.9 7.7 %collective-permute-start.18 = (bf16[288,1152]{1,0:T(8,128)(2,1)S(1)}, bf16[288,1152]{1,0:T(8,128)(2,1)S(1)}, u32[]{:S(2)}, u32[]{:S(2)}) collective-permute-start(bf16[288,1152]{1,0:T(8,128)(2,1)S(1)} %bitcast.16), channel_id=1, source_target_pairs={{0,1},{1,0},{2,3},{3,2},{4,5},{5,4},{6,7},{7,6},{8,9},{9,8},{10,11... | collective-permute-start | bytes 1990664 | tf_op jit(solution)/shard_map/share_first/ppermute | solution.py:53
  103.6 0.1 fusion
  103.7 0.4 collective-permute-start.14
  104.0 2.4 %collective-permute-start.15 = (bf16[144,1152]{1,0:T(8,128)(2,1)S(1)}, bf16[144,1152]{1,0:T(8,128)(2,1)S(1)}, u32[]{:S(2)}, u32[]{:S(2)}) collective-permute-start(bf16[144,1152]{1,0:T(8,128)(2,1)S(1)} %bitcast.23), channel_id=1, source_target_pairs={{0,48},{1,193},{2,50},{3,195},{4,52},{5,197},{6,54},{7,199},{8,56}... | collective-permute-start | bytes 995336 | tf_op jit(solution)/shard_map/share_first/ppermute | solution.py:53
  106.4 0.0 collective-permute-start.17
  106.4 1.4 %collective-permute-start.16 = (bf16[144,1152]{1,0:T(8,128)(2,1)S(1)}, bf16[144,1152]{1,0:T(8,128)(2,1)S(1)}, u32[]{:S(2)}, u32[]{:S(2)}) collective-permute-start(bf16[144,1152]{1,0:T(8,128)(2,1)S(1)} %bitcast.24), channel_id=1, source_target_pairs={{0,16},{1,65},{2,18},{3,67},{4,20},{5,69},{6,22},{7,71},{8,24},{9,... | collective-permute-start | bytes 995336 | tf_op jit(solution)/shard_map/share_first/ppermute | solution.py:53
  107.9 3.3 %collective-permute-done.14.refs_1_ = bf16[144,1152]{1,0:T(8,128)(2,1)S(1)} collective-permute-done((bf16[144,1152]{1,0:T(8,128)(2,1)S(1)}, bf16[144,1152]{1,0:T(8,128)(2,1)S(1)}, u32[]{:S(2)}, u32[]{:S(2)}) %collective-permute-start.14) | collective-permute-done | bytes 331808 | tf_op jit(solution)/shard_map/share_first/ppermute | solution.py:53
  111.2 0.0 collective-permute-start.19
  111.2 2.7 %collective-permute-start.20 = (bf16[144,1152]{1,0:T(8,128)(2,1)S(1)}, bf16[144,1152]{1,0:T(8,128)(2,1)S(1)}, u32[]{:S(2)}, u32[]{:S(2)}) collective-permute-start(bf16[144,1152]{1,0:T(8,128)(2,1)S(1)} %collective-permute-done.15.refs_2_), channel_id=1, source_target_pairs={{0,48},{1,193},{2,50},{3,195},{4,52},{5,197},{6,54},{7,199},{8,56}... | collective-permute-start | bytes 995336 | tf_op jit(solution)/shard_map/share_first/ppermute | solution.py:53
  113.9 0.1 collective-permute-done.17.refs_4_
  114.0 1.3 %collective-permute-start.24 = (bf16[144,1152]{1,0:T(8,128)(2,1)S(1)}, bf16[144,1152]{1,0:T(8,128)(2,1)S(1)}, u32[]{:S(2)}, u32[]{:S(2)}) collective-permute-start(bf16[144,1152]{1,0:T(8,128)(2,1)S(1)} %collective-permute-done.17.refs_4_), channel_id=1, source_target_pairs={{0,1},{1,0},{2,3},{3,2},{4,5},{5,4},{6,7},{7,6},{8,9},{9,8},{10,11... | collective-permute-start | bytes 995336 | tf_op jit(solution)/shard_map/share_first/ppermute | solution.py:53
  115.3 0.0 collective-permute-done.16.refs_3_
  115.3 0.3 collective-permute-start.21
  115.6 0.0 collective-permute-done.18.refs_5_
  115.6 0.2 collective-permute-start.23
  115.8 1.5 %write.4 = (bf16[1152,1152]{1,0:T(8,128)(2,1)}, bf16[1152,1152]{1,0:T(8,128)(2,1)}) custom-call(bf16[288,1152]{1,0:T(8,128)(2,1)S(1)} %bitcast.17, bf16[144,1152]{1,0:T(8,128)(2,1)S(1)} %collective-permute-done.14.refs_1_, bf16[144,1152]{1,0:T(8,128)(2,1)S(1)} %collective-permute-done.15.refs_2_, bf16[144,1152]{1,0:T(8,128)(2,1)S(1)} %collective-permute-done.16.refs_3_, ...), custom_call_target="tpu_custom_call" | custom-call | tf_op jit(solution)/shard_map/write/pallas_call | solution.py:69
  117.4 1.3 %collective-permute-done.19.refs_1_ = bf16[144,1152]{1,0:T(8,128)(2,1)S(1)} collective-permute-done((bf16[144,1152]{1,0:T(8,128)(2,1)S(1)}, bf16[144,1152]{1,0:T(8,128)(2,1)S(1)}, u32[]{:S(2)}, u32[]{:S(2)}) %collective-permute-start.19) | collective-permute-done | bytes 331808 | tf_op jit(solution)/shard_map/share_first/ppermute | solution.py:53
  118.7 1.7 %collective-permute-start.22 = (bf16[144,1152]{1,0:T(8,128)(2,1)S(1)}, bf16[144,1152]{1,0:T(8,128)(2,1)S(1)}, u32[]{:S(2)}, u32[]{:S(2)}) collective-permute-start(bf16[144,1152]{1,0:T(8,128)(2,1)S(1)} %collective-permute-done.15.refs_2_), channel_id=1, source_target_pairs={{0,1},{1,0},{2,3},{3,2},{4,5},{5,4},{6,7},{7,6},{8,9},{9,8},{10,11... | collective-permute-start | bytes 995336 | tf_op jit(solution)/shard_map/share_first/ppermute | solution.py:53
  120.4 0.0 collective-permute-done.20.refs_2_
  120.4 0.1 collective-permute-start.25
  120.5 0.4 collective-permute-start.26
  120.9 0.7 collective-permute-done.22.refs_5_
  121.7 1.3 %write.6 = (bf16[1152,1152]{1,0:T(8,128)(2,1)}, bf16[1152,1152]{1,0:T(8,128)(2,1)}) custom-call(bf16[1152,1152]{1,0:T(8,128)(2,1)} %get-tuple-element.58.refs_0_, bf16[1152,1152]{1,0:T(8,128)(2,1)} %get-tuple-element.59.refs_1_, bf16[144,1152]{1,0:T(8,128)(2,1)S(1)} %get-tuple-element.60.refs_2_, ...), custom_call_target="tpu_custom_call", output_to_operand_aliasing={{0}: (0, {}), {1}: (1, {})} | custom-call | tf_op jit(solution)/shard_map/write/pallas_call | solution.py:69
  123.0 0.0 collective-permute-done.25.refs_2_
  123.0 0.9 write.7
  (14 shorter events, 0.2 us)
Async XLA Ops:
  1.6 13.2 %collective-permute-start.4 = (bf16[144,1152]{1,0:T(8,128)(2,1)S(1)}, bf16[144,1152]{1,0:T(8,128)(2,1)S(1)}, u32[]{:S(2)}, u32[]{:S(2)}) collective-permute-start(bf16[144,1152]{1,0:T(8,128)(2,1)S(1)} %band_exchange.1.image_own), channel_id=1, source_target_pairs={{0,1},{1,0},{2,3},{3,2},{4,5},{5,4},{6,7},{7,6},{8,9},{9,8},{10,11... | collective-permute-start | bytes 995336 | tf_op jit(solution)/shard_map/band_exchange/ppermute | solution.py:53
  5.0 9.9 %collective-permute-start.3 = (bf16[128,1152]{1,0:T(8,128)(2,1)}, bf16[128,1152]{1,0:T(8,128)(2,1)S(1)}, u32[]{:S(2)}, u32[]{:S(2)}) collective-permute-start(bf16[128,1152]{1,0:T(8,128)(2,1)} %text_hbm.1), channel_id=1, source_target_pairs={{0,1},{1,0},{2,3},{3,2},{4,5},{5,4},{6,7},{7,6},{8,9},{9,8},{10,11... | collective-permute-start | bytes 884744 | tf_op jit(solution)/shard_map/band_exchange/ppermute | solution.py:53
  5.1 15.7 %collective-permute-start.2 = (bf16[128,1152]{1,0:T(8,128)(2,1)}, bf16[128,1152]{1,0:T(8,128)(2,1)S(1)}, u32[]{:S(2)}, u32[]{:S(2)}) collective-permute-start(bf16[128,1152]{1,0:T(8,128)(2,1)} %text_hbm.1), channel_id=1, source_target_pairs={{0,2},{1,3},{2,4},{3,5},{4,6},{5,7},{6,8},{7,9},{8,10},{9,11},{10,... | collective-permute-start | bytes 884744 | tf_op jit(solution)/shard_map/band_exchange/ppermute | solution.py:53
  5.1 17.9 %collective-permute-start.1 = (bf16[128,1152]{1,0:T(8,128)(2,1)}, bf16[128,1152]{1,0:T(8,128)(2,1)S(1)}, u32[]{:S(2)}, u32[]{:S(2)}) collective-permute-start(bf16[128,1152]{1,0:T(8,128)(2,1)} %text_hbm.1), channel_id=1, source_target_pairs={{0,254},{1,255},{2,0},{3,1},{4,2},{5,3},{6,4},{7,5},{8,6},{9,7},{1... | collective-permute-start | bytes 884744 | tf_op jit(solution)/shard_map/band_exchange/ppermute | solution.py:53
  13.6 12.8 %collective-permute-start = (bf16[128,1152]{1,0:T(8,128)(2,1)}, bf16[128,1152]{1,0:T(8,128)(2,1)S(1)}, u32[]{:S(2)}, u32[]{:S(2)}) collective-permute-start(bf16[128,1152]{1,0:T(8,128)(2,1)} %text_hbm.1), channel_id=1, source_target_pairs={{0,253},{1,4},{2,255},{3,6},{4,1},{5,8},{6,3},{7,10},{8,5},{9,12},... | collective-permute-start | bytes 884744 | tf_op jit(solution)/shard_map/band_exchange/ppermute | solution.py:53
  23.0 4.4 %collective-permute-start.6 = (bf16[128,1152]{1,0:T(8,128)(2,1)S(1)}, bf16[128,1152]{1,0:T(8,128)(2,1)S(1)}, u32[]{:S(2)}, u32[]{:S(2)}) collective-permute-start(bf16[128,1152]{1,0:T(8,128)(2,1)S(1)} %get-tuple-element.34.below), channel_id=1, source_target_pairs={{0,1},{1,0},{2,3},{3,2},{4,5},{5,4},{6,7},{7,6},{8,9},{9,8},{10,11... | collective-permute-start | bytes 884744 | tf_op jit(solution)/shard_map/swap_neighbours/ppermute | solution.py:53
  24.2 3.2 %collective-permute-start.7 = (bf16[128,1152]{1,0:T(8,128)(2,1)S(1)}, bf16[128,1152]{1,0:T(8,128)(2,1)S(1)}, u32[]{:S(2)}, u32[]{:S(2)}) collective-permute-start(bf16[128,1152]{1,0:T(8,128)(2,1)S(1)} %get-tuple-element.35.above), channel_id=1, source_target_pairs={{0,1},{1,0},{2,3},{3,2},{4,5},{5,4},{6,7},{7,6},{8,9},{9,8},{10,11... | collective-permute-start | bytes 884744 | tf_op jit(solution)/shard_map/swap_neighbours/ppermute | solution.py:53
  26.4 3.3 %collective-permute-start.5 = (bf16[128,1152]{1,0:T(8,128)(2,1)S(1)}, bf16[128,1152]{1,0:T(8,128)(2,1)S(1)}, u32[]{:S(2)}, u32[]{:S(2)}) collective-permute-start(bf16[128,1152]{1,0:T(8,128)(2,1)S(1)} %received.3.far), channel_id=1, source_target_pairs={{0,1},{1,0},{2,3},{3,2},{4,5},{5,4},{6,7},{7,6},{8,9},{9,8},{10,11... | collective-permute-start | bytes 884744 | tf_op jit(solution)/shard_map/received/ppermute | solution.py:53
  35.3 7.6 %collective-permute-start.8 = (bf16[144,1152]{1,0:T(8,128)(2,1)S(1)}, bf16[144,1152]{1,0:T(8,128)(2,1)S(1)}, u32[]{:S(2)}, u32[]{:S(2)}) collective-permute-start(bf16[144,1152]{1,0:T(8,128)(2,1)S(1)} %get-tuple-element.51), channel_id=1, source_target_pairs={{0,16},{1,65},{2,18},{3,67},{4,20},{5,69},{6,22},{7,71},{8,24},{9,... | collective-permute-start | bytes 995336 | tf_op jit(solution)/shard_map/sum_first/ppermute | solution.py:53
  35.4 7.5 %collective-permute-start.9 = (bf16[144,1152]{1,0:T(8,128)(2,1)S(1)}, bf16[144,1152]{1,0:T(8,128)(2,1)S(1)}, u32[]{:S(2)}, u32[]{:S(2)}) collective-permute-start(bf16[144,1152]{1,0:T(8,128)(2,1)S(1)} %get-tuple-element.53), channel_id=1, source_target_pairs={{0,48},{1,193},{2,50},{3,195},{4,52},{5,197},{6,54},{7,199},{8,56}... | collective-permute-start | bytes 995336 | tf_op jit(solution)/shard_map/sum_first/ppermute | solution.py:53
  38.1 8.4 %collective-permute-start.11 = (bf16[144,1152]{1,0:T(8,128)(2,1)S(1)}, bf16[144,1152]{1,0:T(8,128)(2,1)S(1)}, u32[]{:S(2)}, u32[]{:S(2)}) collective-permute-start(bf16[144,1152]{1,0:T(8,128)(2,1)S(1)} %get-tuple-element.55), channel_id=1, source_target_pairs={{0,16},{1,65},{2,18},{3,67},{4,20},{5,69},{6,22},{7,71},{8,24},{9,... | collective-permute-start | bytes 995336 | tf_op jit(solution)/shard_map/sum_first/ppermute | solution.py:53
  38.1 8.4 %collective-permute-start.12 = (bf16[144,1152]{1,0:T(8,128)(2,1)S(1)}, bf16[144,1152]{1,0:T(8,128)(2,1)S(1)}, u32[]{:S(2)}, u32[]{:S(2)}) collective-permute-start(bf16[144,1152]{1,0:T(8,128)(2,1)S(1)} %get-tuple-element.56), channel_id=1, source_target_pairs={{0,48},{1,193},{2,50},{3,195},{4,52},{5,197},{6,54},{7,199},{8,56}... | collective-permute-start | bytes 995336 | tf_op jit(solution)/shard_map/sum_first/ppermute | solution.py:53
  43.1 7.3 %collective-permute-start.10 = (bf16[144,1152]{1,0:T(8,128)(2,1)S(1)}, bf16[144,1152]{1,0:T(8,128)(2,1)S(1)}, u32[]{:S(2)}, u32[]{:S(2)}) collective-permute-start(bf16[144,1152]{1,0:T(8,128)(2,1)S(1)} %get-tuple-element.54), channel_id=1, source_target_pairs={{0,16},{1,65},{2,18},{3,67},{4,20},{5,69},{6,22},{7,71},{8,24},{9,... | collective-permute-start | bytes 995336 | tf_op jit(solution)/shard_map/sum_first/ppermute | solution.py:53
  43.2 7.2 %collective-permute-start.13 = (bf16[144,1152]{1,0:T(8,128)(2,1)S(1)}, bf16[144,1152]{1,0:T(8,128)(2,1)S(1)}, u32[]{:S(2)}, u32[]{:S(2)}) collective-permute-start(bf16[144,1152]{1,0:T(8,128)(2,1)S(1)} %get-tuple-element.57), channel_id=1, source_target_pairs={{0,48},{1,193},{2,50},{3,195},{4,52},{5,197},{6,54},{7,199},{8,56}... | collective-permute-start | bytes 995336 | tf_op jit(solution)/shard_map/sum_first/ppermute | solution.py:53
  95.9 19.8 %collective-permute-start.18 = (bf16[288,1152]{1,0:T(8,128)(2,1)S(1)}, bf16[288,1152]{1,0:T(8,128)(2,1)S(1)}, u32[]{:S(2)}, u32[]{:S(2)}) collective-permute-start(bf16[288,1152]{1,0:T(8,128)(2,1)S(1)} %bitcast.16), channel_id=1, source_target_pairs={{0,1},{1,0},{2,3},{3,2},{4,5},{5,4},{6,7},{7,6},{8,9},{9,8},{10,11... | collective-permute-start | bytes 1990664 | tf_op jit(solution)/shard_map/share_first/ppermute | solution.py:53
  103.7 7.6 %collective-permute-start.14 = (bf16[144,1152]{1,0:T(8,128)(2,1)S(1)}, bf16[144,1152]{1,0:T(8,128)(2,1)S(1)}, u32[]{:S(2)}, u32[]{:S(2)}) collective-permute-start(bf16[144,1152]{1,0:T(8,128)(2,1)S(1)} %bitcast.25), channel_id=1, source_target_pairs={{0,16},{1,65},{2,18},{3,67},{4,20},{5,69},{6,22},{7,71},{8,24},{9,... | collective-permute-start | bytes 995336 | tf_op jit(solution)/shard_map/share_first/ppermute | solution.py:53
  104.0 7.2 %collective-permute-start.15 = (bf16[144,1152]{1,0:T(8,128)(2,1)S(1)}, bf16[144,1152]{1,0:T(8,128)(2,1)S(1)}, u32[]{:S(2)}, u32[]{:S(2)}) collective-permute-start(bf16[144,1152]{1,0:T(8,128)(2,1)S(1)} %bitcast.23), channel_id=1, source_target_pairs={{0,48},{1,193},{2,50},{3,195},{4,52},{5,197},{6,54},{7,199},{8,56}... | collective-permute-start | bytes 995336 | tf_op jit(solution)/shard_map/share_first/ppermute | solution.py:53
  106.4 7.6 %collective-permute-start.17 = (bf16[144,1152]{1,0:T(8,128)(2,1)S(1)}, bf16[144,1152]{1,0:T(8,128)(2,1)S(1)}, u32[]{:S(2)}, u32[]{:S(2)}) collective-permute-start(bf16[144,1152]{1,0:T(8,128)(2,1)S(1)} %bitcast.26), channel_id=1, source_target_pairs={{0,48},{1,193},{2,50},{3,195},{4,52},{5,197},{6,54},{7,199},{8,56}... | collective-permute-start | bytes 995336 | tf_op jit(solution)/shard_map/share_first/ppermute | solution.py:53
  106.4 8.9 %collective-permute-start.16 = (bf16[144,1152]{1,0:T(8,128)(2,1)S(1)}, bf16[144,1152]{1,0:T(8,128)(2,1)S(1)}, u32[]{:S(2)}, u32[]{:S(2)}) collective-permute-start(bf16[144,1152]{1,0:T(8,128)(2,1)S(1)} %bitcast.24), channel_id=1, source_target_pairs={{0,16},{1,65},{2,18},{3,67},{4,20},{5,69},{6,22},{7,71},{8,24},{9,... | collective-permute-start | bytes 995336 | tf_op jit(solution)/shard_map/share_first/ppermute | solution.py:53
  111.2 7.5 %collective-permute-start.19 = (bf16[144,1152]{1,0:T(8,128)(2,1)S(1)}, bf16[144,1152]{1,0:T(8,128)(2,1)S(1)}, u32[]{:S(2)}, u32[]{:S(2)}) collective-permute-start(bf16[144,1152]{1,0:T(8,128)(2,1)S(1)} %collective-permute-done.14.refs_1_), channel_id=1, source_target_pairs={{0,16},{1,65},{2,18},{3,67},{4,20},{5,69},{6,22},{7,71},{8,24},{9,... | collective-permute-start | bytes 995336 | tf_op jit(solution)/shard_map/share_first/ppermute | solution.py:53
  111.2 9.2 %collective-permute-start.20 = (bf16[144,1152]{1,0:T(8,128)(2,1)S(1)}, bf16[144,1152]{1,0:T(8,128)(2,1)S(1)}, u32[]{:S(2)}, u32[]{:S(2)}) collective-permute-start(bf16[144,1152]{1,0:T(8,128)(2,1)S(1)} %collective-permute-done.15.refs_2_), channel_id=1, source_target_pairs={{0,48},{1,193},{2,50},{3,195},{4,52},{5,197},{6,54},{7,199},{8,56}... | collective-permute-start | bytes 995336 | tf_op jit(solution)/shard_map/share_first/ppermute | solution.py:53
  114.0 6.5 %collective-permute-start.24 = (bf16[144,1152]{1,0:T(8,128)(2,1)S(1)}, bf16[144,1152]{1,0:T(8,128)(2,1)S(1)}, u32[]{:S(2)}, u32[]{:S(2)}) collective-permute-start(bf16[144,1152]{1,0:T(8,128)(2,1)S(1)} %collective-permute-done.17.refs_4_), channel_id=1, source_target_pairs={{0,1},{1,0},{2,3},{3,2},{4,5},{5,4},{6,7},{7,6},{8,9},{9,8},{10,11... | collective-permute-start | bytes 995336 | tf_op jit(solution)/shard_map/share_first/ppermute | solution.py:53
  115.3 5.6 %collective-permute-start.21 = (bf16[144,1152]{1,0:T(8,128)(2,1)S(1)}, bf16[144,1152]{1,0:T(8,128)(2,1)S(1)}, u32[]{:S(2)}, u32[]{:S(2)}) collective-permute-start(bf16[144,1152]{1,0:T(8,128)(2,1)S(1)} %collective-permute-done.14.refs_1_), channel_id=1, source_target_pairs={{0,1},{1,0},{2,3},{3,2},{4,5},{5,4},{6,7},{7,6},{8,9},{9,8},{10,11... | collective-permute-start | bytes 995336 | tf_op jit(solution)/shard_map/share_first/ppermute | solution.py:53
  115.6 5.3 %collective-permute-start.23 = (bf16[144,1152]{1,0:T(8,128)(2,1)S(1)}, bf16[144,1152]{1,0:T(8,128)(2,1)S(1)}, u32[]{:S(2)}, u32[]{:S(2)}) collective-permute-start(bf16[144,1152]{1,0:T(8,128)(2,1)S(1)} %collective-permute-done.16.refs_3_), channel_id=1, source_target_pairs={{0,1},{1,0},{2,3},{3,2},{4,5},{5,4},{6,7},{7,6},{8,9},{9,8},{10,11... | collective-permute-start | bytes 995336 | tf_op jit(solution)/shard_map/share_first/ppermute | solution.py:53
  118.7 3.0 %collective-permute-start.22 = (bf16[144,1152]{1,0:T(8,128)(2,1)S(1)}, bf16[144,1152]{1,0:T(8,128)(2,1)S(1)}, u32[]{:S(2)}, u32[]{:S(2)}) collective-permute-start(bf16[144,1152]{1,0:T(8,128)(2,1)S(1)} %collective-permute-done.15.refs_2_), channel_id=1, source_target_pairs={{0,1},{1,0},{2,3},{3,2},{4,5},{5,4},{6,7},{7,6},{8,9},{9,8},{10,11... | collective-permute-start | bytes 995336 | tf_op jit(solution)/shard_map/share_first/ppermute | solution.py:53
  120.4 2.6 %collective-permute-start.25 = (bf16[144,1152]{1,0:T(8,128)(2,1)S(1)}, bf16[144,1152]{1,0:T(8,128)(2,1)S(1)}, u32[]{:S(2)}, u32[]{:S(2)}) collective-permute-start(bf16[144,1152]{1,0:T(8,128)(2,1)S(1)} %get-tuple-element.60.refs_2_), channel_id=1, source_target_pairs={{0,1},{1,0},{2,3},{3,2},{4,5},{5,4},{6,7},{7,6},{8,9},{9,8},{10,11... | collective-permute-start | bytes 995336 | tf_op jit(solution)/shard_map/write/ppermute | solution.py:53
  120.5 2.5 %collective-permute-start.26 = (bf16[144,1152]{1,0:T(8,128)(2,1)S(1)}, bf16[144,1152]{1,0:T(8,128)(2,1)S(1)}, u32[]{:S(2)}, u32[]{:S(2)}) collective-permute-start(bf16[144,1152]{1,0:T(8,128)(2,1)S(1)} %get-tuple-element.61.refs_3_), channel_id=1, source_target_pairs={{0,1},{1,0},{2,3},{3,2},{4,5},{5,4},{6,7},{7,6},{8,9},{9,8},{10,11... | collective-permute-start | bytes 995336 | tf_op jit(solution)/shard_map/write/ppermute | solution.py:53

commit v10 on v9

--- a/solution.py
+++ b/solution.py
@@ -107,11 +107,12 @@
     return projected, inverse
 
 
-def make_head(head, pairs):
+def make_head(head, pairs, before=None):
     step = 128
     for k in range(head.shape[0] // step):
         at = pl.ds(k * step, step)
-        head[at, :] = sum(contract(x[:, at], back[...], 0, 0) for x, back in pairs)
+        new = sum(contract(x[:, at], back[...], 0, 0) for x, back in pairs)
+        head[at, :] = new if before is None else before[at, :] + new
 
 
 def join_positions(image_hbm, position_hbm, out, position, sems):
@@ -207,9 +208,20 @@
     visit(log_scale, shift, x, text_w, image_emb, lambda c: c, back, grad, grad_before)
 
 
+def received_kernel(
+    log_scale, shift, below, above, text_w, image_emb, grad_before, x_1, back_1,
+    grad, head, x, back,
+):
+    pair_kernel(log_scale, shift, below, above, text_w, image_emb, grad_before, grad, x, back)
+
+    @pl.when(on_text())
+    def _():
+        make_head(head, [(x_1, back_1), (x, back)])
+
+
 def far_kernel(
     log_scale, shift, far, far_other, text_w, image_emb, grad_before,
-    image_near, image_projected, image_inverse, x_1, back_1, x_2, back_2, x_3, back_3,
+    image_near, image_projected, image_inverse, head_before, x_1, back_1,
     own, right_top, right_bottom, left_top, left_bottom, far_right, far_left,
     grad, head, x, back,
 ):
@@ -226,7 +238,7 @@
 
     @pl.when(on_text())
     def _():
-        make_head(head, [(x_1, back_1), (x_2, back_2), (x_3, back_3), (x, back)])
+        make_head(head, [(x_1, back_1), (x, back)], head_before)
 
     @pl.when(jnp.logical_not(on_text()))
     def _():
@@ -351,13 +363,19 @@
         above, below = after(image_inverse, above, below)
         below_other = send(below, SWAP)
         above_other = send(above, SWAP)
-    visits = call(pair_kernel, [pair_f32, pair, pair], flops=4 * 10**9)
     with jax.named_scope("received"):
-        grad, *first = visits(scalars, (), below, above, weight, image_emb, grad)
+        grad, head = call(
+            received_kernel,
+            [pair_f32, total],
+            [pltpu.VMEM(*pair), pltpu.VMEM(*pair)],
+            flops=4 * 10**9,
+        )(scalars, (), below, above, weight, image_emb, grad, *near)
         [far] = after(grad, far)
         far_other = send(far, SWAP)
     with jax.named_scope("partners"):
-        grad, *second = visits(scalars, (), below_other, above_other, weight, image_emb, grad)
+        grad, *second = call(pair_kernel, [pair_f32, pair, pair], flops=4 * 10**9)(
+            scalars, (), below_other, above_other, weight, image_emb, grad
+        )
     with jax.named_scope("far"):
         own, right_top, right_bottom, left_top, left_bottom, far_right, far_left = call(
             far_kernel,
@@ -366,7 +384,7 @@
             flops=4 * 10**9,
         )(
             scalars, (), far, far_other, weight, image_emb, grad, image_near, image_projected,
-            image_inverse, *near, *first, *second,
+            image_inverse, head, *second,
         )
     with jax.named_scope("sum_first"):
         from_left = send(far_right, RIGHT)

time: 124 us -> 123 us (level)
  transfers between devices with their start and end apart: 27 -> 27, of which waited for: 9 -> 9; matrix products, arithmetic and copies ran while one was open for 0% -> 0% of each run, Pallas kernels for 10% -> 11%
where the time goes in v10:
time: 123 us
  blocking collectives  45.3 us (37%)
  starting transfers between devices  40.5 us (33%)
  Pallas kernels  20.4 us (17%)
  waiting for transfers between devices  14.3 us (12%)
  between operations  2.33 us (2%)
    all_to_all x4, blocking collectives, exchange(): lax.all_to_all(parts, 'dp', 0, 0, axis_index_groups=members, tiled=True)  45.3 us
    ppermute x27, starting transfers between devices, send(): return lax.ppermute(block, 'dp', pairs)  40.5 us
    pallas_call x13, Pallas kernels, run(): pl.pallas_call(body, out_shape=[jax.ShapeDtypeStruct(s, d) for s, d in ou...  20.4 us
    ppermute x27, waiting for transfers between devices, send(): return lax.ppermute(block, 'dp', pairs)  14.3 us
  transfers between devices with their start and end apart: 27, of which 9 were waited for; matrix products, arithmetic and copies ran while one was open for 0% of the time, Pallas kernels for 11%

profile of v10, /device:TPU:1, one launch (start us, length us, event | category | flops | bytes accessed | tf_op | source)
XLA Modules:
  0.0 123.1 jit_solution(11395707036423581396)
XLA Ops:
  0.6 1.0 band_exchange.1.image_own
  1.6 3.3 %collective-permute-start.4 = (bf16[144,1152]{1,0:T(8,128)(2,1)S(1)}, bf16[144,1152]{1,0:T(8,128)(2,1)S(1)}, u32[]{:S(2)}, u32[]{:S(2)}) collective-permute-start(bf16[144,1152]{1,0:T(8,128)(2,1)S(1)} %band_exchange.1.image_own), channel_id=1, source_target_pairs={{0,1},{1,0},{2,3},{3,2},{4,5},{5,4},{6,7},{7,6},{8,9},{9,8},{10,11... | collective-permute-start | bytes 995336 | tf_op jit(solution)/shard_map/band_exchange/ppermute | solution.py:53
  5.0 0.1 collective-permute-start.3
  5.1 0.0 collective-permute-start.2
  5.1 8.5 %collective-permute-start.1 = (bf16[128,1152]{1,0:T(8,128)(2,1)}, bf16[128,1152]{1,0:T(8,128)(2,1)S(1)}, u32[]{:S(2)}, u32[]{:S(2)}) collective-permute-start(bf16[128,1152]{1,0:T(8,128)(2,1)} %text_hbm.1), channel_id=1, source_target_pairs={{0,254},{1,255},{2,0},{3,1},{4,2},{5,3},{6,4},{7,5},{8,6},{9,7},{1... | collective-permute-start | bytes 884744 | tf_op jit(solution)/shard_map/band_exchange/ppermute | solution.py:53
  13.6 0.0 collective-permute-start
  14.9 0.0 collective-permute-done.3.text_other
  14.9 0.0 collective-permute-done.4.image_other
  14.9 5.0 %near.1 = (bf16[256,1152]{1,0:T(8,128)(2,1)S(1)}, bf16[1152,1152]{1,0:T(8,128)(2,1)S(1)}, bf16[256,1152]{1,0:T(8,128)(2,1)S(1)}, f32[256,1152]{1,0:T(8,128)S(1)}...) custom-call(f32[1]{0:T(128)S(6)} %copy.27.log_scale, ...), custom_call_target="tpu_custom_call" | custom-call | flops 4000000000 | tf_op jit(solution)/shard_map/near/pallas_call | solution.py:69
  19.9 0.9 collective-permute-done.2.refs_1_
  20.8 2.2 %collective-permute-done.1.refs_0_ = bf16[128,1152]{1,0:T(8,128)(2,1)S(1)} collective-permute-done((bf16[128,1152]{1,0:T(8,128)(2,1)}, bf16[128,1152]{1,0:T(8,128)(2,1)S(1)}, u32[]{:S(2)}, u32[]{:S(2)}) %collective-permute-start.1) | collective-permute-done | bytes 294944 | tf_op jit(solution)/shard_map/band_exchange/ppermute | solution.py:53
  23.0 1.2 %collective-permute-start.6 = (bf16[128,1152]{1,0:T(8,128)(2,1)S(1)}, bf16[128,1152]{1,0:T(8,128)(2,1)S(1)}, u32[]{:S(2)}, u32[]{:S(2)}) collective-permute-start(bf16[128,1152]{1,0:T(8,128)(2,1)S(1)} %get-tuple-element.33.below), channel_id=1, source_target_pairs={{0,1},{1,0},{2,3},{3,2},{4,5},{5,4},{6,7},{7,6},{8,9},{9,8},{10,11... | collective-permute-start | bytes 884744 | tf_op jit(solution)/shard_map/swap_neighbours/ppermute | solution.py:53
  24.2 0.0 collective-permute-start.7
  24.3 3.8 %received.2 = (f32[256,1152]{1,0:T(8,128)S(1)}, f32[1152,1152]{1,0:T(8,128)S(1)}) custom-call(f32[1]{0:T(128)S(6)} %copy.27.log_scale, f32[1]{0:T(128)S(6)} %copy.28.shift, bf16[128,1152]{1,0:T(8,128)(2,1)S(1)} %get-tuple-element.33.below, bf16[128,1152]{1,0:T(8,128)(2,1)S(1)} %get-tuple-element.34.above, bf16[1152,1152]{1,0:T(8,128)(2,1)S(1)} %get-tuple-element.35.text_w, ...), custom_call_target="tpu_custom_call" | custom-call | flops 4000000000 | tf_op jit(solution)/shard_map/received/pallas_call | solution.py:69
  28.1 0.0 collective-permute-done.refs_0_
  28.1 0.3 collective-permute-start.5
  28.4 0.0 collective-permute-done.6.below
  28.4 0.0 collective-permute-done.7.above
  28.4 2.1 %partners.1 = (f32[256,1152]{1,0:T(8,128)S(1)}, bf16[256,1152]{1,0:T(8,128)(2,1)S(1)}, bf16[256,1152]{1,0:T(8,128)(2,1)S(1)}) custom-call(f32[1]{0:T(128)S(6)} %copy.27.log_scale, f32[1]{0:T(128)S(6)} %copy.28.shift, bf16[128,1152]{1,0:T(8,128)(2,1)S(1)} %collective-permute-done.6.below, bf16[128,1152]{1,0:T(8,128)(2,1)S(1)} %collective-permute-done.7.above, ...), custom_call_target="tpu_custom_call" | custom-call | flops 4000000000 | tf_op jit(solution)/shard_map/partners/pallas_call | solution.py:69
  30.5 0.0 collective-permute-done.5.far_other
  30.5 4.3 %far.1 = (bf16[288,1152]{1,0:T(8,128)(2,1)S(1)}, bf16[144,1152]{1,0:T(8,128)(2,1)S(1)}, bf16[144,1152]{1,0:T(8,128)(2,1)S(1)}, bf16[144,1152]{1,0:T(8,128)(2,1)S...) custom-call(f32[1]{0:T(128)S(6)} %copy.27.log_scale, ...), custom_call_target="tpu_custom_call" | custom-call | flops 4000000000 | tf_op jit(solution)/shard_map/far/pallas_call | solution.py:69
  34.8 0.1 collective-permute-start.8
  34.9 2.7 %collective-permute-start.9 = (bf16[144,1152]{1,0:T(8,128)(2,1)S(1)}, bf16[144,1152]{1,0:T(8,128)(2,1)S(1)}, u32[]{:S(2)}, u32[]{:S(2)}) collective-permute-start(bf16[144,1152]{1,0:T(8,128)(2,1)S(1)} %get-tuple-element.51), channel_id=1, source_target_pairs={{0,48},{1,193},{2,50},{3,195},{4,52},{5,197},{6,54},{7,199},{8,56}... | collective-permute-start | bytes 995336 | tf_op jit(solution)/shard_map/sum_first/ppermute | solution.py:53
  37.5 2.7 %collective-permute-start.12 = (bf16[144,1152]{1,0:T(8,128)(2,1)S(1)}, bf16[144,1152]{1,0:T(8,128)(2,1)S(1)}, u32[]{:S(2)}, u32[]{:S(2)}) collective-permute-start(bf16[144,1152]{1,0:T(8,128)(2,1)S(1)} %get-tuple-element.54), channel_id=1, source_target_pairs={{0,48},{1,193},{2,50},{3,195},{4,52},{5,197},{6,54},{7,199},{8,56}... | collective-permute-start | bytes 995336 | tf_op jit(solution)/shard_map/sum_first/ppermute | solution.py:53
  40.2 2.1 %collective-permute-done.8.b = bf16[144,1152]{1,0:T(8,128)(2,1)S(1)} collective-permute-done((bf16[144,1152]{1,0:T(8,128)(2,1)S(1)}, bf16[144,1152]{1,0:T(8,128)(2,1)S(1)}, u32[]{:S(2)}, u32[]{:S(2)}) %collective-permute-start.8) | collective-permute-done | bytes 331808 | tf_op jit(solution)/shard_map/sum_first/ppermute | solution.py:53
  42.3 0.0 collective-permute-done.9.d
  42.3 0.2 sum_first.2
  42.5 0.1 collective-permute-start.10
  42.6 2.8 %collective-permute-start.13 = (bf16[144,1152]{1,0:T(8,128)(2,1)S(1)}, bf16[144,1152]{1,0:T(8,128)(2,1)S(1)}, u32[]{:S(2)}, u32[]{:S(2)}) collective-permute-start(bf16[144,1152]{1,0:T(8,128)(2,1)S(1)} %get-tuple-element.55), channel_id=1, source_target_pairs={{0,48},{1,193},{2,50},{3,195},{4,52},{5,197},{6,54},{7,199},{8,56}... | collective-permute-start | bytes 995336 | tf_op jit(solution)/shard_map/sum_first/ppermute | solution.py:53
  45.3 0.5 collective-permute-done.11.a_bottom
  45.9 0.0 collective-permute-done.12.b_top
  45.9 4.2 %collective-permute-done.10.a_top = bf16[144,1152]{1,0:T(8,128)(2,1)S(1)} collective-permute-done((bf16[144,1152]{1,0:T(8,128)(2,1)S(1)}, bf16[144,1152]{1,0:T(8,128)(2,1)S(1)}, u32[]{:S(2)}, u32[]{:S(2)}) %collective-permute-start.10) | collective-permute-done | bytes 331808 | tf_op jit(solution)/shard_map/sum_first/ppermute | solution.py:53
  50.1 0.3 sum_first.3
  50.3 10.5 %all_to_all.20 = bf16[4,72,1152]{2,1,0:T(8,128)(2,1)S(1)} all-to-all(bf16[4,72,1152]{2,1,0:T(8,128)(2,1)S(1)} %bitcast.18), channel_id=1, replica_groups={{0,64,128,192},{1,17,33,49},{2,66,130,194},{3,19,35,51},{4,68,132,196},..., dimensions={0} | all-to-all | bytes 1327104 | tf_op jit(solution)/shard_map/sum_second/all_to_all | solution.py:57
  60.9 0.1 reduce_sum.24
  61.0 13.9 %all_to_all.21 = bf16[88,8,128]{2,1,0:T(8,128)(2,1)S(1)} all-to-all(bf16[88,8,128]{2,1,0:T(8,128)(2,1)S(1)} %concatenate.3), channel_id=1, replica_groups={{0,2,4,6,8,10,12,14},{1,3,5,7,9,11,13,15},{16,18,20,22,24,26,28,30},{17..., dimensions={0} | all-to-all | bytes 360448 | tf_op jit(solution)/shard_map/sum_lines/all_to_all | solution.py:57
  74.9 10.9 %all_to_all.22 = bf16[88,8,128]{2,1,0:T(8,128)(2,1)S(1)} all-to-all(bf16[88,8,128]{2,1,0:T(8,128)(2,1)S(1)} %bitcast.20), channel_id=1, replica_groups={{0,2,4,6,8,10,12,14},{1,3,5,7,9,11,13,15},{16,18,20,22,24,26,28,30},{17..., dimensions={0} | all-to-all | bytes 360448 | tf_op jit(solution)/shard_map/share_lines/all_to_all | solution.py:57
  85.8 10.1 %all_to_all.23 = bf16[4,72,1152]{2,1,0:T(8,128)(2,1)S(1)} all-to-all(bf16[4,72,1152]{2,1,0:T(8,128)(2,1)S(1)} %tile.20), channel_id=1, replica_groups={{0,64,128,192},{1,17,33,49},{2,66,130,194},{3,19,35,51},{4,68,132,196},..., dimensions={0} | all-to-all | bytes 1327104 | tf_op jit(solution)/shard_map/share_second/all_to_all | solution.py:57
  95.9 6.5 %collective-permute-start.18 = (bf16[288,1152]{1,0:T(8,128)(2,1)S(1)}, bf16[288,1152]{1,0:T(8,128)(2,1)S(1)}, u32[]{:S(2)}, u32[]{:S(2)}) collective-permute-start(bf16[288,1152]{1,0:T(8,128)(2,1)S(1)} %bitcast.16), channel_id=1, source_target_pairs={{0,1},{1,0},{2,3},{3,2},{4,5},{5,4},{6,7},{7,6},{8,9},{9,8},{10,11... | collective-permute-start | bytes 1990664 | tf_op jit(solution)/shard_map/share_first/ppermute | solution.py:53
  102.4 0.1 fusion
  102.5 0.4 collective-permute-start.14
  102.9 2.4 %collective-permute-start.15 = (bf16[144,1152]{1,0:T(8,128)(2,1)S(1)}, bf16[144,1152]{1,0:T(8,128)(2,1)S(1)}, u32[]{:S(2)}, u32[]{:S(2)}) collective-permute-start(bf16[144,1152]{1,0:T(8,128)(2,1)S(1)} %bitcast.23), channel_id=1, source_target_pairs={{0,48},{1,193},{2,50},{3,195},{4,52},{5,197},{6,54},{7,199},{8,56}... | collective-permute-start | bytes 995336 | tf_op jit(solution)/shard_map/share_first/ppermute | solution.py:53
  105.2 0.0 collective-permute-start.17
  105.3 1.4 %collective-permute-start.16 = (bf16[144,1152]{1,0:T(8,128)(2,1)S(1)}, bf16[144,1152]{1,0:T(8,128)(2,1)S(1)}, u32[]{:S(2)}, u32[]{:S(2)}) collective-permute-start(bf16[144,1152]{1,0:T(8,128)(2,1)S(1)} %bitcast.24), channel_id=1, source_target_pairs={{0,16},{1,65},{2,18},{3,67},{4,20},{5,69},{6,22},{7,71},{8,24},{9,... | collective-permute-start | bytes 995336 | tf_op jit(solution)/shard_map/share_first/ppermute | solution.py:53
  106.7 3.3 %collective-permute-done.14.refs_1_ = bf16[144,1152]{1,0:T(8,128)(2,1)S(1)} collective-permute-done((bf16[144,1152]{1,0:T(8,128)(2,1)S(1)}, bf16[144,1152]{1,0:T(8,128)(2,1)S(1)}, u32[]{:S(2)}, u32[]{:S(2)}) %collective-permute-start.14) | collective-permute-done | bytes 331808 | tf_op jit(solution)/shard_map/share_first/ppermute | solution.py:53
  110.0 0.0 collective-permute-start.19
  110.0 0.0 collective-permute-done.15.refs_2_
  110.0 2.7 %collective-permute-start.20 = (bf16[144,1152]{1,0:T(8,128)(2,1)S(1)}, bf16[144,1152]{1,0:T(8,128)(2,1)S(1)}, u32[]{:S(2)}, u32[]{:S(2)}) collective-permute-start(bf16[144,1152]{1,0:T(8,128)(2,1)S(1)} %collective-permute-done.15.refs_2_), channel_id=1, source_target_pairs={{0,48},{1,193},{2,50},{3,195},{4,52},{5,197},{6,54},{7,199},{8,56}... | collective-permute-start | bytes 995336 | tf_op jit(solution)/shard_map/share_first/ppermute | solution.py:53
  112.7 0.1 collective-permute-done.17.refs_4_
  112.9 2.1 %collective-permute-start.24 = (bf16[144,1152]{1,0:T(8,128)(2,1)S(1)}, bf16[144,1152]{1,0:T(8,128)(2,1)S(1)}, u32[]{:S(2)}, u32[]{:S(2)}) collective-permute-start(bf16[144,1152]{1,0:T(8,128)(2,1)S(1)} %collective-permute-done.17.refs_4_), channel_id=1, source_target_pairs={{0,1},{1,0},{2,3},{3,2},{4,5},{5,4},{6,7},{7,6},{8,9},{9,8},{10,11... | collective-permute-start | bytes 995336 | tf_op jit(solution)/shard_map/share_first/ppermute | solution.py:53
  115.0 0.0 collective-permute-done.16.refs_3_
  115.0 0.9 collective-permute-start.21
  115.8 0.0 collective-permute-done.18.refs_5_
  115.9 0.0 collective-permute-start.23
  115.9 1.5 %write.4 = (bf16[1152,1152]{1,0:T(8,128)(2,1)}, bf16[1152,1152]{1,0:T(8,128)(2,1)}) custom-call(bf16[288,1152]{1,0:T(8,128)(2,1)S(1)} %bitcast.17, bf16[144,1152]{1,0:T(8,128)(2,1)S(1)} %collective-permute-done.14.refs_1_, bf16[144,1152]{1,0:T(8,128)(2,1)S(1)} %collective-permute-done.15.refs_2_, bf16[144,1152]{1,0:T(8,128)(2,1)S(1)} %collective-permute-done.16.refs_3_, ...), custom_call_target="tpu_custom_call" | custom-call | tf_op jit(solution)/shard_map/write/pallas_call | solution.py:69
  117.4 0.1 collective-permute-done.19.refs_1_
  117.5 1.9 %collective-permute-start.22 = (bf16[144,1152]{1,0:T(8,128)(2,1)S(1)}, bf16[144,1152]{1,0:T(8,128)(2,1)S(1)}, u32[]{:S(2)}, u32[]{:S(2)}) collective-permute-start(bf16[144,1152]{1,0:T(8,128)(2,1)S(1)} %collective-permute-done.15.refs_2_), channel_id=1, source_target_pairs={{0,1},{1,0},{2,3},{3,2},{4,5},{5,4},{6,7},{7,6},{8,9},{9,8},{10,11... | collective-permute-start | bytes 995336 | tf_op jit(solution)/shard_map/share_first/ppermute | solution.py:53
  119.4 0.0 collective-permute-done.20.refs_2_
  119.4 0.1 collective-permute-start.25
  119.5 0.4 collective-permute-start.26
  119.9 0.7 collective-permute-done.22.refs_5_
  120.7 1.3 %write.6 = (bf16[1152,1152]{1,0:T(8,128)(2,1)}, bf16[1152,1152]{1,0:T(8,128)(2,1)}) custom-call(bf16[1152,1152]{1,0:T(8,128)(2,1)} %get-tuple-element.56.refs_0_, bf16[1152,1152]{1,0:T(8,128)(2,1)} %get-tuple-element.57.refs_1_, bf16[144,1152]{1,0:T(8,128)(2,1)S(1)} %get-tuple-element.58.refs_2_, ...), custom_call_target="tpu_custom_call", output_to_operand_aliasing={{0}: (0, {}), {1}: (1, {})} | custom-call | tf_op jit(solution)/shard_map/write/pallas_call | solution.py:69
  122.0 0.0 collective-permute-done.25.refs_2_
  122.0 0.9 write.7
  (14 shorter events, 0.2 us)
Async XLA Ops:
  1.6 13.2 %collective-permute-start.4 = (bf16[144,1152]{1,0:T(8,128)(2,1)S(1)}, bf16[144,1152]{1,0:T(8,128)(2,1)S(1)}, u32[]{:S(2)}, u32[]{:S(2)}) collective-permute-start(bf16[144,1152]{1,0:T(8,128)(2,1)S(1)} %band_exchange.1.image_own), channel_id=1, source_target_pairs={{0,1},{1,0},{2,3},{3,2},{4,5},{5,4},{6,7},{7,6},{8,9},{9,8},{10,11... | collective-permute-start | bytes 995336 | tf_op jit(solution)/shard_map/band_exchange/ppermute | solution.py:53
  5.0 9.9 %collective-permute-start.3 = (bf16[128,1152]{1,0:T(8,128)(2,1)}, bf16[128,1152]{1,0:T(8,128)(2,1)S(1)}, u32[]{:S(2)}, u32[]{:S(2)}) collective-permute-start(bf16[128,1152]{1,0:T(8,128)(2,1)} %text_hbm.1), channel_id=1, source_target_pairs={{0,1},{1,0},{2,3},{3,2},{4,5},{5,4},{6,7},{7,6},{8,9},{9,8},{10,11... | collective-permute-start | bytes 884744 | tf_op jit(solution)/shard_map/band_exchange/ppermute | solution.py:53
  5.1 15.7 %collective-permute-start.2 = (bf16[128,1152]{1,0:T(8,128)(2,1)}, bf16[128,1152]{1,0:T(8,128)(2,1)S(1)}, u32[]{:S(2)}, u32[]{:S(2)}) collective-permute-start(bf16[128,1152]{1,0:T(8,128)(2,1)} %text_hbm.1), channel_id=1, source_target_pairs={{0,2},{1,3},{2,4},{3,5},{4,6},{5,7},{6,8},{7,9},{8,10},{9,11},{10,... | collective-permute-start | bytes 884744 | tf_op jit(solution)/shard_map/band_exchange/ppermute | solution.py:53
  5.1 17.9 %collective-permute-start.1 = (bf16[128,1152]{1,0:T(8,128)(2,1)}, bf16[128,1152]{1,0:T(8,128)(2,1)S(1)}, u32[]{:S(2)}, u32[]{:S(2)}) collective-permute-start(bf16[128,1152]{1,0:T(8,128)(2,1)} %text_hbm.1), channel_id=1, source_target_pairs={{0,254},{1,255},{2,0},{3,1},{4,2},{5,3},{6,4},{7,5},{8,6},{9,7},{1... | collective-permute-start | bytes 884744 | tf_op jit(solution)/shard_map/band_exchange/ppermute | solution.py:53
  13.6 14.5 %collective-permute-start = (bf16[128,1152]{1,0:T(8,128)(2,1)}, bf16[128,1152]{1,0:T(8,128)(2,1)S(1)}, u32[]{:S(2)}, u32[]{:S(2)}) collective-permute-start(bf16[128,1152]{1,0:T(8,128)(2,1)} %text_hbm.1), channel_id=1, source_target_pairs={{0,253},{1,4},{2,255},{3,6},{4,1},{5,8},{6,3},{7,10},{8,5},{9,12},... | collective-permute-start | bytes 884744 | tf_op jit(solution)/shard_map/band_exchange/ppermute | solution.py:53
  23.0 5.4 %collective-permute-start.6 = (bf16[128,1152]{1,0:T(8,128)(2,1)S(1)}, bf16[128,1152]{1,0:T(8,128)(2,1)S(1)}, u32[]{:S(2)}, u32[]{:S(2)}) collective-permute-start(bf16[128,1152]{1,0:T(8,128)(2,1)S(1)} %get-tuple-element.33.below), channel_id=1, source_target_pairs={{0,1},{1,0},{2,3},{3,2},{4,5},{5,4},{6,7},{7,6},{8,9},{9,8},{10,11... | collective-permute-start | bytes 884744 | tf_op jit(solution)/shard_map/swap_neighbours/ppermute | solution.py:53
  24.2 4.1 %collective-permute-start.7 = (bf16[128,1152]{1,0:T(8,128)(2,1)S(1)}, bf16[128,1152]{1,0:T(8,128)(2,1)S(1)}, u32[]{:S(2)}, u32[]{:S(2)}) collective-permute-start(bf16[128,1152]{1,0:T(8,128)(2,1)S(1)} %get-tuple-element.34.above), channel_id=1, source_target_pairs={{0,1},{1,0},{2,3},{3,2},{4,5},{5,4},{6,7},{7,6},{8,9},{9,8},{10,11... | collective-permute-start | bytes 884744 | tf_op jit(solution)/shard_map/swap_neighbours/ppermute | solution.py:53
  28.1 2.4 %collective-permute-start.5 = (bf16[128,1152]{1,0:T(8,128)(2,1)S(1)}, bf16[128,1152]{1,0:T(8,128)(2,1)S(1)}, u32[]{:S(2)}, u32[]{:S(2)}) collective-permute-start(bf16[128,1152]{1,0:T(8,128)(2,1)S(1)} %received.3.far), channel_id=1, source_target_pairs={{0,1},{1,0},{2,3},{3,2},{4,5},{5,4},{6,7},{7,6},{8,9},{9,8},{10,11... | collective-permute-start | bytes 884744 | tf_op jit(solution)/shard_map/received/ppermute | solution.py:53
  34.8 7.6 %collective-permute-start.8 = (bf16[144,1152]{1,0:T(8,128)(2,1)S(1)}, bf16[144,1152]{1,0:T(8,128)(2,1)S(1)}, u32[]{:S(2)}, u32[]{:S(2)}) collective-permute-start(bf16[144,1152]{1,0:T(8,128)(2,1)S(1)} %get-tuple-element.49), channel_id=1, source_target_pairs={{0,16},{1,65},{2,18},{3,67},{4,20},{5,69},{6,22},{7,71},{8,24},{9,... | collective-permute-start | bytes 995336 | tf_op jit(solution)/shard_map/sum_first/ppermute | solution.py:53
  34.9 7.5 %collective-permute-start.9 = (bf16[144,1152]{1,0:T(8,128)(2,1)S(1)}, bf16[144,1152]{1,0:T(8,128)(2,1)S(1)}, u32[]{:S(2)}, u32[]{:S(2)}) collective-permute-start(bf16[144,1152]{1,0:T(8,128)(2,1)S(1)} %get-tuple-element.51), channel_id=1, source_target_pairs={{0,48},{1,193},{2,50},{3,195},{4,52},{5,197},{6,54},{7,199},{8,56}... | collective-permute-start | bytes 995336 | tf_op jit(solution)/shard_map/sum_first/ppermute | solution.py:53
  37.5 8.4 %collective-permute-start.11 = (bf16[144,1152]{1,0:T(8,128)(2,1)S(1)}, bf16[144,1152]{1,0:T(8,128)(2,1)S(1)}, u32[]{:S(2)}, u32[]{:S(2)}) collective-permute-start(bf16[144,1152]{1,0:T(8,128)(2,1)S(1)} %get-tuple-element.53), channel_id=1, source_target_pairs={{0,16},{1,65},{2,18},{3,67},{4,20},{5,69},{6,22},{7,71},{8,24},{9,... | collective-permute-start | bytes 995336 | tf_op jit(solution)/shard_map/sum_first/ppermute | solution.py:53
  37.5 8.4 %collective-permute-start.12 = (bf16[144,1152]{1,0:T(8,128)(2,1)S(1)}, bf16[144,1152]{1,0:T(8,128)(2,1)S(1)}, u32[]{:S(2)}, u32[]{:S(2)}) collective-permute-start(bf16[144,1152]{1,0:T(8,128)(2,1)S(1)} %get-tuple-element.54), channel_id=1, source_target_pairs={{0,48},{1,193},{2,50},{3,195},{4,52},{5,197},{6,54},{7,199},{8,56}... | collective-permute-start | bytes 995336 | tf_op jit(solution)/shard_map/sum_first/ppermute | solution.py:53
  42.5 7.6 %collective-permute-start.10 = (bf16[144,1152]{1,0:T(8,128)(2,1)S(1)}, bf16[144,1152]{1,0:T(8,128)(2,1)S(1)}, u32[]{:S(2)}, u32[]{:S(2)}) collective-permute-start(bf16[144,1152]{1,0:T(8,128)(2,1)S(1)} %get-tuple-element.52), channel_id=1, source_target_pairs={{0,16},{1,65},{2,18},{3,67},{4,20},{5,69},{6,22},{7,71},{8,24},{9,... | collective-permute-start | bytes 995336 | tf_op jit(solution)/shard_map/sum_first/ppermute | solution.py:53
  42.6 7.5 %collective-permute-start.13 = (bf16[144,1152]{1,0:T(8,128)(2,1)S(1)}, bf16[144,1152]{1,0:T(8,128)(2,1)S(1)}, u32[]{:S(2)}, u32[]{:S(2)}) collective-permute-start(bf16[144,1152]{1,0:T(8,128)(2,1)S(1)} %get-tuple-element.55), channel_id=1, source_target_pairs={{0,48},{1,193},{2,50},{3,195},{4,52},{5,197},{6,54},{7,199},{8,56}... | collective-permute-start | bytes 995336 | tf_op jit(solution)/shard_map/sum_first/ppermute | solution.py:53
  95.9 19.9 %collective-permute-start.18 = (bf16[288,1152]{1,0:T(8,128)(2,1)S(1)}, bf16[288,1152]{1,0:T(8,128)(2,1)S(1)}, u32[]{:S(2)}, u32[]{:S(2)}) collective-permute-start(bf16[288,1152]{1,0:T(8,128)(2,1)S(1)} %bitcast.16), channel_id=1, source_target_pairs={{0,1},{1,0},{2,3},{3,2},{4,5},{5,4},{6,7},{7,6},{8,9},{9,8},{10,11... | collective-permute-start | bytes 1990664 | tf_op jit(solution)/shard_map/share_first/ppermute | solution.py:53
  102.5 7.6 %collective-permute-start.14 = (bf16[144,1152]{1,0:T(8,128)(2,1)S(1)}, bf16[144,1152]{1,0:T(8,128)(2,1)S(1)}, u32[]{:S(2)}, u32[]{:S(2)}) collective-permute-start(bf16[144,1152]{1,0:T(8,128)(2,1)S(1)} %bitcast.25), channel_id=1, source_target_pairs={{0,16},{1,65},{2,18},{3,67},{4,20},{5,69},{6,22},{7,71},{8,24},{9,... | collective-permute-start | bytes 995336 | tf_op jit(solution)/shard_map/share_first/ppermute | solution.py:53
  102.9 7.2 %collective-permute-start.15 = (bf16[144,1152]{1,0:T(8,128)(2,1)S(1)}, bf16[144,1152]{1,0:T(8,128)(2,1)S(1)}, u32[]{:S(2)}, u32[]{:S(2)}) collective-permute-start(bf16[144,1152]{1,0:T(8,128)(2,1)S(1)} %bitcast.23), channel_id=1, source_target_pairs={{0,48},{1,193},{2,50},{3,195},{4,52},{5,197},{6,54},{7,199},{8,56}... | collective-permute-start | bytes 995336 | tf_op jit(solution)/shard_map/share_first/ppermute | solution.py:53
  105.2 7.6 %collective-permute-start.17 = (bf16[144,1152]{1,0:T(8,128)(2,1)S(1)}, bf16[144,1152]{1,0:T(8,128)(2,1)S(1)}, u32[]{:S(2)}, u32[]{:S(2)}) collective-permute-start(bf16[144,1152]{1,0:T(8,128)(2,1)S(1)} %bitcast.26), channel_id=1, source_target_pairs={{0,48},{1,193},{2,50},{3,195},{4,52},{5,197},{6,54},{7,199},{8,56}... | collective-permute-start | bytes 995336 | tf_op jit(solution)/shard_map/share_first/ppermute | solution.py:53
  105.3 9.7 %collective-permute-start.16 = (bf16[144,1152]{1,0:T(8,128)(2,1)S(1)}, bf16[144,1152]{1,0:T(8,128)(2,1)S(1)}, u32[]{:S(2)}, u32[]{:S(2)}) collective-permute-start(bf16[144,1152]{1,0:T(8,128)(2,1)S(1)} %bitcast.24), channel_id=1, source_target_pairs={{0,16},{1,65},{2,18},{3,67},{4,20},{5,69},{6,22},{7,71},{8,24},{9,... | collective-permute-start | bytes 995336 | tf_op jit(solution)/shard_map/share_first/ppermute | solution.py:53
  110.0 7.5 %collective-permute-start.19 = (bf16[144,1152]{1,0:T(8,128)(2,1)S(1)}, bf16[144,1152]{1,0:T(8,128)(2,1)S(1)}, u32[]{:S(2)}, u32[]{:S(2)}) collective-permute-start(bf16[144,1152]{1,0:T(8,128)(2,1)S(1)} %collective-permute-done.14.refs_1_), channel_id=1, source_target_pairs={{0,16},{1,65},{2,18},{3,67},{4,20},{5,69},{6,22},{7,71},{8,24},{9,... | collective-permute-start | bytes 995336 | tf_op jit(solution)/shard_map/share_first/ppermute | solution.py:53
  110.0 9.4 %collective-permute-start.20 = (bf16[144,1152]{1,0:T(8,128)(2,1)S(1)}, bf16[144,1152]{1,0:T(8,128)(2,1)S(1)}, u32[]{:S(2)}, u32[]{:S(2)}) collective-permute-start(bf16[144,1152]{1,0:T(8,128)(2,1)S(1)} %collective-permute-done.15.refs_2_), channel_id=1, source_target_pairs={{0,48},{1,193},{2,50},{3,195},{4,52},{5,197},{6,54},{7,199},{8,56}... | collective-permute-start | bytes 995336 | tf_op jit(solution)/shard_map/share_first/ppermute | solution.py:53
  112.9 6.6 %collective-permute-start.24 = (bf16[144,1152]{1,0:T(8,128)(2,1)S(1)}, bf16[144,1152]{1,0:T(8,128)(2,1)S(1)}, u32[]{:S(2)}, u32[]{:S(2)}) collective-permute-start(bf16[144,1152]{1,0:T(8,128)(2,1)S(1)} %collective-permute-done.17.refs_4_), channel_id=1, source_target_pairs={{0,1},{1,0},{2,3},{3,2},{4,5},{5,4},{6,7},{7,6},{8,9},{9,8},{10,11... | collective-permute-start | bytes 995336 | tf_op jit(solution)/shard_map/share_first/ppermute | solution.py:53
  115.0 4.9 %collective-permute-start.21 = (bf16[144,1152]{1,0:T(8,128)(2,1)S(1)}, bf16[144,1152]{1,0:T(8,128)(2,1)S(1)}, u32[]{:S(2)}, u32[]{:S(2)}) collective-permute-start(bf16[144,1152]{1,0:T(8,128)(2,1)S(1)} %collective-permute-done.14.refs_1_), channel_id=1, source_target_pairs={{0,1},{1,0},{2,3},{3,2},{4,5},{5,4},{6,7},{7,6},{8,9},{9,8},{10,11... | collective-permute-start | bytes 995336 | tf_op jit(solution)/shard_map/share_first/ppermute | solution.py:53
  115.9 4.1 %collective-permute-start.23 = (bf16[144,1152]{1,0:T(8,128)(2,1)S(1)}, bf16[144,1152]{1,0:T(8,128)(2,1)S(1)}, u32[]{:S(2)}, u32[]{:S(2)}) collective-permute-start(bf16[144,1152]{1,0:T(8,128)(2,1)S(1)} %collective-permute-done.16.refs_3_), channel_id=1, source_target_pairs={{0,1},{1,0},{2,3},{3,2},{4,5},{5,4},{6,7},{7,6},{8,9},{9,8},{10,11... | collective-permute-start | bytes 995336 | tf_op jit(solution)/shard_map/share_first/ppermute | solution.py:53
  117.5 3.1 %collective-permute-start.22 = (bf16[144,1152]{1,0:T(8,128)(2,1)S(1)}, bf16[144,1152]{1,0:T(8,128)(2,1)S(1)}, u32[]{:S(2)}, u32[]{:S(2)}) collective-permute-start(bf16[144,1152]{1,0:T(8,128)(2,1)S(1)} %collective-permute-done.15.refs_2_), channel_id=1, source_target_pairs={{0,1},{1,0},{2,3},{3,2},{4,5},{5,4},{6,7},{7,6},{8,9},{9,8},{10,11... | collective-permute-start | bytes 995336 | tf_op jit(solution)/shard_map/share_first/ppermute | solution.py:53
  119.4 2.6 %collective-permute-start.25 = (bf16[144,1152]{1,0:T(8,128)(2,1)S(1)}, bf16[144,1152]{1,0:T(8,128)(2,1)S(1)}, u32[]{:S(2)}, u32[]{:S(2)}) collective-permute-start(bf16[144,1152]{1,0:T(8,128)(2,1)S(1)} %get-tuple-element.58.refs_2_), channel_id=1, source_target_pairs={{0,1},{1,0},{2,3},{3,2},{4,5},{5,4},{6,7},{7,6},{8,9},{9,8},{10,11... | collective-permute-start | bytes 995336 | tf_op jit(solution)/shard_map/write/ppermute | solution.py:53
  119.5 2.5 %collective-permute-start.26 = (bf16[144,1152]{1,0:T(8,128)(2,1)S(1)}, bf16[144,1152]{1,0:T(8,128)(2,1)S(1)}, u32[]{:S(2)}, u32[]{:S(2)}) collective-permute-start(bf16[144,1152]{1,0:T(8,128)(2,1)S(1)} %get-tuple-element.59.refs_3_), channel_id=1, source_target_pairs={{0,1},{1,0},{2,3},{3,2},{4,5},{5,4},{6,7},{7,6},{8,9},{9,8},{10,11... | collective-permute-start | bytes 995336 | tf_op jit(solution)/shard_map/write/ppermute | solution.py:53

commit v11 on v10

--- a/solution.py
+++ b/solution.py
@@ -266,9 +266,8 @@
     own[...] = part(0, 0, slab)
 
 
-def add_kernel(a, b, c, d, ab, cd):
-    ab[...] = (a[...].astype(f32) + b[...].astype(f32)).astype(bf16)
-    cd[...] = (c[...].astype(f32) + d[...].astype(f32)).astype(bf16)
+def add_kernel(a, b, out):
+    out[...] = (a[...].astype(f32) + b[...].astype(f32)).astype(bf16)
 
 
 def join_kernel(own, a_top, a_bottom, b_top, b_bottom, out):
@@ -391,9 +390,8 @@
         from_right = send(far_left, LEFT)
         a_bottom = send(right_bottom, RIGHT)
         b_top = send(left_top, LEFT)
-        right_top, left_bottom = call(add_kernel, [half_piece] * 2)(
-            (), (), right_top, from_left, left_bottom, from_right
-        )
+        [right_top] = call(add_kernel, [half_piece])((), (), right_top, from_left)
+        [left_bottom] = call(add_kernel, [half_piece])((), (), left_bottom, from_right)
         a_top = send(right_top, RIGHT)
         b_bottom = send(left_bottom, LEFT)
         [part] = call(join_kernel, [piece])((), (), own, a_top, a_bottom, b_top, b_bottom)
@@ -430,7 +428,8 @@
         outs = write((), [OWN, LEFT_TOP, RIGHT_BOTTOM, LEFT_BOTTOM, RIGHT_TOP], [OWN])(
             own, left_top, right_bottom, left_bottom, right_top, own_other, shape=matrix
         )
-        across_top, across_bottom = after(outs[0], across_top, across_bottom, in_hbm=True)
+        [across_top] = after(outs[0], across_top, in_hbm=True)
+        [across_bottom] = after(outs[0], across_bottom, in_hbm=True)
         across_others = [send(across_top, SWAP), send(across_bottom, SWAP)]
         outs = write(
             tuple(outs),

time: 123 us -> 123 us (level)
    pallas_call x13 -> x15, Pallas kernels: 20.4 us -> 20.4 us  [run(): pl.pallas_call(body, out_shape=[jax.ShapeDtypeStruct(s, d) for s, d in ou...]
where the time goes in v11:
time: 123 us
  blocking collectives  45.3 us (37%)
  starting transfers between devices  40.5 us (33%)
  Pallas kernels  20.4 us (17%)
  waiting for transfers between devices  14.2 us (12%)
  between operations  2.34 us (2%)
    all_to_all x4, blocking collectives, exchange(): lax.all_to_all(parts, 'dp', 0, 0, axis_index_groups=members, tiled=True)  45.3 us
    ppermute x27, starting transfers between devices, send(): return lax.ppermute(block, 'dp', pairs)  40.5 us
    pallas_call x15, Pallas kernels, run(): pl.pallas_call(body, out_shape=[jax.ShapeDtypeStruct(s, d) for s, d in ou...  20.4 us
    ppermute x27, waiting for transfers between devices, send(): return lax.ppermute(block, 'dp', pairs)  14.2 us
  transfers between devices with their start and end apart: 27, of which 9 were waited for; matrix products, arithmetic and copies ran while one was open for 0% of the time, Pallas kernels for 11%

profile of v11, /device:TPU:1, one launch (start us, length us, event | category | flops | bytes accessed | tf_op | source)
XLA Modules:
  0.0 123.0 jit_solution(7280921920514840741)
XLA Ops:
  0.6 1.0 band_exchange.1.image_own
  1.6 3.3 %collective-permute-start.4 = (bf16[144,1152]{1,0:T(8,128)(2,1)S(1)}, bf16[144,1152]{1,0:T(8,128)(2,1)S(1)}, u32[]{:S(2)}, u32[]{:S(2)}) collective-permute-start(bf16[144,1152]{1,0:T(8,128)(2,1)S(1)} %band_exchange.1.image_own), channel_id=1, source_target_pairs={{0,1},{1,0},{2,3},{3,2},{4,5},{5,4},{6,7},{7,6},{8,9},{9,8},{10,11... | collective-permute-start | bytes 995336 | tf_op jit(solution)/shard_map/band_exchange/ppermute | solution.py:53
  5.0 0.1 collective-permute-start.3
  5.1 0.0 collective-permute-start.2
  5.1 8.5 %collective-permute-start.1 = (bf16[128,1152]{1,0:T(8,128)(2,1)}, bf16[128,1152]{1,0:T(8,128)(2,1)S(1)}, u32[]{:S(2)}, u32[]{:S(2)}) collective-permute-start(bf16[128,1152]{1,0:T(8,128)(2,1)} %text_hbm.1), channel_id=1, source_target_pairs={{0,254},{1,255},{2,0},{3,1},{4,2},{5,3},{6,4},{7,5},{8,6},{9,7},{1... | collective-permute-start | bytes 884744 | tf_op jit(solution)/shard_map/band_exchange/ppermute | solution.py:53
  14.9 0.0 collective-permute-done.3.text_other
  14.9 0.0 collective-permute-done.4.image_other
  14.9 5.0 %near.1 = (bf16[256,1152]{1,0:T(8,128)(2,1)S(1)}, bf16[1152,1152]{1,0:T(8,128)(2,1)S(1)}, bf16[256,1152]{1,0:T(8,128)(2,1)S(1)}, f32[256,1152]{1,0:T(8,128)S(1)}...) custom-call(f32[1]{0:T(128)S(6)} %copy.27.log_scale, ...), custom_call_target="tpu_custom_call" | custom-call | flops 4000000000 | tf_op jit(solution)/shard_map/near/pallas_call | solution.py:69
  19.9 0.9 collective-permute-done.2.refs_1_
  20.8 2.2 %collective-permute-done.1.refs_0_ = bf16[128,1152]{1,0:T(8,128)(2,1)S(1)} collective-permute-done((bf16[128,1152]{1,0:T(8,128)(2,1)}, bf16[128,1152]{1,0:T(8,128)(2,1)S(1)}, u32[]{:S(2)}, u32[]{:S(2)}) %collective-permute-start.1) | collective-permute-done | bytes 294944 | tf_op jit(solution)/shard_map/band_exchange/ppermute | solution.py:53
  23.0 1.2 %collective-permute-start.6 = (bf16[128,1152]{1,0:T(8,128)(2,1)S(1)}, bf16[128,1152]{1,0:T(8,128)(2,1)S(1)}, u32[]{:S(2)}, u32[]{:S(2)}) collective-permute-start(bf16[128,1152]{1,0:T(8,128)(2,1)S(1)} %get-tuple-element.29.below), channel_id=1, source_target_pairs={{0,1},{1,0},{2,3},{3,2},{4,5},{5,4},{6,7},{7,6},{8,9},{9,8},{10,11... | collective-permute-start | bytes 884744 | tf_op jit(solution)/shard_map/swap_neighbours/ppermute | solution.py:53
  24.2 0.0 collective-permute-start.7
  24.3 3.8 %received.2 = (f32[256,1152]{1,0:T(8,128)S(1)}, f32[1152,1152]{1,0:T(8,128)S(1)}) custom-call(f32[1]{0:T(128)S(6)} %copy.27.log_scale, f32[1]{0:T(128)S(6)} %copy.28.shift, bf16[128,1152]{1,0:T(8,128)(2,1)S(1)} %get-tuple-element.29.below, bf16[128,1152]{1,0:T(8,128)(2,1)S(1)} %get-tuple-element.30.above, bf16[1152,1152]{1,0:T(8,128)(2,1)S(1)} %get-tuple-element.31.text_w, ...), custom_call_target="tpu_custom_call" | custom-call | flops 4000000000 | tf_op jit(solution)/shard_map/received/pallas_call | solution.py:69
  28.1 0.0 collective-permute-done.refs_0_
  28.1 0.3 collective-permute-start.5
  28.4 0.0 collective-permute-done.6.below
  28.4 0.0 collective-permute-done.7.above
  28.4 2.1 %partners.1 = (f32[256,1152]{1,0:T(8,128)S(1)}, bf16[256,1152]{1,0:T(8,128)(2,1)S(1)}, bf16[256,1152]{1,0:T(8,128)(2,1)S(1)}) custom-call(f32[1]{0:T(128)S(6)} %copy.27.log_scale, f32[1]{0:T(128)S(6)} %copy.28.shift, bf16[128,1152]{1,0:T(8,128)(2,1)S(1)} %collective-permute-done.6.below, bf16[128,1152]{1,0:T(8,128)(2,1)S(1)} %collective-permute-done.7.above, ...), custom_call_target="tpu_custom_call" | custom-call | flops 4000000000 | tf_op jit(solution)/shard_map/partners/pallas_call | solution.py:69
  30.5 0.0 collective-permute-done.5.far_other
  30.5 4.3 %far.1 = (bf16[288,1152]{1,0:T(8,128)(2,1)S(1)}, bf16[144,1152]{1,0:T(8,128)(2,1)S(1)}, bf16[144,1152]{1,0:T(8,128)(2,1)S(1)}, bf16[144,1152]{1,0:T(8,128)(2,1)S...) custom-call(f32[1]{0:T(128)S(6)} %copy.27.log_scale, ...), custom_call_target="tpu_custom_call" | custom-call | flops 4000000000 | tf_op jit(solution)/shard_map/far/pallas_call | solution.py:69
  34.8 0.1 collective-permute-start.8
  34.9 2.7 %collective-permute-start.12 = (bf16[144,1152]{1,0:T(8,128)(2,1)S(1)}, bf16[144,1152]{1,0:T(8,128)(2,1)S(1)}, u32[]{:S(2)}, u32[]{:S(2)}) collective-permute-start(bf16[144,1152]{1,0:T(8,128)(2,1)S(1)} %get-tuple-element.49), channel_id=1, source_target_pairs={{0,48},{1,193},{2,50},{3,195},{4,52},{5,197},{6,54},{7,199},{8,56}... | collective-permute-start | bytes 995336 | tf_op jit(solution)/shard_map/sum_first/ppermute | solution.py:53
  37.6 0.0 collective-permute-start.10
  37.6 2.7 %collective-permute-start.11 = (bf16[144,1152]{1,0:T(8,128)(2,1)S(1)}, bf16[144,1152]{1,0:T(8,128)(2,1)S(1)}, u32[]{:S(2)}, u32[]{:S(2)}) collective-permute-start(bf16[144,1152]{1,0:T(8,128)(2,1)S(1)} %get-tuple-element.47), channel_id=1, source_target_pairs={{0,48},{1,193},{2,50},{3,195},{4,52},{5,197},{6,54},{7,199},{8,56}... | collective-permute-start | bytes 995336 | tf_op jit(solution)/shard_map/sum_first/ppermute | solution.py:53
  40.2 2.1 %collective-permute-done.8.b = bf16[144,1152]{1,0:T(8,128)(2,1)S(1)} collective-permute-done((bf16[144,1152]{1,0:T(8,128)(2,1)S(1)}, bf16[144,1152]{1,0:T(8,128)(2,1)S(1)}, u32[]{:S(2)}, u32[]{:S(2)}) %collective-permute-start.8) | collective-permute-done | bytes 331808 | tf_op jit(solution)/shard_map/sum_first/ppermute | solution.py:53
  42.4 0.1 sum_first.3
  42.4 0.1 collective-permute-start.9
  42.5 0.0 collective-permute-done.12.b
  42.5 0.1 sum_first.4
  42.6 2.7 %collective-permute-start.13 = (bf16[144,1152]{1,0:T(8,128)(2,1)S(1)}, bf16[144,1152]{1,0:T(8,128)(2,1)S(1)}, u32[]{:S(2)}, u32[]{:S(2)}) collective-permute-start(bf16[144,1152]{1,0:T(8,128)(2,1)S(1)} %sum_first.4), channel_id=1, source_target_pairs={{0,48},{1,193},{2,50},{3,195},{4,52},{5,197},{6,54},{7,199},{8,56}... | collective-permute-start | bytes 995336 | tf_op jit(solution)/shard_map/sum_first/ppermute | solution.py:53
  45.4 0.6 collective-permute-done.10.a_bottom
  45.9 4.1 %collective-permute-done.9.a_top = bf16[144,1152]{1,0:T(8,128)(2,1)S(1)} collective-permute-done((bf16[144,1152]{1,0:T(8,128)(2,1)S(1)}, bf16[144,1152]{1,0:T(8,128)(2,1)S(1)}, u32[]{:S(2)}, u32[]{:S(2)}) %collective-permute-start.9) | collective-permute-done | bytes 331808 | tf_op jit(solution)/shard_map/sum_first/ppermute | solution.py:53
  50.0 0.0 collective-permute-done.13.b_bottom
  50.0 0.3 sum_first.5
  50.3 10.5 %all_to_all.20 = bf16[4,72,1152]{2,1,0:T(8,128)(2,1)S(1)} all-to-all(bf16[4,72,1152]{2,1,0:T(8,128)(2,1)S(1)} %bitcast.18), channel_id=1, replica_groups={{0,64,128,192},{1,17,33,49},{2,66,130,194},{3,19,35,51},{4,68,132,196},..., dimensions={0} | all-to-all | bytes 1327104 | tf_op jit(solution)/shard_map/sum_second/all_to_all | solution.py:57
  60.8 0.1 reduce_sum.24
  60.9 13.7 %all_to_all.21 = bf16[88,8,128]{2,1,0:T(8,128)(2,1)S(1)} all-to-all(bf16[88,8,128]{2,1,0:T(8,128)(2,1)S(1)} %concatenate.3), channel_id=1, replica_groups={{0,2,4,6,8,10,12,14},{1,3,5,7,9,11,13,15},{16,18,20,22,24,26,28,30},{17..., dimensions={0} | all-to-all | bytes 360448 | tf_op jit(solution)/shard_map/sum_lines/all_to_all | solution.py:57
  74.7 10.9 %all_to_all.22 = bf16[88,8,128]{2,1,0:T(8,128)(2,1)S(1)} all-to-all(bf16[88,8,128]{2,1,0:T(8,128)(2,1)S(1)} %bitcast.20), channel_id=1, replica_groups={{0,2,4,6,8,10,12,14},{1,3,5,7,9,11,13,15},{16,18,20,22,24,26,28,30},{17..., dimensions={0} | all-to-all | bytes 360448 | tf_op jit(solution)/shard_map/share_lines/all_to_all | solution.py:57
  85.7 10.1 %all_to_all.23 = bf16[4,72,1152]{2,1,0:T(8,128)(2,1)S(1)} all-to-all(bf16[4,72,1152]{2,1,0:T(8,128)(2,1)S(1)} %tile.20), channel_id=1, replica_groups={{0,64,128,192},{1,17,33,49},{2,66,130,194},{3,19,35,51},{4,68,132,196},..., dimensions={0} | all-to-all | bytes 1327104 | tf_op jit(solution)/shard_map/share_second/all_to_all | solution.py:57
  95.8 6.6 %collective-permute-start.18 = (bf16[288,1152]{1,0:T(8,128)(2,1)S(1)}, bf16[288,1152]{1,0:T(8,128)(2,1)S(1)}, u32[]{:S(2)}, u32[]{:S(2)}) collective-permute-start(bf16[288,1152]{1,0:T(8,128)(2,1)S(1)} %bitcast.16), channel_id=1, source_target_pairs={{0,1},{1,0},{2,3},{3,2},{4,5},{5,4},{6,7},{7,6},{8,9},{9,8},{10,11... | collective-permute-start | bytes 1990664 | tf_op jit(solution)/shard_map/share_first/ppermute | solution.py:53
  102.4 0.1 fusion
  102.4 0.4 collective-permute-start.14
  102.8 2.4 %collective-permute-start.15 = (bf16[144,1152]{1,0:T(8,128)(2,1)S(1)}, bf16[144,1152]{1,0:T(8,128)(2,1)S(1)}, u32[]{:S(2)}, u32[]{:S(2)}) collective-permute-start(bf16[144,1152]{1,0:T(8,128)(2,1)S(1)} %bitcast.23), channel_id=1, source_target_pairs={{0,48},{1,193},{2,50},{3,195},{4,52},{5,197},{6,54},{7,199},{8,56}... | collective-permute-start | bytes 995336 | tf_op jit(solution)/shard_map/share_first/ppermute | solution.py:53
  105.2 0.0 collective-permute-start.17
  105.2 1.4 %collective-permute-start.16 = (bf16[144,1152]{1,0:T(8,128)(2,1)S(1)}, bf16[144,1152]{1,0:T(8,128)(2,1)S(1)}, u32[]{:S(2)}, u32[]{:S(2)}) collective-permute-start(bf16[144,1152]{1,0:T(8,128)(2,1)S(1)} %bitcast.24), channel_id=1, source_target_pairs={{0,16},{1,65},{2,18},{3,67},{4,20},{5,69},{6,22},{7,71},{8,24},{9,... | collective-permute-start | bytes 995336 | tf_op jit(solution)/shard_map/share_first/ppermute | solution.py:53
  106.7 3.3 %collective-permute-done.14.refs_1_ = bf16[144,1152]{1,0:T(8,128)(2,1)S(1)} collective-permute-done((bf16[144,1152]{1,0:T(8,128)(2,1)S(1)}, bf16[144,1152]{1,0:T(8,128)(2,1)S(1)}, u32[]{:S(2)}, u32[]{:S(2)}) %collective-permute-start.14) | collective-permute-done | bytes 331808 | tf_op jit(solution)/shard_map/share_first/ppermute | solution.py:53
  110.0 0.0 collective-permute-start.19
  110.0 0.0 collective-permute-done.15.refs_2_
  110.0 2.7 %collective-permute-start.20 = (bf16[144,1152]{1,0:T(8,128)(2,1)S(1)}, bf16[144,1152]{1,0:T(8,128)(2,1)S(1)}, u32[]{:S(2)}, u32[]{:S(2)}) collective-permute-start(bf16[144,1152]{1,0:T(8,128)(2,1)S(1)} %collective-permute-done.15.refs_2_), channel_id=1, source_target_pairs={{0,48},{1,193},{2,50},{3,195},{4,52},{5,197},{6,54},{7,199},{8,56}... | collective-permute-start | bytes 995336 | tf_op jit(solution)/shard_map/share_first/ppermute | solution.py:53
  112.7 0.1 collective-permute-done.17.refs_4_
  112.8 1.3 %collective-permute-start.24 = (bf16[144,1152]{1,0:T(8,128)(2,1)S(1)}, bf16[144,1152]{1,0:T(8,128)(2,1)S(1)}, u32[]{:S(2)}, u32[]{:S(2)}) collective-permute-start(bf16[144,1152]{1,0:T(8,128)(2,1)S(1)} %collective-permute-done.17.refs_4_), channel_id=1, source_target_pairs={{0,1},{1,0},{2,3},{3,2},{4,5},{5,4},{6,7},{7,6},{8,9},{9,8},{10,11... | collective-permute-start | bytes 995336 | tf_op jit(solution)/shard_map/share_first/ppermute | solution.py:53
  114.1 0.0 collective-permute-done.16.refs_3_
  114.1 1.7 %collective-permute-start.21 = (bf16[144,1152]{1,0:T(8,128)(2,1)S(1)}, bf16[144,1152]{1,0:T(8,128)(2,1)S(1)}, u32[]{:S(2)}, u32[]{:S(2)}) collective-permute-start(bf16[144,1152]{1,0:T(8,128)(2,1)S(1)} %collective-permute-done.14.refs_1_), channel_id=1, source_target_pairs={{0,1},{1,0},{2,3},{3,2},{4,5},{5,4},{6,7},{7,6},{8,9},{9,8},{10,11... | collective-permute-start | bytes 995336 | tf_op jit(solution)/shard_map/share_first/ppermute | solution.py:53
  115.8 0.0 collective-permute-start.23
  115.8 1.5 %write.5 = (bf16[1152,1152]{1,0:T(8,128)(2,1)}, bf16[1152,1152]{1,0:T(8,128)(2,1)}) custom-call(bf16[288,1152]{1,0:T(8,128)(2,1)S(1)} %bitcast.17, bf16[144,1152]{1,0:T(8,128)(2,1)S(1)} %collective-permute-done.14.refs_1_, bf16[144,1152]{1,0:T(8,128)(2,1)S(1)} %collective-permute-done.15.refs_2_, bf16[144,1152]{1,0:T(8,128)(2,1)S(1)} %collective-permute-done.16.refs_3_, ...), custom_call_target="tpu_custom_call" | custom-call | tf_op jit(solution)/shard_map/write/pallas_call | solution.py:69
  117.3 0.1 collective-permute-done.19.refs_1_
  117.5 1.9 %collective-permute-start.22 = (bf16[144,1152]{1,0:T(8,128)(2,1)S(1)}, bf16[144,1152]{1,0:T(8,128)(2,1)S(1)}, u32[]{:S(2)}, u32[]{:S(2)}) collective-permute-start(bf16[144,1152]{1,0:T(8,128)(2,1)S(1)} %collective-permute-done.15.refs_2_), channel_id=1, source_target_pairs={{0,1},{1,0},{2,3},{3,2},{4,5},{5,4},{6,7},{7,6},{8,9},{9,8},{10,11... | collective-permute-start | bytes 995336 | tf_op jit(solution)/shard_map/share_first/ppermute | solution.py:53
  119.3 0.0 collective-permute-done.20.refs_1_
  119.3 0.1 collective-permute-start.25
  119.4 0.4 collective-permute-start.26
  119.9 0.7 collective-permute-done.22.refs_5_
  120.6 1.3 %write.8 = (bf16[1152,1152]{1,0:T(8,128)(2,1)}, bf16[1152,1152]{1,0:T(8,128)(2,1)}) custom-call(bf16[1152,1152]{1,0:T(8,128)(2,1)} %get-tuple-element.50.refs_0_, bf16[1152,1152]{1,0:T(8,128)(2,1)} %get-tuple-element.51.refs_1_, bf16[144,1152]{1,0:T(8,128)(2,1)S(1)} %write.6.refs_2_, ...), custom_call_target="tpu_custom_call", output_to_operand_aliasing={{0}: (0, {}), {1}: (1, {})} | custom-call | tf_op jit(solution)/shard_map/write/pallas_call | solution.py:69
  121.9 0.0 collective-permute-done.26.refs_3_
  121.9 0.9 write.9
  (16 shorter events, 0.2 us)
Async XLA Ops:
  1.6 13.2 %collective-permute-start.4 = (bf16[144,1152]{1,0:T(8,128)(2,1)S(1)}, bf16[144,1152]{1,0:T(8,128)(2,1)S(1)}, u32[]{:S(2)}, u32[]{:S(2)}) collective-permute-start(bf16[144,1152]{1,0:T(8,128)(2,1)S(1)} %band_exchange.1.image_own), channel_id=1, source_target_pairs={{0,1},{1,0},{2,3},{3,2},{4,5},{5,4},{6,7},{7,6},{8,9},{9,8},{10,11... | collective-permute-start | bytes 995336 | tf_op jit(solution)/shard_map/band_exchange/ppermute | solution.py:53
  5.0 9.9 %collective-permute-start.3 = (bf16[128,1152]{1,0:T(8,128)(2,1)}, bf16[128,1152]{1,0:T(8,128)(2,1)S(1)}, u32[]{:S(2)}, u32[]{:S(2)}) collective-permute-start(bf16[128,1152]{1,0:T(8,128)(2,1)} %text_hbm.1), channel_id=1, source_target_pairs={{0,1},{1,0},{2,3},{3,2},{4,5},{5,4},{6,7},{7,6},{8,9},{9,8},{10,11... | collective-permute-start | bytes 884744 | tf_op jit(solution)/shard_map/band_exchange/ppermute | solution.py:53
  5.1 15.7 %collective-permute-start.2 = (bf16[128,1152]{1,0:T(8,128)(2,1)}, bf16[128,1152]{1,0:T(8,128)(2,1)S(1)}, u32[]{:S(2)}, u32[]{:S(2)}) collective-permute-start(bf16[128,1152]{1,0:T(8,128)(2,1)} %text_hbm.1), channel_id=1, source_target_pairs={{0,2},{1,3},{2,4},{3,5},{4,6},{5,7},{6,8},{7,9},{8,10},{9,11},{10,... | collective-permute-start | bytes 884744 | tf_op jit(solution)/shard_map/band_exchange/ppermute | solution.py:53
  5.1 17.9 %collective-permute-start.1 = (bf16[128,1152]{1,0:T(8,128)(2,1)}, bf16[128,1152]{1,0:T(8,128)(2,1)S(1)}, u32[]{:S(2)}, u32[]{:S(2)}) collective-permute-start(bf16[128,1152]{1,0:T(8,128)(2,1)} %text_hbm.1), channel_id=1, source_target_pairs={{0,254},{1,255},{2,0},{3,1},{4,2},{5,3},{6,4},{7,5},{8,6},{9,7},{1... | collective-permute-start | bytes 884744 | tf_op jit(solution)/shard_map/band_exchange/ppermute | solution.py:53
  13.6 14.5 %collective-permute-start = (bf16[128,1152]{1,0:T(8,128)(2,1)}, bf16[128,1152]{1,0:T(8,128)(2,1)S(1)}, u32[]{:S(2)}, u32[]{:S(2)}) collective-permute-start(bf16[128,1152]{1,0:T(8,128)(2,1)} %text_hbm.1), channel_id=1, source_target_pairs={{0,253},{1,4},{2,255},{3,6},{4,1},{5,8},{6,3},{7,10},{8,5},{9,12},... | collective-permute-start | bytes 884744 | tf_op jit(solution)/shard_map/band_exchange/ppermute | solution.py:53
  23.0 5.4 %collective-permute-start.6 = (bf16[128,1152]{1,0:T(8,128)(2,1)S(1)}, bf16[128,1152]{1,0:T(8,128)(2,1)S(1)}, u32[]{:S(2)}, u32[]{:S(2)}) collective-permute-start(bf16[128,1152]{1,0:T(8,128)(2,1)S(1)} %get-tuple-element.29.below), channel_id=1, source_target_pairs={{0,1},{1,0},{2,3},{3,2},{4,5},{5,4},{6,7},{7,6},{8,9},{9,8},{10,11... | collective-permute-start | bytes 884744 | tf_op jit(solution)/shard_map/swap_neighbours/ppermute | solution.py:53
  24.2 4.1 %collective-permute-start.7 = (bf16[128,1152]{1,0:T(8,128)(2,1)S(1)}, bf16[128,1152]{1,0:T(8,128)(2,1)S(1)}, u32[]{:S(2)}, u32[]{:S(2)}) collective-permute-start(bf16[128,1152]{1,0:T(8,128)(2,1)S(1)} %get-tuple-element.30.above), channel_id=1, source_target_pairs={{0,1},{1,0},{2,3},{3,2},{4,5},{5,4},{6,7},{7,6},{8,9},{9,8},{10,11... | collective-permute-start | bytes 884744 | tf_op jit(solution)/shard_map/swap_neighbours/ppermute | solution.py:53
  28.1 2.4 %collective-permute-start.5 = (bf16[128,1152]{1,0:T(8,128)(2,1)S(1)}, bf16[128,1152]{1,0:T(8,128)(2,1)S(1)}, u32[]{:S(2)}, u32[]{:S(2)}) collective-permute-start(bf16[128,1152]{1,0:T(8,128)(2,1)S(1)} %received.3.far), channel_id=1, source_target_pairs={{0,1},{1,0},{2,3},{3,2},{4,5},{5,4},{6,7},{7,6},{8,9},{9,8},{10,11... | collective-permute-start | bytes 884744 | tf_op jit(solution)/shard_map/received/ppermute | solution.py:53
  34.8 7.6 %collective-permute-start.8 = (bf16[144,1152]{1,0:T(8,128)(2,1)S(1)}, bf16[144,1152]{1,0:T(8,128)(2,1)S(1)}, u32[]{:S(2)}, u32[]{:S(2)}) collective-permute-start(bf16[144,1152]{1,0:T(8,128)(2,1)S(1)} %get-tuple-element.45), channel_id=1, source_target_pairs={{0,16},{1,65},{2,18},{3,67},{4,20},{5,69},{6,22},{7,71},{8,24},{9,... | collective-permute-start | bytes 995336 | tf_op jit(solution)/shard_map/sum_first/ppermute | solution.py:53
  34.9 7.6 %collective-permute-start.12 = (bf16[144,1152]{1,0:T(8,128)(2,1)S(1)}, bf16[144,1152]{1,0:T(8,128)(2,1)S(1)}, u32[]{:S(2)}, u32[]{:S(2)}) collective-permute-start(bf16[144,1152]{1,0:T(8,128)(2,1)S(1)} %get-tuple-element.49), channel_id=1, source_target_pairs={{0,48},{1,193},{2,50},{3,195},{4,52},{5,197},{6,54},{7,199},{8,56}... | collective-permute-start | bytes 995336 | tf_op jit(solution)/shard_map/sum_first/ppermute | solution.py:53
  37.6 8.4 %collective-permute-start.10 = (bf16[144,1152]{1,0:T(8,128)(2,1)S(1)}, bf16[144,1152]{1,0:T(8,128)(2,1)S(1)}, u32[]{:S(2)}, u32[]{:S(2)}) collective-permute-start(bf16[144,1152]{1,0:T(8,128)(2,1)S(1)} %get-tuple-element.46), channel_id=1, source_target_pairs={{0,16},{1,65},{2,18},{3,67},{4,20},{5,69},{6,22},{7,71},{8,24},{9,... | collective-permute-start | bytes 995336 | tf_op jit(solution)/shard_map/sum_first/ppermute | solution.py:53
  37.6 8.4 %collective-permute-start.11 = (bf16[144,1152]{1,0:T(8,128)(2,1)S(1)}, bf16[144,1152]{1,0:T(8,128)(2,1)S(1)}, u32[]{:S(2)}, u32[]{:S(2)}) collective-permute-start(bf16[144,1152]{1,0:T(8,128)(2,1)S(1)} %get-tuple-element.47), channel_id=1, source_target_pairs={{0,48},{1,193},{2,50},{3,195},{4,52},{5,197},{6,54},{7,199},{8,56}... | collective-permute-start | bytes 995336 | tf_op jit(solution)/shard_map/sum_first/ppermute | solution.py:53
  42.4 7.6 %collective-permute-start.9 = (bf16[144,1152]{1,0:T(8,128)(2,1)S(1)}, bf16[144,1152]{1,0:T(8,128)(2,1)S(1)}, u32[]{:S(2)}, u32[]{:S(2)}) collective-permute-start(bf16[144,1152]{1,0:T(8,128)(2,1)S(1)} %sum_first.3), channel_id=1, source_target_pairs={{0,16},{1,65},{2,18},{3,67},{4,20},{5,69},{6,22},{7,71},{8,24},{9,... | collective-permute-start | bytes 995336 | tf_op jit(solution)/shard_map/sum_first/ppermute | solution.py:53
  42.6 7.4 %collective-permute-start.13 = (bf16[144,1152]{1,0:T(8,128)(2,1)S(1)}, bf16[144,1152]{1,0:T(8,128)(2,1)S(1)}, u32[]{:S(2)}, u32[]{:S(2)}) collective-permute-start(bf16[144,1152]{1,0:T(8,128)(2,1)S(1)} %sum_first.4), channel_id=1, source_target_pairs={{0,48},{1,193},{2,50},{3,195},{4,52},{5,197},{6,54},{7,199},{8,56}... | collective-permute-start | bytes 995336 | tf_op jit(solution)/shard_map/sum_first/ppermute | solution.py:53
  95.8 20.0 %collective-permute-start.18 = (bf16[288,1152]{1,0:T(8,128)(2,1)S(1)}, bf16[288,1152]{1,0:T(8,128)(2,1)S(1)}, u32[]{:S(2)}, u32[]{:S(2)}) collective-permute-start(bf16[288,1152]{1,0:T(8,128)(2,1)S(1)} %bitcast.16), channel_id=1, source_target_pairs={{0,1},{1,0},{2,3},{3,2},{4,5},{5,4},{6,7},{7,6},{8,9},{9,8},{10,11... | collective-permute-start | bytes 1990664 | tf_op jit(solution)/shard_map/share_first/ppermute | solution.py:53
  102.4 7.6 %collective-permute-start.14 = (bf16[144,1152]{1,0:T(8,128)(2,1)S(1)}, bf16[144,1152]{1,0:T(8,128)(2,1)S(1)}, u32[]{:S(2)}, u32[]{:S(2)}) collective-permute-start(bf16[144,1152]{1,0:T(8,128)(2,1)S(1)} %bitcast.25), channel_id=1, source_target_pairs={{0,16},{1,65},{2,18},{3,67},{4,20},{5,69},{6,22},{7,71},{8,24},{9,... | collective-permute-start | bytes 995336 | tf_op jit(solution)/shard_map/share_first/ppermute | solution.py:53
  102.8 7.2 %collective-permute-start.15 = (bf16[144,1152]{1,0:T(8,128)(2,1)S(1)}, bf16[144,1152]{1,0:T(8,128)(2,1)S(1)}, u32[]{:S(2)}, u32[]{:S(2)}) collective-permute-start(bf16[144,1152]{1,0:T(8,128)(2,1)S(1)} %bitcast.23), channel_id=1, source_target_pairs={{0,48},{1,193},{2,50},{3,195},{4,52},{5,197},{6,54},{7,199},{8,56}... | collective-permute-start | bytes 995336 | tf_op jit(solution)/shard_map/share_first/ppermute | solution.py:53
  105.2 7.6 %collective-permute-start.17 = (bf16[144,1152]{1,0:T(8,128)(2,1)S(1)}, bf16[144,1152]{1,0:T(8,128)(2,1)S(1)}, u32[]{:S(2)}, u32[]{:S(2)}) collective-permute-start(bf16[144,1152]{1,0:T(8,128)(2,1)S(1)} %bitcast.26), channel_id=1, source_target_pairs={{0,48},{1,193},{2,50},{3,195},{4,52},{5,197},{6,54},{7,199},{8,56}... | collective-permute-start | bytes 995336 | tf_op jit(solution)/shard_map/share_first/ppermute | solution.py:53
  105.2 8.9 %collective-permute-start.16 = (bf16[144,1152]{1,0:T(8,128)(2,1)S(1)}, bf16[144,1152]{1,0:T(8,128)(2,1)S(1)}, u32[]{:S(2)}, u32[]{:S(2)}) collective-permute-start(bf16[144,1152]{1,0:T(8,128)(2,1)S(1)} %bitcast.24), channel_id=1, source_target_pairs={{0,16},{1,65},{2,18},{3,67},{4,20},{5,69},{6,22},{7,71},{8,24},{9,... | collective-permute-start | bytes 995336 | tf_op jit(solution)/shard_map/share_first/ppermute | solution.py:53
  110.0 7.5 %collective-permute-start.19 = (bf16[144,1152]{1,0:T(8,128)(2,1)S(1)}, bf16[144,1152]{1,0:T(8,128)(2,1)S(1)}, u32[]{:S(2)}, u32[]{:S(2)}) collective-permute-start(bf16[144,1152]{1,0:T(8,128)(2,1)S(1)} %collective-permute-done.14.refs_1_), channel_id=1, source_target_pairs={{0,16},{1,65},{2,18},{3,67},{4,20},{5,69},{6,22},{7,71},{8,24},{9,... | collective-permute-start | bytes 995336 | tf_op jit(solution)/shard_map/share_first/ppermute | solution.py:53
  110.0 9.3 %collective-permute-start.20 = (bf16[144,1152]{1,0:T(8,128)(2,1)S(1)}, bf16[144,1152]{1,0:T(8,128)(2,1)S(1)}, u32[]{:S(2)}, u32[]{:S(2)}) collective-permute-start(bf16[144,1152]{1,0:T(8,128)(2,1)S(1)} %collective-permute-done.15.refs_2_), channel_id=1, source_target_pairs={{0,48},{1,193},{2,50},{3,195},{4,52},{5,197},{6,54},{7,199},{8,56}... | collective-permute-start | bytes 995336 | tf_op jit(solution)/shard_map/share_first/ppermute | solution.py:53
  112.8 6.6 %collective-permute-start.24 = (bf16[144,1152]{1,0:T(8,128)(2,1)S(1)}, bf16[144,1152]{1,0:T(8,128)(2,1)S(1)}, u32[]{:S(2)}, u32[]{:S(2)}) collective-permute-start(bf16[144,1152]{1,0:T(8,128)(2,1)S(1)} %collective-permute-done.17.refs_4_), channel_id=1, source_target_pairs={{0,1},{1,0},{2,3},{3,2},{4,5},{5,4},{6,7},{7,6},{8,9},{9,8},{10,11... | collective-permute-start | bytes 995336 | tf_op jit(solution)/shard_map/share_first/ppermute | solution.py:53
  114.1 5.8 %collective-permute-start.21 = (bf16[144,1152]{1,0:T(8,128)(2,1)S(1)}, bf16[144,1152]{1,0:T(8,128)(2,1)S(1)}, u32[]{:S(2)}, u32[]{:S(2)}) collective-permute-start(bf16[144,1152]{1,0:T(8,128)(2,1)S(1)} %collective-permute-done.14.refs_1_), channel_id=1, source_target_pairs={{0,1},{1,0},{2,3},{3,2},{4,5},{5,4},{6,7},{7,6},{8,9},{9,8},{10,11... | collective-permute-start | bytes 995336 | tf_op jit(solution)/shard_map/share_first/ppermute | solution.py:53
  115.8 4.1 %collective-permute-start.23 = (bf16[144,1152]{1,0:T(8,128)(2,1)S(1)}, bf16[144,1152]{1,0:T(8,128)(2,1)S(1)}, u32[]{:S(2)}, u32[]{:S(2)}) collective-permute-start(bf16[144,1152]{1,0:T(8,128)(2,1)S(1)} %collective-permute-done.16.refs_3_), channel_id=1, source_target_pairs={{0,1},{1,0},{2,3},{3,2},{4,5},{5,4},{6,7},{7,6},{8,9},{9,8},{10,11... | collective-permute-start | bytes 995336 | tf_op jit(solution)/shard_map/share_first/ppermute | solution.py:53
  117.5 3.1 %collective-permute-start.22 = (bf16[144,1152]{1,0:T(8,128)(2,1)S(1)}, bf16[144,1152]{1,0:T(8,128)(2,1)S(1)}, u32[]{:S(2)}, u32[]{:S(2)}) collective-permute-start(bf16[144,1152]{1,0:T(8,128)(2,1)S(1)} %collective-permute-done.15.refs_2_), channel_id=1, source_target_pairs={{0,1},{1,0},{2,3},{3,2},{4,5},{5,4},{6,7},{7,6},{8,9},{9,8},{10,11... | collective-permute-start | bytes 995336 | tf_op jit(solution)/shard_map/share_first/ppermute | solution.py:53
  119.3 2.6 %collective-permute-start.25 = (bf16[144,1152]{1,0:T(8,128)(2,1)S(1)}, bf16[144,1152]{1,0:T(8,128)(2,1)S(1)}, u32[]{:S(2)}, u32[]{:S(2)}) collective-permute-start(bf16[144,1152]{1,0:T(8,128)(2,1)S(1)} %write.6.refs_2_), channel_id=1, source_target_pairs={{0,1},{1,0},{2,3},{3,2},{4,5},{5,4},{6,7},{7,6},{8,9},{9,8},{10,11... | collective-permute-start | bytes 995336 | tf_op jit(solution)/shard_map/write/ppermute | solution.py:53
  119.4 2.5 %collective-permute-start.26 = (bf16[144,1152]{1,0:T(8,128)(2,1)S(1)}, bf16[144,1152]{1,0:T(8,128)(2,1)S(1)}, u32[]{:S(2)}, u32[]{:S(2)}) collective-permute-start(bf16[144,1152]{1,0:T(8,128)(2,1)S(1)} %write.7.refs_3_), channel_id=1, source_target_pairs={{0,1},{1,0},{2,3},{3,2},{4,5},{5,4},{6,7},{7,6},{8,9},{9,8},{10,11... | collective-permute-start | bytes 995336 | tf_op jit(solution)/shard_map/write/ppermute | solution.py:53

commit v12 on v7

--- a/solution.py
+++ b/solution.py
@@ -113,6 +113,22 @@
         at = pl.ds(k * step, step)
         new = contract(x[:, at], back[...], 0, 0)
         head[at, :] = new if before is None else before[at, :] + new
+
+
+def join_positions(image_hbm, position_hbm, out, position, sems):
+    rows = position.shape[0]
+    moves = [
+        pltpu.make_async_copy(position_hbm, position, sems.at[0]),
+        pltpu.make_async_copy(image_hbm, out.at[pl.ds(0, rows), :], sems.at[1]),
+    ]
+    for move in moves:
+        move.start()
+    tail = pl.ds(rows, TAIL)
+    out[tail, :] = jnp.zeros((TAIL, out.shape[1]), bf16)
+    moves[0].wait()
+    row = position[...].reshape(1, rows).astype(f32)
+    out[tail, pl.ds(0, rows)] = jnp.broadcast_to(row, (TAIL, rows)).astype(bf16)
+    moves[1].wait()
 
 
 def visit(log_scale, shift, x, text_w, image_emb, finish, back, grad, grad_before):
@@ -250,9 +266,8 @@
     own[...] = part(0, 0, slab)
 
 
-def add_kernel(a, b, c, d, ab, cd):
-    ab[...] = (a[...].astype(f32) + b[...].astype(f32)).astype(bf16)
-    cd[...] = (c[...].astype(f32) + d[...].astype(f32)).astype(bf16)
+def add_kernel(a, b, out):
+    out[...] = (a[...].astype(f32) + b[...].astype(f32)).astype(bf16)
 
 
 def join_kernel(own, a_top, a_bottom, b_top, b_bottom, out):
@@ -325,8 +340,11 @@
     piece, half_piece = ((slab, width), bf16), ((half, width), bf16)
     with jax.named_scope("band_exchange"):
         text_other = send(text_x, SWAP)
-        tail = jnp.pad(position.astype(bf16)[None], ((0, TAIL - 1), (0, width - rows)))
-        image_own = jnp.concatenate([image_x, tail])
+        [image_own] = call(
+            join_positions,
+            [((rows + TAIL, width), bf16)],
+            [pltpu.VMEM((rows,), jnp.int32), pltpu.SemaphoreType.DMA((2,))],
+        )((), (image_x, position))
         image_other = send(image_own, SWAP)
         below = send(text_x, shifted(2))
         above = send(text_x, shifted(-2))
@@ -373,9 +391,8 @@
         from_right = send(far_left, LEFT)
         a_bottom = send(right_bottom, RIGHT)
         b_top = send(left_top, LEFT)
-        right_top, left_bottom = call(add_kernel, [half_piece] * 2)(
-            (), (), right_top, from_left, left_bottom, from_right
-        )
+        [right_top] = call(add_kernel, [half_piece])((), (), right_top, from_left)
+        [left_bottom] = call(add_kernel, [half_piece])((), (), left_bottom, from_right)
         a_top = send(right_top, RIGHT)
         b_bottom = send(left_bottom, LEFT)
         [part] = call(join_kernel, [piece])((), (), own, a_top, a_bottom, b_top, b_bottom)

time: 123 us -> 125 us (1.016)
  waiting for transfers between devices: 13.7 us -> 16.4 us
  blocking collectives: 45.2 us -> 46.9 us
  starting transfers between devices: 39.8 us -> 38.1 us
  other arithmetic: 1.78 us -> 0.13 us
    ppermute x27, waiting for transfers between devices: 13.7 us -> 16.4 us  [send(): return lax.ppermute(block, 'dp', pairs)]
    ppermute x27, starting transfers between devices: 39.8 us -> 38.1 us  [send(): return lax.ppermute(block, 'dp', pairs)]
    all_to_all x4, blocking collectives: 45.2 us -> 46.9 us  [exchange(): lax.all_to_all(parts, 'dp', 0, 0, axis_index_groups=members, tiled=True)]
    pallas_call x12 -> x14, Pallas kernels: 19.6 us -> 20.6 us  [run(): pl.pallas_call(body, out_shape=[jax.ShapeDtypeStruct(s, d) for s, d in ou...]
  transfers between devices with their start and end apart: 27 -> 27, of which waited for: 8 -> 9; matrix products, arithmetic and copies ran while one was open for 0% -> 0% of each run, Pallas kernels for 12% -> 12%
where the time goes in v12:
time: 125 us
  blocking collectives  46.9 us (38%)
  starting transfers between devices  38.1 us (30%)
  Pallas kernels  20.6 us (16%)
  waiting for transfers between devices  16.4 us (13%)
  between operations  2.33 us (2%)
    all_to_all x4, blocking collectives, exchange(): lax.all_to_all(parts, 'dp', 0, 0, axis_index_groups=members, tiled=True)  46.9 us
    ppermute x27, starting transfers between devices, send(): return lax.ppermute(block, 'dp', pairs)  38.1 us
    pallas_call x14, Pallas kernels, run(): pl.pallas_call(body, out_shape=[jax.ShapeDtypeStruct(s, d) for s, d in ou...  20.6 us
    ppermute x27, waiting for transfers between devices, send(): return lax.ppermute(block, 'dp', pairs)  16.4 us
  transfers between devices with their start and end apart: 27, of which 9 were waited for; matrix products, arithmetic and copies ran while one was open for 0% of the time, Pallas kernels for 12%

profile of v12, /device:TPU:1, one launch (start us, length us, event | category | flops | bytes accessed | tf_op | source)
XLA Modules:
  0.0 124.7 jit_solution(12693608905074974486)
XLA Ops:
  0.6 1.0 band_exchange.1.image_own
  1.6 3.3 %collective-permute-start.4 = (bf16[144,1152]{1,0:T(8,128)(2,1)S(1)}, bf16[144,1152]{1,0:T(8,128)(2,1)S(1)}, u32[]{:S(2)}, u32[]{:S(2)}) collective-permute-start(bf16[144,1152]{1,0:T(8,128)(2,1)S(1)} %band_exchange.1.image_own), channel_id=1, source_target_pairs={{0,1},{1,0},{2,3},{3,2},{4,5},{5,4},{6,7},{7,6},{8,9},{9,8},{10,11... | collective-permute-start | bytes 995336 | tf_op jit(solution)/shard_map/band_exchange/ppermute | solution.py:53
  5.0 0.1 collective-permute-start.3
  5.1 0.0 collective-permute-start.1
  5.1 8.5 %collective-permute-start.2 = (bf16[128,1152]{1,0:T(8,128)(2,1)}, bf16[128,1152]{1,0:T(8,128)(2,1)S(1)}, u32[]{:S(2)}, u32[]{:S(2)}) collective-permute-start(bf16[128,1152]{1,0:T(8,128)(2,1)} %text_hbm.1), channel_id=1, source_target_pairs={{0,254},{1,255},{2,0},{3,1},{4,2},{5,3},{6,4},{7,5},{8,6},{9,7},{1... | collective-permute-start | bytes 884744 | tf_op jit(solution)/shard_map/band_exchange/ppermute | solution.py:53
  13.6 0.0 collective-permute-start
  14.9 0.0 collective-permute-done.3.text_other
  14.9 0.0 collective-permute-done.4.image_other
  14.9 6.0 %near.1 = (bf16[256,1152]{1,0:T(8,128)(2,1)S(1)}, bf16[1152,1152]{1,0:T(8,128)(2,1)S(1)}, bf16[256,1152]{1,0:T(8,128)(2,1)S(1)}, f32[256,1152]{1,0:T(8,128)S(1)}...) custom-call(f32[1]{0:T(128)S(6)} %copy.27.log_scale, f32[1]{0:T(128)S(6)} %copy.28.shift, ...), custom_call_target="tpu_custom_call" | custom-call | flops 4000000000 | tf_op jit(solution)/shard_map/near/pallas_call | solution.py:69
  20.9 0.0 collective-permute-done.1.refs_0_
  20.9 2.1 %collective-permute-done.2.refs_1_ = bf16[128,1152]{1,0:T(8,128)(2,1)S(1)} collective-permute-done((bf16[128,1152]{1,0:T(8,128)(2,1)}, bf16[128,1152]{1,0:T(8,128)(2,1)S(1)}, u32[]{:S(2)}, u32[]{:S(2)}) %collective-permute-start.2) | collective-permute-done | bytes 294944 | tf_op jit(solution)/shard_map/band_exchange/ppermute | solution.py:53
  23.0 1.2 collective-permute-start.6
  24.2 0.0 collective-permute-start.7
  24.3 3.1 %received.2 = (f32[256,1152]{1,0:T(8,128)S(1)}, f32[1152,1152]{1,0:T(8,128)S(1)}) custom-call(f32[1]{0:T(128)S(6)} %copy.27.log_scale, f32[1]{0:T(128)S(6)} %copy.28.shift, bf16[128,1152]{1,0:T(8,128)(2,1)S(1)} %get-tuple-element.29.below, bf16[128,1152]{1,0:T(8,128)(2,1)S(1)} %get-tuple-element.30.above, bf16[1152,1152]{1,0:T(8,128)(2,1)S(1)} %get-tuple-element.31.text_w, ...), custom_call_target="tpu_custom_call" | custom-call | flops 4000000000 | tf_op jit(solution)/shard_map/received/pallas_call | solution.py:69
  27.3 0.0 collective-permute-done.refs_0_
  27.3 0.3 collective-permute-start.5
  27.6 0.0 collective-permute-done.7.above
  27.6 3.1 %partners.1 = (f32[256,1152]{1,0:T(8,128)S(1)}, f32[1152,1152]{1,0:T(8,128)S(1)}) custom-call(f32[1]{0:T(128)S(6)} %copy.27.log_scale, f32[1]{0:T(128)S(6)} %copy.28.shift, bf16[128,1152]{1,0:T(8,128)(2,1)S(1)} %collective-permute-done.6.below, bf16[128,1152]{1,0:T(8,128)(2,1)S(1)} %collective-permute-done.7.above, ...), custom_call_target="tpu_custom_call" | custom-call | flops 4000000000 | tf_op jit(solution)/shard_map/partners/pallas_call | solution.py:69
  30.7 0.0 collective-permute-done.5.far_other
  30.7 3.4 %far.1 = (bf16[288,1152]{1,0:T(8,128)(2,1)S(1)}, bf16[144,1152]{1,0:T(8,128)(2,1)S(1)}, bf16[144,1152]{1,0:T(8,128)(2,1)S(1)}, bf16[144,1152]{1,0:T(8,128)(2,1)S...) custom-call(f32[1]{0:T(128)S(6)} %copy.27.log_scale, ...), custom_call_target="tpu_custom_call" | custom-call | flops 4000000000 | tf_op jit(solution)/shard_map/far/pallas_call | solution.py:69
  34.1 0.6 collective-permute-start.12
  34.7 1.0 collective-permute-start.8
  35.6 0.0 collective-permute-start.10
  35.7 2.6 %collective-permute-start.11 = (bf16[144,1152]{1,0:T(8,128)(2,1)S(1)}, bf16[144,1152]{1,0:T(8,128)(2,1)S(1)}, u32[]{:S(2)}, u32[]{:S(2)}) collective-permute-start(bf16[144,1152]{1,0:T(8,128)(2,1)S(1)} %get-tuple-element.45), channel_id=1, source_target_pairs={{0,48},{1,193},{2,50},{3,195},{4,52},{5,197},{6,54},{7,199},{8,56}... | collective-permute-start | bytes 995336 | tf_op jit(solution)/shard_map/sum_first/ppermute | solution.py:53
  38.3 2.1 %collective-permute-done.12.b = bf16[144,1152]{1,0:T(8,128)(2,1)S(1)} collective-permute-done((bf16[144,1152]{1,0:T(8,128)(2,1)S(1)}, bf16[144,1152]{1,0:T(8,128)(2,1)S(1)}, u32[]{:S(2)}, u32[]{:S(2)}) %collective-permute-start.12) | collective-permute-done | bytes 331808 | tf_op jit(solution)/shard_map/sum_first/ppermute | solution.py:53
  40.4 0.1 sum_first.4
  40.5 1.8 %collective-permute-start.13 = (bf16[144,1152]{1,0:T(8,128)(2,1)S(1)}, bf16[144,1152]{1,0:T(8,128)(2,1)S(1)}, u32[]{:S(2)}, u32[]{:S(2)}) collective-permute-start(bf16[144,1152]{1,0:T(8,128)(2,1)S(1)} %sum_first.4), channel_id=1, source_target_pairs={{0,48},{1,193},{2,50},{3,195},{4,52},{5,197},{6,54},{7,199},{8,56}... | collective-permute-start | bytes 995336 | tf_op jit(solution)/shard_map/sum_first/ppermute | solution.py:53
  42.3 0.1 sum_first.3
  42.4 0.1 collective-permute-start.9
  42.5 3.1 %collective-permute-done.10.a_bottom = bf16[144,1152]{1,0:T(8,128)(2,1)S(1)} collective-permute-done((bf16[144,1152]{1,0:T(8,128)(2,1)S(1)}, bf16[144,1152]{1,0:T(8,128)(2,1)S(1)}, u32[]{:S(2)}, u32[]{:S(2)}) %collective-permute-start.10) | collective-permute-done | bytes 331808 | tf_op jit(solution)/shard_map/sum_first/ppermute | solution.py:53
  45.6 0.0 collective-permute-done.11.b_top
  45.6 2.0 %collective-permute-done.13.b_bottom = bf16[144,1152]{1,0:T(8,128)(2,1)S(1)} collective-permute-done((bf16[144,1152]{1,0:T(8,128)(2,1)S(1)}, bf16[144,1152]{1,0:T(8,128)(2,1)S(1)}, u32[]{:S(2)}, u32[]{:S(2)}) %collective-permute-start.13) | collective-permute-done | bytes 331808 | tf_op jit(solution)/shard_map/sum_first/ppermute | solution.py:53
  47.5 2.4 %collective-permute-done.9.a_top = bf16[144,1152]{1,0:T(8,128)(2,1)S(1)} collective-permute-done((bf16[144,1152]{1,0:T(8,128)(2,1)S(1)}, bf16[144,1152]{1,0:T(8,128)(2,1)S(1)}, u32[]{:S(2)}, u32[]{:S(2)}) %collective-permute-start.9) | collective-permute-done | bytes 331808 | tf_op jit(solution)/shard_map/sum_first/ppermute | solution.py:53
  49.9 0.2 sum_first.5
  50.2 10.6 %all_to_all.20 = bf16[4,72,1152]{2,1,0:T(8,128)(2,1)S(1)} all-to-all(bf16[4,72,1152]{2,1,0:T(8,128)(2,1)S(1)} %bitcast.18), channel_id=1, replica_groups={{0,64,128,192},{1,17,33,49},{2,66,130,194},{3,19,35,51},{4,68,132,196},..., dimensions={0} | all-to-all | bytes 1327104 | tf_op jit(solution)/shard_map/sum_second/all_to_all | solution.py:57
  60.8 0.1 reduce_sum.24
  60.9 15.4 %all_to_all.21 = bf16[88,8,128]{2,1,0:T(8,128)(2,1)S(1)} all-to-all(bf16[88,8,128]{2,1,0:T(8,128)(2,1)S(1)} %concatenate.3), channel_id=1, replica_groups={{0,2,4,6,8,10,12,14},{1,3,5,7,9,11,13,15},{16,18,20,22,24,26,28,30},{17..., dimensions={0} | all-to-all | bytes 360448 | tf_op jit(solution)/shard_map/sum_lines/all_to_all | solution.py:57
  76.3 10.8 %all_to_all.22 = bf16[88,8,128]{2,1,0:T(8,128)(2,1)S(1)} all-to-all(bf16[88,8,128]{2,1,0:T(8,128)(2,1)S(1)} %bitcast.20), channel_id=1, replica_groups={{0,2,4,6,8,10,12,14},{1,3,5,7,9,11,13,15},{16,18,20,22,24,26,28,30},{17..., dimensions={0} | all-to-all | bytes 360448 | tf_op jit(solution)/shard_map/share_lines/all_to_all | solution.py:57
  87.3 10.1 %all_to_all.23 = bf16[4,72,1152]{2,1,0:T(8,128)(2,1)S(1)} all-to-all(bf16[4,72,1152]{2,1,0:T(8,128)(2,1)S(1)} %tile.20), channel_id=1, replica_groups={{0,64,128,192},{1,17,33,49},{2,66,130,194},{3,19,35,51},{4,68,132,196},..., dimensions={0} | all-to-all | bytes 1327104 | tf_op jit(solution)/shard_map/share_second/all_to_all | solution.py:57
  97.4 6.9 %collective-permute-start.18 = (bf16[288,1152]{1,0:T(8,128)(2,1)S(1)}, bf16[288,1152]{1,0:T(8,128)(2,1)S(1)}, u32[]{:S(2)}, u32[]{:S(2)}) collective-permute-start(bf16[288,1152]{1,0:T(8,128)(2,1)S(1)} %bitcast.16), channel_id=1, source_target_pairs={{0,1},{1,0},{2,3},{3,2},{4,5},{5,4},{6,7},{7,6},{8,9},{9,8},{10,11... | collective-permute-start | bytes 1990664 | tf_op jit(solution)/shard_map/share_first/ppermute | solution.py:53
  104.2 0.1 fusion
  104.3 0.4 collective-permute-start.14
  104.7 2.4 %collective-permute-start.15 = (bf16[144,1152]{1,0:T(8,128)(2,1)S(1)}, bf16[144,1152]{1,0:T(8,128)(2,1)S(1)}, u32[]{:S(2)}, u32[]{:S(2)}) collective-permute-start(bf16[144,1152]{1,0:T(8,128)(2,1)S(1)} %bitcast.25), channel_id=1, source_target_pairs={{0,48},{1,193},{2,50},{3,195},{4,52},{5,197},{6,54},{7,199},{8,56}... | collective-permute-start | bytes 995336 | tf_op jit(solution)/shard_map/share_first/ppermute | solution.py:53
  107.1 2.7 %collective-permute-start.17 = (bf16[144,1152]{1,0:T(8,128)(2,1)S(1)}, bf16[144,1152]{1,0:T(8,128)(2,1)S(1)}, u32[]{:S(2)}, u32[]{:S(2)}) collective-permute-start(bf16[144,1152]{1,0:T(8,128)(2,1)S(1)} %bitcast.24), channel_id=1, source_target_pairs={{0,48},{1,193},{2,50},{3,195},{4,52},{5,197},{6,54},{7,199},{8,56}... | collective-permute-start | bytes 995336 | tf_op jit(solution)/shard_map/share_first/ppermute | solution.py:53
  109.7 2.1 %collective-permute-done.14.refs_1_ = bf16[144,1152]{1,0:T(8,128)(2,1)S(1)} collective-permute-done((bf16[144,1152]{1,0:T(8,128)(2,1)S(1)}, bf16[144,1152]{1,0:T(8,128)(2,1)S(1)}, u32[]{:S(2)}, u32[]{:S(2)}) %collective-permute-start.14) | collective-permute-done | bytes 331808 | tf_op jit(solution)/shard_map/share_first/ppermute | solution.py:53
  111.8 0.0 collective-permute-start.19
  111.9 0.0 collective-permute-done.15.refs_2_
  111.9 2.7 %collective-permute-start.20 = (bf16[144,1152]{1,0:T(8,128)(2,1)S(1)}, bf16[144,1152]{1,0:T(8,128)(2,1)S(1)}, u32[]{:S(2)}, u32[]{:S(2)}) collective-permute-start(bf16[144,1152]{1,0:T(8,128)(2,1)S(1)} %collective-permute-done.15.refs_2_), channel_id=1, source_target_pairs={{0,48},{1,193},{2,50},{3,195},{4,52},{5,197},{6,54},{7,199},{8,56}... | collective-permute-start | bytes 995336 | tf_op jit(solution)/shard_map/share_first/ppermute | solution.py:53
  114.5 0.9 collective-permute-done.16.refs_3_
  115.4 0.9 collective-permute-start.21
  116.3 0.0 collective-permute-done.17.refs_4_
  116.3 0.0 collective-permute-start.22
  116.3 0.0 collective-permute-done.18.refs_5_
  116.3 0.5 collective-permute-start.23
  116.8 1.5 %write.4 = (bf16[1152,1152]{1,0:T(8,128)(2,1)}, bf16[1152,1152]{1,0:T(8,128)(2,1)}) custom-call(bf16[288,1152]{1,0:T(8,128)(2,1)S(1)} %bitcast.17, bf16[144,1152]{1,0:T(8,128)(2,1)S(1)} %collective-permute-done.14.refs_1_, bf16[144,1152]{1,0:T(8,128)(2,1)S(1)} %collective-permute-done.15.refs_2_, bf16[144,1152]{1,0:T(8,128)(2,1)S(1)} %collective-permute-done.16.refs_3_, ...), custom_call_target="tpu_custom_call" | custom-call | tf_op jit(solution)/shard_map/write/pallas_call | solution.py:69
  118.3 1.0 collective-permute-done.19.refs_1_
  119.3 1.7 %collective-permute-start.24 = (bf16[144,1152]{1,0:T(8,128)(2,1)S(1)}, bf16[144,1152]{1,0:T(8,128)(2,1)S(1)}, u32[]{:S(2)}, u32[]{:S(2)}) collective-permute-start(bf16[144,1152]{1,0:T(8,128)(2,1)S(1)} %collective-permute-done.17.refs_4_), channel_id=1, source_target_pairs={{0,1},{1,0},{2,3},{3,2},{4,5},{5,4},{6,7},{7,6},{8,9},{9,8},{10,11... | collective-permute-start | bytes 995336 | tf_op jit(solution)/shard_map/share_first/ppermute | solution.py:53
  121.0 0.0 collective-permute-done.20.refs_2_
  121.0 0.1 collective-permute-start.25
  121.1 0.4 collective-permute-start.26
  121.6 0.7 collective-permute-done.24.refs_7_
  122.3 1.3 %write.6 = (bf16[1152,1152]{1,0:T(8,128)(2,1)}, bf16[1152,1152]{1,0:T(8,128)(2,1)}) custom-call(bf16[1152,1152]{1,0:T(8,128)(2,1)} %get-tuple-element.48.refs_0_, bf16[1152,1152]{1,0:T(8,128)(2,1)} %get-tuple-element.49.refs_1_, bf16[144,1152]{1,0:T(8,128)(2,1)S(1)} %get-tuple-element.50.refs_2_, ...), custom_call_target="tpu_custom_call", output_to_operand_aliasing={{0}: (0, {}), {1}: (1, {})} | custom-call | tf_op jit(solution)/shard_map/write/pallas_call | solution.py:69
  123.6 0.0 collective-permute-done.25.refs_2_
  123.7 0.9 write.7
  (15 shorter events, 0.2 us)
Async XLA Ops:
  1.6 13.2 %collective-permute-start.4 = (bf16[144,1152]{1,0:T(8,128)(2,1)S(1)}, bf16[144,1152]{1,0:T(8,128)(2,1)S(1)}, u32[]{:S(2)}, u32[]{:S(2)}) collective-permute-start(bf16[144,1152]{1,0:T(8,128)(2,1)S(1)} %band_exchange.1.image_own), channel_id=1, source_target_pairs={{0,1},{1,0},{2,3},{3,2},{4,5},{5,4},{6,7},{7,6},{8,9},{9,8},{10,11... | collective-permute-start | bytes 995336 | tf_op jit(solution)/shard_map/band_exchange/ppermute | solution.py:53
  5.0 9.9 %collective-permute-start.3 = (bf16[128,1152]{1,0:T(8,128)(2,1)}, bf16[128,1152]{1,0:T(8,128)(2,1)S(1)}, u32[]{:S(2)}, u32[]{:S(2)}) collective-permute-start(bf16[128,1152]{1,0:T(8,128)(2,1)} %text_hbm.1), channel_id=1, source_target_pairs={{0,1},{1,0},{2,3},{3,2},{4,5},{5,4},{6,7},{7,6},{8,9},{9,8},{10,11... | collective-permute-start | bytes 884744 | tf_op jit(solution)/shard_map/band_exchange/ppermute | solution.py:53
  5.1 15.8 %collective-permute-start.1 = (bf16[128,1152]{1,0:T(8,128)(2,1)}, bf16[128,1152]{1,0:T(8,128)(2,1)S(1)}, u32[]{:S(2)}, u32[]{:S(2)}) collective-permute-start(bf16[128,1152]{1,0:T(8,128)(2,1)} %text_hbm.1), channel_id=1, source_target_pairs={{0,2},{1,3},{2,4},{3,5},{4,6},{5,7},{6,8},{7,9},{8,10},{9,11},{10,... | collective-permute-start | bytes 884744 | tf_op jit(solution)/shard_map/band_exchange/ppermute | solution.py:53
  5.1 17.9 %collective-permute-start.2 = (bf16[128,1152]{1,0:T(8,128)(2,1)}, bf16[128,1152]{1,0:T(8,128)(2,1)S(1)}, u32[]{:S(2)}, u32[]{:S(2)}) collective-permute-start(bf16[128,1152]{1,0:T(8,128)(2,1)} %text_hbm.1), channel_id=1, source_target_pairs={{0,254},{1,255},{2,0},{3,1},{4,2},{5,3},{6,4},{7,5},{8,6},{9,7},{1... | collective-permute-start | bytes 884744 | tf_op jit(solution)/shard_map/band_exchange/ppermute | solution.py:53
  13.6 13.8 %collective-permute-start = (bf16[128,1152]{1,0:T(8,128)(2,1)}, bf16[128,1152]{1,0:T(8,128)(2,1)S(1)}, u32[]{:S(2)}, u32[]{:S(2)}) collective-permute-start(bf16[128,1152]{1,0:T(8,128)(2,1)} %text_hbm.1), channel_id=1, source_target_pairs={{0,253},{1,4},{2,255},{3,6},{4,1},{5,8},{6,3},{7,10},{8,5},{9,12},... | collective-permute-start | bytes 884744 | tf_op jit(solution)/shard_map/band_exchange/ppermute | solution.py:53
  23.0 4.6 %collective-permute-start.6 = (bf16[128,1152]{1,0:T(8,128)(2,1)S(1)}, bf16[128,1152]{1,0:T(8,128)(2,1)S(1)}, u32[]{:S(2)}, u32[]{:S(2)}) collective-permute-start(bf16[128,1152]{1,0:T(8,128)(2,1)S(1)} %get-tuple-element.29.below), channel_id=1, source_target_pairs={{0,1},{1,0},{2,3},{3,2},{4,5},{5,4},{6,7},{7,6},{8,9},{9,8},{10,11... | collective-permute-start | bytes 884744 | tf_op jit(solution)/shard_map/swap_neighbours/ppermute | solution.py:53
  24.2 3.4 %collective-permute-start.7 = (bf16[128,1152]{1,0:T(8,128)(2,1)S(1)}, bf16[128,1152]{1,0:T(8,128)(2,1)S(1)}, u32[]{:S(2)}, u32[]{:S(2)}) collective-permute-start(bf16[128,1152]{1,0:T(8,128)(2,1)S(1)} %get-tuple-element.30.above), channel_id=1, source_target_pairs={{0,1},{1,0},{2,3},{3,2},{4,5},{5,4},{6,7},{7,6},{8,9},{9,8},{10,11... | collective-permute-start | bytes 884744 | tf_op jit(solution)/shard_map/swap_neighbours/ppermute | solution.py:53
  27.3 3.4 %collective-permute-start.5 = (bf16[128,1152]{1,0:T(8,128)(2,1)S(1)}, bf16[128,1152]{1,0:T(8,128)(2,1)S(1)}, u32[]{:S(2)}, u32[]{:S(2)}) collective-permute-start(bf16[128,1152]{1,0:T(8,128)(2,1)S(1)} %received.3.far), channel_id=1, source_target_pairs={{0,1},{1,0},{2,3},{3,2},{4,5},{5,4},{6,7},{7,6},{8,9},{9,8},{10,11... | collective-permute-start | bytes 884744 | tf_op jit(solution)/shard_map/received/ppermute | solution.py:53
  34.1 6.3 %collective-permute-start.12 = (bf16[144,1152]{1,0:T(8,128)(2,1)S(1)}, bf16[144,1152]{1,0:T(8,128)(2,1)S(1)}, u32[]{:S(2)}, u32[]{:S(2)}) collective-permute-start(bf16[144,1152]{1,0:T(8,128)(2,1)S(1)} %get-tuple-element.47), channel_id=1, source_target_pairs={{0,48},{1,193},{2,50},{3,195},{4,52},{5,197},{6,54},{7,199},{8,56}... | collective-permute-start | bytes 995336 | tf_op jit(solution)/shard_map/sum_first/ppermute | solution.py:53
  34.7 7.6 %collective-permute-start.8 = (bf16[144,1152]{1,0:T(8,128)(2,1)S(1)}, bf16[144,1152]{1,0:T(8,128)(2,1)S(1)}, u32[]{:S(2)}, u32[]{:S(2)}) collective-permute-start(bf16[144,1152]{1,0:T(8,128)(2,1)S(1)} %get-tuple-element.43), channel_id=1, source_target_pairs={{0,16},{1,65},{2,18},{3,67},{4,20},{5,69},{6,22},{7,71},{8,24},{9,... | collective-permute-start | bytes 995336 | tf_op jit(solution)/shard_map/sum_first/ppermute | solution.py:53
  35.6 9.9 %collective-permute-start.10 = (bf16[144,1152]{1,0:T(8,128)(2,1)S(1)}, bf16[144,1152]{1,0:T(8,128)(2,1)S(1)}, u32[]{:S(2)}, u32[]{:S(2)}) collective-permute-start(bf16[144,1152]{1,0:T(8,128)(2,1)S(1)} %get-tuple-element.44), channel_id=1, source_target_pairs={{0,16},{1,65},{2,18},{3,67},{4,20},{5,69},{6,22},{7,71},{8,24},{9,... | collective-permute-start | bytes 995336 | tf_op jit(solution)/shard_map/sum_first/ppermute | solution.py:53
  35.7 9.9 %collective-permute-start.11 = (bf16[144,1152]{1,0:T(8,128)(2,1)S(1)}, bf16[144,1152]{1,0:T(8,128)(2,1)S(1)}, u32[]{:S(2)}, u32[]{:S(2)}) collective-permute-start(bf16[144,1152]{1,0:T(8,128)(2,1)S(1)} %get-tuple-element.45), channel_id=1, source_target_pairs={{0,48},{1,193},{2,50},{3,195},{4,52},{5,197},{6,54},{7,199},{8,56}... | collective-permute-start | bytes 995336 | tf_op jit(solution)/shard_map/sum_first/ppermute | solution.py:53
  40.5 7.0 %collective-permute-start.13 = (bf16[144,1152]{1,0:T(8,128)(2,1)S(1)}, bf16[144,1152]{1,0:T(8,128)(2,1)S(1)}, u32[]{:S(2)}, u32[]{:S(2)}) collective-permute-start(bf16[144,1152]{1,0:T(8,128)(2,1)S(1)} %sum_first.4), channel_id=1, source_target_pairs={{0,48},{1,193},{2,50},{3,195},{4,52},{5,197},{6,54},{7,199},{8,56}... | collective-permute-start | bytes 995336 | tf_op jit(solution)/shard_map/sum_first/ppermute | solution.py:53
  42.4 7.6 %collective-permute-start.9 = (bf16[144,1152]{1,0:T(8,128)(2,1)S(1)}, bf16[144,1152]{1,0:T(8,128)(2,1)S(1)}, u32[]{:S(2)}, u32[]{:S(2)}) collective-permute-start(bf16[144,1152]{1,0:T(8,128)(2,1)S(1)} %sum_first.3), channel_id=1, source_target_pairs={{0,16},{1,65},{2,18},{3,67},{4,20},{5,69},{6,22},{7,71},{8,24},{9,... | collective-permute-start | bytes 995336 | tf_op jit(solution)/shard_map/sum_first/ppermute | solution.py:53
  97.4 18.9 %collective-permute-start.18 = (bf16[288,1152]{1,0:T(8,128)(2,1)S(1)}, bf16[288,1152]{1,0:T(8,128)(2,1)S(1)}, u32[]{:S(2)}, u32[]{:S(2)}) collective-permute-start(bf16[288,1152]{1,0:T(8,128)(2,1)S(1)} %bitcast.16), channel_id=1, source_target_pairs={{0,1},{1,0},{2,3},{3,2},{4,5},{5,4},{6,7},{7,6},{8,9},{9,8},{10,11... | collective-permute-start | bytes 1990664 | tf_op jit(solution)/shard_map/share_first/ppermute | solution.py:53
  104.3 7.6 %collective-permute-start.14 = (bf16[144,1152]{1,0:T(8,128)(2,1)S(1)}, bf16[144,1152]{1,0:T(8,128)(2,1)S(1)}, u32[]{:S(2)}, u32[]{:S(2)}) collective-permute-start(bf16[144,1152]{1,0:T(8,128)(2,1)S(1)} %bitcast.23), channel_id=1, source_target_pairs={{0,16},{1,65},{2,18},{3,67},{4,20},{5,69},{6,22},{7,71},{8,24},{9,... | collective-permute-start | bytes 995336 | tf_op jit(solution)/shard_map/share_first/ppermute | solution.py:53
  104.7 7.2 %collective-permute-start.15 = (bf16[144,1152]{1,0:T(8,128)(2,1)S(1)}, bf16[144,1152]{1,0:T(8,128)(2,1)S(1)}, u32[]{:S(2)}, u32[]{:S(2)}) collective-permute-start(bf16[144,1152]{1,0:T(8,128)(2,1)S(1)} %bitcast.25), channel_id=1, source_target_pairs={{0,48},{1,193},{2,50},{3,195},{4,52},{5,197},{6,54},{7,199},{8,56}... | collective-permute-start | bytes 995336 | tf_op jit(solution)/shard_map/share_first/ppermute | solution.py:53
  107.1 8.4 %collective-permute-start.16 = (bf16[144,1152]{1,0:T(8,128)(2,1)S(1)}, bf16[144,1152]{1,0:T(8,128)(2,1)S(1)}, u32[]{:S(2)}, u32[]{:S(2)}) collective-permute-start(bf16[144,1152]{1,0:T(8,128)(2,1)S(1)} %bitcast.26), channel_id=1, source_target_pairs={{0,16},{1,65},{2,18},{3,67},{4,20},{5,69},{6,22},{7,71},{8,24},{9,... | collective-permute-start | bytes 995336 | tf_op jit(solution)/shard_map/share_first/ppermute | solution.py:53
  107.1 9.2 %collective-permute-start.17 = (bf16[144,1152]{1,0:T(8,128)(2,1)S(1)}, bf16[144,1152]{1,0:T(8,128)(2,1)S(1)}, u32[]{:S(2)}, u32[]{:S(2)}) collective-permute-start(bf16[144,1152]{1,0:T(8,128)(2,1)S(1)} %bitcast.24), channel_id=1, source_target_pairs={{0,48},{1,193},{2,50},{3,195},{4,52},{5,197},{6,54},{7,199},{8,56}... | collective-permute-start | bytes 995336 | tf_op jit(solution)/shard_map/share_first/ppermute | solution.py:53
  111.8 7.5 %collective-permute-start.19 = (bf16[144,1152]{1,0:T(8,128)(2,1)S(1)}, bf16[144,1152]{1,0:T(8,128)(2,1)S(1)}, u32[]{:S(2)}, u32[]{:S(2)}) collective-permute-start(bf16[144,1152]{1,0:T(8,128)(2,1)S(1)} %collective-permute-done.14.refs_1_), channel_id=1, source_target_pairs={{0,16},{1,65},{2,18},{3,67},{4,20},{5,69},{6,22},{7,71},{8,24},{9,... | collective-permute-start | bytes 995336 | tf_op jit(solution)/shard_map/share_first/ppermute | solution.py:53
  111.9 9.2 %collective-permute-start.20 = (bf16[144,1152]{1,0:T(8,128)(2,1)S(1)}, bf16[144,1152]{1,0:T(8,128)(2,1)S(1)}, u32[]{:S(2)}, u32[]{:S(2)}) collective-permute-start(bf16[144,1152]{1,0:T(8,128)(2,1)S(1)} %collective-permute-done.15.refs_2_), channel_id=1, source_target_pairs={{0,48},{1,193},{2,50},{3,195},{4,52},{5,197},{6,54},{7,199},{8,56}... | collective-permute-start | bytes 995336 | tf_op jit(solution)/shard_map/share_first/ppermute | solution.py:53
  115.4 5.7 %collective-permute-start.21 = (bf16[144,1152]{1,0:T(8,128)(2,1)S(1)}, bf16[144,1152]{1,0:T(8,128)(2,1)S(1)}, u32[]{:S(2)}, u32[]{:S(2)}) collective-permute-start(bf16[144,1152]{1,0:T(8,128)(2,1)S(1)} %collective-permute-done.14.refs_1_), channel_id=1, source_target_pairs={{0,1},{1,0},{2,3},{3,2},{4,5},{5,4},{6,7},{7,6},{8,9},{9,8},{10,11... | collective-permute-start | bytes 995336 | tf_op jit(solution)/shard_map/share_first/ppermute | solution.py:53
  116.3 5.3 %collective-permute-start.22 = (bf16[144,1152]{1,0:T(8,128)(2,1)S(1)}, bf16[144,1152]{1,0:T(8,128)(2,1)S(1)}, u32[]{:S(2)}, u32[]{:S(2)}) collective-permute-start(bf16[144,1152]{1,0:T(8,128)(2,1)S(1)} %collective-permute-done.15.refs_2_), channel_id=1, source_target_pairs={{0,1},{1,0},{2,3},{3,2},{4,5},{5,4},{6,7},{7,6},{8,9},{9,8},{10,11... | collective-permute-start | bytes 995336 | tf_op jit(solution)/shard_map/share_first/ppermute | solution.py:53
  116.3 5.3 %collective-permute-start.23 = (bf16[144,1152]{1,0:T(8,128)(2,1)S(1)}, bf16[144,1152]{1,0:T(8,128)(2,1)S(1)}, u32[]{:S(2)}, u32[]{:S(2)}) collective-permute-start(bf16[144,1152]{1,0:T(8,128)(2,1)S(1)} %collective-permute-done.16.refs_3_), channel_id=1, source_target_pairs={{0,1},{1,0},{2,3},{3,2},{4,5},{5,4},{6,7},{7,6},{8,9},{9,8},{10,11... | collective-permute-start | bytes 995336 | tf_op jit(solution)/shard_map/share_first/ppermute | solution.py:53
  119.3 3.0 %collective-permute-start.24 = (bf16[144,1152]{1,0:T(8,128)(2,1)S(1)}, bf16[144,1152]{1,0:T(8,128)(2,1)S(1)}, u32[]{:S(2)}, u32[]{:S(2)}) collective-permute-start(bf16[144,1152]{1,0:T(8,128)(2,1)S(1)} %collective-permute-done.17.refs_4_), channel_id=1, source_target_pairs={{0,1},{1,0},{2,3},{3,2},{4,5},{5,4},{6,7},{7,6},{8,9},{9,8},{10,11... | collective-permute-start | bytes 995336 | tf_op jit(solution)/shard_map/share_first/ppermute | solution.py:53
  121.0 2.6 %collective-permute-start.25 = (bf16[144,1152]{1,0:T(8,128)(2,1)S(1)}, bf16[144,1152]{1,0:T(8,128)(2,1)S(1)}, u32[]{:S(2)}, u32[]{:S(2)}) collective-permute-start(bf16[144,1152]{1,0:T(8,128)(2,1)S(1)} %get-tuple-element.50.refs_2_), channel_id=1, source_target_pairs={{0,1},{1,0},{2,3},{3,2},{4,5},{5,4},{6,7},{7,6},{8,9},{9,8},{10,11... | collective-permute-start | bytes 995336 | tf_op jit(solution)/shard_map/write/ppermute | solution.py:53
  121.1 2.5 %collective-permute-start.26 = (bf16[144,1152]{1,0:T(8,128)(2,1)S(1)}, bf16[144,1152]{1,0:T(8,128)(2,1)S(1)}, u32[]{:S(2)}, u32[]{:S(2)}) collective-permute-start(bf16[144,1152]{1,0:T(8,128)(2,1)S(1)} %get-tuple-element.51.refs_3_), channel_id=1, source_target_pairs={{0,1},{1,0},{2,3},{3,2},{4,5},{5,4},{6,7},{7,6},{8,9},{9,8},{10,11... | collective-permute-start | bytes 995336 | tf_op jit(solution)/shard_map/write/ppermute | solution.py:53

commit v13 on v11

--- a/solution.py
+++ b/solution.py
@@ -41,7 +41,6 @@
 SECOND = groups(lambda y, x, z, c: (c, z, x if c == 0 else y))
 LINES = groups(lambda y, x, z, c: (c, x, y))
 FAR = [(i, (i + 3) % N if i % 2 else (i - 3) % N) for i in range(N)]
-TAIL = 16
 TEXT = 1
 
 
@@ -115,22 +114,6 @@
         head[at, :] = new if before is None else before[at, :] + new
 
 
-def join_positions(image_hbm, position_hbm, out, position, sems):
-    rows = position.shape[0]
-    moves = [
-        pltpu.make_async_copy(position_hbm, position, sems.at[0]),
-        pltpu.make_async_copy(image_hbm, out.at[pl.ds(0, rows), :], sems.at[1]),
-    ]
-    for move in moves:
-        move.start()
-    tail = pl.ds(rows, TAIL)
-    out[tail, :] = jnp.zeros((TAIL, out.shape[1]), bf16)
-    moves[0].wait()
-    row = position[...].reshape(1, rows).astype(f32)
-    out[tail, pl.ds(0, rows)] = jnp.broadcast_to(row, (TAIL, rows)).astype(bf16)
-    moves[1].wait()
-
-
 def visit(log_scale, shift, x, text_w, image_emb, finish, back, grad, grad_before):
     scale = factor(log_scale)
     projected, inverse = embed(x[...], text_w[...])
@@ -152,39 +135,36 @@
 
 
 def near_kernel(
-    log_scale, shift, text_hbm, text_w_hbm, image_w_hbm, text_other, image_own, image_other,
+    log_scale, shift, text_hbm, image_hbm, text_w_hbm, image_w_hbm, text_other, image_other,
+    position, position_other,
     image_near, text_w, image_emb, image_projected, image_inverse, grad, text_near, back,
     image_w, sems,
 ):
     rows = text_other.shape[0]
     first, second = pl.ds(0, rows), pl.ds(rows, rows)
     moves = [
-        pltpu.make_async_copy(image_w_hbm, image_w, sems.at[0]),
-        pltpu.make_async_copy(text_hbm, text_near.at[first, :], sems.at[1]),
-        pltpu.make_async_copy(text_w_hbm, text_w, sems.at[2]),
+        pltpu.make_async_copy(image_hbm, image_near.at[first, :], sems.at[0]),
+        pltpu.make_async_copy(image_w_hbm, image_w, sems.at[1]),
+        pltpu.make_async_copy(text_hbm, text_near.at[first, :], sems.at[2]),
+        pltpu.make_async_copy(text_w_hbm, text_w, sems.at[3]),
     ]
     for move in moves:
         move.start()
-    image_near[first, :] = image_own[first, :]
-    image_near[second, :] = image_other[first, :]
+    image_near[second, :] = image_other[...]
     text_near[second, :] = text_other[...]
     moves[0].wait()
+    moves[1].wait()
     projected, inverse = embed(image_near[...], image_w[...])
     image_emb[...] = (projected * inverse).astype(bf16)
     image_projected[...] = projected
     image_inverse[...] = inverse
-    moves[1].wait()
     moves[2].wait()
+    moves[3].wait()
 
     def with_labels(sigmoid):
         column = lax.broadcasted_iota(jnp.int32, (2 * rows, rows), 0)
-
-        def positions(block):
-            tail = block[pl.ds(rows, TAIL), pl.ds(0, rows)]
-            return tail.astype(f32)[:1].astype(jnp.int32)
-
-        own = (column == positions(image_own)).astype(f32)
-        other = (column == positions(image_other) + rows).astype(f32)
+        own = (column == position[...]).astype(f32)
+        other = (column == position_other[...] + rows).astype(f32)
         return sigmoid - jnp.concatenate([own, other], axis=1).T
 
     visit(log_scale, shift, text_near, text_w, image_emb, with_labels, back, grad, None)
@@ -340,12 +320,8 @@
     piece, half_piece = ((slab, width), bf16), ((half, width), bf16)
     with jax.named_scope("band_exchange"):
         text_other = send(text_x, SWAP)
-        [image_own] = call(
-            join_positions,
-            [((rows + TAIL, width), bf16)],
-            [pltpu.VMEM((rows,), jnp.int32), pltpu.SemaphoreType.DMA((2,))],
-        )((), (image_x, position))
-        image_other = send(image_own, SWAP)
+        image_other = send(image_x, SWAP)
+        position_other = send(position, SWAP)
         below = send(text_x, shifted(2))
         above = send(text_x, shifted(-2))
         far = send(text_x, FAR)
@@ -353,10 +329,11 @@
         image_near, weight, image_emb, image_projected, image_inverse, grad, *near = call(
             near_kernel,
             [pair, matrix, pair, pair_f32, ((2 * rows, 1), f32), pair_f32, pair, pair],
-            [pltpu.VMEM(*matrix), pltpu.SemaphoreType.DMA((3,))],
+            [pltpu.VMEM(*matrix), pltpu.SemaphoreType.DMA((4,))],
             flops=4 * 10**9,
         )(
-            scalars, (text_x, text_w, image_w), text_other, image_own, image_other
+            scalars, (text_x, image_x, text_w, image_w), text_other, image_other,
+            position[None], position_other[None],
         )
     with jax.named_scope("swap_neighbours"):
         above, below = after(image_inverse, above, below)

time: 123 us -> 122 us (level)
  starting transfers between devices: 40.5 us -> 43.8 us
  blocking collectives: 45.3 us -> 42.6 us
  waiting for transfers between devices: 14.2 us -> 12.5 us
    ppermute x27 -> x28, starting transfers between devices: 40.5 us -> 43.8 us  [send(): return lax.ppermute(block, 'dp', pairs)]
    all_to_all x4, blocking collectives: 45.3 us -> 42.6 us  [exchange(): lax.all_to_all(parts, 'dp', 0, 0, axis_index_groups=members, tiled=True)]
    ppermute x27 -> x28, waiting for transfers between devices: 14.2 us -> 12.5 us  [send(): return lax.ppermute(block, 'dp', pairs)]
    pallas_call x15 -> x14, Pallas kernels: 20.4 us -> 19.5 us  [run(): pl.pallas_call(body, out_shape=[jax.ShapeDtypeStruct(s, d) for s, d in ou...]
  transfers between devices with their start and end apart: 27 -> 28, of which waited for: 9 -> 9; matrix products, arithmetic and copies ran while one was open for 0% -> 0% of each run, Pallas kernels for 11% -> 12%
where the time goes in v13:
time: 122 us
  starting transfers between devices  43.8 us (36%)
  blocking collectives  42.6 us (35%)
  Pallas kernels  19.5 us (16%)
  waiting for transfers between devices  12.5 us (10%)
  between operations  2.33 us (2%)
    ppermute x28, starting transfers between devices, send(): return lax.ppermute(block, 'dp', pairs)  43.8 us
    all_to_all x4, blocking collectives, exchange(): lax.all_to_all(parts, 'dp', 0, 0, axis_index_groups=members, tiled=True)  42.6 us
    pallas_call x14, Pallas kernels, run(): pl.pallas_call(body, out_shape=[jax.ShapeDtypeStruct(s, d) for s, d in ou...  19.5 us
    ppermute x28, waiting for transfers between devices, send(): return lax.ppermute(block, 'dp', pairs)  12.5 us
  transfers between devices with their start and end apart: 28, of which 9 were waited for; matrix products, arithmetic and copies ran while one was open for 0% of the time, Pallas kernels for 12%

profile of v13, /device:TPU:1, one launch (start us, length us, event | category | flops | bytes accessed | tf_op | source)
XLA Modules:
  0.0 121.7 jit_solution(1613915591651705590)
XLA Ops:
  0.6 3.3 %collective-permute-start.4 = (bf16[128,1152]{1,0:T(8,128)(2,1)}, bf16[128,1152]{1,0:T(8,128)(2,1)S(1)}, u32[]{:S(2)}, u32[]{:S(2)}) collective-permute-start(bf16[128,1152]{1,0:T(8,128)(2,1)} %image_hbm.1), channel_id=1, source_target_pairs={{0,1},{1,0},{2,3},{3,2},{4,5},{5,4},{6,7},{7,6},{8,9},{9,8},{10,11... | collective-permute-start | bytes 884744 | tf_op jit(solution)/shard_map/band_exchange/ppermute | solution.py:52
  4.0 0.1 collective-permute-start.3
  4.1 0.4 collective-permute-start.5
  4.5 0.0 collective-permute-start.2
  4.5 8.5 %collective-permute-start.1 = (bf16[128,1152]{1,0:T(8,128)(2,1)}, bf16[128,1152]{1,0:T(8,128)(2,1)S(1)}, u32[]{:S(2)}, u32[]{:S(2)}) collective-permute-start(bf16[128,1152]{1,0:T(8,128)(2,1)} %text_hbm.1), channel_id=1, source_target_pairs={{0,254},{1,255},{2,0},{3,1},{4,2},{5,3},{6,4},{7,5},{8,6},{9,7},{1... | collective-permute-start | bytes 884744 | tf_op jit(solution)/shard_map/band_exchange/ppermute | solution.py:52
  14.3 0.0 collective-permute-done.5
  14.3 0.1 collective-permute-start
  14.4 0.0 collective-permute-done.4.image_other
  14.4 0.0 collective-permute-done.3.text_other
  14.4 0.6 copy-done
  15.1 5.2 %near.1 = (bf16[256,1152]{1,0:T(8,128)(2,1)S(1)}, bf16[1152,1152]{1,0:T(8,128)(2,1)S(1)}, bf16[256,1152]{1,0:T(8,128)(2,1)S(1)}, f32[256,1152]{1,0:T(8,128)S(1)}...) custom-call(f32[1]{0:T(128)S(6)} %copy.27.log_scale, ...), custom_call_target="tpu_custom_call" | custom-call | flops 4000000000 | tf_op jit(solution)/shard_map/near/pallas_call | solution.py:68
  20.2 0.2 collective-permute-done.2.refs_1_
  20.5 1.2 collective-permute-done.1.refs_0_
  21.6 1.0 collective-permute-start.7
  22.6 0.1 collective-permute-start.8
  22.7 3.8 %received.2 = (f32[256,1152]{1,0:T(8,128)S(1)}, f32[1152,1152]{1,0:T(8,128)S(1)}) custom-call(f32[1]{0:T(128)S(6)} %copy.27.log_scale, f32[1]{0:T(128)S(6)} %copy.28.shift, bf16[128,1152]{1,0:T(8,128)(2,1)S(1)} %get-tuple-element.29.below, bf16[128,1152]{1,0:T(8,128)(2,1)S(1)} %get-tuple-element.30.above, bf16[1152,1152]{1,0:T(8,128)(2,1)S(1)} %get-tuple-element.31.text_w, ...), custom_call_target="tpu_custom_call" | custom-call | flops 4000000000 | tf_op jit(solution)/shard_map/received/pallas_call | solution.py:68
  26.6 0.0 collective-permute-done.refs_0_
  26.6 3.4 %collective-permute-start.6 = (bf16[128,1152]{1,0:T(8,128)(2,1)S(1)}, bf16[128,1152]{1,0:T(8,128)(2,1)S(1)}, u32[]{:S(2)}, u32[]{:S(2)}) collective-permute-start(bf16[128,1152]{1,0:T(8,128)(2,1)S(1)} %received.3.far), channel_id=1, source_target_pairs={{0,1},{1,0},{2,3},{3,2},{4,5},{5,4},{6,7},{7,6},{8,9},{9,8},{10,11... | collective-permute-start | bytes 884744 | tf_op jit(solution)/shard_map/received/ppermute | solution.py:52
  30.0 0.0 collective-permute-done.7.below
  30.0 0.0 collective-permute-done.8.above
  30.0 2.1 %partners.1 = (f32[256,1152]{1,0:T(8,128)S(1)}, bf16[256,1152]{1,0:T(8,128)(2,1)S(1)}, bf16[256,1152]{1,0:T(8,128)(2,1)S(1)}) custom-call(f32[1]{0:T(128)S(6)} %copy.27.log_scale, f32[1]{0:T(128)S(6)} %copy.28.shift, bf16[128,1152]{1,0:T(8,128)(2,1)S(1)} %collective-permute-done.7.below, bf16[128,1152]{1,0:T(8,128)(2,1)S(1)} %collective-permute-done.8.above, ...), custom_call_target="tpu_custom_call" | custom-call | flops 4000000000 | tf_op jit(solution)/shard_map/partners/pallas_call | solution.py:68
  32.2 4.3 %far.1 = (bf16[288,1152]{1,0:T(8,128)(2,1)S(1)}, bf16[144,1152]{1,0:T(8,128)(2,1)S(1)}, bf16[144,1152]{1,0:T(8,128)(2,1)S(1)}, bf16[144,1152]{1,0:T(8,128)(2,1)S...) custom-call(f32[1]{0:T(128)S(6)} %copy.27.log_scale, ...), custom_call_target="tpu_custom_call" | custom-call | flops 4000000000 | tf_op jit(solution)/shard_map/far/pallas_call | solution.py:68
  36.5 0.1 collective-permute-start.9
  36.5 2.7 %collective-permute-start.13 = (bf16[144,1152]{1,0:T(8,128)(2,1)S(1)}, bf16[144,1152]{1,0:T(8,128)(2,1)S(1)}, u32[]{:S(2)}, u32[]{:S(2)}) collective-permute-start(bf16[144,1152]{1,0:T(8,128)(2,1)S(1)} %get-tuple-element.49), channel_id=1, source_target_pairs={{0,48},{1,193},{2,50},{3,195},{4,52},{5,197},{6,54},{7,199},{8,56}... | collective-permute-start | bytes 995336 | tf_op jit(solution)/shard_map/sum_first/ppermute | solution.py:52
  39.2 0.0 collective-permute-start.11
  39.2 2.7 %collective-permute-start.12 = (bf16[144,1152]{1,0:T(8,128)(2,1)S(1)}, bf16[144,1152]{1,0:T(8,128)(2,1)S(1)}, u32[]{:S(2)}, u32[]{:S(2)}) collective-permute-start(bf16[144,1152]{1,0:T(8,128)(2,1)S(1)} %get-tuple-element.47), channel_id=1, source_target_pairs={{0,48},{1,193},{2,50},{3,195},{4,52},{5,197},{6,54},{7,199},{8,56}... | collective-permute-start | bytes 995336 | tf_op jit(solution)/shard_map/sum_first/ppermute | solution.py:52
  41.9 2.1 %collective-permute-done.9.b = bf16[144,1152]{1,0:T(8,128)(2,1)S(1)} collective-permute-done((bf16[144,1152]{1,0:T(8,128)(2,1)S(1)}, bf16[144,1152]{1,0:T(8,128)(2,1)S(1)}, u32[]{:S(2)}, u32[]{:S(2)}) %collective-permute-start.9) | collective-permute-done | bytes 331808 | tf_op jit(solution)/shard_map/sum_first/ppermute | solution.py:52
  44.0 0.1 sum_first.3
  44.1 0.1 collective-permute-start.10
  44.2 0.0 collective-permute-done.13.b
  44.2 0.1 sum_first.4
  44.3 2.7 %collective-permute-start.14 = (bf16[144,1152]{1,0:T(8,128)(2,1)S(1)}, bf16[144,1152]{1,0:T(8,128)(2,1)S(1)}, u32[]{:S(2)}, u32[]{:S(2)}) collective-permute-start(bf16[144,1152]{1,0:T(8,128)(2,1)S(1)} %sum_first.4), channel_id=1, source_target_pairs={{0,48},{1,193},{2,50},{3,195},{4,52},{5,197},{6,54},{7,199},{8,56}... | collective-permute-start | bytes 995336 | tf_op jit(solution)/shard_map/sum_first/ppermute | solution.py:52
  47.0 0.5 collective-permute-done.11.a_bottom
  47.5 0.0 collective-permute-done.12.b_top
  47.5 4.2 %collective-permute-done.10.a_top = bf16[144,1152]{1,0:T(8,128)(2,1)S(1)} collective-permute-done((bf16[144,1152]{1,0:T(8,128)(2,1)S(1)}, bf16[144,1152]{1,0:T(8,128)(2,1)S(1)}, u32[]{:S(2)}, u32[]{:S(2)}) %collective-permute-start.10) | collective-permute-done | bytes 331808 | tf_op jit(solution)/shard_map/sum_first/ppermute | solution.py:52
  51.6 0.3 sum_first.5
  51.9 10.6 %all_to_all.20 = bf16[4,72,1152]{2,1,0:T(8,128)(2,1)S(1)} all-to-all(bf16[4,72,1152]{2,1,0:T(8,128)(2,1)S(1)} %bitcast.20), channel_id=1, replica_groups={{0,64,128,192},{1,17,33,49},{2,66,130,194},{3,19,35,51},{4,68,132,196},..., dimensions={0} | all-to-all | bytes 1327104 | tf_op jit(solution)/shard_map/sum_second/all_to_all | solution.py:56
  62.5 0.1 reduce_sum.24
  62.6 10.9 %all_to_all.21 = bf16[88,8,128]{2,1,0:T(8,128)(2,1)S(1)} all-to-all(bf16[88,8,128]{2,1,0:T(8,128)(2,1)S(1)} %concatenate.3), channel_id=1, replica_groups={{0,2,4,6,8,10,12,14},{1,3,5,7,9,11,13,15},{16,18,20,22,24,26,28,30},{17..., dimensions={0} | all-to-all | bytes 360448 | tf_op jit(solution)/shard_map/sum_lines/all_to_all | solution.py:56
  73.6 10.9 %all_to_all.22 = bf16[88,8,128]{2,1,0:T(8,128)(2,1)S(1)} all-to-all(bf16[88,8,128]{2,1,0:T(8,128)(2,1)S(1)} %bitcast.24), channel_id=1, replica_groups={{0,2,4,6,8,10,12,14},{1,3,5,7,9,11,13,15},{16,18,20,22,24,26,28,30},{17..., dimensions={0} | all-to-all | bytes 360448 | tf_op jit(solution)/shard_map/share_lines/all_to_all | solution.py:56
  84.7 10.1 %all_to_all.23 = bf16[4,72,1152]{2,1,0:T(8,128)(2,1)S(1)} all-to-all(bf16[4,72,1152]{2,1,0:T(8,128)(2,1)S(1)} %tile.20), channel_id=1, replica_groups={{0,64,128,192},{1,17,33,49},{2,66,130,194},{3,19,35,51},{4,68,132,196},..., dimensions={0} | all-to-all | bytes 1327104 | tf_op jit(solution)/shard_map/share_second/all_to_all | solution.py:56
  94.8 6.3 %collective-permute-start.19 = (bf16[288,1152]{1,0:T(8,128)(2,1)S(1)}, bf16[288,1152]{1,0:T(8,128)(2,1)S(1)}, u32[]{:S(2)}, u32[]{:S(2)}) collective-permute-start(bf16[288,1152]{1,0:T(8,128)(2,1)S(1)} %bitcast.18), channel_id=1, source_target_pairs={{0,1},{1,0},{2,3},{3,2},{4,5},{5,4},{6,7},{7,6},{8,9},{9,8},{10,11... | collective-permute-start | bytes 1990664 | tf_op jit(solution)/shard_map/share_first/ppermute | solution.py:52
  101.1 0.1 fusion
  101.1 0.4 collective-permute-start.15
  101.5 2.4 %collective-permute-start.16 = (bf16[144,1152]{1,0:T(8,128)(2,1)S(1)}, bf16[144,1152]{1,0:T(8,128)(2,1)S(1)}, u32[]{:S(2)}, u32[]{:S(2)}) collective-permute-start(bf16[144,1152]{1,0:T(8,128)(2,1)S(1)} %bitcast.27), channel_id=1, source_target_pairs={{0,48},{1,193},{2,50},{3,195},{4,52},{5,197},{6,54},{7,199},{8,56}... | collective-permute-start | bytes 995336 | tf_op jit(solution)/shard_map/share_first/ppermute | solution.py:52
  103.9 0.0 collective-permute-start.18
  103.9 1.4 %collective-permute-start.17 = (bf16[144,1152]{1,0:T(8,128)(2,1)S(1)}, bf16[144,1152]{1,0:T(8,128)(2,1)S(1)}, u32[]{:S(2)}, u32[]{:S(2)}) collective-permute-start(bf16[144,1152]{1,0:T(8,128)(2,1)S(1)} %bitcast.28), channel_id=1, source_target_pairs={{0,16},{1,65},{2,18},{3,67},{4,20},{5,69},{6,22},{7,71},{8,24},{9,... | collective-permute-start | bytes 995336 | tf_op jit(solution)/shard_map/share_first/ppermute | solution.py:52
  105.3 3.3 %collective-permute-done.15.refs_1_ = bf16[144,1152]{1,0:T(8,128)(2,1)S(1)} collective-permute-done((bf16[144,1152]{1,0:T(8,128)(2,1)S(1)}, bf16[144,1152]{1,0:T(8,128)(2,1)S(1)}, u32[]{:S(2)}, u32[]{:S(2)}) %collective-permute-start.15) | collective-permute-done | bytes 331808 | tf_op jit(solution)/shard_map/share_first/ppermute | solution.py:52
  108.7 2.7 %collective-permute-start.21 = (bf16[144,1152]{1,0:T(8,128)(2,1)S(1)}, bf16[144,1152]{1,0:T(8,128)(2,1)S(1)}, u32[]{:S(2)}, u32[]{:S(2)}) collective-permute-start(bf16[144,1152]{1,0:T(8,128)(2,1)S(1)} %collective-permute-done.16.refs_2_), channel_id=1, source_target_pairs={{0,48},{1,193},{2,50},{3,195},{4,52},{5,197},{6,54},{7,199},{8,56}... | collective-permute-start | bytes 995336 | tf_op jit(solution)/shard_map/share_first/ppermute | solution.py:52
  111.3 0.1 collective-permute-done.18.refs_4_
  111.5 1.3 %collective-permute-start.25 = (bf16[144,1152]{1,0:T(8,128)(2,1)S(1)}, bf16[144,1152]{1,0:T(8,128)(2,1)S(1)}, u32[]{:S(2)}, u32[]{:S(2)}) collective-permute-start(bf16[144,1152]{1,0:T(8,128)(2,1)S(1)} %collective-permute-done.18.refs_4_), channel_id=1, source_target_pairs={{0,1},{1,0},{2,3},{3,2},{4,5},{5,4},{6,7},{7,6},{8,9},{9,8},{10,11... | collective-permute-start | bytes 995336 | tf_op jit(solution)/shard_map/share_first/ppermute | solution.py:52
  112.8 0.0 collective-permute-done.17.refs_3_
  112.8 1.7 %collective-permute-start.22 = (bf16[144,1152]{1,0:T(8,128)(2,1)S(1)}, bf16[144,1152]{1,0:T(8,128)(2,1)S(1)}, u32[]{:S(2)}, u32[]{:S(2)}) collective-permute-start(bf16[144,1152]{1,0:T(8,128)(2,1)S(1)} %collective-permute-done.15.refs_1_), channel_id=1, source_target_pairs={{0,1},{1,0},{2,3},{3,2},{4,5},{5,4},{6,7},{7,6},{8,9},{9,8},{10,11... | collective-permute-start | bytes 995336 | tf_op jit(solution)/shard_map/share_first/ppermute | solution.py:52
  114.5 0.0 collective-permute-done.19.refs_5_
  114.5 0.0 collective-permute-start.24
  114.5 1.5 %write.5 = (bf16[1152,1152]{1,0:T(8,128)(2,1)}, bf16[1152,1152]{1,0:T(8,128)(2,1)}) custom-call(bf16[288,1152]{1,0:T(8,128)(2,1)S(1)} %bitcast.19, bf16[144,1152]{1,0:T(8,128)(2,1)S(1)} %collective-permute-done.15.refs_1_, bf16[144,1152]{1,0:T(8,128)(2,1)S(1)} %collective-permute-done.16.refs_2_, bf16[144,1152]{1,0:T(8,128)(2,1)S(1)} %collective-permute-done.17.refs_3_, ...), custom_call_target="tpu_custom_call" | custom-call | tf_op jit(solution)/shard_map/write/pallas_call | solution.py:68
  116.0 0.1 collective-permute-done.20.refs_1_
  116.1 1.9 %collective-permute-start.23 = (bf16[144,1152]{1,0:T(8,128)(2,1)S(1)}, bf16[144,1152]{1,0:T(8,128)(2,1)S(1)}, u32[]{:S(2)}, u32[]{:S(2)}) collective-permute-start(bf16[144,1152]{1,0:T(8,128)(2,1)S(1)} %collective-permute-done.16.refs_2_), channel_id=1, source_target_pairs={{0,1},{1,0},{2,3},{3,2},{4,5},{5,4},{6,7},{7,6},{8,9},{9,8},{10,11... | collective-permute-start | bytes 995336 | tf_op jit(solution)/shard_map/share_first/ppermute | solution.py:52
  118.0 0.1 collective-permute-start.26
  118.1 0.4 collective-permute-start.27
  118.5 0.0 collective-permute-done.24.refs_6_
  118.5 0.7 collective-permute-done.23.refs_5_
  119.3 1.3 %write.8 = (bf16[1152,1152]{1,0:T(8,128)(2,1)}, bf16[1152,1152]{1,0:T(8,128)(2,1)}) custom-call(bf16[1152,1152]{1,0:T(8,128)(2,1)} %get-tuple-element.50.refs_0_, bf16[1152,1152]{1,0:T(8,128)(2,1)} %get-tuple-element.51.refs_1_, bf16[144,1152]{1,0:T(8,128)(2,1)S(1)} %write.6.refs_2_, ...), custom_call_target="tpu_custom_call", output_to_operand_aliasing={{0}: (0, {}), {1}: (1, {})} | custom-call | tf_op jit(solution)/shard_map/write/pallas_call | solution.py:68
  120.6 0.9 write.9
  (19 shorter events, 0.2 us)
Async XLA Ops:
  0.6 13.8 %collective-permute-start.4 = (bf16[128,1152]{1,0:T(8,128)(2,1)}, bf16[128,1152]{1,0:T(8,128)(2,1)S(1)}, u32[]{:S(2)}, u32[]{:S(2)}) collective-permute-start(bf16[128,1152]{1,0:T(8,128)(2,1)} %image_hbm.1), channel_id=1, source_target_pairs={{0,1},{1,0},{2,3},{3,2},{4,5},{5,4},{6,7},{7,6},{8,9},{9,8},{10,11... | collective-permute-start | bytes 884744 | tf_op jit(solution)/shard_map/band_exchange/ppermute | solution.py:52
  4.0 10.4 %collective-permute-start.3 = (bf16[128,1152]{1,0:T(8,128)(2,1)}, bf16[128,1152]{1,0:T(8,128)(2,1)S(1)}, u32[]{:S(2)}, u32[]{:S(2)}) collective-permute-start(bf16[128,1152]{1,0:T(8,128)(2,1)} %text_hbm.1), channel_id=1, source_target_pairs={{0,1},{1,0},{2,3},{3,2},{4,5},{5,4},{6,7},{7,6},{8,9},{9,8},{10,11... | collective-permute-start | bytes 884744 | tf_op jit(solution)/shard_map/band_exchange/ppermute | solution.py:52
  4.1 10.2 %collective-permute-start.5 = (s32[128]{0:T(128)}, s32[128]{0:T(128)S(1)}, u32[]{:S(2)}, u32[]{:S(2)}) collective-permute-start(s32[128]{0:T(128)} %param.11), channel_id=1, source_target_pairs={{0,1},{1,0},{2,3},{3,2},{4,5},{5,4},{6,7},{7,6},{8,9},{9,8},{10,11... | collective-permute-start | bytes 1544 | tf_op jit(solution)/shard_map/band_exchange/ppermute | solution.py:52
  4.5 16.0 %collective-permute-start.2 = (bf16[128,1152]{1,0:T(8,128)(2,1)}, bf16[128,1152]{1,0:T(8,128)(2,1)S(1)}, u32[]{:S(2)}, u32[]{:S(2)}) collective-permute-start(bf16[128,1152]{1,0:T(8,128)(2,1)} %text_hbm.1), channel_id=1, source_target_pairs={{0,2},{1,3},{2,4},{3,5},{4,6},{5,7},{6,8},{7,9},{8,10},{9,11},{10,... | collective-permute-start | bytes 884744 | tf_op jit(solution)/shard_map/band_exchange/ppermute | solution.py:52
  4.5 17.2 %collective-permute-start.1 = (bf16[128,1152]{1,0:T(8,128)(2,1)}, bf16[128,1152]{1,0:T(8,128)(2,1)S(1)}, u32[]{:S(2)}, u32[]{:S(2)}) collective-permute-start(bf16[128,1152]{1,0:T(8,128)(2,1)} %text_hbm.1), channel_id=1, source_target_pairs={{0,254},{1,255},{2,0},{3,1},{4,2},{5,3},{6,4},{7,5},{8,6},{9,7},{1... | collective-permute-start | bytes 884744 | tf_op jit(solution)/shard_map/band_exchange/ppermute | solution.py:52
  14.3 12.3 %collective-permute-start = (bf16[128,1152]{1,0:T(8,128)(2,1)}, bf16[128,1152]{1,0:T(8,128)(2,1)S(1)}, u32[]{:S(2)}, u32[]{:S(2)}) collective-permute-start(bf16[128,1152]{1,0:T(8,128)(2,1)} %text_hbm.1), channel_id=1, source_target_pairs={{0,253},{1,4},{2,255},{3,6},{4,1},{5,8},{6,3},{7,10},{8,5},{9,12},... | collective-permute-start | bytes 884744 | tf_op jit(solution)/shard_map/band_exchange/ppermute | solution.py:52
  14.4 0.7 copy-start
  21.6 8.4 %collective-permute-start.7 = (bf16[128,1152]{1,0:T(8,128)(2,1)S(1)}, bf16[128,1152]{1,0:T(8,128)(2,1)S(1)}, u32[]{:S(2)}, u32[]{:S(2)}) collective-permute-start(bf16[128,1152]{1,0:T(8,128)(2,1)S(1)} %get-tuple-element.29.below), channel_id=1, source_target_pairs={{0,1},{1,0},{2,3},{3,2},{4,5},{5,4},{6,7},{7,6},{8,9},{9,8},{10,11... | collective-permute-start | bytes 884744 | tf_op jit(solution)/shard_map/swap_neighbours/ppermute | solution.py:52
  22.6 7.4 %collective-permute-start.8 = (bf16[128,1152]{1,0:T(8,128)(2,1)S(1)}, bf16[128,1152]{1,0:T(8,128)(2,1)S(1)}, u32[]{:S(2)}, u32[]{:S(2)}) collective-permute-start(bf16[128,1152]{1,0:T(8,128)(2,1)S(1)} %get-tuple-element.30.above), channel_id=1, source_target_pairs={{0,1},{1,0},{2,3},{3,2},{4,5},{5,4},{6,7},{7,6},{8,9},{9,8},{10,11... | collective-permute-start | bytes 884744 | tf_op jit(solution)/shard_map/swap_neighbours/ppermute | solution.py:52
  26.6 5.6 %collective-permute-start.6 = (bf16[128,1152]{1,0:T(8,128)(2,1)S(1)}, bf16[128,1152]{1,0:T(8,128)(2,1)S(1)}, u32[]{:S(2)}, u32[]{:S(2)}) collective-permute-start(bf16[128,1152]{1,0:T(8,128)(2,1)S(1)} %received.3.far), channel_id=1, source_target_pairs={{0,1},{1,0},{2,3},{3,2},{4,5},{5,4},{6,7},{7,6},{8,9},{9,8},{10,11... | collective-permute-start | bytes 884744 | tf_op jit(solution)/shard_map/received/ppermute | solution.py:52
  36.5 7.6 %collective-permute-start.9 = (bf16[144,1152]{1,0:T(8,128)(2,1)S(1)}, bf16[144,1152]{1,0:T(8,128)(2,1)S(1)}, u32[]{:S(2)}, u32[]{:S(2)}) collective-permute-start(bf16[144,1152]{1,0:T(8,128)(2,1)S(1)} %get-tuple-element.45), channel_id=1, source_target_pairs={{0,16},{1,65},{2,18},{3,67},{4,20},{5,69},{6,22},{7,71},{8,24},{9,... | collective-permute-start | bytes 995336 | tf_op jit(solution)/shard_map/sum_first/ppermute | solution.py:52
  36.5 7.6 %collective-permute-start.13 = (bf16[144,1152]{1,0:T(8,128)(2,1)S(1)}, bf16[144,1152]{1,0:T(8,128)(2,1)S(1)}, u32[]{:S(2)}, u32[]{:S(2)}) collective-permute-start(bf16[144,1152]{1,0:T(8,128)(2,1)S(1)} %get-tuple-element.49), channel_id=1, source_target_pairs={{0,48},{1,193},{2,50},{3,195},{4,52},{5,197},{6,54},{7,199},{8,56}... | collective-permute-start | bytes 995336 | tf_op jit(solution)/shard_map/sum_first/ppermute | solution.py:52
  39.2 8.3 %collective-permute-start.11 = (bf16[144,1152]{1,0:T(8,128)(2,1)S(1)}, bf16[144,1152]{1,0:T(8,128)(2,1)S(1)}, u32[]{:S(2)}, u32[]{:S(2)}) collective-permute-start(bf16[144,1152]{1,0:T(8,128)(2,1)S(1)} %get-tuple-element.46), channel_id=1, source_target_pairs={{0,16},{1,65},{2,18},{3,67},{4,20},{5,69},{6,22},{7,71},{8,24},{9,... | collective-permute-start | bytes 995336 | tf_op jit(solution)/shard_map/sum_first/ppermute | solution.py:52
  39.2 8.3 %collective-permute-start.12 = (bf16[144,1152]{1,0:T(8,128)(2,1)S(1)}, bf16[144,1152]{1,0:T(8,128)(2,1)S(1)}, u32[]{:S(2)}, u32[]{:S(2)}) collective-permute-start(bf16[144,1152]{1,0:T(8,128)(2,1)S(1)} %get-tuple-element.47), channel_id=1, source_target_pairs={{0,48},{1,193},{2,50},{3,195},{4,52},{5,197},{6,54},{7,199},{8,56}... | collective-permute-start | bytes 995336 | tf_op jit(solution)/shard_map/sum_first/ppermute | solution.py:52
  44.1 7.6 %collective-permute-start.10 = (bf16[144,1152]{1,0:T(8,128)(2,1)S(1)}, bf16[144,1152]{1,0:T(8,128)(2,1)S(1)}, u32[]{:S(2)}, u32[]{:S(2)}) collective-permute-start(bf16[144,1152]{1,0:T(8,128)(2,1)S(1)} %sum_first.3), channel_id=1, source_target_pairs={{0,16},{1,65},{2,18},{3,67},{4,20},{5,69},{6,22},{7,71},{8,24},{9,... | collective-permute-start | bytes 995336 | tf_op jit(solution)/shard_map/sum_first/ppermute | solution.py:52
  44.3 7.4 %collective-permute-start.14 = (bf16[144,1152]{1,0:T(8,128)(2,1)S(1)}, bf16[144,1152]{1,0:T(8,128)(2,1)S(1)}, u32[]{:S(2)}, u32[]{:S(2)}) collective-permute-start(bf16[144,1152]{1,0:T(8,128)(2,1)S(1)} %sum_first.4), channel_id=1, source_target_pairs={{0,48},{1,193},{2,50},{3,195},{4,52},{5,197},{6,54},{7,199},{8,56}... | collective-permute-start | bytes 995336 | tf_op jit(solution)/shard_map/sum_first/ppermute | solution.py:52
  94.8 19.7 %collective-permute-start.19 = (bf16[288,1152]{1,0:T(8,128)(2,1)S(1)}, bf16[288,1152]{1,0:T(8,128)(2,1)S(1)}, u32[]{:S(2)}, u32[]{:S(2)}) collective-permute-start(bf16[288,1152]{1,0:T(8,128)(2,1)S(1)} %bitcast.18), channel_id=1, source_target_pairs={{0,1},{1,0},{2,3},{3,2},{4,5},{5,4},{6,7},{7,6},{8,9},{9,8},{10,11... | collective-permute-start | bytes 1990664 | tf_op jit(solution)/shard_map/share_first/ppermute | solution.py:52
  101.1 7.6 %collective-permute-start.15 = (bf16[144,1152]{1,0:T(8,128)(2,1)S(1)}, bf16[144,1152]{1,0:T(8,128)(2,1)S(1)}, u32[]{:S(2)}, u32[]{:S(2)}) collective-permute-start(bf16[144,1152]{1,0:T(8,128)(2,1)S(1)} %bitcast.29), channel_id=1, source_target_pairs={{0,16},{1,65},{2,18},{3,67},{4,20},{5,69},{6,22},{7,71},{8,24},{9,... | collective-permute-start | bytes 995336 | tf_op jit(solution)/shard_map/share_first/ppermute | solution.py:52
  101.5 7.2 %collective-permute-start.16 = (bf16[144,1152]{1,0:T(8,128)(2,1)S(1)}, bf16[144,1152]{1,0:T(8,128)(2,1)S(1)}, u32[]{:S(2)}, u32[]{:S(2)}) collective-permute-start(bf16[144,1152]{1,0:T(8,128)(2,1)S(1)} %bitcast.27), channel_id=1, source_target_pairs={{0,48},{1,193},{2,50},{3,195},{4,52},{5,197},{6,54},{7,199},{8,56}... | collective-permute-start | bytes 995336 | tf_op jit(solution)/shard_map/share_first/ppermute | solution.py:52
  103.9 7.6 %collective-permute-start.18 = (bf16[144,1152]{1,0:T(8,128)(2,1)S(1)}, bf16[144,1152]{1,0:T(8,128)(2,1)S(1)}, u32[]{:S(2)}, u32[]{:S(2)}) collective-permute-start(bf16[144,1152]{1,0:T(8,128)(2,1)S(1)} %bitcast.30), channel_id=1, source_target_pairs={{0,48},{1,193},{2,50},{3,195},{4,52},{5,197},{6,54},{7,199},{8,56}... | collective-permute-start | bytes 995336 | tf_op jit(solution)/shard_map/share_first/ppermute | solution.py:52
  103.9 8.9 %collective-permute-start.17 = (bf16[144,1152]{1,0:T(8,128)(2,1)S(1)}, bf16[144,1152]{1,0:T(8,128)(2,1)S(1)}, u32[]{:S(2)}, u32[]{:S(2)}) collective-permute-start(bf16[144,1152]{1,0:T(8,128)(2,1)S(1)} %bitcast.28), channel_id=1, source_target_pairs={{0,16},{1,65},{2,18},{3,67},{4,20},{5,69},{6,22},{7,71},{8,24},{9,... | collective-permute-start | bytes 995336 | tf_op jit(solution)/shard_map/share_first/ppermute | solution.py:52
  108.7 7.5 %collective-permute-start.20 = (bf16[144,1152]{1,0:T(8,128)(2,1)S(1)}, bf16[144,1152]{1,0:T(8,128)(2,1)S(1)}, u32[]{:S(2)}, u32[]{:S(2)}) collective-permute-start(bf16[144,1152]{1,0:T(8,128)(2,1)S(1)} %collective-permute-done.15.refs_1_), channel_id=1, source_target_pairs={{0,16},{1,65},{2,18},{3,67},{4,20},{5,69},{6,22},{7,71},{8,24},{9,... | collective-permute-start | bytes 995336 | tf_op jit(solution)/shard_map/share_first/ppermute | solution.py:52
  108.7 9.4 %collective-permute-start.21 = (bf16[144,1152]{1,0:T(8,128)(2,1)S(1)}, bf16[144,1152]{1,0:T(8,128)(2,1)S(1)}, u32[]{:S(2)}, u32[]{:S(2)}) collective-permute-start(bf16[144,1152]{1,0:T(8,128)(2,1)S(1)} %collective-permute-done.16.refs_2_), channel_id=1, source_target_pairs={{0,48},{1,193},{2,50},{3,195},{4,52},{5,197},{6,54},{7,199},{8,56}... | collective-permute-start | bytes 995336 | tf_op jit(solution)/shard_map/share_first/ppermute | solution.py:52
  111.5 6.6 %collective-permute-start.25 = (bf16[144,1152]{1,0:T(8,128)(2,1)S(1)}, bf16[144,1152]{1,0:T(8,128)(2,1)S(1)}, u32[]{:S(2)}, u32[]{:S(2)}) collective-permute-start(bf16[144,1152]{1,0:T(8,128)(2,1)S(1)} %collective-permute-done.18.refs_4_), channel_id=1, source_target_pairs={{0,1},{1,0},{2,3},{3,2},{4,5},{5,4},{6,7},{7,6},{8,9},{9,8},{10,11... | collective-permute-start | bytes 995336 | tf_op jit(solution)/shard_map/share_first/ppermute | solution.py:52
  112.8 5.8 %collective-permute-start.22 = (bf16[144,1152]{1,0:T(8,128)(2,1)S(1)}, bf16[144,1152]{1,0:T(8,128)(2,1)S(1)}, u32[]{:S(2)}, u32[]{:S(2)}) collective-permute-start(bf16[144,1152]{1,0:T(8,128)(2,1)S(1)} %collective-permute-done.15.refs_1_), channel_id=1, source_target_pairs={{0,1},{1,0},{2,3},{3,2},{4,5},{5,4},{6,7},{7,6},{8,9},{9,8},{10,11... | collective-permute-start | bytes 995336 | tf_op jit(solution)/shard_map/share_first/ppermute | solution.py:52
  114.5 4.1 %collective-permute-start.24 = (bf16[144,1152]{1,0:T(8,128)(2,1)S(1)}, bf16[144,1152]{1,0:T(8,128)(2,1)S(1)}, u32[]{:S(2)}, u32[]{:S(2)}) collective-permute-start(bf16[144,1152]{1,0:T(8,128)(2,1)S(1)} %collective-permute-done.17.refs_3_), channel_id=1, source_target_pairs={{0,1},{1,0},{2,3},{3,2},{4,5},{5,4},{6,7},{7,6},{8,9},{9,8},{10,11... | collective-permute-start | bytes 995336 | tf_op jit(solution)/shard_map/share_first/ppermute | solution.py:52
  116.1 3.1 %collective-permute-start.23 = (bf16[144,1152]{1,0:T(8,128)(2,1)S(1)}, bf16[144,1152]{1,0:T(8,128)(2,1)S(1)}, u32[]{:S(2)}, u32[]{:S(2)}) collective-permute-start(bf16[144,1152]{1,0:T(8,128)(2,1)S(1)} %collective-permute-done.16.refs_2_), channel_id=1, source_target_pairs={{0,1},{1,0},{2,3},{3,2},{4,5},{5,4},{6,7},{7,6},{8,9},{9,8},{10,11... | collective-permute-start | bytes 995336 | tf_op jit(solution)/shard_map/share_first/ppermute | solution.py:52
  118.0 2.6 %collective-permute-start.26 = (bf16[144,1152]{1,0:T(8,128)(2,1)S(1)}, bf16[144,1152]{1,0:T(8,128)(2,1)S(1)}, u32[]{:S(2)}, u32[]{:S(2)}) collective-permute-start(bf16[144,1152]{1,0:T(8,128)(2,1)S(1)} %write.6.refs_2_), channel_id=1, source_target_pairs={{0,1},{1,0},{2,3},{3,2},{4,5},{5,4},{6,7},{7,6},{8,9},{9,8},{10,11... | collective-permute-start | bytes 995336 | tf_op jit(solution)/shard_map/write/ppermute | solution.py:52
  118.1 2.5 %collective-permute-start.27 = (bf16[144,1152]{1,0:T(8,128)(2,1)S(1)}, bf16[144,1152]{1,0:T(8,128)(2,1)S(1)}, u32[]{:S(2)}, u32[]{:S(2)}) collective-permute-start(bf16[144,1152]{1,0:T(8,128)(2,1)S(1)} %write.7.refs_3_), channel_id=1, source_target_pairs={{0,1},{1,0},{2,3},{3,2},{4,5},{5,4},{6,7},{7,6},{8,9},{9,8},{10,11... | collective-permute-start | bytes 995336 | tf_op jit(solution)/shard_map/write/ppermute | solution.py:52

commit v14 on v13

--- a/solution.py
+++ b/solution.py
@@ -135,10 +135,10 @@
 
 
 def near_kernel(
-    log_scale, shift, text_hbm, image_hbm, text_w_hbm, image_w_hbm, text_other, image_other,
-    position, position_other,
+    log_scale, shift, text_hbm, image_hbm, text_w_hbm, image_w_hbm, position_hbm,
+    text_other, image_other, position_other,
     image_near, text_w, image_emb, image_projected, image_inverse, grad, text_near, back,
-    image_w, sems,
+    image_w, position, sems,
 ):
     rows = text_other.shape[0]
     first, second = pl.ds(0, rows), pl.ds(rows, rows)
@@ -147,6 +147,7 @@
         pltpu.make_async_copy(image_w_hbm, image_w, sems.at[1]),
         pltpu.make_async_copy(text_hbm, text_near.at[first, :], sems.at[2]),
         pltpu.make_async_copy(text_w_hbm, text_w, sems.at[3]),
+        pltpu.make_async_copy(position_hbm, position, sems.at[4]),
     ]
     for move in moves:
         move.start()
@@ -160,10 +161,11 @@
     image_inverse[...] = inverse
     moves[2].wait()
     moves[3].wait()
+    moves[4].wait()
 
     def with_labels(sigmoid):
         column = lax.broadcasted_iota(jnp.int32, (2 * rows, rows), 0)
-        own = (column == position[...]).astype(f32)
+        own = (column == position[...].reshape(1, rows)).astype(f32)
         other = (column == position_other[...] + rows).astype(f32)
         return sigmoid - jnp.concatenate([own, other], axis=1).T
 
@@ -329,11 +331,11 @@
         image_near, weight, image_emb, image_projected, image_inverse, grad, *near = call(
             near_kernel,
             [pair, matrix, pair, pair_f32, ((2 * rows, 1), f32), pair_f32, pair, pair],
-            [pltpu.VMEM(*matrix), pltpu.SemaphoreType.DMA((4,))],
+            [pltpu.VMEM(*matrix), pltpu.VMEM((rows,), jnp.int32), pltpu.SemaphoreType.DMA((5,))],
             flops=4 * 10**9,
         )(
-            scalars, (text_x, image_x, text_w, image_w), text_other, image_other,
-            position[None], position_other[None],
+            scalars, (text_x, image_x, text_w, image_w, position), text_other, image_other,
+            position_other[None],
         )
     with jax.named_scope("swap_neighbours"):
         above, below = after(image_inverse, above, below)

time: 122 us -> 122 us (level)
  no operation moved by 1% of the time
where the time goes in v14:
time: 122 us
  starting transfers between devices  43.7 us (36%)
  blocking collectives  42.6 us (35%)
  Pallas kernels  19.5 us (16%)
  waiting for transfers between devices  13.2 us (11%)
  between operations  2.33 us (2%)
    ppermute x28, starting transfers between devices, send(): return lax.ppermute(block, 'dp', pairs)  43.7 us
    all_to_all x4, blocking collectives, exchange(): lax.all_to_all(parts, 'dp', 0, 0, axis_index_groups=members, tiled=True)  42.6 us
    pallas_call x14, Pallas kernels, run(): pl.pallas_call(body, out_shape=[jax.ShapeDtypeStruct(s, d) for s, d in ou...  19.5 us
    ppermute x28, waiting for transfers between devices, send(): return lax.ppermute(block, 'dp', pairs)  13.2 us
  transfers between devices with their start and end apart: 28, of which 9 were waited for; matrix products, arithmetic and copies ran while one was open for 0% of the time, Pallas kernels for 12%

profile of v14, /device:TPU:1, one launch (start us, length us, event | category | flops | bytes accessed | tf_op | source)
XLA Modules:
  0.0 121.7 jit_solution(13096232583985775881)
XLA Ops:
  0.6 3.3 %collective-permute-start.4 = (bf16[128,1152]{1,0:T(8,128)(2,1)}, bf16[128,1152]{1,0:T(8,128)(2,1)S(1)}, u32[]{:S(2)}, u32[]{:S(2)}) collective-permute-start(bf16[128,1152]{1,0:T(8,128)(2,1)} %image_hbm.1), channel_id=1, source_target_pairs={{0,1},{1,0},{2,3},{3,2},{4,5},{5,4},{6,7},{7,6},{8,9},{9,8},{10,11... | collective-permute-start | bytes 884744 | tf_op jit(solution)/shard_map/band_exchange/ppermute | solution.py:52
  4.0 0.1 collective-permute-start.3
  4.1 0.4 collective-permute-start.5
  4.5 0.0 collective-permute-start.2
  4.5 8.5 %collective-permute-start.1 = (bf16[128,1152]{1,0:T(8,128)(2,1)}, bf16[128,1152]{1,0:T(8,128)(2,1)S(1)}, u32[]{:S(2)}, u32[]{:S(2)}) collective-permute-start(bf16[128,1152]{1,0:T(8,128)(2,1)} %text_hbm.1), channel_id=1, source_target_pairs={{0,254},{1,255},{2,0},{3,1},{4,2},{5,3},{6,4},{7,5},{8,6},{9,7},{1... | collective-permute-start | bytes 884744 | tf_op jit(solution)/shard_map/band_exchange/ppermute | solution.py:52
  14.3 0.0 collective-permute-done.5
  14.3 0.1 collective-permute-start
  14.4 0.0 collective-permute-done.4.image_other
  14.4 0.0 collective-permute-done.3.text_other
  14.4 5.2 %near.1 = (bf16[256,1152]{1,0:T(8,128)(2,1)S(1)}, bf16[1152,1152]{1,0:T(8,128)(2,1)S(1)}, bf16[256,1152]{1,0:T(8,128)(2,1)S(1)}, f32[256,1152]{1,0:T(8,128)S(1)}...) custom-call(f32[1]{0:T(128)S(6)} %copy.27.log_scale, ...), custom_call_target="tpu_custom_call" | custom-call | flops 4000000000 | tf_op jit(solution)/shard_map/near/pallas_call | solution.py:68
  19.6 0.9 collective-permute-done.2.refs_1_
  20.5 1.2 collective-permute-done.1.refs_0_
  21.6 0.9 collective-permute-start.7
  22.5 0.0 collective-permute-start.8
  22.5 3.8 %received.2 = (f32[256,1152]{1,0:T(8,128)S(1)}, f32[1152,1152]{1,0:T(8,128)S(1)}) custom-call(f32[1]{0:T(128)S(6)} %copy.27.log_scale, f32[1]{0:T(128)S(6)} %copy.28.shift, bf16[128,1152]{1,0:T(8,128)(2,1)S(1)} %get-tuple-element.29.below, bf16[128,1152]{1,0:T(8,128)(2,1)S(1)} %get-tuple-element.30.above, bf16[1152,1152]{1,0:T(8,128)(2,1)S(1)} %get-tuple-element.31.text_w, ...), custom_call_target="tpu_custom_call" | custom-call | flops 4000000000 | tf_op jit(solution)/shard_map/received/pallas_call | solution.py:68
  26.3 0.0 collective-permute-done.refs_0_
  26.4 3.7 %collective-permute-start.6 = (bf16[128,1152]{1,0:T(8,128)(2,1)S(1)}, bf16[128,1152]{1,0:T(8,128)(2,1)S(1)}, u32[]{:S(2)}, u32[]{:S(2)}) collective-permute-start(bf16[128,1152]{1,0:T(8,128)(2,1)S(1)} %received.3.far), channel_id=1, source_target_pairs={{0,1},{1,0},{2,3},{3,2},{4,5},{5,4},{6,7},{7,6},{8,9},{9,8},{10,11... | collective-permute-start | bytes 884744 | tf_op jit(solution)/shard_map/received/ppermute | solution.py:52
  30.0 0.0 collective-permute-done.7.below
  30.0 2.1 %partners.1 = (f32[256,1152]{1,0:T(8,128)S(1)}, bf16[256,1152]{1,0:T(8,128)(2,1)S(1)}, bf16[256,1152]{1,0:T(8,128)(2,1)S(1)}) custom-call(f32[1]{0:T(128)S(6)} %copy.27.log_scale, f32[1]{0:T(128)S(6)} %copy.28.shift, bf16[128,1152]{1,0:T(8,128)(2,1)S(1)} %collective-permute-done.7.below, bf16[128,1152]{1,0:T(8,128)(2,1)S(1)} %collective-permute-done.8.above, ...), custom_call_target="tpu_custom_call" | custom-call | flops 4000000000 | tf_op jit(solution)/shard_map/partners/pallas_call | solution.py:68
  32.2 4.3 %far.1 = (bf16[288,1152]{1,0:T(8,128)(2,1)S(1)}, bf16[144,1152]{1,0:T(8,128)(2,1)S(1)}, bf16[144,1152]{1,0:T(8,128)(2,1)S(1)}, bf16[144,1152]{1,0:T(8,128)(2,1)S...) custom-call(f32[1]{0:T(128)S(6)} %copy.27.log_scale, ...), custom_call_target="tpu_custom_call" | custom-call | flops 4000000000 | tf_op jit(solution)/shard_map/far/pallas_call | solution.py:68
  36.5 0.1 collective-permute-start.9
  36.5 2.7 %collective-permute-start.13 = (bf16[144,1152]{1,0:T(8,128)(2,1)S(1)}, bf16[144,1152]{1,0:T(8,128)(2,1)S(1)}, u32[]{:S(2)}, u32[]{:S(2)}) collective-permute-start(bf16[144,1152]{1,0:T(8,128)(2,1)S(1)} %get-tuple-element.49), channel_id=1, source_target_pairs={{0,48},{1,193},{2,50},{3,195},{4,52},{5,197},{6,54},{7,199},{8,56}... | collective-permute-start | bytes 995336 | tf_op jit(solution)/shard_map/sum_first/ppermute | solution.py:52
  39.2 2.7 %collective-permute-start.12 = (bf16[144,1152]{1,0:T(8,128)(2,1)S(1)}, bf16[144,1152]{1,0:T(8,128)(2,1)S(1)}, u32[]{:S(2)}, u32[]{:S(2)}) collective-permute-start(bf16[144,1152]{1,0:T(8,128)(2,1)S(1)} %get-tuple-element.47), channel_id=1, source_target_pairs={{0,48},{1,193},{2,50},{3,195},{4,52},{5,197},{6,54},{7,199},{8,56}... | collective-permute-start | bytes 995336 | tf_op jit(solution)/shard_map/sum_first/ppermute | solution.py:52
  41.9 2.1 %collective-permute-done.9.b = bf16[144,1152]{1,0:T(8,128)(2,1)S(1)} collective-permute-done((bf16[144,1152]{1,0:T(8,128)(2,1)S(1)}, bf16[144,1152]{1,0:T(8,128)(2,1)S(1)}, u32[]{:S(2)}, u32[]{:S(2)}) %collective-permute-start.9) | collective-permute-done | bytes 331808 | tf_op jit(solution)/shard_map/sum_first/ppermute | solution.py:52
  44.0 0.1 sum_first.3
  44.1 0.1 collective-permute-start.10
  44.2 0.1 sum_first.4
  44.3 2.7 %collective-permute-start.14 = (bf16[144,1152]{1,0:T(8,128)(2,1)S(1)}, bf16[144,1152]{1,0:T(8,128)(2,1)S(1)}, u32[]{:S(2)}, u32[]{:S(2)}) collective-permute-start(bf16[144,1152]{1,0:T(8,128)(2,1)S(1)} %sum_first.4), channel_id=1, source_target_pairs={{0,48},{1,193},{2,50},{3,195},{4,52},{5,197},{6,54},{7,199},{8,56}... | collective-permute-start | bytes 995336 | tf_op jit(solution)/shard_map/sum_first/ppermute | solution.py:52
  47.0 0.4 collective-permute-done.11.a_bottom
  47.4 4.2 %collective-permute-done.10.a_top = bf16[144,1152]{1,0:T(8,128)(2,1)S(1)} collective-permute-done((bf16[144,1152]{1,0:T(8,128)(2,1)S(1)}, bf16[144,1152]{1,0:T(8,128)(2,1)S(1)}, u32[]{:S(2)}, u32[]{:S(2)}) %collective-permute-start.10) | collective-permute-done | bytes 331808 | tf_op jit(solution)/shard_map/sum_first/ppermute | solution.py:52
  51.6 0.0 collective-permute-done.14.b_bottom
  51.6 0.3 sum_first.5
  51.9 10.6 %all_to_all.20 = bf16[4,72,1152]{2,1,0:T(8,128)(2,1)S(1)} all-to-all(bf16[4,72,1152]{2,1,0:T(8,128)(2,1)S(1)} %bitcast.19), channel_id=1, replica_groups={{0,64,128,192},{1,17,33,49},{2,66,130,194},{3,19,35,51},{4,68,132,196},..., dimensions={0} | all-to-all | bytes 1327104 | tf_op jit(solution)/shard_map/sum_second/all_to_all | solution.py:56
  62.5 0.1 reduce_sum.24
  62.6 10.9 %all_to_all.21 = bf16[88,8,128]{2,1,0:T(8,128)(2,1)S(1)} all-to-all(bf16[88,8,128]{2,1,0:T(8,128)(2,1)S(1)} %concatenate.3), channel_id=1, replica_groups={{0,2,4,6,8,10,12,14},{1,3,5,7,9,11,13,15},{16,18,20,22,24,26,28,30},{17..., dimensions={0} | all-to-all | bytes 360448 | tf_op jit(solution)/shard_map/sum_lines/all_to_all | solution.py:56
  73.6 10.9 %all_to_all.22 = bf16[88,8,128]{2,1,0:T(8,128)(2,1)S(1)} all-to-all(bf16[88,8,128]{2,1,0:T(8,128)(2,1)S(1)} %bitcast.22), channel_id=1, replica_groups={{0,2,4,6,8,10,12,14},{1,3,5,7,9,11,13,15},{16,18,20,22,24,26,28,30},{17..., dimensions={0} | all-to-all | bytes 360448 | tf_op jit(solution)/shard_map/share_lines/all_to_all | solution.py:56
  84.7 10.1 %all_to_all.23 = bf16[4,72,1152]{2,1,0:T(8,128)(2,1)S(1)} all-to-all(bf16[4,72,1152]{2,1,0:T(8,128)(2,1)S(1)} %tile.20), channel_id=1, replica_groups={{0,64,128,192},{1,17,33,49},{2,66,130,194},{3,19,35,51},{4,68,132,196},..., dimensions={0} | all-to-all | bytes 1327104 | tf_op jit(solution)/shard_map/share_second/all_to_all | solution.py:56
  94.7 6.3 %collective-permute-start.19 = (bf16[288,1152]{1,0:T(8,128)(2,1)S(1)}, bf16[288,1152]{1,0:T(8,128)(2,1)S(1)}, u32[]{:S(2)}, u32[]{:S(2)}) collective-permute-start(bf16[288,1152]{1,0:T(8,128)(2,1)S(1)} %bitcast.17), channel_id=1, source_target_pairs={{0,1},{1,0},{2,3},{3,2},{4,5},{5,4},{6,7},{7,6},{8,9},{9,8},{10,11... | collective-permute-start | bytes 1990664 | tf_op jit(solution)/shard_map/share_first/ppermute | solution.py:52
  101.0 0.1 fusion
  101.1 0.4 collective-permute-start.15
  101.5 2.4 %collective-permute-start.16 = (bf16[144,1152]{1,0:T(8,128)(2,1)S(1)}, bf16[144,1152]{1,0:T(8,128)(2,1)S(1)}, u32[]{:S(2)}, u32[]{:S(2)}) collective-permute-start(bf16[144,1152]{1,0:T(8,128)(2,1)S(1)} %bitcast.25), channel_id=1, source_target_pairs={{0,48},{1,193},{2,50},{3,195},{4,52},{5,197},{6,54},{7,199},{8,56}... | collective-permute-start | bytes 995336 | tf_op jit(solution)/shard_map/share_first/ppermute | solution.py:52
  103.9 0.0 collective-permute-start.18
  103.9 1.4 %collective-permute-start.17 = (bf16[144,1152]{1,0:T(8,128)(2,1)S(1)}, bf16[144,1152]{1,0:T(8,128)(2,1)S(1)}, u32[]{:S(2)}, u32[]{:S(2)}) collective-permute-start(bf16[144,1152]{1,0:T(8,128)(2,1)S(1)} %bitcast.26), channel_id=1, source_target_pairs={{0,16},{1,65},{2,18},{3,67},{4,20},{5,69},{6,22},{7,71},{8,24},{9,... | collective-permute-start | bytes 995336 | tf_op jit(solution)/shard_map/share_first/ppermute | solution.py:52
  105.3 3.3 %collective-permute-done.15.refs_1_ = bf16[144,1152]{1,0:T(8,128)(2,1)S(1)} collective-permute-done((bf16[144,1152]{1,0:T(8,128)(2,1)S(1)}, bf16[144,1152]{1,0:T(8,128)(2,1)S(1)}, u32[]{:S(2)}, u32[]{:S(2)}) %collective-permute-start.15) | collective-permute-done | bytes 331808 | tf_op jit(solution)/shard_map/share_first/ppermute | solution.py:52
  108.7 2.7 %collective-permute-start.21 = (bf16[144,1152]{1,0:T(8,128)(2,1)S(1)}, bf16[144,1152]{1,0:T(8,128)(2,1)S(1)}, u32[]{:S(2)}, u32[]{:S(2)}) collective-permute-start(bf16[144,1152]{1,0:T(8,128)(2,1)S(1)} %collective-permute-done.16.refs_2_), channel_id=1, source_target_pairs={{0,48},{1,193},{2,50},{3,195},{4,52},{5,197},{6,54},{7,199},{8,56}... | collective-permute-start | bytes 995336 | tf_op jit(solution)/shard_map/share_first/ppermute | solution.py:52
  111.3 0.1 collective-permute-done.18.refs_4_
  111.5 1.3 %collective-permute-start.25 = (bf16[144,1152]{1,0:T(8,128)(2,1)S(1)}, bf16[144,1152]{1,0:T(8,128)(2,1)S(1)}, u32[]{:S(2)}, u32[]{:S(2)}) collective-permute-start(bf16[144,1152]{1,0:T(8,128)(2,1)S(1)} %collective-permute-done.18.refs_4_), channel_id=1, source_target_pairs={{0,1},{1,0},{2,3},{3,2},{4,5},{5,4},{6,7},{7,6},{8,9},{9,8},{10,11... | collective-permute-start | bytes 995336 | tf_op jit(solution)/shard_map/share_first/ppermute | solution.py:52
  112.8 0.0 collective-permute-done.17.refs_3_
  112.8 1.7 %collective-permute-start.22 = (bf16[144,1152]{1,0:T(8,128)(2,1)S(1)}, bf16[144,1152]{1,0:T(8,128)(2,1)S(1)}, u32[]{:S(2)}, u32[]{:S(2)}) collective-permute-start(bf16[144,1152]{1,0:T(8,128)(2,1)S(1)} %collective-permute-done.15.refs_1_), channel_id=1, source_target_pairs={{0,1},{1,0},{2,3},{3,2},{4,5},{5,4},{6,7},{7,6},{8,9},{9,8},{10,11... | collective-permute-start | bytes 995336 | tf_op jit(solution)/shard_map/share_first/ppermute | solution.py:52
  114.4 0.0 collective-permute-done.19.refs_5_
  114.4 0.0 collective-permute-start.24
  114.4 1.5 %write.5 = (bf16[1152,1152]{1,0:T(8,128)(2,1)}, bf16[1152,1152]{1,0:T(8,128)(2,1)}) custom-call(bf16[288,1152]{1,0:T(8,128)(2,1)S(1)} %bitcast.18, bf16[144,1152]{1,0:T(8,128)(2,1)S(1)} %collective-permute-done.15.refs_1_, bf16[144,1152]{1,0:T(8,128)(2,1)S(1)} %collective-permute-done.16.refs_2_, bf16[144,1152]{1,0:T(8,128)(2,1)S(1)} %collective-permute-done.17.refs_3_, ...), custom_call_target="tpu_custom_call" | custom-call | tf_op jit(solution)/shard_map/write/pallas_call | solution.py:68
  116.0 0.1 collective-permute-done.20.refs_1_
  116.1 1.9 %collective-permute-start.23 = (bf16[144,1152]{1,0:T(8,128)(2,1)S(1)}, bf16[144,1152]{1,0:T(8,128)(2,1)S(1)}, u32[]{:S(2)}, u32[]{:S(2)}) collective-permute-start(bf16[144,1152]{1,0:T(8,128)(2,1)S(1)} %collective-permute-done.16.refs_2_), channel_id=1, source_target_pairs={{0,1},{1,0},{2,3},{3,2},{4,5},{5,4},{6,7},{7,6},{8,9},{9,8},{10,11... | collective-permute-start | bytes 995336 | tf_op jit(solution)/shard_map/share_first/ppermute | solution.py:52
  118.0 0.1 collective-permute-start.26
  118.1 0.0 collective-permute-done.25.refs_7_
  118.1 0.4 collective-permute-start.27
  118.5 0.0 collective-permute-done.22.refs_4_
  118.5 0.0 collective-permute-done.24.refs_6_
  118.5 0.7 collective-permute-done.23.refs_5_
  119.2 1.3 %write.8 = (bf16[1152,1152]{1,0:T(8,128)(2,1)}, bf16[1152,1152]{1,0:T(8,128)(2,1)}) custom-call(bf16[1152,1152]{1,0:T(8,128)(2,1)} %get-tuple-element.50.refs_0_, bf16[1152,1152]{1,0:T(8,128)(2,1)} %get-tuple-element.51.refs_1_, bf16[144,1152]{1,0:T(8,128)(2,1)S(1)} %write.6.refs_2_, ...), custom_call_target="tpu_custom_call", output_to_operand_aliasing={{0}: (0, {}), {1}: (1, {})} | custom-call | tf_op jit(solution)/shard_map/write/pallas_call | solution.py:68
  120.6 0.0 collective-permute-done.26.refs_2_
  120.6 0.0 collective-permute-done.27.refs_3_
  120.6 0.9 write.9
  (17 shorter events, 0.2 us)
Async XLA Ops:
  0.6 13.8 %collective-permute-start.4 = (bf16[128,1152]{1,0:T(8,128)(2,1)}, bf16[128,1152]{1,0:T(8,128)(2,1)S(1)}, u32[]{:S(2)}, u32[]{:S(2)}) collective-permute-start(bf16[128,1152]{1,0:T(8,128)(2,1)} %image_hbm.1), channel_id=1, source_target_pairs={{0,1},{1,0},{2,3},{3,2},{4,5},{5,4},{6,7},{7,6},{8,9},{9,8},{10,11... | collective-permute-start | bytes 884744 | tf_op jit(solution)/shard_map/band_exchange/ppermute | solution.py:52
  4.0 10.4 %collective-permute-start.3 = (bf16[128,1152]{1,0:T(8,128)(2,1)}, bf16[128,1152]{1,0:T(8,128)(2,1)S(1)}, u32[]{:S(2)}, u32[]{:S(2)}) collective-permute-start(bf16[128,1152]{1,0:T(8,128)(2,1)} %text_hbm.1), channel_id=1, source_target_pairs={{0,1},{1,0},{2,3},{3,2},{4,5},{5,4},{6,7},{7,6},{8,9},{9,8},{10,11... | collective-permute-start | bytes 884744 | tf_op jit(solution)/shard_map/band_exchange/ppermute | solution.py:52
  4.1 10.2 %collective-permute-start.5 = (s32[128]{0:T(128)}, s32[128]{0:T(128)S(1)}, u32[]{:S(2)}, u32[]{:S(2)}) collective-permute-start(s32[128]{0:T(128)} %position_hbm.1), channel_id=1, source_target_pairs={{0,1},{1,0},{2,3},{3,2},{4,5},{5,4},{6,7},{7,6},{8,9},{9,8},{10,11... | collective-permute-start | bytes 1544 | tf_op jit(solution)/shard_map/band_exchange/ppermute | solution.py:52
  4.5 16.0 %collective-permute-start.2 = (bf16[128,1152]{1,0:T(8,128)(2,1)}, bf16[128,1152]{1,0:T(8,128)(2,1)S(1)}, u32[]{:S(2)}, u32[]{:S(2)}) collective-permute-start(bf16[128,1152]{1,0:T(8,128)(2,1)} %text_hbm.1), channel_id=1, source_target_pairs={{0,2},{1,3},{2,4},{3,5},{4,6},{5,7},{6,8},{7,9},{8,10},{9,11},{10,... | collective-permute-start | bytes 884744 | tf_op jit(solution)/shard_map/band_exchange/ppermute | solution.py:52
  4.5 17.2 %collective-permute-start.1 = (bf16[128,1152]{1,0:T(8,128)(2,1)}, bf16[128,1152]{1,0:T(8,128)(2,1)S(1)}, u32[]{:S(2)}, u32[]{:S(2)}) collective-permute-start(bf16[128,1152]{1,0:T(8,128)(2,1)} %text_hbm.1), channel_id=1, source_target_pairs={{0,254},{1,255},{2,0},{3,1},{4,2},{5,3},{6,4},{7,5},{8,6},{9,7},{1... | collective-permute-start | bytes 884744 | tf_op jit(solution)/shard_map/band_exchange/ppermute | solution.py:52
  14.3 12.1 %collective-permute-start = (bf16[128,1152]{1,0:T(8,128)(2,1)}, bf16[128,1152]{1,0:T(8,128)(2,1)S(1)}, u32[]{:S(2)}, u32[]{:S(2)}) collective-permute-start(bf16[128,1152]{1,0:T(8,128)(2,1)} %text_hbm.1), channel_id=1, source_target_pairs={{0,253},{1,4},{2,255},{3,6},{4,1},{5,8},{6,3},{7,10},{8,5},{9,12},... | collective-permute-start | bytes 884744 | tf_op jit(solution)/shard_map/band_exchange/ppermute | solution.py:52
  21.6 8.4 %collective-permute-start.7 = (bf16[128,1152]{1,0:T(8,128)(2,1)S(1)}, bf16[128,1152]{1,0:T(8,128)(2,1)S(1)}, u32[]{:S(2)}, u32[]{:S(2)}) collective-permute-start(bf16[128,1152]{1,0:T(8,128)(2,1)S(1)} %get-tuple-element.29.below), channel_id=1, source_target_pairs={{0,1},{1,0},{2,3},{3,2},{4,5},{5,4},{6,7},{7,6},{8,9},{9,8},{10,11... | collective-permute-start | bytes 884744 | tf_op jit(solution)/shard_map/swap_neighbours/ppermute | solution.py:52
  22.5 7.5 %collective-permute-start.8 = (bf16[128,1152]{1,0:T(8,128)(2,1)S(1)}, bf16[128,1152]{1,0:T(8,128)(2,1)S(1)}, u32[]{:S(2)}, u32[]{:S(2)}) collective-permute-start(bf16[128,1152]{1,0:T(8,128)(2,1)S(1)} %get-tuple-element.30.above), channel_id=1, source_target_pairs={{0,1},{1,0},{2,3},{3,2},{4,5},{5,4},{6,7},{7,6},{8,9},{9,8},{10,11... | collective-permute-start | bytes 884744 | tf_op jit(solution)/shard_map/swap_neighbours/ppermute | solution.py:52
  26.4 5.8 %collective-permute-start.6 = (bf16[128,1152]{1,0:T(8,128)(2,1)S(1)}, bf16[128,1152]{1,0:T(8,128)(2,1)S(1)}, u32[]{:S(2)}, u32[]{:S(2)}) collective-permute-start(bf16[128,1152]{1,0:T(8,128)(2,1)S(1)} %received.3.far), channel_id=1, source_target_pairs={{0,1},{1,0},{2,3},{3,2},{4,5},{5,4},{6,7},{7,6},{8,9},{9,8},{10,11... | collective-permute-start | bytes 884744 | tf_op jit(solution)/shard_map/received/ppermute | solution.py:52
  36.5 7.6 %collective-permute-start.9 = (bf16[144,1152]{1,0:T(8,128)(2,1)S(1)}, bf16[144,1152]{1,0:T(8,128)(2,1)S(1)}, u32[]{:S(2)}, u32[]{:S(2)}) collective-permute-start(bf16[144,1152]{1,0:T(8,128)(2,1)S(1)} %get-tuple-element.45), channel_id=1, source_target_pairs={{0,16},{1,65},{2,18},{3,67},{4,20},{5,69},{6,22},{7,71},{8,24},{9,... | collective-permute-start | bytes 995336 | tf_op jit(solution)/shard_map/sum_first/ppermute | solution.py:52
  36.5 7.6 %collective-permute-start.13 = (bf16[144,1152]{1,0:T(8,128)(2,1)S(1)}, bf16[144,1152]{1,0:T(8,128)(2,1)S(1)}, u32[]{:S(2)}, u32[]{:S(2)}) collective-permute-start(bf16[144,1152]{1,0:T(8,128)(2,1)S(1)} %get-tuple-element.49), channel_id=1, source_target_pairs={{0,48},{1,193},{2,50},{3,195},{4,52},{5,197},{6,54},{7,199},{8,56}... | collective-permute-start | bytes 995336 | tf_op jit(solution)/shard_map/sum_first/ppermute | solution.py:52
  39.2 8.2 %collective-permute-start.11 = (bf16[144,1152]{1,0:T(8,128)(2,1)S(1)}, bf16[144,1152]{1,0:T(8,128)(2,1)S(1)}, u32[]{:S(2)}, u32[]{:S(2)}) collective-permute-start(bf16[144,1152]{1,0:T(8,128)(2,1)S(1)} %get-tuple-element.46), channel_id=1, source_target_pairs={{0,16},{1,65},{2,18},{3,67},{4,20},{5,69},{6,22},{7,71},{8,24},{9,... | collective-permute-start | bytes 995336 | tf_op jit(solution)/shard_map/sum_first/ppermute | solution.py:52
  39.2 8.2 %collective-permute-start.12 = (bf16[144,1152]{1,0:T(8,128)(2,1)S(1)}, bf16[144,1152]{1,0:T(8,128)(2,1)S(1)}, u32[]{:S(2)}, u32[]{:S(2)}) collective-permute-start(bf16[144,1152]{1,0:T(8,128)(2,1)S(1)} %get-tuple-element.47), channel_id=1, source_target_pairs={{0,48},{1,193},{2,50},{3,195},{4,52},{5,197},{6,54},{7,199},{8,56}... | collective-permute-start | bytes 995336 | tf_op jit(solution)/shard_map/sum_first/ppermute | solution.py:52
  44.1 7.6 %collective-permute-start.10 = (bf16[144,1152]{1,0:T(8,128)(2,1)S(1)}, bf16[144,1152]{1,0:T(8,128)(2,1)S(1)}, u32[]{:S(2)}, u32[]{:S(2)}) collective-permute-start(bf16[144,1152]{1,0:T(8,128)(2,1)S(1)} %sum_first.3), channel_id=1, source_target_pairs={{0,16},{1,65},{2,18},{3,67},{4,20},{5,69},{6,22},{7,71},{8,24},{9,... | collective-permute-start | bytes 995336 | tf_op jit(solution)/shard_map/sum_first/ppermute | solution.py:52
  44.3 7.4 %collective-permute-start.14 = (bf16[144,1152]{1,0:T(8,128)(2,1)S(1)}, bf16[144,1152]{1,0:T(8,128)(2,1)S(1)}, u32[]{:S(2)}, u32[]{:S(2)}) collective-permute-start(bf16[144,1152]{1,0:T(8,128)(2,1)S(1)} %sum_first.4), channel_id=1, source_target_pairs={{0,48},{1,193},{2,50},{3,195},{4,52},{5,197},{6,54},{7,199},{8,56}... | collective-permute-start | bytes 995336 | tf_op jit(solution)/shard_map/sum_first/ppermute | solution.py:52
  94.7 19.7 %collective-permute-start.19 = (bf16[288,1152]{1,0:T(8,128)(2,1)S(1)}, bf16[288,1152]{1,0:T(8,128)(2,1)S(1)}, u32[]{:S(2)}, u32[]{:S(2)}) collective-permute-start(bf16[288,1152]{1,0:T(8,128)(2,1)S(1)} %bitcast.17), channel_id=1, source_target_pairs={{0,1},{1,0},{2,3},{3,2},{4,5},{5,4},{6,7},{7,6},{8,9},{9,8},{10,11... | collective-permute-start | bytes 1990664 | tf_op jit(solution)/shard_map/share_first/ppermute | solution.py:52
  101.1 7.6 %collective-permute-start.15 = (bf16[144,1152]{1,0:T(8,128)(2,1)S(1)}, bf16[144,1152]{1,0:T(8,128)(2,1)S(1)}, u32[]{:S(2)}, u32[]{:S(2)}) collective-permute-start(bf16[144,1152]{1,0:T(8,128)(2,1)S(1)} %bitcast.27), channel_id=1, source_target_pairs={{0,16},{1,65},{2,18},{3,67},{4,20},{5,69},{6,22},{7,71},{8,24},{9,... | collective-permute-start | bytes 995336 | tf_op jit(solution)/shard_map/share_first/ppermute | solution.py:52
  101.5 7.2 %collective-permute-start.16 = (bf16[144,1152]{1,0:T(8,128)(2,1)S(1)}, bf16[144,1152]{1,0:T(8,128)(2,1)S(1)}, u32[]{:S(2)}, u32[]{:S(2)}) collective-permute-start(bf16[144,1152]{1,0:T(8,128)(2,1)S(1)} %bitcast.25), channel_id=1, source_target_pairs={{0,48},{1,193},{2,50},{3,195},{4,52},{5,197},{6,54},{7,199},{8,56}... | collective-permute-start | bytes 995336 | tf_op jit(solution)/shard_map/share_first/ppermute | solution.py:52
  103.9 7.6 %collective-permute-start.18 = (bf16[144,1152]{1,0:T(8,128)(2,1)S(1)}, bf16[144,1152]{1,0:T(8,128)(2,1)S(1)}, u32[]{:S(2)}, u32[]{:S(2)}) collective-permute-start(bf16[144,1152]{1,0:T(8,128)(2,1)S(1)} %bitcast.28), channel_id=1, source_target_pairs={{0,48},{1,193},{2,50},{3,195},{4,52},{5,197},{6,54},{7,199},{8,56}... | collective-permute-start | bytes 995336 | tf_op jit(solution)/shard_map/share_first/ppermute | solution.py:52
  103.9 8.9 %collective-permute-start.17 = (bf16[144,1152]{1,0:T(8,128)(2,1)S(1)}, bf16[144,1152]{1,0:T(8,128)(2,1)S(1)}, u32[]{:S(2)}, u32[]{:S(2)}) collective-permute-start(bf16[144,1152]{1,0:T(8,128)(2,1)S(1)} %bitcast.26), channel_id=1, source_target_pairs={{0,16},{1,65},{2,18},{3,67},{4,20},{5,69},{6,22},{7,71},{8,24},{9,... | collective-permute-start | bytes 995336 | tf_op jit(solution)/shard_map/share_first/ppermute | solution.py:52
  108.6 7.5 %collective-permute-start.20 = (bf16[144,1152]{1,0:T(8,128)(2,1)S(1)}, bf16[144,1152]{1,0:T(8,128)(2,1)S(1)}, u32[]{:S(2)}, u32[]{:S(2)}) collective-permute-start(bf16[144,1152]{1,0:T(8,128)(2,1)S(1)} %collective-permute-done.15.refs_1_), channel_id=1, source_target_pairs={{0,16},{1,65},{2,18},{3,67},{4,20},{5,69},{6,22},{7,71},{8,24},{9,... | collective-permute-start | bytes 995336 | tf_op jit(solution)/shard_map/share_first/ppermute | solution.py:52
  108.7 9.3 %collective-permute-start.21 = (bf16[144,1152]{1,0:T(8,128)(2,1)S(1)}, bf16[144,1152]{1,0:T(8,128)(2,1)S(1)}, u32[]{:S(2)}, u32[]{:S(2)}) collective-permute-start(bf16[144,1152]{1,0:T(8,128)(2,1)S(1)} %collective-permute-done.16.refs_2_), channel_id=1, source_target_pairs={{0,48},{1,193},{2,50},{3,195},{4,52},{5,197},{6,54},{7,199},{8,56}... | collective-permute-start | bytes 995336 | tf_op jit(solution)/shard_map/share_first/ppermute | solution.py:52
  111.5 6.6 %collective-permute-start.25 = (bf16[144,1152]{1,0:T(8,128)(2,1)S(1)}, bf16[144,1152]{1,0:T(8,128)(2,1)S(1)}, u32[]{:S(2)}, u32[]{:S(2)}) collective-permute-start(bf16[144,1152]{1,0:T(8,128)(2,1)S(1)} %collective-permute-done.18.refs_4_), channel_id=1, source_target_pairs={{0,1},{1,0},{2,3},{3,2},{4,5},{5,4},{6,7},{7,6},{8,9},{9,8},{10,11... | collective-permute-start | bytes 995336 | tf_op jit(solution)/shard_map/share_first/ppermute | solution.py:52
  112.8 5.8 %collective-permute-start.22 = (bf16[144,1152]{1,0:T(8,128)(2,1)S(1)}, bf16[144,1152]{1,0:T(8,128)(2,1)S(1)}, u32[]{:S(2)}, u32[]{:S(2)}) collective-permute-start(bf16[144,1152]{1,0:T(8,128)(2,1)S(1)} %collective-permute-done.15.refs_1_), channel_id=1, source_target_pairs={{0,1},{1,0},{2,3},{3,2},{4,5},{5,4},{6,7},{7,6},{8,9},{9,8},{10,11... | collective-permute-start | bytes 995336 | tf_op jit(solution)/shard_map/share_first/ppermute | solution.py:52
  114.4 4.1 %collective-permute-start.24 = (bf16[144,1152]{1,0:T(8,128)(2,1)S(1)}, bf16[144,1152]{1,0:T(8,128)(2,1)S(1)}, u32[]{:S(2)}, u32[]{:S(2)}) collective-permute-start(bf16[144,1152]{1,0:T(8,128)(2,1)S(1)} %collective-permute-done.17.refs_3_), channel_id=1, source_target_pairs={{0,1},{1,0},{2,3},{3,2},{4,5},{5,4},{6,7},{7,6},{8,9},{9,8},{10,11... | collective-permute-start | bytes 995336 | tf_op jit(solution)/shard_map/share_first/ppermute | solution.py:52
  116.1 3.1 %collective-permute-start.23 = (bf16[144,1152]{1,0:T(8,128)(2,1)S(1)}, bf16[144,1152]{1,0:T(8,128)(2,1)S(1)}, u32[]{:S(2)}, u32[]{:S(2)}) collective-permute-start(bf16[144,1152]{1,0:T(8,128)(2,1)S(1)} %collective-permute-done.16.refs_2_), channel_id=1, source_target_pairs={{0,1},{1,0},{2,3},{3,2},{4,5},{5,4},{6,7},{7,6},{8,9},{9,8},{10,11... | collective-permute-start | bytes 995336 | tf_op jit(solution)/shard_map/share_first/ppermute | solution.py:52
  118.0 2.6 %collective-permute-start.26 = (bf16[144,1152]{1,0:T(8,128)(2,1)S(1)}, bf16[144,1152]{1,0:T(8,128)(2,1)S(1)}, u32[]{:S(2)}, u32[]{:S(2)}) collective-permute-start(bf16[144,1152]{1,0:T(8,128)(2,1)S(1)} %write.6.refs_2_), channel_id=1, source_target_pairs={{0,1},{1,0},{2,3},{3,2},{4,5},{5,4},{6,7},{7,6},{8,9},{9,8},{10,11... | collective-permute-start | bytes 995336 | tf_op jit(solution)/shard_map/write/ppermute | solution.py:52
  118.1 2.5 %collective-permute-start.27 = (bf16[144,1152]{1,0:T(8,128)(2,1)S(1)}, bf16[144,1152]{1,0:T(8,128)(2,1)S(1)}, u32[]{:S(2)}, u32[]{:S(2)}) collective-permute-start(bf16[144,1152]{1,0:T(8,128)(2,1)S(1)} %write.7.refs_3_), channel_id=1, source_target_pairs={{0,1},{1,0},{2,3},{3,2},{4,5},{5,4},{6,7},{7,6},{8,9},{9,8},{10,11... | collective-permute-start | bytes 995336 | tf_op jit(solution)/shard_map/write/ppermute | solution.py:52
